TPU v7x, 32 devices: a whole 2x2x4 slice. The times are simulated.
32 devices in a mesh: dp: 4 (over y, x), row: 2 (over core), col: 4 (over z).
Axes of the slice: x: 2, y: 2, z: 4, core: 2. Of those that a mesh axis runs over, the one named last changes fastest.
Arguments:
- tokens: bfloat16 [16384, 1536], P(('dp', 'row', 'col')), may hold values from -6 to 6
- norm_gain: bfloat16 [1536], replicated, may hold values from 0.5 to 1.5
- w_gate: bfloat16 [1536, 3072], P('row', 'col'), may hold values from -0.15625 to 0.15625
- w_value: bfloat16 [1536, 3072], P('row', 'col'), may hold values from -0.15625 to 0.15625
- w_state: bfloat16 [1536, 256], P('row', 'col'), may hold values from -0.15625 to 0.15625
- w_step: bfloat16 [1536, 48], P('row', 'col'), may hold values from -0.15625 to 0.15625
- conv_value: bfloat16 [3072, 4], P('col'), may hold values from -3 to 3
- bias_value: bfloat16 [3072], P('col'), may hold values from -3 to 3
- conv_state: bfloat16 [256, 4], P('col'), may hold values from -3 to 3
- bias_state: bfloat16 [256], P('col'), may hold values from -3 to 3
- a_log: bfloat16 [48], P('col'), may hold values from -4 to 2.765625
- d_skip: bfloat16 [48], P('col'), may hold values from 0.5 to 1.5
- dt_bias: bfloat16 [48], P('col'), may hold values from -5 to -1
- mix_gain: bfloat16 [3072], P('col'), may hold values from 0.5 to 1.5
- w_out: bfloat16 [3072, 1536], P('col', 'row'), may hold values from -0.109375 to 0.109375
- cotangent: bfloat16 [16384, 1536], P(('dp', 'row', 'col')), may hold values from -6 to 6
Outputs:
- block_out: bfloat16 [16384, 1536], P(('dp', 'row', 'col'))
- tokens_grad: float32 [16384, 1536], P(('dp', 'row', 'col'))
- grad_norm_gain: float32 [1536], replicated
- grad_w_gate: float32 [1536, 3072], P('row', 'col')
- grad_w_value: float32 [1536, 3072], P('row', 'col')
- grad_w_state: float32 [1536, 256], P('row', 'col')
- grad_w_step: float32 [1536, 48], P('row', 'col')
- grad_conv_value: float32 [3072, 4], P('col')
- grad_bias_value: float32 [3072], P('col')
- grad_conv_state: float32 [256, 4], P('col')
- grad_bias_state: float32 [256], P('col')
- grad_a_log: float32 [48], P('col')
- grad_d_skip: float32 [48], P('col')
- grad_dt_bias: float32 [48], P('col')
- grad_mix_gain: float32 [3072], P('col')
- grad_w_out: float32 [3072, 1536], P('col', 'row')
All inputs are finite; a program needn't handle non-finite values.
Results may differ from a plain program's by a relative error of at most 0.003.
The roundings to bfloat16 on the way count: a program that leaves them out, or rounds other values in their place, can miss the bound.
Values may be sent and summed in bfloat16 or wider, within the bound.
A program may use at most 256 MiB of HBM per device.

v0:
```python
from functools import partial

import jax
import jax.numpy as jnp
from jax import lax
from jax.sharding import PartitionSpec as P

N = 128
Q = 256
SEQ_LEN = 2048
DI = 3072


EPSILON = 1e-05
HIGHEST = lax.Precision.HIGHEST
precise = partial(jnp.einsum, precision=HIGHEST)


def causal_mask(block_size):
    return lax.broadcasted_iota(jnp.int32, (block_size, block_size), 0) >= lax.broadcasted_iota(
        jnp.int32, (block_size, block_size), 1
    )


def silu_slope(values):
    sigmoid_values = jax.nn.sigmoid(values)
    return sigmoid_values * (1.0 + values * (1.0 - sigmoid_values))


def causal_conv(inputs, kernel, offsets):
    tap_count = kernel.shape[1]
    length = inputs.shape[1]
    padded = jnp.pad(inputs, ((0, 0), (tap_count - 1, 0), (0, 0)))
    running = jnp.zeros_like(inputs) + offsets
    for offset in range(tap_count):
        running = running + kernel[:, offset] * padded[:, offset : offset + length]
    return running


def conv_backward(grad_pre, inputs, kernel):
    tap_count = kernel.shape[1]
    length = inputs.shape[1]
    padded = jnp.pad(inputs, ((0, 0), (tap_count - 1, 0), (0, 0)))
    grad_padded = jnp.pad(grad_pre, ((0, 0), (0, tap_count - 1), (0, 0)))
    grad_kernel = jnp.stack(
        [
            jnp.sum(grad_pre * padded[:, offset : offset + length], axis=(0, 1))
            for offset in range(tap_count)
        ],
        axis=1,
    )
    grad_offsets = jnp.sum(grad_pre, axis=(0, 1))
    grad_inputs = jnp.zeros_like(inputs)
    for offset in range(tap_count):
        first_at = tap_count - 1 - offset
        grad_inputs = grad_inputs + kernel[:, offset] * grad_padded[:, first_at : first_at + length]
    return (grad_inputs, grad_kernel, grad_offsets)


def ssd_pieces(head_values, step_sizes, decay_rate, b_matrix, c_matrix, block_size):
    length, head_count, head_size = head_values.shape
    blocks = length // block_size
    x_blocks = head_values.reshape(blocks, block_size, head_count, head_size)
    step_blocks = step_sizes.reshape(blocks, block_size, head_count)
    b_blocks = b_matrix.reshape(blocks, block_size, -1)
    c_blocks = c_matrix.reshape(blocks, block_size, -1)
    cumulative = jnp.cumsum(step_blocks * decay_rate, axis=1)
    cum_heads = jnp.transpose(cumulative, (0, 2, 1))
    step_heads = jnp.transpose(step_blocks, (0, 2, 1))
    causal = causal_mask(block_size)
    affinity = jnp.einsum(
        "cin,cjn->cij",
        c_blocks.astype(jnp.bfloat16),
        b_blocks.astype(jnp.bfloat16),
        preferred_element_type=jnp.float32,
    )
    spread = cum_heads[:, :, :, None] - cum_heads[:, :, None, :]
    weights_decay = jnp.where(causal, jnp.exp(jnp.where(causal, spread, 0.0)), 0.0)
    mixing = affinity[:, None] * weights_decay * step_heads[:, :, None, :]
    tail_decay = jnp.exp(cumulative[:, -1:, :] - cumulative)
    tail_weight = tail_decay * step_blocks
    fresh_state = precise("cjn,cjh,cjhp->chnp", b_blocks, tail_weight, x_blocks)
    block_fall = jnp.exp(cumulative[:, -1, :])

    def advance(carried, scan_item):
        fall_rate, added_state = scan_item
        return (fall_rate[:, None, None] * carried + added_state, carried)

    _, before = lax.scan(
        advance, jnp.zeros(fresh_state.shape[1:], jnp.float32), (block_fall, fresh_state)
    )
    reached = precise("cin,chnp->cihp", c_blocks, before)
    growth = jnp.exp(cumulative)
    output = precise("chij,cjhp->cihp", mixing, x_blocks) + reached * growth[..., None]
    stored = (
        x_blocks,
        step_blocks,
        b_blocks,
        c_blocks,
        affinity,
        weights_decay,
        mixing,
        tail_decay,
        tail_weight,
        block_fall,
        before,
        reached,
        growth,
    )
    return (output.reshape(length, head_count, head_size), stored)


def ssd_backward(grad_output, head_values, step_sizes, decay_rate, b_matrix, c_matrix, block_size):
    length, head_count, head_size = head_values.shape
    _, stored = ssd_pieces(head_values, step_sizes, decay_rate, b_matrix, c_matrix, block_size)
    (
        x_blocks,
        step_blocks,
        b_blocks,
        c_blocks,
        affinity,
        weights_decay,
        mixing,
        tail_decay,
        tail_weight,
        block_fall,
        before,
        reached,
        growth,
    ) = stored
    grad_blocks = grad_output.reshape(x_blocks.shape)
    grad_grown = grad_blocks * growth[..., None]
    grad_before = precise("cin,cihp->chnp", c_blocks, grad_grown)
    grad_c = precise("cihp,chnp->cin", grad_grown, before)
    grad_cum = jnp.sum(grad_blocks * reached, axis=-1) * growth

    def retreat(later_grad, scan_item):
        fall_rate, direct, prior_state = scan_item
        grad_fall = jnp.sum(later_grad * prior_state, axis=(1, 2))
        return (direct + fall_rate[:, None, None] * later_grad, (later_grad, grad_fall))

    _, (grad_fresh, grad_fall_all) = lax.scan(
        retreat,
        jnp.zeros(before.shape[1:], jnp.float32),
        (block_fall, grad_before, before),
        reverse=True,
    )
    last_add = grad_fall_all * block_fall
    grad_b = precise("chnp,cjh,cjhp->cjn", grad_fresh, tail_weight, x_blocks)
    grad_x = precise("chnp,cjn,cjh->cjhp", grad_fresh, b_blocks, tail_weight)
    grad_tail = precise("chnp,cjn,cjhp->cjh", grad_fresh, b_blocks, x_blocks)
    grad_step = grad_tail * tail_decay
    grad_span = grad_tail * tail_weight
    grad_cum = grad_cum - grad_span
    last_add = last_add + jnp.sum(grad_span, axis=1)
    grad_mixing = precise("cihp,cjhp->chij", grad_blocks, x_blocks)
    grad_x = grad_x + precise("chij,cihp->cjhp", mixing, grad_blocks)
    weighted = grad_mixing * weights_decay
    step_heads = jnp.transpose(step_blocks, (0, 2, 1))
    grad_affinity = jnp.sum(weighted * step_heads[:, :, None, :], axis=1)
    grad_step = grad_step + jnp.transpose(jnp.sum(weighted * affinity[:, None], axis=2), (0, 2, 1))
    grad_spread = grad_mixing * mixing
    grad_cum = grad_cum + jnp.transpose(
        jnp.sum(grad_spread, axis=3) - jnp.sum(grad_spread, axis=2), (0, 2, 1)
    )
    grad_cum = grad_cum + jnp.pad(last_add[:, None, :], ((0, 0), (block_size - 1, 0), (0, 0)))
    grad_c = grad_c + precise("cij,cjn->cin", grad_affinity, b_blocks)
    grad_b = grad_b + precise("cij,cin->cjn", grad_affinity, c_blocks)
    grad_rate = lax.cumsum(grad_cum, axis=1, reverse=True)
    grad_step = grad_step + grad_rate * decay_rate
    grad_decay = jnp.sum(grad_rate * step_blocks, axis=(0, 1))
    return (
        grad_x.reshape(length, head_count, head_size),
        grad_step.reshape(length, head_count),
        grad_decay,
        grad_b.reshape(length, -1),
        grad_c.reshape(length, -1),
    )


def stacked(values, copies):
    return jnp.broadcast_to(values[None], (copies,) + values.shape)


def per_device(
    tokens,
    norm_gain,
    w_gate,
    w_value,
    w_state,
    w_step,
    conv_value,
    bias_value,
    conv_state,
    bias_state,
    a_log,
    d_skip,
    dt_bias,
    mix_gain,
    w_out,
    cotangent,
):
    tok_local = tokens.shape[0]
    model_width = tokens.shape[1]
    row_count_axis = lax.axis_size("row")
    rows_float = tokens.astype(jnp.float32)
    norm_scale = norm_gain.astype(jnp.float32)
    inv_rms = lax.rsqrt(jnp.mean(rows_float * rows_float, axis=-1, keepdims=True) + EPSILON)
    unit_rows = rows_float * inv_rms
    normed = (unit_rows * norm_scale).astype(jnp.bfloat16)
    gate_full, value_full, state_full, step_full, out_full = (
        lax.all_gather(w_gate, "row", axis=0, tiled=True),
        lax.all_gather(w_value, "row", axis=0, tiled=True),
        lax.all_gather(w_state, "row", axis=0, tiled=True),
        lax.all_gather(w_step, "row", axis=0, tiled=True),
        lax.all_gather(w_out, "row", axis=1, tiled=True),
    )
    group_rows = lax.all_gather(normed, "col", axis=0, tiled=True)
    group_len = group_rows.shape[0]
    seq_count = group_len // SEQ_LEN
    gate_raw = jnp.dot(group_rows, gate_full, preferred_element_type=jnp.float32)
    value_raw = jnp.dot(group_rows, value_full, preferred_element_type=jnp.float32)
    step_raw = jnp.dot(group_rows, step_full, preferred_element_type=jnp.float32)
    value_kernel = conv_value.astype(jnp.float32)
    value_in = value_raw.reshape(seq_count, SEQ_LEN, -1)
    value_pre = causal_conv(value_in, value_kernel, bias_value.astype(jnp.float32))
    value_act = jax.nn.silu(value_pre).astype(jnp.bfloat16)
    state_kernel = conv_state.astype(jnp.float32)
    state_raw = jnp.dot(group_rows, state_full, preferred_element_type=jnp.float32)
    state_in = state_raw.reshape(seq_count, SEQ_LEN, -1)
    state_pre = causal_conv(state_in, state_kernel, bias_state.astype(jnp.float32))
    state_own = jax.nn.silu(state_pre).astype(jnp.bfloat16).reshape(group_len, -1)
    state_act = lax.all_gather(state_own, "col", axis=1, tiled=True)
    step_input = step_raw + dt_bias.astype(jnp.float32)
    step_value = jax.nn.softplus(step_input)
    decay_rate = -jnp.exp(a_log.astype(jnp.float32))
    head_local = a_log.shape[0]
    head_size = value_act.shape[-1] // head_local
    value_heads = value_act.astype(jnp.float32).reshape(seq_count, SEQ_LEN, head_local, head_size)
    state_seq = state_act.astype(jnp.float32).reshape(seq_count, SEQ_LEN, 2 * N)
    step_seq = step_value.reshape(seq_count, SEQ_LEN, head_local)

    def forward_one(scan_item):
        heads_in, steps_in, states_in = scan_item
        output, _ = ssd_pieces(
            heads_in, steps_in, decay_rate, states_in[:, :N], states_in[:, N:], Q
        )
        return output

    scanned = lax.map(forward_one, (value_heads, step_seq, state_seq))
    skip_gain = d_skip.astype(jnp.float32)
    y_flat = (scanned + skip_gain[:, None] * value_heads).reshape(group_len, -1)
    gate_act = jax.nn.silu(gate_raw)
    gated = y_flat * gate_act
    square_sum = lax.psum(jnp.sum(gated * gated, axis=-1), "col")
    inv_gate = lax.rsqrt(square_sum / DI + EPSILON)[:, None]
    mix_scale = mix_gain.astype(jnp.float32)
    unit_gate = gated * inv_gate
    mix_rows = (unit_gate * mix_scale).astype(jnp.bfloat16)
    branch_out = lax.psum_scatter(
        jnp.dot(mix_rows, out_full, preferred_element_type=jnp.float32),
        "col",
        scatter_dimension=0,
        tiled=True,
    )
    block_out = (rows_float + branch_out).astype(jnp.bfloat16)
    cot_rows = lax.all_gather(cotangent, "col", axis=0, tiled=True)
    grad_mix = jnp.einsum("td,cd->tc", cot_rows, out_full, preferred_element_type=jnp.float32)
    grad_out = jnp.einsum("tc,td->cd", mix_rows, cot_rows, preferred_element_type=jnp.float32)
    grad_mix_gain = jnp.sum(grad_mix * unit_gate, axis=0)
    grad_unit = grad_mix * mix_scale
    inner_sum = lax.psum(jnp.sum(grad_unit * gated, axis=-1), "col")
    grad_gated = inv_gate * grad_unit - gated * inv_gate**3 * (inner_sum / DI)[:, None]
    grad_y = grad_gated * gate_act
    grad_gate_raw = (grad_gated * y_flat * silu_slope(gate_raw)).astype(jnp.bfloat16)
    grad_heads = grad_y.reshape(seq_count, SEQ_LEN, head_local, head_size)
    grad_skip = jnp.sum(grad_heads * value_heads, axis=(0, 1, 3))

    def backward_one(scan_item):
        grad_in, heads_in, steps_in, states_in = scan_item
        return ssd_backward(
            grad_in, heads_in, steps_in, decay_rate, states_in[:, :N], states_in[:, N:], Q
        )

    grad_scan, grad_steps, grad_decays, grad_bmat, grad_cmat = lax.map(
        backward_one, (grad_heads, value_heads, step_seq, state_seq)
    )
    grad_value_act = grad_scan + skip_gain[:, None] * grad_heads
    grad_a_log = jnp.sum(grad_decays, axis=0) * decay_rate
    grad_step_pre = grad_steps.reshape(group_len, -1) * jax.nn.sigmoid(step_input)
    grad_dt_bias = jnp.sum(grad_step_pre, axis=0)
    grad_step_raw = grad_step_pre.astype(jnp.bfloat16)
    grad_state_all = jnp.concatenate([grad_bmat, grad_cmat], axis=-1).reshape(group_len, 2 * N)
    grad_state_own = lax.psum_scatter(grad_state_all, "col", scatter_dimension=1, tiled=True)
    grad_state_pre = grad_state_own.reshape(seq_count, SEQ_LEN, -1) * silu_slope(state_pre)
    grad_state_in, grad_conv_state, grad_bias_state = conv_backward(
        grad_state_pre, state_in, state_kernel
    )
    grad_state_raw = grad_state_in.reshape(group_len, -1).astype(jnp.bfloat16)
    grad_value_pre = grad_value_act.reshape(seq_count, SEQ_LEN, -1) * silu_slope(value_pre)
    grad_value_in, grad_conv_value, grad_bias_value = conv_backward(
        grad_value_pre, value_in, value_kernel
    )
    grad_value_raw = grad_value_in.reshape(group_len, -1).astype(jnp.bfloat16)
    projections = (
        (grad_gate_raw, gate_full),
        (grad_value_raw, value_full),
        (grad_state_raw, state_full),
        (grad_step_raw, step_full),
    )
    running = jnp.zeros((tok_local * lax.axis_size("col"), model_width), jnp.float32)
    for input_grad_part, input_weights in projections:
        running = running + jnp.einsum(
            "tc,dc->td", input_grad_part, input_weights, preferred_element_type=jnp.float32
        )
    grad_normed = lax.psum_scatter(running, "col", scatter_dimension=0, tiled=True)
    weight_grads = [
        jnp.einsum("td,tc->dc", group_rows, grad_part, preferred_element_type=jnp.float32)
        for grad_part, weights in projections
    ]
    grad_unit_rows = grad_normed * norm_scale
    tokens_grad = cotangent.astype(jnp.float32) + inv_rms * (
        grad_unit_rows - unit_rows * jnp.mean(grad_unit_rows * unit_rows, axis=-1, keepdims=True)
    )
    norm_part = jnp.sum(grad_normed * unit_rows, axis=0)
    reduced_rows = (
        lax.psum_scatter(weight_grads[0], "row", scatter_dimension=0, tiled=True),
        lax.psum_scatter(weight_grads[1], "row", scatter_dimension=0, tiled=True),
        lax.psum_scatter(weight_grads[2], "row", scatter_dimension=0, tiled=True),
        lax.psum_scatter(weight_grads[3], "row", scatter_dimension=0, tiled=True),
        lax.psum_scatter(grad_out, "row", scatter_dimension=1, tiled=True),
        lax.psum_scatter(
            stacked(grad_mix_gain, row_count_axis), "row", scatter_dimension=0, tiled=True
        ),
        lax.psum_scatter(
            stacked(grad_conv_value, row_count_axis), "row", scatter_dimension=0, tiled=True
        ),
        lax.psum_scatter(
            stacked(grad_bias_value, row_count_axis), "row", scatter_dimension=0, tiled=True
        ),
        lax.psum_scatter(
            stacked(grad_conv_state, row_count_axis), "row", scatter_dimension=0, tiled=True
        ),
        lax.psum_scatter(
            stacked(grad_bias_state, row_count_axis), "row", scatter_dimension=0, tiled=True
        ),
        lax.psum_scatter(
            stacked(grad_a_log, row_count_axis), "row", scatter_dimension=0, tiled=True
        ),
        lax.psum_scatter(
            stacked(grad_skip, row_count_axis), "row", scatter_dimension=0, tiled=True
        ),
        lax.psum_scatter(
            stacked(grad_dt_bias, row_count_axis), "row", scatter_dimension=0, tiled=True
        ),
    )
    (
        sum_gate,
        sum_value,
        sum_state,
        sum_step,
        sum_out,
        sum_mix,
        sum_conv_value,
        sum_bias_value,
        sum_conv_state,
        sum_bias_state,
        sum_a_log,
        sum_skip,
        sum_dt_bias,
    ) = lax.psum(
        (
            reduced_rows[0],
            reduced_rows[1],
            reduced_rows[2],
            reduced_rows[3],
            reduced_rows[4],
            reduced_rows[5][0],
            reduced_rows[6][0],
            reduced_rows[7][0],
            reduced_rows[8][0],
            reduced_rows[9][0],
            reduced_rows[10][0],
            reduced_rows[11][0],
            reduced_rows[12][0],
        ),
        "dp",
    )
    norm_total = lax.psum(norm_part, ("dp", "row", "col"))
    return (
        block_out,
        tokens_grad,
        norm_total,
        sum_gate,
        sum_value,
        sum_state,
        sum_step,
        sum_conv_value,
        sum_bias_value,
        sum_conv_state,
        sum_bias_state,
        sum_a_log,
        sum_skip,
        sum_dt_bias,
        sum_mix,
        sum_out,
    )


def solution(mesh):
    return jax.shard_map(
        per_device,
        mesh=mesh,
        in_specs=(
            P(("dp", "row", "col"), None),
            P(),
            P("row", "col"),
            P("row", "col"),
            P("row", "col"),
            P("row", "col"),
            P("col", None),
            P("col"),
            P("col", None),
            P("col"),
            P("col"),
            P("col"),
            P("col"),
            P("col"),
            P("col", "row"),
            P(("dp", "row", "col"), None),
        ),
        out_specs=(
            P(("dp", "row", "col"), None),
            P(("dp", "row", "col"), None),
            P(),
            P("row", "col"),
            P("row", "col"),
            P("row", "col"),
            P("row", "col"),
            P("col", None),
            P("col"),
            P("col", None),
            P("col"),
            P("col"),
            P("col"),
            P("col"),
            P("col"),
            P("col", "row"),
        ),
        check_vma=False,
    )
```

profile of v0, /device:TPU:0, one launch (start us, length us, event | category | flops | bytes accessed | tf_op | source)
XLA Modules:
  0.0 1298.7 jit_solution(16055600817272455886)
XLA Ops:
  16.4 115.2 %all-gather.8.cloned.1.call-done = bf16[2048,1536]{1,0:T(8,128)(2,1)} async-done(((bf16[512,1536]{1,0:T(8,128)(2,1)}), bf16[2048,1536]{1,0:T(8,128)(2,1)}) %all-gather.8.cloned.1.call-update) | async-done | bytes 6291472 | tf_op jit(solution)/shard_map/all_gather | solution.py:218
  131.6 4.8 fusion.111
  143.3 5.2 compare_select_fusion
  148.7 4.7 reduce-window.14
  154.9 7.8 fusion.110
  162.8 6.2 multiply_convert_fusion.2
  169.0 4.8 copy.225
  181.5 7.4 fusion.67
  192.4 19.6 %while.59 = (s32[]{:T(128)}, f32[12,128,64]{2,1,0:T(8,128)S(1)}, f32[8,12,128,64]{3,2,1,0:T(8,128)}, f32[8,12]{1,0:T(8,128)S(1)}, f32[8,12,128,64]{2,3,1,0:T(8,128)}, /*index=5*/s32[]{:T(128)}, s32[]{:T(128)}) while((s32[]{:T(128)}, f32[12,128,64]{2,1,0:T(8,128)S(1)}, f32[8,12,128,64]{3,2,1,0:T(8,128)}, f32[8,12]{1,0:T(8,128)S(1)}, ...), condition=%wide.region_4.5_spmd.clone, body=%wide.region_3.4_spmd.clone.sunk | while | flops 393219 | bytes 3932912 | solution.py:89
  212.0 4.9 copy.246
  231.8 20.5 %bitcast_add_fusion.3 = f32[8,256,12,64]{1,3,2,0:T(8,128)S(1)} fusion(f32[8,256,12,64]{1,3,2,0:T(8,128)S(1)} %bitcast.272, f32[8,256,12]{1,2,0:T(8,128)S(1)} %get-tuple-element.449, f32[8,12,256]{2,1,0:T(8,128)S(1)} %copy-done.41, f32[8,12,256]{2,1,0:T(8,128)S(1)} %copy-done.37, f32[8,256,256]{2,1,0:T(8,128)S(1)} %fusion.112, ...), kind=kOutput, calls=%fused_computation.41 | convolution fusion | flops 4866441216 | bytes 18186240 | tf_op jit(solution)/shard_map/while/body/eval_jaxpr/chij,cjhp->cihp/dot_general | solution.py:94
  256.7 5.8 copy.307
  262.5 6.7 copy.248
  269.2 13.1 %multiply_reduce_fusion.10 = (f32[2048]{0:T(1024)}, f32[2048,768]{1,0:T(8,128)}, f32[2048,768]{1,0:T(8,128)}) fusion(f32[2048,768]{1,0:T(8,128)} %copy.248, bf16[1,2048,768]{2,1,0:T(8,128)(2,1)S(1)} %copy-done.3, f32[768]{0:T(1024)S(1)} %mul.580, bf16[2048,1536]{1,0:T(8,128)(2,1)} %all-gather.8.cloned.1.call-done, ...), kind=kOutput, calls=%fused_computation.57 | convolution fusion | flops 4847564800 | bytes 30682112 | tf_op jit(solution)/shard_map/dot_general | solution.py:221
  282.3 11.7 psum.112
  294.6 23.1 %all-gather.16.cloned.1.call-done = bf16[2048,1536]{1,0:T(8,128)(2,1)} async-done(((bf16[512,1536]{1,0:T(8,128)(2,1)}), bf16[2048,1536]{1,0:T(8,128)(2,1)}) %all-gather.16.cloned.1.call-update) | async-done | bytes 6291472 | tf_op jit(solution)/shard_map/all_gather | solution.py:267
  317.7 12.6 multiply_reduce_fusion.3
  330.3 9.0 psum.113
  339.3 15.1 %fusion.22 = (f32[768]{0:T(1024)}, f32[2048,768]{1,0:T(8,128)}, bf16[2048,768]{1,0:T(8,128)(2,1)}) fusion(bf16[1,2048,768]{2,1,0:T(8,128)(2,1)S(1)} %copy-done.3, f32[2048,768]{1,0:T(8,128)} %get-tuple-element.459, f32[2048]{0:T(1024)S(1)} %broadcast_multiply_fusion, f32[2048,768]{1,0:T(8,128)} %get-tuple-element.431, f32[2048]{0:T(1024)} %get-tuple-element.451, ...), kind=kLoop, calls=%fused_computation.38 | loop fusion | flops 34602240 | bytes 37782528 | tf_op jit(solution)/shard_map/reduce_sum | solution.py:277
  354.3 6.6 copy.249
  361.0 6.1 copy.308
  367.1 30.2 %fusion.7 = (f32[8,12,256]{2,1,0:T(8,128)}, f32[8,12,256]{2,1,0:T(8,128)}, f32[8,12,256]{2,1,0:T(8,128)}, f32[8,256,256]{2,1,0:T(8,128)}) fusion(f32[8,12,256]{2,1,0:T(8,128)S(1)} %copy-done.42, f32[8,12,256]{2,1,0:T(8,128)S(1)} %copy-done.37, f32[8,256,256]{2,1,0:T(8,128)S(1)} %copy-done.26, pred[256,256]{1,0:T(8,128)(4,1)S(1)} %copy-done.52, ...), kind=kOutput, calls=%fused_computation.20 | convolution fusion | flops 4913029120 | bytes 14188544 | tf_op jit(solution)/shard_map/while/body/eval_jaxpr/cihp,cjhp->chij/dot_general | solution.py:156
  397.3 21.9 %fusion.68 = f32[8,256,128]{2,1,0:T(8,128)} fusion(f32[8,12,128,64]{3,2,1,0:T(8,128)S(1)} %bitcast.261, f32[8,256,12,64]{1,0,3,2:T(8,128)S(1)} %bitcast.252, f32[8,256,12]{1,2,0:T(8,128)S(1)} %get-tuple-element.449), kind=kOutput, calls=%fused_computation.107 | convolution fusion | flops 2417491968 | bytes 10584064 | tf_op jit(solution)/shard_map/while/body/eval_jaxpr/cihp,chnp->cin/dot_general | solution.py:134
  419.2 6.4 fusion.64
  429.0 35.2 %while.60 = (s32[]{:T(128)}, f32[12,128,64]{2,1,0:T(8,128)S(1)}, f32[8,12,128,64]{3,2,1,0:T(8,128)}, f32[8,12]{1,0:T(8,128)S(1)}, f32[8,12,128,64]{2,3,1,0:T(8,1...) while((s32[]{:T(128)}, f32[12,128,64]{2,1,0:T(8,128)S(1)}, ...), condition=%wide.region_12.13_spmd.clone, body=%wide.region_10.12_spmd.clone.sunk | while | flops 589816 | bytes 4325808 | solution.py:142
  464.2 23.6 %fusion.71 = f32[8,256,128]{2,1,0:T(8,128)} fusion(f32[8,12,128,64]{3,2,1,0:T(8,128)} %get-tuple-element.247, f32[8,256,12]{1,2,0:T(8,128)S(1)} %get-tuple-element.450, bf16[8,256,12,64]{1,0,3,2:T(8,128)(2,1)} %bitcast.263), kind=kOutput, calls=%fused_computation.108 | convolution fusion | flops 2419064832 | bytes 7438336 | tf_op jit(solution)/shard_map/while/body/eval_jaxpr/chnp,cjh,cjhp->cjn/dot_general | solution.py:149
  487.8 6.4 copy.255
  505.4 4.8 fusion.115
  512.8 24.2 %bitcast_add_fusion.2 = f32[8,256,12,64]{1,3,2,0:T(8,128)S(1)} fusion(f32[8,256,12,64]{1,3,2,0:T(8,128)S(1)} %bitcast.274, f32[8,256,12]{1,2,0:T(8,128)S(1)} %get-tuple-element.450, f32[8,12,256]{2,1,0:T(8,128)S(1)} %copy-done.42, f32[8,12,256]{2,1,0:T(8,128)S(1)} %copy-done.37, f32[8,256,256]{2,1,0:T(8,128)S(1)} %copy-done.27, ...), kind=kOutput, calls=%fused_computation.40 | convolution fusion | flops 4866441216 | bytes 21331968 | tf_op jit(solution)/shard_map/while/body/eval_jaxpr/chij,cihp->cjhp/dot_general | solution.py:157
  541.4 5.6 copy.309
  547.0 6.6 copy.258
  553.6 16.7 %fusion.103 = (f32[768]{0:T(1024)}, f32[768]{0:T(1024)S(1)}, f32[768]{0:T(1024)}, f32[768]{0:T(1024)S(1)}, f32[768]{0:T(1024)}, /*index=5*/f32[1,2048,768]{2,1,0:T(8,128)S(1)}) fusion(f32[2048,768]{1,0:T(8,128)} %copy-done.1, f32[1,2048,768]{2,1,0:T(8,128)} %bitcast.259, f32[1,2048,768]{2,1,0:T(8,128)} %get-tuple-element.433, f32[2048,768]{1,0:T(8,128)} %copy.258, ...), kind=kLoop, calls=%fused_computation.201 | loop fusion | flops 29880576 | bytes 37767168 | tf_op jit(solution)/shard_map/reduce_sum | solution.py:52
  582.9 8.7 fusion.49
  591.7 10.9 fusion.101
  602.7 9.2 fusion.116
  617.4 10.4 multiply_reduce_fusion.2
  628.5 19.9 %reduce-window.16 = f32[8,12,2,128]{3,1,2,0:T(8,128)S(1)} reduce-window(f32[8,12,2,128]{3,1,2,0:T(8,128)S(1)} %copy.274, f32[]{:T(128)} %constant.135.clone.1), window={size=1x1x1x128 pad=0_0x0_0x0_0x0_127}, to_apply=%region_20.21 | reduce-window | flops 3121152 | bytes 196612 | tf_op jit(solution)/shard_map/reduce-window.2
  653.8 10.4 fusion.51
  664.2 8.1 fusion.114
  672.3 6.4 fusion.77
  678.8 17.8 %add_add_fusion = f32[2048,1536]{1,0:T(8,128)} fusion(f32[2048,1536]{1,0:T(8,128)} %fusion.77, f32[2048,1536]{1,0:T(8,128)} %fusion.114, f32[2048,1536]{1,0:T(8,128)} %fusion.51, bf16[1536,12]{0,1:T(8,128)(2,1)S(1)} %copy-done.35, bf16[2048,12]{0,1:T(8,128)(2,1)S(1)} %get-tuple-element.425), kind=kOutput, calls=%fused_computation.22 | convolution fusion | flops 84934656 | bytes 50417664 | tf_op jit(solution)/shard_map/tc,dc->td/dot_general | solution.py:313
  698.2 10.9 fusion.102
  719.9 18.6 %all-reduce.13 = (f32[768,12]{0,1:T(8,128)}, f32[768,4]{0,1:T(4,128)}, f32[768]{0:T(1024)}, f32[64,4]{0,1:T(4,128)}, f32[64]{0:T(128)}, /*index=5*/f32[12]{0:T(128)}, f32[12]{0:T(128)}, f32[12]{0:T(128)}, f32[768]{0:T(1024)}) all-reduce(f32[768,12]{0,1:T(8,128)} %reduce-scatter.21.cloned.1.call-do, ...), channel_id=1, replica_groups=mesh['dp'=4,'row'=2,'col'=4] {'dp'}, use_global_device_ids=true, to_apply=%region_33.34 | all-reduce | flops 14180 | bytes 113440 | tf_op jit(solution)/shard_map/psum | solution.py:371
  738.5 169.3 %reduce-scatter.13.cloned.1.call-done = f32[512,1536]{1,0:T(8,128)} async-done(((f32[2048,1536]{1,0:T(8,128)}), f32[512,1536]{1,0:T(8,128)}) %reduce-scatter.13.cloned.1.call-update) | async-done | bytes 3145744 | tf_op jit(solution)/shard_map/reduce_scatter | solution.py:316
  910.6 50.2 %psum.114 = f32[1536]{0:T(1024)} all-reduce(f32[1536]{0:T(1024)S(1)} %get-tuple-element.365), channel_id=1, replica_groups=mesh['dp'=4,'row'=2,'col'=4] {'dp','row','col'}, use_global_device_ids=true, to_apply=%region_25.26 | all-reduce | flops 1536 | bytes 12288 | tf_op jit(solution)/shard_map/psum | solution.py:389
  960.8 163.3 %reduce-scatter.9.cloned.1.call-done = f32[512,1536]{1,0:T(8,128)} async-done(((f32[2048,1536]{1,0:T(8,128)}), f32[512,1536]{1,0:T(8,128)}) %reduce-scatter.9.cloned.1.call-update) | async-done | bytes 3145744 | tf_op jit(solution)/shard_map/reduce_scatter | solution.py:260
  1124.1 6.1 fusion.45
  1130.2 154.9 %all-reduce.18.cloned.1.call-done = (f32[768,768]{1,0:T(8,128)}, f32[768,768]{1,0:T(8,128)}, f32[768,64]{0,1:T(8,128)}, f32[768,768]{1,0:T(8,128)}) async-done(((f32[768,768]{1,0:T(8,128)}, f32[768,768]{1,0:T(8,128)}, f32[768,64]{0,1:T(8,128)}, f32[768,768]{1,0:T(8,128)}), (f32[768,768]{1,0:T(8,128)}, f32[768,768]{1,0:T(8,128)}, f32[768,64]{0,1:T(8,128)}, ...) | async-done | bytes 7274512 | tf_op jit(solution)/shard_map/psum | solution.py:371
  (456 shorter events, 169.7 us)
Async XLA Ops:
  7.2 124.4 %all-gather.8.cloned.1.call-start = ((), (), s32[]{:S(2)}) async-start(), calls=%async_computation.8 | async-start | bytes 7864320 | tf_op jit(solution)/shard_map/all_gather | solution.py:218
  13.4 141.5 %all-gather.10.cloned.1.call-start = ((), (), s32[]{:S(2)}) async-start(), calls=%async_computation.9 | async-start | bytes 3538944 | tf_op jit(solution)/shard_map/all_gather | solution.py:213
  14.1 165.1 %all-gather.18.cloned.1.call-start = ((), (), s32[]{:S(2)}) async-start(), calls=%async_computation.21 | async-start | bytes 1310720 | tf_op jit(solution)/shard_map/all_gather | solution.py:233
  16.3 124.1 %copy-start.29 = (bf16[1536,64]{0,1:T(8,128)(2,1)}, bf16[1536,64]{0,1:T(8,128)(2,1)S(1)}, u32[]{:S(2)}) copy-start(bf16[1536,64]{0,1:T(8,128)(2,1)S(1)} %all_gather.26) | copy-start | bytes 589828
  16.3 124.1 %copy-start.74 = (f32[64]{0:T(128)}, f32[64]{0:T(128)S(1)}, u32[]{:S(2)}) copy-start(f32[64]{0:T(128)S(1)} %get-tuple-element.453) | copy-start | bytes 772
  16.3 124.1 %copy-start.76 = (f32[64]{0:T(128)}, f32[64]{0:T(128)S(1)}, u32[]{:S(2)}) copy-start(f32[64]{0:T(128)S(1)} %get-tuple-element.454) | copy-start | bytes 772
  16.3 124.1 %copy-start.78 = (f32[64]{0:T(128)}, f32[64]{0:T(128)S(1)}, u32[]{:S(2)}) copy-start(f32[64]{0:T(128)S(1)} %get-tuple-element.455) | copy-start | bytes 772
  16.3 124.1 %copy-start.79 = (f32[64]{0:T(128)}, f32[64]{0:T(128)S(1)}, u32[]{:S(2)}) copy-start(f32[64]{0:T(128)S(1)} %get-tuple-element.456) | copy-start | bytes 772
  16.3 124.8 %copy-start.64 = (bf16[768,12]{0,1:T(8,128)(2,1)S(1)}, bf16[768,12]{0,1:T(8,128)(2,1)}, u32[]{:S(2)}) copy-start(bf16[768,12]{0,1:T(8,128)(2,1)} %param.25) | copy-start | bytes 55300
  16.3 126.6 %copy-start.96 = (bf16[12]{0:T(256)(128)(2,1)S(1)}, bf16[12]{0:T(256)(128)(2,1)}, u32[]{:S(2)}) copy-start(bf16[12]{0:T(256)(128)(2,1)} %param.32) | copy-start | bytes 76
  16.3 126.6 %copy-start.97 = (bf16[12]{0:T(256)(128)(2,1)S(1)}, bf16[12]{0:T(256)(128)(2,1)}, u32[]{:S(2)}) copy-start(bf16[12]{0:T(256)(128)(2,1)} %param.30) | copy-start | bytes 76
  16.3 126.6 %copy-start.73 = (bf16[768,4]{0,1:T(4,128)(2,1)S(1)}, bf16[768,4]{0,1:T(4,128)(2,1)}, u32[]{:S(2)}) copy-start(bf16[768,4]{0,1:T(4,128)(2,1)} %param.26) | copy-start | bytes 18436
  16.4 126.7 %copy-start.86 = (bf16[768]{0:T(1024)(128)(2,1)S(1)}, bf16[768]{0:T(1024)(128)(2,1)}, u32[]{:S(2)}) copy-start(bf16[768]{0:T(1024)(128)(2,1)} %param.27) | copy-start | bytes 4612
  16.4 126.8 %copy-start.92 = (bf16[12]{0:T(256)(128)(2,1)S(1)}, bf16[12]{0:T(256)(128)(2,1)}, u32[]{:S(2)}) copy-start(bf16[12]{0:T(256)(128)(2,1)} %param.31) | copy-start | bytes 76
  16.4 126.9 %copy-start.87 = (bf16[768]{0:T(1024)(128)(2,1)S(1)}, bf16[768]{0:T(1024)(128)(2,1)}, u32[]{:S(2)}) copy-start(bf16[768]{0:T(1024)(128)(2,1)} %param.33) | copy-start | bytes 4612
  138.6 130.6 %all-gather.12.cloned.1.call-start = ((), (), s32[]{:S(2)}) async-start(), calls=%async_computation.10 | async-start | bytes 3538944 | tf_op jit(solution)/shard_map/all_gather | solution.py:212
  139.2 155.4 %all-gather.14.cloned.1.call-start = ((), (), s32[]{:S(2)}) async-start(), calls=%async_computation.11 | async-start | bytes 3538944 | tf_op jit(solution)/shard_map/all_gather | solution.py:216
  139.8 177.9 %all-gather.16.cloned.1.call-start = ((), (), s32[]{:S(2)}) async-start(), calls=%async_computation.13 | async-start | bytes 7864320 | tf_op jit(solution)/shard_map/all_gather | solution.py:267
  140.4 434.1 %reduce-scatter.11.cloned.1.call-start = ((), (), s32[]{:S(2)}) async-start(), calls=%async_computation.14 | async-start | bytes 2621440 | tf_op jit(solution)/shard_map/reduce_scatter | solution.py:294
  143.1 19.7 %copy-start.53 = (f32[768]{0:T(1024)}, f32[768]{0:T(1024)S(1)}, u32[]{:S(2)}) copy-start(f32[768]{0:T(1024)S(1)} %get-tuple-element.375) | copy-start | bytes 9220
  143.1 19.7 %copy-start.55 = (f32[768]{0:T(1024)}, f32[768]{0:T(1024)S(1)}, u32[]{:S(2)}) copy-start(f32[768]{0:T(1024)S(1)} %get-tuple-element.376) | copy-start | bytes 9220
  143.1 19.7 %copy-start.57 = (f32[768]{0:T(1024)}, f32[768]{0:T(1024)S(1)}, u32[]{:S(2)}) copy-start(f32[768]{0:T(1024)S(1)} %get-tuple-element.377) | copy-start | bytes 9220
  143.1 19.7 %copy-start.59 = (f32[768]{0:T(1024)}, f32[768]{0:T(1024)S(1)}, u32[]{:S(2)}) copy-start(f32[768]{0:T(1024)S(1)} %get-tuple-element.378) | copy-start | bytes 9220
  143.3 196.0 %copy-start.68 = (f32[768]{0:T(1024)}, f32[768]{0:T(1024)S(1)}, u32[]{:S(2)}) copy-start(f32[768]{0:T(1024)S(1)} %convert_element_type.109) | copy-start | bytes 9220
  154.9 23.6 %copy-start.47 = (f32[8,12]{0,1:T(8,128)}, f32[8,12]{0,1:T(8,128)S(1)}, u32[]{:S(2)}) copy-start(f32[8,12]{0,1:T(8,128)S(1)} %copy.239) | copy-start | bytes 1156
  361.0 36.4 %slice-start.2 = ((s8[6291456]{0:T(1024)(128)(4,1)}), s8[4194304]{0:T(1024)(128)(4,1)S(1)}, s32[]{:S(2)}) async-start(s8[6291456]{0:T(1024)(128)(4,1)} %bitcast.260), calls=%async_computation.25 | async-start | bytes 8388608
  367.1 52.1 %copy-start = (f32[96,8,8,256]{3,2,1,0:T(8,128)}, f32[96,8,8,256]{3,2,1,0:T(8,128)S(1)}, u32[]{:S(2)}) copy-start(f32[96,8,8,256]{3,2,1,0:T(8,128)S(1)} %copy.308) | copy-start | bytes 18874372
  367.1 30.2 %slice-start.3 = ((s8[6291456]{0:T(1024)(128)(4,1)}), s8[2097152]{0:T(1024)(128)(4,1)S(1)}, s32[]{:S(2)}) async-start(s8[6291456]{0:T(1024)(128)(4,1)} %bitcast.260), calls=%async_computation.26 | async-start | bytes 4194304
  397.3 21.9 %copy-start.15 = (bf16[16,8,8,256]{3,2,1,0:T(8,128)(2,1)S(1)}, bf16[16,8,8,256]{3,2,1,0:T(8,128)(2,1)}, u32[]{:S(2)}) copy-start(bf16[16,8,8,256]{3,2,1,0:T(8,128)(2,1)} %copy.304) | copy-start | bytes 1572868
  464.2 30.0 %copy-start.71 = (f32[8,12]{1,0:T(8,128)}, f32[8,12]{1,0:T(8,128)S(1)}, u32[]{:S(2)}) copy-start(f32[8,12]{1,0:T(8,128)S(1)} %get-tuple-element.248) | copy-start | bytes 1156
  505.4 204.1 %reduce-scatter.19.cloned.1.call-start = ((), (), s32[]{:S(2)}) async-start(), calls=%async_computation.18 | async-start | bytes 589824 | tf_op jit(solution)/shard_map/reduce_scatter | solution.py:329
  553.6 16.7 %copy-start.60 = (f32[768]{0:T(1024)S(1)}, f32[768]{0:T(1024)}, u32[]{:S(2)}) copy-start(f32[768]{0:T(1024)} %copy-done.59) | copy-start | bytes 9220
  582.9 126.6 %reduce-scatter.17.cloned.1.call-start = ((), (), s32[]{:S(2)}) async-start(), calls=%async_computation.17 | async-start | bytes 7077888 | tf_op jit(solution)/shard_map/reduce_scatter | solution.py:328
  591.7 117.8 %reduce-scatter.23.cloned.1.call-start = ((), (), s32[]{:S(2)}) async-start(), calls=%async_computation.20 | async-start | bytes 7077888 | tf_op jit(solution)/shard_map/reduce_scatter | solution.py:331
  602.6 106.9 %reduce-scatter.15.cloned.1.call-start = ((), (), s32[]{:S(2)}) async-start(), calls=%async_computation.16 | async-start | bytes 7077888 | tf_op jit(solution)/shard_map/reduce_scatter | solution.py:327
  611.9 108.0 %reduce-scatter.21.cloned.1.call-start = ((), (), s32[]{:S(2)}) async-start(), calls=%async_computation.19 | async-start | bytes 147456 | tf_op jit(solution)/shard_map/reduce_scatter | solution.py:330
  617.3 31.5 %copy-start.32 = (f32[8,256,12]{1,0,2:T(8,128)S(1)}, f32[8,256,12]{1,0,2:T(8,128)}, u32[]{:S(2)}) copy-start(f32[8,256,12]{1,0,2:T(8,128)} %copy-done.31) | copy-start | bytes 294916
  617.3 31.5 %copy-start.43 = (f32[8,12,256]{2,1,0:T(8,128)S(1)}, f32[8,12,256]{2,1,0:T(8,128)}, u32[]{:S(2)}) copy-start(f32[8,12,256]{2,1,0:T(8,128)} %get-tuple-element.353) | copy-start | bytes 294916
  617.3 31.5 %copy-start.50 = (f32[8,12]{1,0:T(8,128)S(1)}, f32[8,12]{1,0:T(8,128)}, u32[]{:S(2)}) copy-start(f32[8,12]{1,0:T(8,128)} %copy-done.49) | copy-start | bytes 1156
  617.4 31.5 %copy-start.89 = (f32[12]{0:T(128)S(1)}, f32[12]{0:T(128)}, u32[]{:S(2)}) copy-start(f32[12]{0:T(128)} %copy-done.88) | copy-start | bytes 148
  617.4 31.9 %copy-start.33 = (f32[2048,12]{0,1:T(8,128)S(1)}, f32[2048,12]{0,1:T(8,128)}, u32[]{:S(2)}) copy-start(f32[2048,12]{0,1:T(8,128)} %get-tuple-element.458) | copy-start | bytes 294916
  653.8 254.0 %reduce-scatter.13.cloned.1.call-start = ((), (), s32[]{:S(2)}) async-start(), calls=%async_computation.15 | async-start | bytes 15728640 | tf_op jit(solution)/shard_map/reduce_scatter | solution.py:316
  696.6 427.5 %reduce-scatter.9.cloned.1.call-start = ((), (), s32[]{:S(2)}) async-start(), calls=%async_computation.12 | async-start | bytes 15728640 | tf_op jit(solution)/shard_map/reduce_scatter | solution.py:260
  709.3 198.5 %copy-start.7 = (bf16[512,1536]{1,0:T(8,128)(2,1)S(1)}, bf16[512,1536]{1,0:T(8,128)(2,1)}, u32[]{:S(2)}) copy-start(bf16[512,1536]{1,0:T(8,128)(2,1)} %param.20) | copy-start | bytes 4718596
  709.3 198.5 %copy-start.40 = (f32[1536]{0:T(1024)S(1)}, f32[1536]{0:T(1024)}, u32[]{:S(2)}) copy-start(f32[1536]{0:T(1024)} %copy-done.39) | copy-start | bytes 18436
  709.4 198.5 %copy-start.62 = (f32[512]{0:T(512)S(1)}, f32[512]{0:T(512)}, u32[]{:S(2)}) copy-start(f32[512]{0:T(512)} %copy-done.61) | copy-start | bytes 6148
  709.4 414.7 %copy-start.16 = (bf16[512,1536]{1,0:T(8,128)(2,1)S(1)}, bf16[512,1536]{1,0:T(8,128)(2,1)}, u32[]{:S(2)}) copy-start(bf16[512,1536]{1,0:T(8,128)(2,1)} %param.35) | copy-start | bytes 4718596
  709.4 575.7 %all-reduce.18.cloned.1.call-start = ((), (), s32[]{:S(2)}) async-start(), calls=%async_computation.22 | async-start | bytes 14548992 | tf_op jit(solution)/shard_map/psum | solution.py:371
  (71 other events, 444.6 us)
Sparse Core Ops, SparseCore 0:
  13.5 118.0 all-gather.7
  133.1 9.1 all-gather.9
  144.5 29.1 all-gather.17
  175.1 10.4 all-gather.11
  187.0 12.1 all-gather.13
  200.6 116.9 all-gather.15
  505.5 43.1 reduce-scatter.10
  583.0 7.0 reduce-scatter.18
  592.4 13.7 reduce-scatter.16
  608.4 13.7 reduce-scatter.22
  624.5 13.7 reduce-scatter.14
  653.9 6.6 reduce-scatter.20
  696.7 211.0 reduce-scatter.12
  910.1 213.9 reduce-scatter.8
  1128.3 156.7 all-reduce.17
where the time goes:
time: 1310 us; the launch traced here: 1300 us
  waiting for transfers between devices  629 us (48%)
  matrix products  286 us (22%)
  local copies, waits for them, and re-layouts  140 us (11%)
  other arithmetic  130 us (10%)
  blocking collectives  96.8 us (7%)
  between operations  15.9 us (1%)
    reduce_scatter x1, waiting for transfers between devices, per_device(): lax.psum_scatter(running, 'col', scatter_dimension=0, tiled=True)  169 us
    reduce_scatter x1, waiting for transfers between devices, per_device(): lax.psum_scatter(jnp.dot(mix_rows, out_full, preferred_element_type=jnp.f...  163 us
    psum x1, waiting for transfers between devices, per_device(): lax.psum((reduced_rows[0], reduced_rows[1], reduced_rows[2], reduced_rows...  155 us
    all_gather x1, waiting for transfers between devices, per_device(): group_rows = lax.all_gather(normed, 'col', axis=0, tiled=True)  115 us
    psum x1, blocking collectives, per_device(): norm_total = lax.psum(norm_part, ('dp', 'row', 'col'))  50.2 us
    unnamed x224, local copies, waits for them, and re-layouts  45.7 us
    dot_general x4, matrix products, per_device(): jnp.einsum('tc,dc->td', input_grad_part, input_weights, preferred_element...  42.7 us
    dot_general x1, matrix products, ssd_backward(): grad_mixing = precise('cihp,cjhp->chij', grad_blocks, x_blocks)  30.2 us
  transfers between devices with their start and end apart: 15, of which 5 were waited for; matrix products, arithmetic and copies ran while one was open for 26% of the time, Pallas kernels for 0%

commit v1 on v0

v1 whole, which is shorter than its diff:
```python
from functools import partial

import jax
import jax.numpy as jnp
from jax import lax
from jax.experimental import pallas as pl
from jax.experimental.pallas import tpu as pltpu
from jax.sharding import PartitionSpec as P

BF = jnp.bfloat16
F32 = jnp.float32
EPSILON = 1e-05
N = 128
Q = 128
HEAD = 64
HALO = 16
TILE = 256
HIGHEST = lax.Precision.HIGHEST
VMEM_LIMIT = 56 * 2**20


def mm(a, b):
    return lax.dot_general(a, b, (((1,), (0,)), ((), ())), preferred_element_type=F32)


def mm_nt(a, b):
    return lax.dot_general(a, b, (((1,), (1,)), ((), ())), preferred_element_type=F32)


def mm_exact(a, b):
    return lax.dot_general(
        a, b, (((1,), (0,)), ((), ())), precision=HIGHEST, preferred_element_type=F32
    )


def split2(values):
    high = values.astype(BF)
    return high, (values - high.astype(F32)).astype(BF)


def sigmoid(values):
    return 1.0 / (1.0 + jnp.exp(-values))


def iota2(shape, axis):
    return lax.broadcasted_iota(jnp.int32, shape, axis)


def params(*names):
    return pltpu.CompilerParams(
        dimension_semantics=names or ("arbitrary",), vmem_limit_bytes=VMEM_LIMIT
    )


def cost(micros):
    return pl.CostEstimate(flops=0, bytes_accessed=int(micros * 3.0e6), transcendentals=0)


def whole(shape):
    return pl.BlockSpec(shape, lambda *_: (0,) * len(shape))


def columns(rows, width=TILE):
    return pl.BlockSpec((rows, width), lambda j: (0, j))


def sds(shape, dtype=F32):
    return jax.ShapeDtypeStruct(shape, dtype)


def conv_rows(raw_ref, taps, start, size):
    total = taps[4:5, :] + jnp.zeros((size, taps.shape[1]), F32)
    for k in range(4):
        total = total + taps[k : k + 1, :] * raw_ref[pl.ds(HALO - 3 + k + start, size), :]
    return total


def project_kernel(
    normed_ref, w_ref, taps_ref, wstep_ref, head_ref,
    raw_ref, act_ref, stepin_ref, step_ref, cum_ref, grow_ref, offs_ref,
):
    tokens = act_ref.shape[0]
    raw_ref[...] = mm(normed_ref[...], w_ref[...])
    taps = taps_ref[...]
    for at in range(0, tokens, Q):
        pre = conv_rows(raw_ref, taps, at, Q)
        act_ref[at : at + Q, :] = (pre * sigmoid(pre)).astype(BF)

    @pl.when(pl.program_id(0) == 0)
    def _():
        step_in = mm(normed_ref[HALO:, :], wstep_ref[...]) + head_ref[0:1, :]
        small = jnp.exp(-jnp.abs(step_in))
        plus = 1.0 + small
        log_part = jnp.where(plus == 1.0, small, jnp.log(plus) * (small / jnp.where(plus == 1.0, 1.0, plus - 1.0)))
        step = jnp.maximum(step_in, 0.0) + log_part
        stepin_ref[...] = step_in
        step_ref[...] = step
        falls = step * head_ref[1:2, :]
        lower = (iota2((Q, Q), 0) >= iota2((Q, Q), 1)).astype(F32)
        before = jnp.zeros((1, 128), F32)
        offs_ref[...] = jnp.zeros_like(offs_ref)
        for b in range(tokens // Q):
            rows = slice(b * Q, b * Q + Q)
            cum = mm_exact(lower, falls[rows, :])
            cum_ref[rows, :] = cum
            high, low = split2(jnp.exp(cum + before))
            grow_ref[rows, 0:128] = high
            grow_ref[rows, 128:256] = low
            before = before + cum[Q - 1 : Q, :]
            offs_ref[b + 1 : b + 2, :] = before


def project(normed, weights, taps, w_step, head_rows):
    rows, width = normed.shape
    tokens = rows - HALO
    total = weights.shape[1]
    return pl.pallas_call(
        project_kernel,
        grid=(total // TILE,),
        in_specs=[
            whole((rows, width)),
            columns(width),
            columns(8),
            whole((width, 128)),
            whole((8, 128)),
        ],
        out_specs=[
            columns(rows),
            columns(tokens),
            whole((tokens, 128)),
            whole((tokens, 128)),
            whole((tokens, 128)),
            whole((tokens, 256)),
            whole((16, 128)),
        ],
        out_shape=[
            sds((rows, total)),
            sds((tokens, total), BF),
            sds((tokens, 128)),
            sds((tokens, 128)),
            sds((tokens, 128)),
            sds((tokens, 256), BF),
            sds((16, 128)),
        ],
        compiler_params=params(),
        cost_estimate=cost(9),
        name="project",
    )(normed, weights, taps, w_step, head_rows)


def expand(per_head, spread):
    high, low = split2(per_head)
    return mm(jnp.concatenate([high, low], 1), spread)


def transpose_bf(values):
    return values.astype(F32).T.astype(BF)


def states_kernel(x_ref, b_ref, step_ref, cum_ref, spread_ref, states_ref, final_ref, held):
    at = pl.program_id(0)
    last = pl.num_programs(0) - 1

    @pl.when(at == 0)
    def _():
        held[...] = jnp.zeros_like(held)

    states_ref[0] = held[...]

    @pl.when(at == last)
    def _():
        final_ref[...] = held[...]

    @pl.when(at < last)
    def _():
        cum = cum_ref[...]
        end = cum[Q - 1 : Q, :]
        tail = jnp.exp(end - cum) * step_ref[...]
        fall = jnp.broadcast_to(jnp.exp(end), (8, 128))
        b_t = transpose_bf(b_ref[...])
        b_t2 = jnp.concatenate([b_t, b_t], 1)
        for start in range(0, x_ref.shape[1], TILE):
            lanes = slice(start, start + TILE)
            spread = spread_ref[:, lanes]
            scaled = expand(tail, spread) * x_ref[:, lanes].astype(F32)
            high, low = split2(scaled)
            fresh = mm(b_t2, jnp.concatenate([high, low], 0))
            held[:, lanes] = held[:, lanes] * expand(fall, spread)[0:1, :] + fresh


def scan_states(act, step, cum, spread, channels):
    blocks = act.shape[0] // Q
    clamp = lambda i: jnp.minimum(i, blocks - 1)
    return pl.pallas_call(
        states_kernel,
        grid=(blocks + 1,),
        in_specs=[
            pl.BlockSpec((Q, channels), lambda i: (clamp(i), 0)),
            pl.BlockSpec((Q, N), lambda i: (clamp(i), channels // N)),
            pl.BlockSpec((Q, 128), lambda i: (clamp(i), 0)),
            pl.BlockSpec((Q, 128), lambda i: (clamp(i), 0)),
            whole((256, channels)),
        ],
        out_specs=[
            pl.BlockSpec((1, N, channels), lambda i: (i, 0, 0)),
            whole((N, channels)),
        ],
        out_shape=[sds((blocks + 1, N, channels)), sds((N, channels))],
        scratch_shapes=[pltpu.VMEM((N, channels), F32)],
        compiler_params=params(),
        cost_estimate=cost(6),
        name="scan_states",
    )(act, act, step, cum, spread)


def forward_kernel(x_ref, b_ref, c_ref, step_ref, cum_ref, spread_ref, state_ref, y_ref):
    b_blk, c_blk = b_ref[...], c_ref[...]
    affinity = mm_nt(c_blk, b_blk)
    causal = iota2((Q, Q), 0) >= iota2((Q, Q), 1)
    first = iota2((Q, 128), 1) < HEAD
    cum = cum_ref[...]
    cum_t = cum.T
    step_t = step_ref[...].T
    growth = jnp.exp(cum)
    c2 = jnp.concatenate([c_blk, c_blk], 1)
    zero = jnp.zeros((Q, 128), BF)
    for start in range(0, x_ref.shape[1], TILE):
        lanes = slice(start, start + TILE)
        s_high, s_low = split2(state_ref[0, :, lanes])
        reached = mm(c2, jnp.concatenate([s_high, s_low], 0)) * expand(growth, spread_ref[:, lanes])
        for pair in range(2):
            at = start + pair * 128
            x_pair = x_ref[:, at : at + 128]
            x0, x1 = jnp.where(first, x_pair, zero), jnp.where(first, zero, x_pair)
            pieces = []
            for half in range(2):
                h = at // HEAD + half
                spread_h = cum[:, h : h + 1] - cum_t[h : h + 1, :]
                decay = jnp.exp(jnp.where(causal, spread_h, -1e30))
                mixing = affinity * decay * step_t[h : h + 1, :]
                pieces += split2(mixing)
            intra = mm(jnp.concatenate(pieces, 1), jnp.concatenate([x0, x0, x1, x1], 0))
            y_ref[:, at : at + 128] = intra + reached[:, pair * 128 : pair * 128 + 128]


def scan_forward(act, step, cum, spread, states, channels):
    tokens = act.shape[0]
    return pl.pallas_call(
        forward_kernel,
        grid=(tokens // Q,),
        in_specs=[
            pl.BlockSpec((Q, channels), lambda i: (i, 0)),
            pl.BlockSpec((Q, N), lambda i: (i, channels // N)),
            pl.BlockSpec((Q, N), lambda i: (i, channels // N + 1)),
            pl.BlockSpec((Q, 128), lambda i: (i, 0)),
            pl.BlockSpec((Q, 128), lambda i: (i, 0)),
            whole((256, channels)),
            pl.BlockSpec((1, N, channels), lambda i: (i, 0, 0)),
        ],
        out_specs=pl.BlockSpec((Q, channels), lambda i: (i, 0)),
        out_shape=sds((tokens, channels)),
        compiler_params=params(),
        cost_estimate=cost(13),
        name="scan_forward",
    )(act, act, act, step, cum, spread, states)


def grad_states_kernel(dy_ref, c_ref, cum_ref, spread_ref, after_ref, first_ref, held):
    at = pl.program_id(0)

    @pl.when(at == 0)
    def _():
        held[...] = jnp.zeros_like(held)

    after_ref[0] = held[...]
    cum = cum_ref[...]
    growth = jnp.exp(cum)
    fall = jnp.broadcast_to(growth[Q - 1 : Q, :], (8, 128))
    c_t = transpose_bf(c_ref[...])
    c_t2 = jnp.concatenate([c_t, c_t], 1)
    for start in range(0, dy_ref.shape[1], TILE):
        lanes = slice(start, start + TILE)
        spread = spread_ref[:, lanes]
        high, low = split2(dy_ref[:, lanes] * expand(growth, spread))
        direct = mm(c_t2, jnp.concatenate([high, low], 0))
        held[:, lanes] = held[:, lanes] * expand(fall, spread)[0:1, :] + direct
    first_ref[...] = held[...]


def scan_grad_states(dy, act, cum, spread):
    tokens, channels = dy.shape
    blocks = tokens // Q
    return pl.pallas_call(
        grad_states_kernel,
        grid=(blocks,),
        in_specs=[
            pl.BlockSpec((Q, channels), lambda i: (blocks - 1 - i, 0)),
            pl.BlockSpec((Q, N), lambda i: (blocks - 1 - i, channels // N + 1)),
            pl.BlockSpec((Q, 128), lambda i: (blocks - 1 - i, 0)),
            whole((256, channels)),
        ],
        out_specs=[
            pl.BlockSpec((1, N, channels), lambda i: (blocks - 1 - i, 0, 0)),
            whole((N, channels)),
        ],
        out_shape=[sds((blocks, N, channels)), sds((N, channels))],
        scratch_shapes=[pltpu.VMEM((N, channels), F32)],
        compiler_params=params(),
        cost_estimate=cost(6),
        name="scan_grad_states",
    )(dy, act, cum, spread)


def backward_near_kernel(
    dy_ref, x_ref, b_ref, c_ref, step_ref, cum_ref, spread_ref, state_ref, early_ref, offs_ref,
    gx_ref, gbc_ref,
):
    at_block = pl.program_id(0)
    b_blk, c_blk = b_ref[...], c_ref[...]
    affinity_t = mm_nt(b_blk, c_blk)
    causal_t = iota2((Q, Q), 1) >= iota2((Q, Q), 0)
    first = iota2((Q, 128), 1) < HEAD
    cum = cum_ref[...]
    cum_t = cum.T
    step = step_ref[...]
    growth = jnp.exp(cum)
    early_fall = jnp.broadcast_to(jnp.exp(offs_ref[pl.ds(at_block, 1), :]), (8, 128))
    zero = jnp.zeros((Q, 128), BF)
    grad_affinity_t = jnp.zeros((Q, Q), F32)
    grad_c = jnp.zeros((Q, N), F32)
    for start in range(0, x_ref.shape[1], TILE):
        lanes = slice(start, start + TILE)
        spread = spread_ref[:, lanes]
        before = state_ref[0, :, lanes] + expand(early_fall, spread)[0:1, :] * early_ref[:, lanes]
        dy_quad = dy_ref[:, lanes]
        s_high, s_low = split2(before)
        g_high, g_low = split2(dy_quad * expand(growth, spread))
        grad_c = grad_c + mm_nt(
            jnp.concatenate([g_high, g_low, g_high], 1), jnp.concatenate([s_high, s_high, s_low], 1)
        )
        for pair in range(2):
            at = start + pair * 128
            d_high, d_low = split2(dy_quad[:, pair * 128 : pair * 128 + 128])
            x_pair = x_ref[:, at : at + 128]
            x0, x1 = jnp.where(first, x_pair, zero), jnp.where(first, zero, x_pair)
            grad_mixing = mm_nt(
                jnp.concatenate([jnp.concatenate([x0, x0], 1), jnp.concatenate([x1, x1], 1)], 0),
                jnp.concatenate([d_high, d_low], 1),
            )
            left, right = [], []
            for half in range(2):
                h = at // HEAD + half
                spread_h = cum_t[h : h + 1, :] - cum[:, h : h + 1]
                decay = jnp.exp(jnp.where(causal_t, spread_h, -1e30))
                m_high, m_low = split2(affinity_t * decay)
                grad_affinity_t = grad_affinity_t + (
                    grad_mixing[half * Q : half * Q + Q, :] * decay * step[:, h : h + 1]
                )
                keep = first if half == 0 else jnp.logical_not(first)
                dh, dl = jnp.where(keep, d_high, zero), jnp.where(keep, d_low, zero)
                left += [m_high, m_low, m_high]
                right += [dh, dh, dl]
            gx_ref[:, at : at + 128] = mm(jnp.concatenate(left, 1), jnp.concatenate(right, 0))
    a_high, a_low = split2(grad_affinity_t)
    gbc_ref[:, 0:N] = mm(jnp.concatenate([a_high, a_low], 1), jnp.concatenate([c_blk, c_blk], 0))
    t_high, t_low = split2(grad_affinity_t.T)
    gbc_ref[:, N : 2 * N] = grad_c + mm(
        jnp.concatenate([t_high, t_low], 1), jnp.concatenate([b_blk, b_blk], 0)
    )


def scan_backward_near(dy, act, step, cum, spread, states, early, offs):
    tokens, channels = dy.shape
    rows = pl.BlockSpec((Q, channels), lambda i: (i, 0))
    return pl.pallas_call(
        backward_near_kernel,
        grid=(tokens // Q,),
        in_specs=[
            rows,
            rows,
            pl.BlockSpec((Q, N), lambda i: (i, channels // N)),
            pl.BlockSpec((Q, N), lambda i: (i, channels // N + 1)),
            pl.BlockSpec((Q, 128), lambda i: (i, 0)),
            pl.BlockSpec((Q, 128), lambda i: (i, 0)),
            whole((256, channels)),
            pl.BlockSpec((1, N, channels), lambda i: (i, 0, 0)),
            whole((N, channels)),
            whole((16, 128)),
        ],
        out_specs=[rows, pl.BlockSpec((Q, 2 * N), lambda i: (i, 0))],
        out_shape=[sds((tokens, channels)), sds((tokens, 2 * N))],
        compiler_params=params(),
        cost_estimate=cost(20),
        name="scan_backward_near",
    )(dy, act, act, act, step, cum, spread, states, early, offs)


def backward_far_kernel(
    dy_ref, x_ref, y_ref, gx_ref, b_ref, step_ref, cum_ref, stepin_ref, spread_ref, gather_ref,
    after_ref, late_ref, state_ref, early_ref, offs_ref, head_ref, skip_ref, gbc_ref,
    ga_ref, gstep_ref, gbc_out_ref, sums_ref,
):
    blocks = pl.num_programs(0)
    at_block = pl.program_id(0)

    @pl.when(at_block == 0)
    def _():
        sums_ref[...] = jnp.zeros_like(sums_ref)

    b_blk = b_ref[...]
    b2 = jnp.concatenate([b_blk, b_blk], 1)
    cum, step = cum_ref[...], step_ref[...]
    tail = jnp.exp(cum[Q - 1 : Q, :] - cum)
    tail_step = tail * step
    offs_after = offs_ref[pl.ds(at_block + 1, 1), :]
    offs_end = offs_ref[pl.ds(blocks, 1), :]
    late_fall = jnp.broadcast_to(jnp.exp(offs_end - offs_after), (8, 128))
    early_fall = jnp.broadcast_to(jnp.exp(offs_after), (8, 128))
    row_dots = jnp.zeros((Q, 128), F32)
    col_dots = jnp.zeros((Q, 128), F32)
    last_add = jnp.zeros((8, 128), F32)
    grad_b = gbc_ref[:, 0:N]
    for start in range(0, x_ref.shape[1], TILE):
        lanes = slice(start, start + TILE)
        spread = spread_ref[:, lanes]
        gather = gather_ref[lanes, :]
        gather2 = jnp.concatenate([gather, gather], 0)
        x_quad = x_ref[:, lanes].astype(F32)
        dy_quad = dy_ref[:, lanes]
        skip = skip_ref[0:1, lanes]
        d_state = after_ref[0, :, lanes] + expand(late_fall, spread)[0:1, :] * late_ref[:, lanes]
        state = state_ref[0, :, lanes] + expand(early_fall, spread)[0:1, :] * early_ref[:, lanes]
        touch = jnp.broadcast_to(jnp.sum(d_state * state, axis=0, keepdims=True), (8, TILE))
        t_high, t_low = split2(touch)
        last_add = last_add + mm(jnp.concatenate([t_high, t_low], 1), gather2)
        s_high, s_low = split2(d_state)
        gx = gx_ref[:, lanes] + expand(tail, spread) * mm(b2, jnp.concatenate([s_high, s_low], 0))
        w_high, w_low = split2(expand(tail_step, spread) * x_quad)
        grad_b = grad_b + mm_nt(
            jnp.concatenate([w_high, w_low, w_high], 1), jnp.concatenate([s_high, s_high, s_low], 1)
        )
        p_high, p_low = split2(dy_quad * (y_ref[:, lanes] - skip * x_quad))
        row_dots = row_dots + mm(jnp.concatenate([p_high, p_low], 1), gather2)
        r_high, r_low = split2(x_quad * gx)
        col_dots = col_dots + mm(jnp.concatenate([r_high, r_low], 1), gather2)
        ga_ref[:, lanes] = expand(step, spread) * gx + skip * dy_quad
    last_row = iota2((Q, 128), 0) == Q - 1
    grad_cum = row_dots - step * col_dots + jnp.where(last_row, last_add[0:1, :], 0.0)
    upper = (iota2((Q, Q), 1) >= iota2((Q, Q), 0)).astype(F32)
    grad_rate = mm_exact(upper, grad_cum)
    grad_step = col_dots + grad_rate * head_ref[1:2, :]
    grad_raw = grad_step * sigmoid(stepin_ref[...])
    gstep_ref[...] = grad_raw.astype(BF)
    sums_ref[0:1, :] += jnp.sum(grad_rate * step, axis=0, keepdims=True)
    sums_ref[1:2, :] += jnp.sum(grad_raw, axis=0, keepdims=True)
    gbc_out_ref[:, 0:N] = grad_b
    gbc_out_ref[:, N : 2 * N] = gbc_ref[:, N : 2 * N]


def scan_backward_far(
    dy, act, y, gx, step, cum, step_in, spread, gather, after, late, states, early, offs, head_rows, skip, gbc
):
    tokens, channels = dy.shape
    rows = pl.BlockSpec((Q, channels), lambda i: (i, 0))
    heads = pl.BlockSpec((Q, 128), lambda i: (i, 0))
    pairs = pl.BlockSpec((Q, 2 * N), lambda i: (i, 0))
    return pl.pallas_call(
        backward_far_kernel,
        grid=(tokens // Q,),
        in_specs=[
            rows,
            rows,
            rows,
            rows,
            pl.BlockSpec((Q, N), lambda i: (i, channels // N)),
            heads,
            heads,
            heads,
            whole((256, channels)),
            whole((channels, 128)),
            pl.BlockSpec((1, N, channels), lambda i: (i, 0, 0)),
            whole((N, channels)),
            pl.BlockSpec((1, N, channels), lambda i: (i + 1, 0, 0)),
            whole((N, channels)),
            whole((16, 128)),
            whole((8, 128)),
            whole((8, channels)),
            pairs,
        ],
        out_specs=[rows, heads, pairs, whole((8, 128))],
        out_shape=[
            sds((tokens, channels)),
            sds((tokens, 128), BF),
            sds((tokens, 2 * N)),
            sds((8, 128)),
        ],
        compiler_params=params(),
        cost_estimate=cost(14),
        name="scan_backward_far",
    )(dy, act, y, gx, act, step, cum, step_in, spread, gather, after, late, states, early, offs, head_rows, skip, gbc)


def gate_kernel(
    normed_ref, cot_ref, wg_ref, wo_ref, y0_ref, x_ref, early_ref, c_ref, grow_ref, spread_ref, vec_ref,
    graw_ref, y_ref, gm_ref, stats_ref, squares, inners,
):
    at = pl.program_id(0)
    tokens = cot_ref.shape[0]

    @pl.when(at == 0)
    def _():
        squares[...] = jnp.zeros_like(squares)
        inners[...] = jnp.zeros_like(inners)

    graw_ref[...] = mm(normed_ref[HALO:, :], wg_ref[...])
    gm_ref[...] = mm_nt(cot_ref[...], wo_ref[...])
    s_high, s_low = split2(early_ref[...])
    s2 = jnp.concatenate([s_high, s_low], 0)
    spread = spread_ref[...]
    skip, gain = vec_ref[0:1, :], vec_ref[1:2, :]
    for row in range(0, tokens, Q):
        rows = slice(row, row + Q)
        c_blk = c_ref[rows, :]
        carried = mm(jnp.concatenate([c_blk, c_blk], 1), s2) * mm(grow_ref[rows, :], spread)
        y = y0_ref[rows, :] + carried + skip * x_ref[rows, :].astype(F32)
        y_ref[rows, :] = y
        raw = graw_ref[rows, :]
        gated = y * raw * sigmoid(raw)
        square = gated * gated
        inner = gm_ref[rows, :] * gain * gated
        squares[rows, :] += square[:, 0:128] + square[:, 128:256]
        inners[rows, :] += inner[:, 0:128] + inner[:, 128:256]

    @pl.when(at == pl.num_programs(0) - 1)
    def _():
        ones = jnp.ones((8, 128), F32)
        nt = (((1,), (1,)), ((), ()))
        square_row = lax.dot_general(ones, squares[...], nt, precision=HIGHEST, preferred_element_type=F32)
        inner_row = lax.dot_general(ones, inners[...], nt, precision=HIGHEST, preferred_element_type=F32)
        stats_ref[...] = jnp.where(iota2(square_row.shape, 0) == 0, square_row, inner_row)


def gate_forward(normed, cot, w_gate, w_out, y0, act, early, grow, spread, vectors):
    rows, width = normed.shape
    tokens, channels = y0.shape
    return pl.pallas_call(
        gate_kernel,
        grid=(channels // TILE,),
        in_specs=[
            whole((rows, width)),
            whole((tokens, width)),
            columns(width),
            pl.BlockSpec((TILE, width), lambda j: (j, 0)),
            columns(tokens),
            columns(tokens),
            columns(N),
            pl.BlockSpec((tokens, N), lambda j: (0, channels // N + 1)),
            whole((tokens, 256)),
            columns(256),
            columns(8),
        ],
        out_specs=[columns(tokens), columns(tokens), columns(tokens), whole((8, tokens))],
        out_shape=[sds((tokens, channels))] * 3 + [sds((8, tokens))],
        scratch_shapes=[pltpu.VMEM((tokens, 128), F32), pltpu.VMEM((tokens, 128), F32)],
        compiler_params=params(),
        cost_estimate=cost(16),
        name="gate_forward",
    )(normed, cot, w_gate, w_out, y0, act, early, act, grow, spread, vectors)


def mix_kernel(
    inner_channels, graw_ref, y_ref, gm_ref, x_ref, stats_ref, vec_ref,
    mixed_ref, gg_ref, dy_ref, sums_ref, stats_col,
):
    tokens = y_ref.shape[0]

    @pl.when(pl.program_id(0) == 0)
    def _():
        stats_col[...] = stats_ref[...].T

    gain = vec_ref[1:2, :]
    gain_sum = jnp.zeros((1, TILE), F32)
    skip_sum = jnp.zeros((1, TILE), F32)
    for row in range(0, tokens, Q):
        rows = slice(row, row + Q)
        inv = lax.rsqrt(stats_col[rows, 0:1] * (1.0 / inner_channels) + EPSILON)
        pull = inv * inv * inv * (stats_col[rows, 1:2] * (1.0 / inner_channels))
        raw = graw_ref[rows, :]
        y = y_ref[rows, :]
        gm = gm_ref[rows, :]
        sig = sigmoid(raw)
        act = raw * sig
        gated = y * act
        unit = gated * inv
        mixed_ref[rows, :] = (unit * gain).astype(BF)
        gain_sum = gain_sum + jnp.sum(gm * unit, axis=0, keepdims=True)
        grad_gated = inv * (gm * gain) - gated * pull
        dy = grad_gated * act
        dy_ref[rows, :] = dy
        gg_ref[rows, :] = (grad_gated * y * (sig * (1.0 + raw * (1.0 - sig)))).astype(BF)
        skip_sum = skip_sum + jnp.sum(dy * x_ref[rows, :].astype(F32), axis=0, keepdims=True)
    sums_ref[...] = jnp.zeros_like(sums_ref)
    sums_ref[0:1, :] = gain_sum
    sums_ref[1:2, :] = skip_sum


def mix_backward(inner_channels, graw, y, gm, act, stats, vectors):
    tokens, channels = y.shape
    return pl.pallas_call(
        partial(mix_kernel, inner_channels),
        grid=(channels // TILE,),
        in_specs=[columns(tokens)] * 4 + [whole((128, tokens)), columns(8)],
        out_specs=[columns(tokens)] * 3 + [columns(8)],
        out_shape=[
            sds((tokens, channels), BF),
            sds((tokens, channels), BF),
            sds((tokens, channels)),
            sds((8, channels)),
        ],
        scratch_shapes=[pltpu.VMEM((tokens, 128), F32)],
        compiler_params=params(),
        cost_estimate=cost(10),
        name="mix_backward",
    )(graw, y, gm, act, stats, vectors)


def conv_back_kernel(ga_ref, raw_ref, taps_ref, gv_ref, sums_ref, g_pad):
    tokens, width = ga_ref.shape
    taps = taps_ref[...]
    g_pad[0:HALO, :] = jnp.zeros((HALO, width), F32)
    g_pad[HALO + tokens :, :] = jnp.zeros((HALO, width), F32)
    sums = [jnp.zeros((1, width), F32)] * 5
    for row in range(0, tokens, Q):
        pre = conv_rows(raw_ref, taps, row, Q)
        sig = sigmoid(pre)
        g = ga_ref[row : row + Q, :] * (sig * (1.0 + pre * (1.0 - sig)))
        g_pad[HALO + row : HALO + row + Q, :] = g
        for k in range(4):
            moved = raw_ref[pl.ds(HALO - 3 + k + row, Q), :]
            sums[k] = sums[k] + jnp.sum(g * moved, axis=0, keepdims=True)
        sums[4] = sums[4] + jnp.sum(g, axis=0, keepdims=True)
    for row in list(range(HALO, HALO + tokens, Q)) + [0]:
        size = HALO if row == 0 else Q
        total = jnp.zeros((size, width), F32)
        for k in range(4):
            total = total + taps[k : k + 1, :] * g_pad[pl.ds(row + 3 - k, size), :]
        gv_ref[row : row + size, :] = total.astype(BF)
    sums_ref[...] = jnp.zeros_like(sums_ref)
    for k in range(5):
        sums_ref[k : k + 1, :] = sums[k]


def conv_back(ga, raw, taps):
    tokens, channels = ga.shape
    width = min(channels, TILE)
    return pl.pallas_call(
        conv_back_kernel,
        grid=(channels // width,),
        in_specs=[columns(tokens, width), columns(tokens + HALO, width), columns(8, width)],
        out_specs=[columns(tokens + HALO, width), columns(8, width)],
        out_shape=[sds((tokens + HALO, channels), BF), sds((8, channels))],
        scratch_shapes=[pltpu.VMEM((tokens + 2 * HALO, width), F32)],
        compiler_params=params(),
        cost_estimate=cost(8 * channels / 1536),
        name="conv_back",
    )(ga, raw, taps)


def flips(size, by):
    return [(i, i ^ by) for i in range(size)]


def butterfly(values, axis):
    size = lax.axis_size(axis)
    by = 1
    while by < size:
        values = values + lax.ppermute(values, axis, flips(size, by))
        by *= 2
    return values


def at_rows(values, index, size):
    return lax.dynamic_slice_in_dim(values, index * size, size, axis=0)


def collect_dp(piece, dp):
    size = lax.axis_size("dp")
    rows = piece.shape[0]
    out = jnp.zeros((size * rows,) + piece.shape[1:], piece.dtype)
    out = lax.dynamic_update_slice_in_dim(out, piece, dp * rows, 0)
    for by in range(1, size):
        other = lax.ppermute(piece, "dp", flips(size, by))
        out = lax.dynamic_update_slice_in_dim(out, other, (dp ^ by) * rows, 0)
    return out


def reduce_dp(values, dp):
    size = lax.axis_size("dp")
    total = lax.dynamic_index_in_dim(values, dp, 0, keepdims=False)
    for by in range(1, size):
        piece = lax.dynamic_index_in_dim(values, dp ^ by, 0, keepdims=False).astype(BF)
        total = total + lax.ppermute(piece, "dp", flips(size, by)).astype(F32)
    return total


def swap_core(values):
    return lax.ppermute(values, "row", [(0, 1), (1, 0)])


def per_device(
    tokens, norm_gain, w_gate, w_value, w_state, w_step, conv_value, bias_value, conv_state,
    bias_state, a_log, d_skip, dt_bias, mix_gain, w_out, cotangent,
):
    cols, rows_n, dps = lax.axis_size("col"), lax.axis_size("row"), lax.axis_size("dp")
    col, row, dp = lax.axis_index("col"), lax.axis_index("row"), lax.axis_index("dp")
    group = cols // 2
    place = lax.rem(col, group)
    local, width = tokens.shape
    span = local * group
    half_width = width // 2
    shard = w_value.shape[1]
    channels = 2 * shard
    heads = a_log.shape[0]
    inner_channels = shard * cols
    state_all = w_state.shape[1] * cols
    mirror = [(i, cols - 1 - i) for i in range(cols)]
    forth = [(i, cols - 1 - i) for i in range(group)]
    back = [(cols - 1 - i, i) for i in range(group)]

    def ring(by):
        return [(i, (i // group) * group + (i % group + by) % group) for i in range(cols)]

    def mine_first(values, axis):
        a, b = jnp.split(values, 2, axis=axis)
        return jnp.where(row == 0, values, jnp.concatenate([b, a], axis=axis))

    def own_then_mirror(own, other):
        return jnp.concatenate([own, other], axis=0)

    tokens_p = mine_first(tokens, 1)
    cot_p = mine_first(cotangent, 1)
    gain_p = mine_first(norm_gain.astype(F32), 0)

    def gather_tokens(values, first_rows):
        out = jnp.zeros((first_rows + span, width), values.dtype)
        out = lax.dynamic_update_slice_in_dim(out, values, first_rows + place * local, 0)
        for by in range(1, group):
            other = lax.ppermute(values, "col", ring(by))
            at = lax.rem(place - by + group, group)
            out = lax.dynamic_update_slice_in_dim(out, other, first_rows + at * local, 0)
        return out

    group_tokens = gather_tokens(tokens_p, HALO)
    halo = sum(
        lax.ppermute(tokens_p[local - HALO :], "col", [(group - 1, group + j)]) for j in range(group)
    )
    group_tokens = lax.dynamic_update_slice_in_dim(group_tokens, halo, 0, 0)

    def import_shard(values):
        piece = values.shape[0] // dps
        return collect_dp(lax.ppermute(at_rows(values, dp, piece), "col", mirror), dp)

    mirror_value = import_shard(w_value)
    value_rows = jnp.concatenate([w_value, mirror_value], axis=1)
    value_other = swap_core(value_rows)
    small = jnp.concatenate([w_state, w_step], axis=1)
    small = lax.all_gather(lax.all_gather(small, "col", axis=0), "row", axis=1, tiled=True)
    small = mine_first(small, 1)
    state_width = w_state.shape[1]
    state_full = jnp.transpose(small[:, :, :state_width], (1, 0, 2)).reshape(width, state_all)
    step_own = lax.dynamic_index_in_dim(small, col, 0, keepdims=False)[:, state_width:]
    step_mirror = lax.dynamic_index_in_dim(small, cols - 1 - col, 0, keepdims=False)[:, state_width:]
    step_full = jnp.pad(
        jnp.concatenate([step_own, step_mirror], axis=1), ((0, 0), (0, 128 - 2 * heads))
    )
    value_full = jnp.concatenate([value_rows, value_other], axis=0)
    weights = jnp.concatenate([value_full, state_full], axis=1)
    gate_out = import_shard(jnp.concatenate([w_gate.reshape(dps, -1, shard), w_out.reshape(dps, -1, half_width)], axis=1).reshape(-1, shard)) if shard == half_width else None
    if gate_out is None:
        mirror_gate, mirror_out = import_shard(w_gate), import_shard(w_out)
    else:
        gate_out = gate_out.reshape(dps, 2, -1, shard)
        mirror_gate = gate_out[:, 0].reshape(half_width, shard)
        mirror_out = gate_out[:, 1].reshape(shard, half_width)
    gate_rows = jnp.concatenate([w_gate, mirror_gate], axis=1)
    gate_full = jnp.concatenate([gate_rows, swap_core(gate_rows)], axis=0)
    out_rows = jnp.concatenate([w_out, mirror_out], axis=0)
    out_full = jnp.concatenate([out_rows, swap_core(out_rows)], axis=1)

    def per_channel(own_taps, own_bias):
        taps = jnp.concatenate([own_taps.astype(F32).T, own_bias.astype(F32)[None]], axis=0)
        return jnp.pad(taps, ((0, 3), (0, 0)))

    packed = jnp.concatenate(
        [
            per_channel(conv_value, bias_value)[:5],
            mix_gain.astype(F32)[None],
            jnp.repeat(d_skip.astype(F32), HEAD)[None],
            jnp.pad(
                jnp.concatenate([a_log.astype(F32), dt_bias.astype(F32)]), (0, shard - 2 * heads)
            )[None],
        ],
        axis=0,
    )
    packed_both = jnp.concatenate([packed, lax.ppermute(packed, "col", mirror)], axis=1)
    state_vec = per_channel(conv_state, bias_state)
    state_vecs = jnp.zeros((8, state_all), F32)
    state_vecs = lax.dynamic_update_slice_in_dim(state_vecs, state_vec, col * state_width, 1)
    state_vecs = butterfly(state_vecs, "col")
    value_taps = jnp.concatenate([packed_both[:5], jnp.zeros((3, channels), F32)], axis=0)
    taps = jnp.concatenate([value_taps, state_vecs], axis=1)
    vectors = jnp.concatenate(
        [packed_both[6:7], packed_both[5:6], jnp.zeros((6, channels), F32)], axis=0
    )
    head_own, head_mirror = packed_both[7, :shard], packed_both[7, shard:]
    a_both = jnp.concatenate([head_own[:heads], head_mirror[:heads]])
    dt_both = jnp.concatenate([head_own[heads : 2 * heads], head_mirror[heads : 2 * heads]])
    rate = -jnp.exp(a_both)
    head_rows = jnp.zeros((8, 128), F32)
    head_rows = head_rows.at[0, : 2 * heads].set(dt_both).at[1, : 2 * heads].set(rate)
    head_of = lax.broadcasted_iota(jnp.int32, (128, channels), 1) // HEAD
    spread_one = (head_of == lax.broadcasted_iota(jnp.int32, (128, channels), 0)).astype(BF)
    spread = jnp.concatenate([spread_one, spread_one], axis=0)
    gather = (
        lax.broadcasted_iota(jnp.int32, (channels, 128), 0) // HEAD
        == lax.broadcasted_iota(jnp.int32, (channels, 128), 1)
    ).astype(BF)

    rows_float = group_tokens.astype(F32)
    inv_rms = lax.rsqrt(jnp.mean(rows_float * rows_float, axis=-1, keepdims=True) + EPSILON)
    normed = (rows_float * inv_rms * gain_p).astype(BF)
    raw, act, step_in, step, cum, grow, offs = project(normed, weights, taps, step_full, head_rows)
    states, final_state = scan_states(act, step, cum, spread, channels)

    def cross(values, pairs):
        moved = lax.ppermute(values, "col", pairs)
        return jnp.concatenate([moved[:, shard:], moved[:, :shard]], axis=1)

    early = cross(final_state, forth)
    y0 = scan_forward(act, step, cum, spread, states, channels)
    group_cot = gather_tokens(cot_p, 0)
    graw, y, gm, stats = gate_forward(
        normed, group_cot, gate_full, out_full, y0, act, early, grow, spread, vectors
    )
    by = 1
    while by < group:
        stats = stats + lax.ppermute(stats, "col", flips(cols, by))
        by *= 2
    stats_pad = jnp.pad(stats, ((0, 120), (0, 0)))
    mixed, grad_gate, dy, mix_sums = mix_backward(inner_channels, graw, y, gm, act, stats_pad, vectors)

    def scatter_rows(make):
        parts = []
        for by in range(1, group):
            part = make(lax.rem(place + by, group)).astype(BF)
            parts.append(lax.ppermute(part, "col", ring(by)))
        total = make(place)
        for part in parts:
            total = total + part.astype(F32)
        return total

    after, first_grad = scan_grad_states(dy, act, cum, spread)
    late = cross(first_grad, back)
    branch = scatter_rows(lambda at: mm(at_rows(mixed, at, local), out_full))
    block_out = mine_first((tokens_p.astype(F32) + branch).astype(BF), 1)

    tn = (((0,), (0,)), ((), ()))

    def weight_grad(left, right):
        return lax.dot_general(left, right, tn, preferred_element_type=F32)

    def reduce_weight(values):
        mine, other = jnp.split(values, 2, axis=0)
        kept = mine + swap_core(other)
        return reduce_dp(kept.reshape(dps, -1, values.shape[1]), dp)

    def settle(own, other):
        total = own + lax.ppermute(other.astype(BF), "col", mirror).astype(F32)
        return collect_dp(total, dp)

    grad_out = weight_grad(mixed, group_cot)
    out_mine, out_other = jnp.split(grad_out, 2, axis=1)
    out_kept = (out_mine + swap_core(out_other)).reshape(2, dps, -1, half_width)
    out_piece = reduce_dp(jnp.transpose(out_kept, (1, 0, 2, 3)), dp)
    sum_out = settle(out_piece[0], out_piece[1])

    gate_piece = reduce_weight(weight_grad(normed[HALO:], grad_gate))
    sum_gate = settle(gate_piece[:, :shard], gate_piece[:, shard:])

    gx, gbc_near = scan_backward_near(dy, act, step, cum, spread, states, early, offs)
    ga, grad_step, gbc, head_sums = scan_backward_far(
        dy, act, y, gx, step, cum, step_in, spread, gather, after, late, states, early, offs,
        head_rows, vectors, gbc_near,
    )
    state_part = state_all // group

    def state_slice(values, at):
        return lax.dynamic_slice_in_dim(values, at * state_part, state_part, axis=1)

    gbc_own = state_slice(gbc, place)
    for by in range(1, group):
        gbc_own = gbc_own + lax.ppermute(state_slice(gbc, lax.rem(place + by, group)), "col", ring(by))
    gv, value_sums = conv_back(ga, raw, taps)
    state_taps = state_slice(state_vecs, place)
    gs, state_sums = conv_back(gbc_own, state_slice(raw[:, channels:], place), state_taps)

    state_here = state_slice(state_full, place)
    nt = (((1,), (1,)), ((), ()))

    def back_dot(left, right):
        return lax.dot_general(left, right, nt, preferred_element_type=F32)

    grad_normed = back_dot(gv, value_full) + back_dot(gs, state_here)
    token_part = back_dot(grad_gate, gate_full) + back_dot(grad_step, step_full)
    grad_normed = grad_normed + jnp.pad(token_part, ((HALO, 0), (0, 0)))
    norm_part = jnp.sum(grad_normed * (rows_float * inv_rms), axis=0)
    halo_part = sum(
        lax.ppermute(grad_normed[:HALO].astype(BF), "col", [(group + j, group - 1)]).astype(F32)
        for j in range(group)
    )
    own_grad = scatter_rows(lambda at: at_rows(grad_normed[HALO:], at, local))
    own_grad = own_grad + jnp.pad(halo_part, ((local - HALO, 0), (0, 0)))

    joint = weight_grad(normed, jnp.concatenate([gv, gs], axis=1))
    joint_step = weight_grad(normed[HALO:], grad_step)
    value_piece = reduce_weight(jnp.concatenate([joint, joint_step], axis=1))
    state_piece = jnp.zeros((half_width // dps, state_all), F32)
    state_piece = lax.dynamic_update_slice_in_dim(
        state_piece, value_piece[:, channels : channels + state_part], place * state_part, 1
    )
    state_piece = lax.dynamic_slice_in_dim(
        butterfly(state_piece, "col"), col * state_width, state_width, axis=1
    )
    step_piece = value_piece[:, channels + state_part :]
    settled = jnp.concatenate([value_piece[:, :shard], step_piece[:, :heads]], axis=1)
    leaving = jnp.concatenate([value_piece[:, shard:channels], step_piece[:, heads : 2 * heads]], axis=1)
    settled = settled + lax.ppermute(leaving.astype(BF), "col", mirror).astype(F32)
    sum_joint = collect_dp(jnp.concatenate([settled, state_piece], axis=1), dp)
    sum_value = sum_joint[:, :shard]
    sum_step = sum_joint[:, shard : shard + heads]
    sum_state = sum_joint[:, shard + heads :]

    wide = jnp.concatenate([value_sums[:5], mix_sums[0:1]], axis=0)
    wide_all = jnp.zeros((6, inner_channels), F32)
    wide_all = lax.dynamic_update_slice_in_dim(wide_all, wide[:, :shard], col * shard, 1)
    wide_all = lax.dynamic_update_slice_in_dim(wide_all, wide[:, shard:], (cols - 1 - col) * shard, 1)
    state_wide = jnp.zeros((5, state_all), F32)
    state_wide = lax.dynamic_update_slice_in_dim(state_wide, state_sums[:5], place * state_part, 1)
    skip_heads = jnp.sum(mix_sums[1].reshape(2 * heads, HEAD), axis=1)
    head_parts = jnp.stack([head_sums[0, : 2 * heads] * rate, skip_heads, head_sums[1, : 2 * heads]])
    head_all = jnp.zeros((3, heads * cols), F32)
    head_all = lax.dynamic_update_slice_in_dim(head_all, head_parts[:, :heads], col * heads, 1)
    head_all = lax.dynamic_update_slice_in_dim(head_all, head_parts[:, heads:], (cols - 1 - col) * heads, 1)
    lengths = [wide_all.size, state_wide.size, head_all.size, width]
    flat = jnp.concatenate(
        [wide_all.reshape(-1), state_wide.reshape(-1), head_all.reshape(-1), mine_first(norm_part, 0)]
    )
    flat = jnp.pad(flat, (0, -flat.size % 1024)).reshape(-1, 128)
    for axis in ("row", "dp", "col"):
        flat = butterfly(flat, axis)
    flat = flat.reshape(-1)
    ends = [sum(lengths[: i + 1]) for i in range(4)]
    wide_all = flat[: ends[0]].reshape(6, inner_channels)
    state_wide = flat[ends[0] : ends[1]].reshape(5, state_all)
    head_all = flat[ends[1] : ends[2]].reshape(3, heads * cols)
    norm_total = flat[ends[2] : ends[3]]
    wide_own = lax.dynamic_slice_in_dim(wide_all, col * shard, shard, axis=1)
    state_own = lax.dynamic_slice_in_dim(state_wide, col * state_width, state_width, axis=1)
    head_own = lax.dynamic_slice_in_dim(head_all, col * heads, heads, axis=1)

    own_float = tokens_p.astype(F32)
    own_inv = lax.rsqrt(jnp.mean(own_float * own_float, axis=-1, keepdims=True) + EPSILON)
    unit = own_float * own_inv
    pulled = own_grad * gain_p
    tokens_grad = cot_p.astype(F32) + own_inv * (
        pulled - unit * jnp.mean(pulled * unit, axis=-1, keepdims=True)
    )
    tokens_grad = mine_first(tokens_grad, 1)
    return (
        block_out,
        tokens_grad,
        norm_total,
        sum_gate,
        sum_value,
        sum_state,
        sum_step,
        wide_own[:4].T,
        wide_own[4],
        state_own[:4].T,
        state_own[4],
        head_own[0],
        head_own[1],
        head_own[2],
        wide_own[5],
        sum_out,
    )


def solution(mesh):
    rows = P(("dp", "row", "col"), None)
    grid = P("row", "col")
    vec = P("col")
    taps = P("col", None)
    return jax.shard_map(
        per_device,
        mesh=mesh,
        in_specs=(
            rows, P(), grid, grid, grid, grid, taps, vec, taps, vec, vec, vec, vec, vec,
            P("col", "row"), rows,
        ),
        out_specs=(
            rows, rows, P(), grid, grid, grid, grid, taps, vec, taps, vec, vec, vec, vec, vec,
            P("col", "row"),
        ),
        check_vma=False,
    )
```

time: 1310 us -> 780 us (0.60)
  waiting for transfers between devices: 629 us -> 158 us
  matrix products: 286 us -> 76.1 us
  Pallas kernels: 0 us -> 172 us
  starting transfers between devices: 0.61 us -> 93.8 us
  blocking collectives: 96.8 us -> 51 us
  other arithmetic: 130 us -> 99.3 us
  local copies, waits for them, and re-layouts: 140 us -> 116 us
  between operations: 15.9 us -> 2.35 us
    reduce_scatter x8 -> x0, waiting for transfers between devices: 333 us -> none  [the longest x1 169 us: per_device(): lax.psum_scatter(running, 'col', scatter_dimension=0, tiled=True)]
    dot_general x25 -> x10, matrix products: 278 us -> 76.1 us  [the longest x4 39.1 us: back_dot(): return lax.dot_general(left, right, nt, preferred_element_type=F32)]
    pallas_call x0 -> x10, Pallas kernels: none -> 172 us  [the longest x1 28.5 us: scan_backward_far(): pl.pallas_call(backward_far_kernel, grid=(tokens // Q,), in_specs=[rows,...]
    ppermute x0 -> x57, waiting for transfers between devices: none -> 158 us  [the longest x15 52.2 us: collect_dp(): other = lax.ppermute(piece, 'dp', flips(size, by))]
    psum x1 -> x0, waiting for transfers between devices: 155 us -> none  [per_device(): lax.psum((reduced_rows[0], reduced_rows[1], reduced_rows[2], reduced_rows...]
    all_gather x6 -> x0, waiting for transfers between devices: 138 us -> none  [the longest x1 115 us: per_device(): group_rows = lax.all_gather(normed, 'col', axis=0, tiled=True)]
    ppermute x0 -> x57, starting transfers between devices: none -> 93.8 us  [the longest x9 20.7 us: butterfly(): values = values + lax.ppermute(values, axis, flips(size, by))]
    psum x4 -> x0, blocking collectives: 89.5 us -> none  [the longest x1 50.2 us: per_device(): norm_total = lax.psum(norm_part, ('dp', 'row', 'col'))]
  transfers between devices with their start and end apart: 15 -> 57, of which waited for: 5 -> 24; matrix products, arithmetic and copies ran while one was open for 26% -> 33% of each run, Pallas kernels for 0% -> 17%
where the time goes in v1:
time: 780 us; the launch traced here: 769 us
  Pallas kernels  172 us (22%)
  waiting for transfers between devices  158 us (20%)
  local copies, waits for them, and re-layouts  116 us (15%)
  other arithmetic  99.3 us (13%)
  starting transfers between devices  93.8 us (12%)
  matrix products  76.1 us (10%)
  blocking collectives  51 us (7%)
    ppermute x15, waiting for transfers between devices, collect_dp(): other = lax.ppermute(piece, 'dp', flips(size, by))  52.2 us
    all_gather x1, blocking collectives, per_device(): lax.all_gather(small, 'col', axis=0)  48.5 us
    ppermute x9, waiting for transfers between devices, reduce_dp(): total = total + lax.ppermute(piece, 'dp', flips(size, by)).astype(F32)  44.4 us
    dot_general x4, matrix products, back_dot(): return lax.dot_general(left, right, nt, preferred_element_type=F32)  39.1 us
    ppermute x9, waiting for transfers between devices, butterfly(): values = values + lax.ppermute(values, axis, flips(size, by))  38.6 us
    pallas_call x1, Pallas kernels, scan_backward_far(): pl.pallas_call(backward_far_kernel, grid=(tokens // Q,), in_specs=[rows,...  28.5 us
    dynamic_update_slice x15, local copies, waits for them, and re-layouts, collect_dp(): out = lax.dynamic_update_slice_in_dim(out, other, (dp ^ by) * rows, 0)  27.9 us
    dot_general x4, matrix products, weight_grad(): return lax.dot_general(left, right, tn, preferred_element_type=F32)  25.8 us
  transfers between devices with their start and end apart: 57, of which 24 were waited for; matrix products, arithmetic and copies ran while one was open for 33% of the time, Pallas kernels for 17%

profile of v1, /device:TPU:0, one launch (start us, length us, event | category | flops | bytes accessed | tf_op | source)
XLA Modules:
  0.0 768.6 jit_solution(15903249986479312473)
XLA Ops:
  27.3 48.5 %all-gather = bf16[3072,76]{0,1:T(8,128)(2,1)S(1)} all-gather(bf16[768,76]{0,1:T(8,128)(2,1)S(1)} %pad_maximum_fusion.12), channel_id=2, replica_groups=mesh['dp'=4,'row'=2,'col'=4] {'col'}, dimensions={0}, use_global_device_ids=true | all-gather | bytes 583680 | tf_op jit(solution)/shard_map/all_gather | solution.py:767
  117.6 7.2 collective-permute-done.12
  128.2 7.6 collective-permute-done.5
  136.7 12.7 %collective-permute-done.6 = bf16[384,768]{1,0:T(8,128)(2,1)S(1)} collective-permute-done((bf16[384,768]{1,0:T(8,128)(2,1)}, bf16[384,768]{1,0:T(8,128)(2,1)S(1)}, u32[]{:S(2)}, u32[]{:S(2)}) %collective-permute-start.6) | collective-permute-done | bytes 589856 | tf_op jit(solution)/shard_map/ppermute | solution.py:692
  158.4 12.4 %collective-permute-done.3 = bf16[512,1536]{1,0:T(8,128)(2,1)S(1)} collective-permute-done((bf16[512,1536]{1,0:T(8,128)(2,1)S(1)}, bf16[512,1536]{1,0:T(8,128)(2,1)S(1)}, u32[]{:S(2)}, u32[]{:S(2)}) %collective-permute-start.3) | collective-permute-done | bytes 1572896 | tf_op jit(solution)/shard_map/ppermute | solution.py:748
  176.0 14.2 %pad_maximum_fusion.1.w_ref = bf16[1536,1792]{1,0:T(8,128)(2,1)} fusion(bf16[1536,256]{1,0:T(8,128)(2,1)S(1)} %copy-done.26, bf16[768,1536]{1,0:T(8,128)(2,1)S(1)} %collective-permute-done.14, bf16[768,768]{1,0:T(8,128)(2,1)S(1)} %constant_dynamic-update-slice_fusion.9, bf16[768,768]{1,0:T(8,128)(2,1)S(1)} %copy-done.19), kind=kLoop, calls=%fused_computation.14 | loop fusion | flops 22020096 | bytes 11010048 | tf_op jit(solution)/shard_map/concatenate | solution.py:777
  190.2 18.9 %project.1 = (f32[1040,1792]{1,0:T(8,128)}, bf16[1024,1792]{1,0:T(8,128)(2,1)}, f32[1024,128]{1,0:T(8,128)}, f32[1024,128]{1,0:T(8,128)}, f32[1024,128]{1,0:T(8,...) custom-call(bf16[1040,1536]{1,0:T(8,128)(2,1)} %fusion.3.normed_ref, bf16[1536,1792]{1,0:T(8,128)(2,1)} %pad_maximum_fusion.1.w_ref, ...), custom_call_target="tpu_custom_call" | custom-call | bytes 27000000 | tf_op jit(solution)/shard_map/project/pallas_call | solution.py:117
  209.2 14.6 %scan_states.1 = (f32[9,128,1536]{2,1,0:T(8,128)}, f32[128,1536]{1,0:T(8,128)}) custom-call(bf16[1024,1792]{1,0:T(8,128)(2,1)} %get-tuple-element.69.x_ref.b_ref.c_ref, bf16[1024,1792]{1,0:T(8,128)(2,1)} %get-tuple-element.69.x_ref.b_ref.c_ref, f32[1024,128]{1,0:T(8,128)} %get-tuple-element.70.step_ref, f32[1024,128]{1,0:T(8,128)} %get-tuple-element.71.cum_ref, ...), custom_call_target="tpu_custom_call" | custom-call | bytes 18000000 | tf_op jit(solution)/shard_map/scan_states/pallas_call | solution.py:194
  223.8 13.1 %scan_forward.1.y0_ref = f32[1024,1536]{1,0:T(8,128)} custom-call(bf16[1024,1792]{1,0:T(8,128)(2,1)} %get-tuple-element.69.x_ref.b_ref.c_ref, bf16[1024,1792]{1,0:T(8,128)(2,1)} %get-tuple-element.69.x_ref.b_ref.c_ref, bf16[1024,1792]{1,0:T(8,128)(2,1)} %get-tuple-element.69.x_ref.b_ref.c_ref, f32[1024,128]{1,0:T(8,128)} %get-tuple-element.70.step_ref, ...), custom_call_target="tpu_custom_call" | custom-call | bytes 39000000 | tf_op jit(solution)/shard_map/scan_forward/pallas_call | solution.py:248
  242.0 12.0 %pad_maximum_fusion.2.wg_ref = bf16[1536,1536]{1,0:T(8,128)(2,1)} fusion(bf16[768,1536]{1,0:T(8,128)(2,1)} %collective-permute-done.8, bf16[768,768]{1,0:T(8,128)(2,1)S(1)} %bitcast.129, bf16[768,768]{1,0:T(8,128)(2,1)S(1)} %copy-done.4), kind=kLoop, calls=%fused_computation.20 | loop fusion | flops 14155776 | bytes 9437184 | tf_op jit(solution)/shard_map/concatenate | solution.py:786
  254.0 12.4 %pad_maximum_fusion.3.wo_ref = bf16[1536,1536]{1,0:T(8,128)(2,1)} fusion(bf16[1536,768]{1,0:T(8,128)(2,1)} %collective-permute-done.9, bf16[768,768]{1,0:T(8,128)(2,1)S(1)} %bitcast.125, bf16[768,768]{1,0:T(8,128)(2,1)S(1)} %copy-done.6), kind=kLoop, calls=%fused_computation.21 | loop fusion | flops 14155776 | bytes 9437184 | tf_op jit(solution)/shard_map/concatenate | solution.py:788
  267.5 23.2 %gate_forward.1 = (f32[1024,1536]{1,0:T(8,128)}, f32[1024,1536]{1,0:T(8,128)}, f32[1024,1536]{1,0:T(8,128)}, f32[8,1024]{1,0:T(8,128)}) custom-call(bf16[1040,1536]{1,0:T(8,128)(2,1)} %fusion.3.normed_ref, bf16[1024,1536]{1,0:T(8,128)(2,1)} %constant_dynamic-update-slice_fusion.17.cot_ref, bf16[1536,1536]{1,0:T(8,128)(2,1)} %pad_maximum_fusion.2.wg_ref, ...), custom_call_target="tpu_custom_call" | custom-call | bytes 48000000 | tf_op jit(solution)/shard_map/gate_forward/pallas_call | solution.py:546
  296.5 15.9 %mix_backward.1 = (bf16[1024,1536]{1,0:T(8,128)(2,1)}, bf16[1024,1536]{1,0:T(8,128)(2,1)}, f32[1024,1536]{1,0:T(8,128)}, f32[8,1536]{1,0:T(8,128)}) custom-call(f32[1024,1536]{1,0:T(8,128)} %get-tuple-element.75.graw_ref, f32[1024,1536]{1,0:T(8,128)} %get-tuple-element.76.y_ref, f32[1024,1536]{1,0:T(8,128)} %get-tuple-element.77.gm_ref, ...), custom_call_target="tpu_custom_call" | custom-call | bytes 30000000 | tf_op jit(solution)/shard_map/mix_backward/pallas_call | solution.py:609
  312.4 5.9 convolution_convert_fusion
  318.3 13.7 %scan_grad_states.1 = (f32[8,128,1536]{2,1,0:T(8,128)}, f32[128,1536]{1,0:T(8,128)}) custom-call(f32[1024,1536]{1,0:T(8,128)} %get-tuple-element.80.dy_ref, bf16[1024,1792]{1,0:T(8,128)(2,1)} %get-tuple-element.69.x_ref.b_ref.c_ref, f32[1024,128]{1,0:T(8,128)} %get-tuple-element.71.cum_ref, bf16[256,1536]{1,0:T(8,128)(2,1)} %add_convert_fusion.spread_ref), custom_call_target="tpu_custom_call" | custom-call | bytes 18000000 | tf_op jit(solution)/shard_map/scan_grad_states/pallas_call | solution.py:293
  332.0 25.2 %scan_backward_near.1 = (f32[1024,1536]{1,0:T(8,128)}, f32[1024,256]{1,0:T(8,128)}) custom-call(f32[1024,1536]{1,0:T(8,128)} %get-tuple-element.80.dy_ref, bf16[1024,1792]{1,0:T(8,128)(2,1)} %get-tuple-element.69.x_ref.b_ref.c_ref, bf16[1024,1792]{1,0:T(8,128)(2,1)} %get-tuple-element.69.x_ref.b_ref.c_ref, ...), custom_call_target="tpu_custom_call" | custom-call | bytes 60000000 | tf_op jit(solution)/shard_map/scan_backward_near/pallas_call | solution.py:375
  359.7 7.0 fusion.27
  372.4 7.0 fusion.91
  387.2 28.5 %scan_backward_far.1 = (f32[1024,1536]{1,0:T(8,128)}, bf16[1024,128]{1,0:T(8,128)(2,1)}, f32[1024,256]{1,0:T(8,128)}, f32[8,128]{1,0:T(8,128)}) custom-call(f32[1024,1536]{1,0:T(8,128)} %get-tuple-element.80.dy_ref, bf16[1024,1792]{1,0:T(8,128)(2,1)} %get-tuple-element.69.x_ref.b_ref.c_ref, f32[1024,1536]{1,0:T(8,128)} %get-tuple-element.76.y_ref, ...), custom_call_target="tpu_custom_call" | custom-call | bytes 42000000 | tf_op jit(solution)/shard_map/scan_backward_far/pallas_call | solution.py:467
  415.8 4.7 fusion.73
  424.6 16.4 %conv_back.2 = (bf16[1040,1536]{1,0:T(8,128)(2,1)}, f32[8,1536]{1,0:T(8,128)}) custom-call(f32[1024,1536]{1,0:T(8,128)} %get-tuple-element.87.ga_ref, f32[1040,1792]{1,0:T(8,128)} %get-tuple-element.88.raw_ref, f32[8,1792]{1,0:T(8,128)} %pad_maximum_fusion.15.taps_ref), custom_call_target="tpu_custom_call" | custom-call | bytes 24000000 | tf_op jit(solution)/shard_map/conv_back/pallas_call | solution.py:656
  443.5 12.9 %convolution_add_fusion.1 = f32[1024,1536]{1,0:T(8,128)} fusion(f32[1024,1536]{1,0:T(8,128)} %fusion.73, bf16[1024,1536]{1,0:T(8,128)(2,1)} %get-tuple-element.92, bf16[768,1536]{1,0:T(8,128)(2,1)} %collective-permute-done.8, bf16[768,768]{1,0:T(8,128)(2,1)} %bitcast.130, bf16[768,768]{1,0:T(8,128)(2,1)} %param.22), kind=kOutput, calls=%fused_computation.27 | convolution fusion | flops 4847566848 | bytes 20447232 | tf_op jit(solution)/shard_map/dot_general | solution.py:911
  463.4 4.7 fusion.48
  468.1 16.8 %fusion.4 = (f32[1536]{0:T(1024)S(1)}, f32[1040,1536]{1,0:T(8,128)}) fusion(bf16[1040,1536]{1,0:T(8,128)(2,1)S(1)} %copy-done.2, f32[1040]{0:T(1024)S(1)} %add_rsqrt_fusion, f32[1024,1536]{1,0:T(8,128)} %convolution_add_fusion.1, f32[1040,1536]{1,0:T(8,128)} %fusion.48, bf16[1040,1536]{1,0:T(8,128)(2,1)} %get-tuple-element.89, ...), kind=kOutput, calls=%fused_computation.9 | convolution fusion | flops 4931074560 | bytes 30189632 | tf_op jit(solution)/shard_map/dot_general | solution.py:911
  485.8 6.0 slice.288
  491.8 9.9 %fusion.15 = f32[1536,1664]{1,0:T(8,128)} fusion(bf16[1040,1536]{1,0:T(8,128)(2,1)S(1)} %copy-done, bf16[1040,128]{1,0:T(8,128)(2,1)S(1)} %copy-done.32, bf16[1040,1536]{1,0:T(8,128)(2,1)S(1)} %copy-done.49), kind=kOutput, calls=%fused_computation.30 | convolution fusion | flops 5323202560 | bytes 16879616 | tf_op jit(solution)/shard_map/dot_general | solution.py:870
  502.6 5.6 pad_maximum_fusion
  520.0 4.9 collective-permute-start.29
  524.8 5.3 fusion.23
  530.3 21.7 %collective-permute-done.29 = f32[168,128]{1,0:T(8,128)S(1)} collective-permute-done((f32[168,128]{1,0:T(8,128)S(1)}, f32[168,128]{1,0:T(8,128)S(1)}, u32[]{:S(2)}, u32[]{:S(2)}) %collective-permute-start.29) | collective-permute-done | bytes 86048 | tf_op jit(solution)/shard_map/ppermute | solution.py:677
  552.0 4.1 collective-permute-start.30
  580.0 4.5 slice_add_fusion
  588.2 5.5 collective-permute-done.34
  595.2 11.2 %collective-permute-done.33 = bf16[192,1536]{1,0:T(8,128)(2,1)S(1)} collective-permute-done((bf16[192,1536]{1,0:T(8,128)(2,1)S(1)}, bf16[192,1536]{1,0:T(8,128)(2,1)S(1)}, u32[]{:S(2)}, u32[]{:S(2)}) %collective-permute-start.33) | collective-permute-done | bytes 589856 | tf_op jit(solution)/shard_map/ppermute | solution.py:702
  615.6 7.2 collective-permute-start.42
  623.4 8.3 %collective-permute-done.51 = bf16[2,192,768]{2,1,0:T(8,128)(2,1)S(1)} collective-permute-done((bf16[2,192,768]{2,1,0:T(8,128)(2,1)}, bf16[2,192,768]{2,1,0:T(8,128)(2,1)S(1)}, u32[]{:S(2)}, u32[]{:S(2)}) %collective-permute-start.51) | collective-permute-done | bytes 589856 | tf_op jit(solution)/shard_map/ppermute | solution.py:702
  638.5 7.9 %collective-permute-done.42 = bf16[192,1792]{1,0:T(8,128)(2,1)S(1)} collective-permute-done((bf16[192,1792]{1,0:T(8,128)(2,1)S(1)}, bf16[192,1792]{1,0:T(8,128)(2,1)S(1)}, u32[]{:S(2)}, u32[]{:S(2)}) %collective-permute-start.42) | collective-permute-done | bytes 688160 | tf_op jit(solution)/shard_map/ppermute | solution.py:702
  648.0 10.6 %collective-permute-done.41 = bf16[192,1792]{1,0:T(8,128)(2,1)S(1)} collective-permute-done((bf16[192,1792]{1,0:T(8,128)(2,1)S(1)}, bf16[192,1792]{1,0:T(8,128)(2,1)S(1)}, u32[]{:S(2)}, u32[]{:S(2)}) %collective-permute-start.41) | collective-permute-done | bytes 688160 | tf_op jit(solution)/shard_map/ppermute | solution.py:702
  671.2 3.9 collective-permute-done.43
  675.1 5.2 collective-permute-start.45
  680.4 7.3 collective-permute-done.45
  694.6 4.6 collective-permute-done.54
  701.6 15.0 %collective-permute-done.55 = f32[192,768]{1,0:T(8,128)S(1)} collective-permute-done((f32[192,768]{1,0:T(8,128)S(1)}, f32[192,768]{1,0:T(8,128)S(1)}, u32[]{:S(2)}, u32[]{:S(2)}) %collective-permute-start.55) | collective-permute-done | bytes 589856 | tf_op jit(solution)/shard_map/ppermute | solution.py:692
  719.8 8.9 %dynamic_update_slice.126 = f32[768,844]{0,1:T(8,128)S(1)} dynamic-update-slice(f32[768,844]{0,1:T(8,128)S(1)} %broadcast_in_dim.78, f32[192,844]{0,1:T(8,128)S(1)} %copy.84, s32[]{:T(128)S(6)} %select_n.181, s32[]{:T(128)} %constant.181.clone.1) | dynamic-update-slice | bytes 1296388 | tf_op jit(solution)/shard_map/dynamic_update_slice | solution.py:690
  730.1 10.1 %dynamic_update_slice.127 = f32[768,844]{0,1:T(8,128)S(1)} dynamic-update-slice(f32[768,844]{0,1:T(8,128)S(1)} %dynamic_update_slice.126, f32[192,844]{0,1:T(8,128)S(1)} %copy.85, s32[]{:T(128)S(6)} %select_n.182, s32[]{:T(128)} %constant.181.clone.1) | dynamic-update-slice | bytes 1296388 | tf_op jit(solution)/shard_map/dynamic_update_slice | solution.py:693
  740.2 4.5 collective-permute-done.47
  746.1 7.5 dynamic_update_slice.128
  755.0 7.2 dynamic_update_slice.129
  (405 shorter events, 223.9 us)
Async XLA Ops:
  6.5 148.3 %collective-permute-start = (bf16[512,1536]{1,0:T(8,128)(2,1)}, bf16[512,1536]{1,0:T(8,128)(2,1)}, u32[]{:S(2)}, u32[]{:S(2)}) collective-permute-start(bf16[512,1536]{1,0:T(8,128)(2,1)} %get-tuple-element.187), channel_id=1, source_target_pairs={{0,1},{1,0},{2,3},{3,2},{4,5},{5,4},{6,7},{7,6},{8,9},{9,8},{10,11... | collective-permute-start | bytes 4718600 | tf_op jit(solution)/shard_map/ppermute | solution.py:748
  10.3 146.1 %collective-permute-start.1 = (bf16[16,1536]{1,0:T(8,128)(2,1)S(1)}, bf16[16,1536]{1,0:T(8,128)(2,1)}, u32[]{:S(2)}, u32[]{:S(2)}) collective-permute-start(bf16[16,1536]{1,0:T(8,128)(2,1)S(1)} %slice.272), channel_id=1, source_target_pairs={{1,2},{5,6},{9,10},{13,14},{17,18},{21,22},{25,26},{29,30}} | collective-permute-start | bytes 147464 | tf_op jit(solution)/shard_map/ppermute | solution.py:755
  15.2 97.8 %collective-permute-start.4 = (bf16[384,768]{1,0:T(8,128)(2,1)}, bf16[384,768]{1,0:T(8,128)(2,1)}, u32[]{:S(2)}, u32[]{:S(2)}) collective-permute-start(bf16[384,768]{1,0:T(8,128)(2,1)} %constant_dynamic-slice_fusion.10), channel_id=1, source_target_pairs={{0,3},{1,2},{2,1},{3,0},{4,7},{5,6},{6,5},{7,4},{8,11},{9,10},{10,... | collective-permute-start | bytes 1769480 | tf_op jit(solution)/shard_map/ppermute | solution.py:761
  19.4 87.3 %collective-permute-start.10 = (bf16[192,768]{1,0:T(8,128)(2,1)}, bf16[192,768]{1,0:T(8,128)(2,1)}, u32[]{:S(2)}, u32[]{:S(2)}) collective-permute-start(bf16[192,768]{1,0:T(8,128)(2,1)} %constant_dynamic-slice_fusion.9), channel_id=1, source_target_pairs={{0,3},{1,2},{2,1},{3,0},{4,7},{5,6},{6,5},{7,4},{8,11},{9,10},{10,... | collective-permute-start | bytes 884744 | tf_op jit(solution)/shard_map/ppermute | solution.py:761
  21.1 69.7 %collective-permute-start.16 = (f32[8,256]{1,0:T(8,128)S(1)}, f32[8,256]{1,0:T(8,128)S(1)}, u32[]{:S(2)}, u32[]{:S(2)}) collective-permute-start(f32[8,256]{1,0:T(8,128)S(1)} %dynamic_update_slice.113), channel_id=1, source_target_pairs={{0,1},{1,0},{2,3},{3,2},{4,5},{5,4},{6,7},{7,6},{8,9},{9,8},{10,11... | collective-permute-start | bytes 24584 | tf_op jit(solution)/shard_map/ppermute | solution.py:677
  110.2 14.6 %collective-permute-start.12 = (bf16[192,768]{1,0:T(8,128)(2,1)}, bf16[192,768]{1,0:T(8,128)(2,1)S(1)}, u32[]{:S(2)}, u32[]{:S(2)}) collective-permute-start(bf16[192,768]{1,0:T(8,128)(2,1)} %collective-permute-done.10), channel_id=1, source_target_pairs={{0,16},{8,24},{16,0},{24,8},{1,17},{9,25},{17,1},{25,9},{2,18},{10... | collective-permute-start | bytes 884744 | tf_op jit(solution)/shard_map/ppermute | solution.py:692
  113.0 13.8 %collective-permute-start.13 = (bf16[192,768]{1,0:T(8,128)(2,1)}, bf16[192,768]{1,0:T(8,128)(2,1)S(1)}, u32[]{:S(2)}, u32[]{:S(2)}) collective-permute-start(bf16[192,768]{1,0:T(8,128)(2,1)} %collective-permute-done.10), channel_id=1, source_target_pairs={{0,24},{8,16},{16,8},{24,0},{1,25},{9,17},{17,9},{25,1},{2,26},{10... | collective-permute-start | bytes 884744 | tf_op jit(solution)/shard_map/ppermute | solution.py:692
  115.2 20.7 %collective-permute-start.5 = (bf16[384,768]{1,0:T(8,128)(2,1)}, bf16[384,768]{1,0:T(8,128)(2,1)S(1)}, u32[]{:S(2)}, u32[]{:S(2)}) collective-permute-start(bf16[384,768]{1,0:T(8,128)(2,1)} %collective-permute-done.4), channel_id=1, source_target_pairs={{0,8},{8,0},{16,24},{24,16},{1,9},{9,1},{17,25},{25,17},{2,10},{10... | collective-permute-start | bytes 1769480 | tf_op jit(solution)/shard_map/ppermute | solution.py:692
  124.8 24.6 %collective-permute-start.6 = (bf16[384,768]{1,0:T(8,128)(2,1)}, bf16[384,768]{1,0:T(8,128)(2,1)S(1)}, u32[]{:S(2)}, u32[]{:S(2)}) collective-permute-start(bf16[384,768]{1,0:T(8,128)(2,1)} %collective-permute-done.4), channel_id=1, source_target_pairs={{0,16},{8,24},{16,0},{24,8},{1,17},{9,25},{17,1},{25,9},{2,18},{10... | collective-permute-start | bytes 1769480 | tf_op jit(solution)/shard_map/ppermute | solution.py:692
  126.8 23.5 %collective-permute-start.7 = (bf16[384,768]{1,0:T(8,128)(2,1)}, bf16[384,768]{1,0:T(8,128)(2,1)S(1)}, u32[]{:S(2)}, u32[]{:S(2)}) collective-permute-start(bf16[384,768]{1,0:T(8,128)(2,1)} %collective-permute-done.4), channel_id=1, source_target_pairs={{0,24},{8,16},{16,8},{24,0},{1,25},{9,17},{17,9},{25,1},{2,26},{10... | collective-permute-start | bytes 1769480 | tf_op jit(solution)/shard_map/ppermute | solution.py:692
  135.8 21.1 %collective-permute-start.2 = (bf16[16,1536]{1,0:T(8,128)(2,1)S(1)}, bf16[16,1536]{1,0:T(8,128)(2,1)S(1)}, u32[]{:S(2)}, u32[]{:S(2)}) collective-permute-start(bf16[16,1536]{1,0:T(8,128)(2,1)S(1)} %slice.272), channel_id=1, source_target_pairs={{1,3},{5,7},{9,11},{13,15},{17,19},{21,23},{25,27},{29,31}} | collective-permute-start | bytes 147464 | tf_op jit(solution)/shard_map/ppermute | solution.py:755
  149.4 21.3 %collective-permute-start.3 = (bf16[512,1536]{1,0:T(8,128)(2,1)S(1)}, bf16[512,1536]{1,0:T(8,128)(2,1)S(1)}, u32[]{:S(2)}, u32[]{:S(2)}) collective-permute-start(bf16[512,1536]{1,0:T(8,128)(2,1)S(1)} %copy-done.17), channel_id=1, source_target_pairs={{0,1},{1,0},{2,3},{3,2},{4,5},{5,4},{6,7},{7,6},{8,9},{9,8},{10,11... | collective-permute-start | bytes 4718600 | tf_op jit(solution)/shard_map/ppermute | solution.py:748
  150.3 24.2 %collective-permute-start.14 = (bf16[768,1536]{1,0:T(8,128)(2,1)S(1)}, bf16[768,1536]{1,0:T(8,128)(2,1)S(1)}, u32[]{:S(2)}, u32[]{:S(2)}) collective-permute-start(bf16[768,1536]{1,0:T(8,128)(2,1)S(1)} %pad_maximum_fusion.7), channel_id=1, source_target_pairs={{0,4},{4,0},{1,5},{5,1},{2,6},{6,2},{3,7},{7,3},{8,12},{12,8},{9,1... | collective-permute-start | bytes 7077896 | tf_op jit(solution)/shard_map/ppermute | solution.py:707
  154.7 87.3 %collective-permute-start.8 = (bf16[768,1536]{1,0:T(8,128)(2,1)}, bf16[768,1536]{1,0:T(8,128)(2,1)}, u32[]{:S(2)}, u32[]{:S(2)}) collective-permute-start(bf16[768,1536]{1,0:T(8,128)(2,1)} %pad_maximum_fusion.5), channel_id=1, source_target_pairs={{0,4},{4,0},{1,5},{5,1},{2,6},{6,2},{3,7},{7,3},{8,12},{12,8},{9,1... | collective-permute-start | bytes 7077896 | tf_op jit(solution)/shard_map/ppermute | solution.py:707
  156.4 97.6 %collective-permute-start.9 = (bf16[1536,768]{1,0:T(8,128)(2,1)}, bf16[1536,768]{1,0:T(8,128)(2,1)}, u32[]{:S(2)}, u32[]{:S(2)}) collective-permute-start(bf16[1536,768]{1,0:T(8,128)(2,1)} %pad_maximum_fusion.6), channel_id=1, source_target_pairs={{0,4},{4,0},{1,5},{5,1},{2,6},{6,2},{3,7},{7,3},{8,12},{12,8},{9,1... | collective-permute-start | bytes 7077896 | tf_op jit(solution)/shard_map/ppermute | solution.py:707
  236.8 29.6 %collective-permute-start.18 = (f32[128,1536]{1,0:T(8,128)S(1)}, f32[128,1536]{1,0:T(8,128)S(1)}, u32[]{:S(2)}, u32[]{:S(2)}) collective-permute-start(f32[128,1536]{1,0:T(8,128)S(1)} %copy-done.52), channel_id=1, source_target_pairs={{0,3},{1,2},{4,7},{5,6},{8,11},{9,10},{12,15},{13,14},{16,19},{17,... | collective-permute-start | bytes 2359304 | tf_op jit(solution)/shard_map/ppermute | solution.py:836
  318.3 201.7 %collective-permute-start.20 = (bf16[512,1536]{1,0:T(8,128)(2,1)}, bf16[512,1536]{1,0:T(8,128)(2,1)}, u32[]{:S(2)}, u32[]{:S(2)}) collective-permute-start(bf16[512,1536]{1,0:T(8,128)(2,1)} %convolution_convert_fusion), channel_id=1, source_target_pairs={{0,1},{1,0},{2,3},{3,2},{4,5},{5,4},{6,7},{7,6},{8,9},{9,8},{10,11... | collective-permute-start | bytes 4718600 | tf_op jit(solution)/shard_map/ppermute | solution.py:856
  357.2 27.9 %collective-permute-start.21 = (f32[128,1536]{1,0:T(8,128)}, f32[128,1536]{1,0:T(8,128)}, u32[]{:S(2)}, u32[]{:S(2)}) collective-permute-start(f32[128,1536]{1,0:T(8,128)} %get-tuple-element.85), channel_id=1, source_target_pairs={{3,0},{2,1},{7,4},{6,5},{11,8},{10,9},{15,12},{14,13},{19,16},{18,... | collective-permute-start | bytes 2359304 | tf_op jit(solution)/shard_map/ppermute | solution.py:836
  372.4 200.6 %collective-permute-start.31 = (f32[768,1536]{1,0:T(8,128)}, f32[768,1536]{1,0:T(8,128)}, u32[]{:S(2)}, u32[]{:S(2)}) collective-permute-start(f32[768,1536]{1,0:T(8,128)} %split.91), channel_id=1, source_target_pairs={{0,4},{4,0},{1,5},{5,1},{2,6},{6,2},{3,7},{7,3},{8,12},{12,8},{9,1... | collective-permute-start | bytes 14155784 | tf_op jit(solution)/shard_map/ppermute | solution.py:707
  384.4 195.6 %collective-permute-start.49 = (f32[1536,768]{1,0:T(8,128)}, f32[1536,768]{1,0:T(8,128)}, u32[]{:S(2)}, u32[]{:S(2)}) collective-permute-start(f32[1536,768]{1,0:T(8,128)} %split.95), channel_id=1, source_target_pairs={{0,4},{4,0},{1,5},{5,1},{2,6},{6,2},{3,7},{7,3},{8,12},{12,8},{9,1... | collective-permute-start | bytes 14155784 | tf_op jit(solution)/shard_map/ppermute | solution.py:707
  421.3 37.6 %collective-permute-start.22 = (f32[1024,128]{1,0:T(8,128)}, f32[1024,128]{1,0:T(8,128)}, u32[]{:S(2)}, u32[]{:S(2)}) collective-permute-start(f32[1024,128]{1,0:T(8,128)} %constant_dynamic-slice_fusion.5), channel_id=1, source_target_pairs={{0,1},{1,0},{2,3},{3,2},{4,5},{5,4},{6,7},{7,6},{8,9},{9,8},{10,11... | collective-permute-start | bytes 1572872 | tf_op jit(solution)/shard_map/ppermute | solution.py:902
  501.7 12.4 %collective-permute-start.25 = (bf16[16,1536]{1,0:T(8,128)(2,1)S(1)}, bf16[16,1536]{1,0:T(8,128)(2,1)S(1)}, u32[]{:S(2)}, u32[]{:S(2)}) collective-permute-start(bf16[16,1536]{1,0:T(8,128)(2,1)S(1)} %slice.355), channel_id=1, source_target_pairs={{3,1},{7,5},{11,9},{15,13},{19,17},{23,21},{27,25},{31,29}} | collective-permute-start | bytes 147464 | tf_op jit(solution)/shard_map/ppermute | solution.py:918
  514.1 49.5 %collective-permute-start.23 = (bf16[512,1536]{1,0:T(8,128)(2,1)S(1)}, bf16[512,1536]{1,0:T(8,128)(2,1)S(1)}, u32[]{:S(2)}, u32[]{:S(2)}) collective-permute-start(bf16[512,1536]{1,0:T(8,128)(2,1)S(1)} %dynamic-slice_convert_fusion), channel_id=1, source_target_pairs={{0,1},{1,0},{2,3},{3,2},{4,5},{5,4},{6,7},{7,6},{8,9},{9,8},{10,11... | collective-permute-start | bytes 4718600 | tf_op jit(solution)/shard_map/ppermute | solution.py:856
  519.9 92.2 %collective-permute-start.39 = (f32[768,1792]{1,0:T(8,128)}, f32[768,1792]{1,0:T(8,128)}, u32[]{:S(2)}, u32[]{:S(2)}) collective-permute-start(f32[768,1792]{1,0:T(8,128)} %pad_maximum_fusion), channel_id=1, source_target_pairs={{0,4},{4,0},{1,5},{5,1},{2,6},{6,2},{3,7},{7,3},{8,12},{12,8},{9,1... | collective-permute-start | bytes 16515080 | tf_op jit(solution)/shard_map/ppermute | solution.py:707
  520.0 32.0 %collective-permute-start.29 = (f32[168,128]{1,0:T(8,128)S(1)}, f32[168,128]{1,0:T(8,128)S(1)}, u32[]{:S(2)}, u32[]{:S(2)}) collective-permute-start(f32[168,128]{1,0:T(8,128)S(1)} %add.335), channel_id=1, source_target_pairs={{0,1},{1,0},{2,3},{3,2},{4,5},{5,4},{6,7},{7,6},{8,9},{9,8},{10,11... | collective-permute-start | bytes 258056 | tf_op jit(solution)/shard_map/ppermute | solution.py:677
  576.5 17.2 %collective-permute-start.34 = (bf16[192,1536]{1,0:T(8,128)(2,1)S(1)}, bf16[192,1536]{1,0:T(8,128)(2,1)S(1)}, u32[]{:S(2)}, u32[]{:S(2)}) collective-permute-start(bf16[192,1536]{1,0:T(8,128)(2,1)S(1)} %get-tuple-element.197), channel_id=1, source_target_pairs={{0,24},{8,16},{16,8},{24,0},{1,25},{9,17},{17,9},{25,1},{2,26},{10... | collective-permute-start | bytes 1769480 | tf_op jit(solution)/shard_map/ppermute | solution.py:702
  578.8 27.6 %collective-permute-start.33 = (bf16[192,1536]{1,0:T(8,128)(2,1)S(1)}, bf16[192,1536]{1,0:T(8,128)(2,1)S(1)}, u32[]{:S(2)}, u32[]{:S(2)}) collective-permute-start(bf16[192,1536]{1,0:T(8,128)(2,1)S(1)} %get-tuple-element.198), channel_id=1, source_target_pairs={{0,16},{8,24},{16,0},{24,8},{1,17},{9,25},{17,1},{25,9},{2,18},{10... | collective-permute-start | bytes 1769480 | tf_op jit(solution)/shard_map/ppermute | solution.py:702
  579.3 28.4 %collective-permute-start.32 = (bf16[192,1536]{1,0:T(8,128)(2,1)S(1)}, bf16[192,1536]{1,0:T(8,128)(2,1)S(1)}, u32[]{:S(2)}, u32[]{:S(2)}) collective-permute-start(bf16[192,1536]{1,0:T(8,128)(2,1)S(1)} %get-tuple-element.196), channel_id=1, source_target_pairs={{0,8},{8,0},{16,24},{24,16},{1,9},{9,1},{17,25},{25,17},{2,10},{10... | collective-permute-start | bytes 1769480 | tf_op jit(solution)/shard_map/ppermute | solution.py:702
  585.9 36.8 %collective-permute-start.52 = (bf16[2,192,768]{2,1,0:T(8,128)(2,1)}, bf16[2,192,768]{2,1,0:T(8,128)(2,1)S(1)}, u32[]{:S(2)}, u32[]{:S(2)}) collective-permute-start(bf16[2,192,768]{2,1,0:T(8,128)(2,1)} %get-tuple-element.195), channel_id=1, source_target_pairs={{0,24},{8,16},{16,8},{24,0},{1,25},{9,17},{17,9},{25,1},{2,26},{10... | collective-permute-start | bytes 1769480 | tf_op jit(solution)/shard_map/ppermute | solution.py:702
  593.7 38.0 %collective-permute-start.51 = (bf16[2,192,768]{2,1,0:T(8,128)(2,1)}, bf16[2,192,768]{2,1,0:T(8,128)(2,1)S(1)}, u32[]{:S(2)}, u32[]{:S(2)}) collective-permute-start(bf16[2,192,768]{2,1,0:T(8,128)(2,1)} %get-tuple-element.194), channel_id=1, source_target_pairs={{0,16},{8,24},{16,0},{24,8},{1,17},{9,25},{17,1},{25,9},{2,18},{10... | collective-permute-start | bytes 1769480 | tf_op jit(solution)/shard_map/ppermute | solution.py:702
  606.4 26.6 %collective-permute-start.50 = (bf16[2,192,768]{2,1,0:T(8,128)(2,1)}, bf16[2,192,768]{2,1,0:T(8,128)(2,1)S(1)}, u32[]{:S(2)}, u32[]{:S(2)}) collective-permute-start(bf16[2,192,768]{2,1,0:T(8,128)(2,1)} %get-tuple-element.193), channel_id=1, source_target_pairs={{0,8},{8,0},{16,24},{24,16},{1,9},{9,1},{17,25},{25,17},{2,10},{10... | collective-permute-start | bytes 1769480 | tf_op jit(solution)/shard_map/ppermute | solution.py:702
  608.8 28.0 %collective-permute-start.35 = (bf16[192,768]{1,0:T(8,128)(2,1)}, bf16[192,768]{1,0:T(8,128)(2,1)}, u32[]{:S(2)}, u32[]{:S(2)}) collective-permute-start(bf16[192,768]{1,0:T(8,128)(2,1)} %slice.354), channel_id=1, source_target_pairs={{0,3},{1,2},{2,1},{3,0},{4,7},{5,6},{6,5},{7,4},{8,11},{9,10},{10,... | collective-permute-start | bytes 884744 | tf_op jit(solution)/shard_map/ppermute | solution.py:878
  615.6 30.9 %collective-permute-start.42 = (bf16[192,1792]{1,0:T(8,128)(2,1)S(1)}, bf16[192,1792]{1,0:T(8,128)(2,1)S(1)}, u32[]{:S(2)}, u32[]{:S(2)}) collective-permute-start(bf16[192,1792]{1,0:T(8,128)(2,1)S(1)} %get-tuple-element.191), channel_id=1, source_target_pairs={{0,24},{8,16},{16,8},{24,0},{1,25},{9,17},{17,9},{25,1},{2,26},{10... | collective-permute-start | bytes 2064392 | tf_op jit(solution)/shard_map/ppermute | solution.py:702
  622.7 35.9 %collective-permute-start.41 = (bf16[192,1792]{1,0:T(8,128)(2,1)S(1)}, bf16[192,1792]{1,0:T(8,128)(2,1)S(1)}, u32[]{:S(2)}, u32[]{:S(2)}) collective-permute-start(bf16[192,1792]{1,0:T(8,128)(2,1)S(1)} %get-tuple-element.192), channel_id=1, source_target_pairs={{0,16},{8,24},{16,0},{24,8},{1,17},{9,25},{17,1},{25,9},{2,18},{10... | collective-permute-start | bytes 2064392 | tf_op jit(solution)/shard_map/ppermute | solution.py:702
  631.7 29.6 %collective-permute-start.40 = (bf16[192,1792]{1,0:T(8,128)(2,1)S(1)}, bf16[192,1792]{1,0:T(8,128)(2,1)S(1)}, u32[]{:S(2)}, u32[]{:S(2)}) collective-permute-start(bf16[192,1792]{1,0:T(8,128)(2,1)S(1)} %get-tuple-element.190), channel_id=1, source_target_pairs={{0,8},{8,0},{16,24},{24,16},{1,9},{9,1},{17,25},{25,17},{2,10},{10... | collective-permute-start | bytes 2064392 | tf_op jit(solution)/shard_map/ppermute | solution.py:702
  633.3 28.9 %collective-permute-start.53 = (bf16[192,768]{1,0:T(8,128)(2,1)S(1)}, bf16[192,768]{1,0:T(8,128)(2,1)S(1)}, u32[]{:S(2)}, u32[]{:S(2)}) collective-permute-start(bf16[192,768]{1,0:T(8,128)(2,1)S(1)} %fusion.50), channel_id=1, source_target_pairs={{0,3},{1,2},{2,1},{3,0},{4,7},{5,6},{6,5},{7,4},{8,11},{9,10},{10,... | collective-permute-start | bytes 884744 | tf_op jit(solution)/shard_map/ppermute | solution.py:878
  638.0 53.0 %collective-permute-start.36 = (f32[192,768]{1,0:T(8,128)S(1)}, f32[192,768]{1,0:T(8,128)S(1)}, u32[]{:S(2)}, u32[]{:S(2)}) collective-permute-start(f32[192,768]{1,0:T(8,128)S(1)} %get-tuple-element.185), channel_id=1, source_target_pairs={{0,8},{8,0},{16,24},{24,16},{1,9},{9,1},{17,25},{25,17},{2,10},{10... | collective-permute-start | bytes 1769480 | tf_op jit(solution)/shard_map/ppermute | solution.py:692
  646.5 45.9 %collective-permute-start.37 = (f32[192,768]{1,0:T(8,128)S(1)}, f32[192,768]{1,0:T(8,128)S(1)}, u32[]{:S(2)}, u32[]{:S(2)}) collective-permute-start(f32[192,768]{1,0:T(8,128)S(1)} %get-tuple-element.185), channel_id=1, source_target_pairs={{0,16},{8,24},{16,0},{24,8},{1,17},{9,25},{17,1},{25,9},{2,18},{10... | collective-permute-start | bytes 1769480 | tf_op jit(solution)/shard_map/ppermute | solution.py:692
  658.6 33.9 %collective-permute-start.38 = (f32[192,768]{1,0:T(8,128)S(1)}, f32[192,768]{1,0:T(8,128)S(1)}, u32[]{:S(2)}, u32[]{:S(2)}) collective-permute-start(f32[192,768]{1,0:T(8,128)S(1)} %get-tuple-element.185), channel_id=1, source_target_pairs={{0,24},{8,16},{16,8},{24,0},{1,25},{9,17},{17,9},{25,1},{2,26},{10... | collective-permute-start | bytes 1769480 | tf_op jit(solution)/shard_map/ppermute | solution.py:692
  661.7 8.8 %collective-permute-start.44 = (f32[192,256]{1,0:T(8,128)S(1)}, f32[192,256]{1,0:T(8,128)S(1)}, u32[]{:S(2)}, u32[]{:S(2)}) collective-permute-start(f32[192,256]{1,0:T(8,128)S(1)} %slice_dynamic-update-slice_fusion), channel_id=1, source_target_pairs={{0,1},{1,0},{2,3},{3,2},{4,5},{5,4},{6,7},{7,6},{8,9},{9,8},{10,11... | collective-permute-start | bytes 589832 | tf_op jit(solution)/shard_map/ppermute | solution.py:677
  662.2 12.9 %collective-permute-start.43 = (bf16[192,780]{1,0:T(8,128)(2,1)S(1)}, bf16[192,780]{1,0:T(8,128)(2,1)S(1)}, u32[]{:S(2)}, u32[]{:S(2)}) collective-permute-start(bf16[192,780]{1,0:T(8,128)(2,1)S(1)} %pad_maximum_fusion.11), channel_id=1, source_target_pairs={{0,3},{1,2},{2,1},{3,0},{4,7},{5,6},{6,5},{7,4},{8,11},{9,10},{10,... | collective-permute-start | bytes 898568 | tf_op jit(solution)/shard_map/ppermute | solution.py:937
  670.5 28.7 %collective-permute-start.54 = (f32[192,768]{1,0:T(8,128)S(1)}, f32[192,768]{1,0:T(8,128)S(1)}, u32[]{:S(2)}, u32[]{:S(2)}) collective-permute-start(f32[192,768]{1,0:T(8,128)S(1)} %get-tuple-element.181), channel_id=1, source_target_pairs={{0,8},{8,0},{16,24},{24,16},{1,9},{9,1},{17,25},{25,17},{2,10},{10... | collective-permute-start | bytes 1769480 | tf_op jit(solution)/shard_map/ppermute | solution.py:692
  675.1 12.5 %collective-permute-start.45 = (f32[192,256]{1,0:T(8,128)S(1)}, f32[192,256]{1,0:T(8,128)S(1)}, u32[]{:S(2)}, u32[]{:S(2)}) collective-permute-start(f32[192,256]{1,0:T(8,128)S(1)} %add_dynamic-update-slice_fusion), channel_id=1, source_target_pairs={{0,2},{1,3},{2,0},{3,1},{4,6},{5,7},{6,4},{7,5},{8,10},{9,11},{10,... | collective-permute-start | bytes 589832 | tf_op jit(solution)/shard_map/ppermute | solution.py:677
  687.7 28.9 %collective-permute-start.55 = (f32[192,768]{1,0:T(8,128)S(1)}, f32[192,768]{1,0:T(8,128)S(1)}, u32[]{:S(2)}, u32[]{:S(2)}) collective-permute-start(f32[192,768]{1,0:T(8,128)S(1)} %get-tuple-element.181), channel_id=1, source_target_pairs={{0,16},{8,24},{16,0},{24,8},{1,17},{9,25},{17,1},{25,9},{2,18},{10... | collective-permute-start | bytes 1769480 | tf_op jit(solution)/shard_map/ppermute | solution.py:692
  691.0 26.4 %collective-permute-start.56 = (f32[192,768]{1,0:T(8,128)S(1)}, f32[192,768]{1,0:T(8,128)S(1)}, u32[]{:S(2)}, u32[]{:S(2)}) collective-permute-start(f32[192,768]{1,0:T(8,128)S(1)} %get-tuple-element.181), channel_id=1, source_target_pairs={{0,24},{8,16},{16,8},{24,0},{1,25},{9,17},{17,9},{25,1},{2,26},{10... | collective-permute-start | bytes 1769480 | tf_op jit(solution)/shard_map/ppermute | solution.py:692
  692.4 36.3 %collective-permute-start.46 = (f32[192,844]{1,0:T(8,128)}, f32[192,844]{1,0:T(8,128)}, u32[]{:S(2)}, u32[]{:S(2)}) collective-permute-start(f32[192,844]{1,0:T(8,128)} %pad_maximum_fusion.10), channel_id=1, source_target_pairs={{0,8},{8,0},{16,24},{24,16},{1,9},{9,1},{17,25},{25,17},{2,10},{10... | collective-permute-start | bytes 1944584 | tf_op jit(solution)/shard_map/ppermute | solution.py:692
  692.5 52.2 %collective-permute-start.47 = (f32[192,844]{1,0:T(8,128)}, f32[192,844]{1,0:T(8,128)}, u32[]{:S(2)}, u32[]{:S(2)}) collective-permute-start(f32[192,844]{1,0:T(8,128)} %pad_maximum_fusion.10), channel_id=1, source_target_pairs={{0,16},{8,24},{16,0},{24,8},{1,17},{9,25},{17,1},{25,9},{2,18},{10... | collective-permute-start | bytes 1944584 | tf_op jit(solution)/shard_map/ppermute | solution.py:692
  699.2 54.4 %collective-permute-start.48 = (f32[192,844]{1,0:T(8,128)}, f32[192,844]{1,0:T(8,128)}, u32[]{:S(2)}, u32[]{:S(2)}) collective-permute-start(f32[192,844]{1,0:T(8,128)} %pad_maximum_fusion.10), channel_id=1, source_target_pairs={{0,24},{8,16},{16,8},{24,0},{1,25},{9,17},{17,9},{25,1},{2,26},{10... | collective-permute-start | bytes 1944584 | tf_op jit(solution)/shard_map/ppermute | solution.py:692
  (70 other events, 1098.4 us)

commit v2 on v1

--- a/solution.py
+++ b/solution.py
@@ -68,6 +68,199 @@
     return jax.ShapeDtypeStruct(shape, dtype)
 
 
+def here():
+    return lax.axis_index("dp"), lax.axis_index("row"), lax.axis_index("col")
+
+
+def lanes_at(index, size):
+    return pl.ds(pl.multiple_of(index * size, 128), size)
+
+
+def greet(others):
+    barrier = pltpu.get_barrier_semaphore()
+    for other in others:
+        pl.semaphore_signal(barrier, inc=1, device_id=other, device_id_type=pl.DeviceIdType.MESH)
+    pl.semaphore_wait(barrier, len(others))
+
+
+def import_kernel(
+    cols, dps, tok, wv, wg, wo, sw, tg, vf, gf, of, sf, zeros, tok_vm, w_vm, wo_vm, s_vm, local, send, recv
+):
+    dp, row, col = here()
+    group = cols // 2
+    place = lax.rem(col, group)
+    half, shard = wv.shape
+    count = tok.shape[0]
+    piece, piece_out = half // dps, wo.shape[0] // dps
+    sibling = (dp, 1 - row, col)
+    mirror = (dp, row, cols - 1 - col)
+    col_peer = lambda by: (dp, row, col ^ by)
+    dp_peer = lambda by: (dp ^ by, row, col)
+    greet(
+        [sibling]
+        + [col_peer(by) for by in range(1, cols)]
+        + [dp_peer(by) for by in range(1, dps)]
+    )
+    used = [0]
+    started = []
+
+    def remote(src, dst, device):
+        i = used[0]
+        used[0] += 1
+        return pltpu.make_async_remote_copy(
+            src_ref=src, dst_ref=dst, send_sem=send.at[i], recv_sem=recv.at[i],
+            device_id=device, device_id_type=pl.DeviceIdType.MESH,
+        )
+
+    def launch(src, dst, device):
+        copy = remote(src, dst, device)
+        copy.start()
+        started.append(copy)
+        return copy
+
+    def keep(i, src, dst):
+        copy = pltpu.make_async_copy(src, dst, local.at[i])
+        copy.start()
+        return copy
+
+    my_rows = pl.ds(row * half, half)
+    my_piece = pl.ds(row * half + dp * piece, piece)
+    out_piece = pl.ds(shard + dp * piece_out, piece_out)
+    my_lanes = lanes_at(row, half)
+    own, other = pl.ds(0, shard), pl.ds(shard, shard)
+    src_piece, src_out = pl.ds(dp * piece, piece), pl.ds(dp * piece_out, piece_out)
+
+    staged = [
+        keep(0, sw.at[src_piece, :], s_vm),
+        keep(2, tok, tok_vm),
+        keep(3, wv, w_vm.at[0]),
+        keep(4, wg, w_vm.at[1]),
+        keep(5, wo, wo_vm),
+    ]
+    s_cross = [
+        launch(sw.at[src_piece, :], sf.at[my_piece, lanes_at(col, 128)], col_peer(by))
+        for by in range(1, cols)
+    ]
+    v_cross = launch(wv.at[src_piece, :], vf.at[my_piece, other], mirror)
+    my_tokens = tg.at[pl.ds(HALO + place * count, count), :]
+    tok_cross = [launch(tok, my_tokens, col_peer(by)) for by in range(1, group)]
+    halo_src = tok.at[pl.ds(count - HALO, HALO), :]
+    halo_dst = tg.at[pl.ds(0, HALO), :]
+    halo_at = used[0]
+    used[0] += group
+    halos = [
+        pltpu.make_async_remote_copy(
+            src_ref=halo_src, dst_ref=halo_dst, send_sem=send.at[halo_at + j], recv_sem=recv.at[halo_at],
+            device_id=(dp, row, group + j), device_id_type=pl.DeviceIdType.MESH,
+        )
+        for j in range(group)
+    ]
+
+    @pl.when(col == group - 1)
+    def _():
+        for copy in halos:
+            copy.start()
+
+    zeros[...] = jnp.zeros_like(zeros)
+
+    @pl.when(col < group)
+    def _():
+        clear = pltpu.make_async_copy(zeros, halo_dst, local.at[1])
+        clear.start()
+        clear.wait()
+
+    v_own = launch(wv, vf.at[my_rows, own], sibling)
+    g_own = launch(wg, gf.at[my_rows, own], sibling)
+    o_own = launch(wo, of.at[own, my_lanes], sibling)
+    for copy in staged:
+        copy.wait()
+    small_own = keep(0, s_vm, sf.at[my_piece, lanes_at(col, 128)])
+    kept = [
+        keep(2, tok_vm, my_tokens),
+        keep(3, w_vm.at[0], vf.at[my_rows, own]),
+        keep(4, w_vm.at[1], gf.at[my_rows, own]),
+        keep(5, wo_vm, of.at[own, my_lanes]),
+    ]
+
+    def spread_out(ref):
+        return [launch(ref, ref, dp_peer(by)) for by in range(1, dps)]
+
+    def arrive(copies):
+        for copy in copies:
+            copy.wait_recv()
+
+    arrive(s_cross)
+    small_own.wait()
+    s_dp = spread_out(sf.at[my_piece, :])
+    arrive([v_cross])
+    g_cross = launch(wg.at[src_piece, :], gf.at[my_piece, other], mirror)
+    v_dp = spread_out(vf.at[my_piece, other])
+    arrive([g_cross])
+    o_cross = launch(wo.at[src_out, :], of.at[out_piece, my_lanes], mirror)
+    g_dp = spread_out(gf.at[my_piece, other])
+    arrive(s_dp)
+    last = [launch(sf.at[my_rows, :], sf.at[my_rows, :], sibling)]
+    arrive(v_dp)
+    last += [launch(vf.at[my_rows, other], vf.at[my_rows, other], sibling)]
+    arrive([o_cross])
+    o_dp = spread_out(of.at[out_piece, my_lanes])
+    arrive(g_dp)
+    last += [launch(gf.at[my_rows, other], gf.at[my_rows, other], sibling)]
+    arrive(o_dp)
+    last += [launch(of.at[other, my_lanes], of.at[other, my_lanes], sibling)]
+    arrive(last)
+    arrive([v_own, g_own, o_own])
+    arrive(tok_cross)
+
+    @pl.when(col >= group)
+    def _():
+        halos[0].wait_recv()
+
+    @pl.when(col == group - 1)
+    def _():
+        for copy in halos:
+            copy.wait_send()
+
+    for copy in kept:
+        copy.wait()
+    for copy in started:
+        copy.wait_send()
+
+
+def import_all(cols, dps, tokens, w_value, w_gate, w_out, small):
+    half, shard = w_value.shape
+    count, width = tokens.shape
+    any_spec = pl.BlockSpec(memory_space=pl.ANY)
+    copies = 3 + (cols - 1) + (cols // 2 - 1) + cols // 2 + 3 + 4 * (dps - 1) + 4
+    return pl.pallas_call(
+        partial(import_kernel, cols, dps),
+        in_specs=[any_spec] * 5,
+        out_specs=[any_spec] * 5,
+        out_shape=[
+            sds((HALO + count * (cols // 2), width), BF),
+            sds((2 * half, 2 * shard), BF),
+            sds((2 * half, 2 * shard), BF),
+            sds((2 * shard, 2 * half), BF),
+            sds((2 * half, cols * 128), BF),
+        ],
+        scratch_shapes=[
+            pltpu.VMEM((HALO, width), BF),
+            pltpu.VMEM((count, width), BF),
+            pltpu.VMEM((2, half, shard), BF),
+            pltpu.VMEM((shard, half), BF),
+            pltpu.VMEM((half // dps, 128), BF),
+            pltpu.SemaphoreType.DMA((6,)),
+            pltpu.SemaphoreType.DMA((copies,)),
+            pltpu.SemaphoreType.DMA((copies,)),
+        ],
+        compiler_params=pltpu.CompilerParams(
+            collective_id=1, has_side_effects=True, vmem_limit_bytes=VMEM_LIMIT
+        ),
+        cost_estimate=cost(55),
+        name="import_all",
+    )(tokens, w_value, w_gate, w_out, small)
+
+
 def conv_rows(raw_ref, taps, start, size):
     total = taps[4:5, :] + jnp.zeros((size, taps.shape[1]), F32)
     for k in range(4):
@@ -76,22 +269,36 @@
 
 
 def project_kernel(
-    normed_ref, w_ref, taps_ref, wstep_ref, head_ref,
-    raw_ref, act_ref, stepin_ref, step_ref, cum_ref, grow_ref, offs_ref,
+    tok_ref, gain_ref, w_ref, small_ref, pick_ref, taps_ref, head_ref,
+    raw_ref, act_ref, normed_ref, stepin_ref, step_ref, cum_ref, grow_ref, offs_ref, inv_ref, picked_ref,
 ):
     tokens = act_ref.shape[0]
-    raw_ref[...] = mm(normed_ref[...], w_ref[...])
-    taps = taps_ref[...]
-    for at in range(0, tokens, Q):
-        pre = conv_rows(raw_ref, taps, at, Q)
-        act_ref[at : at + Q, :] = (pre * sigmoid(pre)).astype(BF)
-
-    @pl.when(pl.program_id(0) == 0)
-    def _():
-        step_in = mm(normed_ref[HALO:, :], wstep_ref[...]) + head_ref[0:1, :]
+    at_tile = pl.program_id(0)
+    last = pl.num_programs(0) - 1
+
+    @pl.when(at_tile == 0)
+    def _():
+        for at in [0] + list(range(HALO, HALO + tokens, Q)):
+            size = HALO if at == 0 else Q
+            values = tok_ref[at : at + size, :].astype(F32)
+            inv = lax.rsqrt(jnp.mean(values * values, axis=-1, keepdims=True) + EPSILON)
+            normed_ref[at : at + size, :] = (values * inv * gain_ref[0:1, :]).astype(BF)
+            inv_ref[at : at + size, :] = jnp.broadcast_to(inv, (size, 128))
+
+    @pl.when(at_tile < last)
+    def _():
+        raw_ref[...] = mm(normed_ref[...], w_ref[...])
+
+    @pl.when(at_tile == last)
+    def _():
+        picked = mm(small_ref[...], pick_ref[...]).astype(BF)
+        picked_ref[...] = picked
+        raw_ref[...] = mm(normed_ref[...], picked[:, :TILE])
+        step_in = mm(normed_ref[HALO:, :], picked[:, TILE:]) + head_ref[0:1, :]
         small = jnp.exp(-jnp.abs(step_in))
         plus = 1.0 + small
-        log_part = jnp.where(plus == 1.0, small, jnp.log(plus) * (small / jnp.where(plus == 1.0, 1.0, plus - 1.0)))
+        safe = jnp.where(plus == 1.0, 1.0, plus - 1.0)
+        log_part = jnp.where(plus == 1.0, small, jnp.log(plus) * (small / safe))
         step = jnp.maximum(step_in, 0.0) + log_part
         stepin_ref[...] = step_in
         step_ref[...] = step
@@ -109,43 +316,57 @@
             before = before + cum[Q - 1 : Q, :]
             offs_ref[b + 1 : b + 2, :] = before
 
-
-def project(normed, weights, taps, w_step, head_rows):
-    rows, width = normed.shape
+    taps = taps_ref[...]
+    for at in range(0, tokens, Q):
+        pre = conv_rows(raw_ref, taps, at, Q)
+        act_ref[at : at + Q, :] = (pre * sigmoid(pre)).astype(BF)
+
+
+def project(group_tokens, gain, weights, small, pick, taps, head_rows):
+    rows, width = group_tokens.shape
     tokens = rows - HALO
-    total = weights.shape[1]
+    total = weights.shape[1] + TILE
+    last = weights.shape[1] // TILE - 1
     return pl.pallas_call(
         project_kernel,
         grid=(total // TILE,),
         in_specs=[
             whole((rows, width)),
-            columns(width),
+            whole((1, width)),
+            pl.BlockSpec((width, TILE), lambda j: (0, jnp.minimum(j, last))),
+            whole(small.shape),
+            whole(pick.shape),
             columns(8),
-            whole((width, 128)),
             whole((8, 128)),
         ],
         out_specs=[
             columns(rows),
             columns(tokens),
+            whole((rows, width)),
             whole((tokens, 128)),
             whole((tokens, 128)),
             whole((tokens, 128)),
             whole((tokens, 256)),
             whole((16, 128)),
+            whole((rows, 128)),
+            whole((width, TILE + 128)),
         ],
         out_shape=[
             sds((rows, total)),
             sds((tokens, total), BF),
+            sds((rows, width), BF),
             sds((tokens, 128)),
             sds((tokens, 128)),
             sds((tokens, 128)),
             sds((tokens, 256), BF),
             sds((16, 128)),
+            sds((rows, 128)),
+            sds((width, TILE + 128), BF),
         ],
         compiler_params=params(),
-        cost_estimate=cost(9),
+        cost_estimate=cost(14),
         name="project",
-    )(normed, weights, taps, w_step, head_rows)
+    )(group_tokens, gain, weights, small, pick, taps, head_rows)
 
 
 def expand(per_head, spread):
@@ -666,6 +887,302 @@
     )(ga, raw, taps)
 
 
+def mm_tn(a, b):
+    return lax.dot_general(a, b, (((0,), (0,)), ((), ())), preferred_element_type=F32)
+
+
+def weight_grad_kernel(skips, widths, left_ref, *refs):
+    rights, out_ref = refs[:-1], refs[-1]
+    rows = left_ref.shape[0]
+    at = 0
+    for skip, width, right in zip(skips, widths, rights):
+        out_ref[:, at : at + width] = mm_tn(left_ref[skip:rows, :], right[...])
+        at += width
+
+
+def weight_grad(left, rights):
+    rows, height = left.shape
+    widths = [right.shape[1] for right in rights]
+    skips = [rows - right.shape[0] for right in rights]
+    return pl.pallas_call(
+        partial(weight_grad_kernel, skips, widths),
+        grid=(height // TILE,),
+        in_specs=[columns(rows)] + [whole(right.shape) for right in rights],
+        out_specs=pl.BlockSpec((TILE, sum(widths)), lambda j: (j, 0)),
+        out_shape=sds((height, sum(widths))),
+        compiler_params=params(),
+        cost_estimate=cost(7),
+        name="weight_grad",
+    )(left, *rights)
+
+
+def input_grad_kernel(
+    gv_ref, gg_ref, gs_ref, gt_ref, v_ref, g_ref, s_ref, t_ref, tok_ref, inv_ref, out_ref, low_ref, sums_ref
+):
+    rows = gv_ref.shape[0]
+    total = mm_nt(gv_ref[...], v_ref[...]) + mm_nt(gs_ref[...], s_ref[...])
+    inner = mm_nt(gg_ref[...], g_ref[...]) + mm_nt(gt_ref[...], t_ref[...])
+    out_ref[0:HALO, :] = total[0:HALO, :]
+    out_ref[HALO:, :] = total[HALO:, :] + inner
+    sums = jnp.zeros((1, TILE), F32)
+    for at in [0] + list(range(HALO, rows, Q)):
+        size = HALO if at == 0 else Q
+        part = out_ref[at : at + size, :]
+        low_ref[at : at + size, :] = part.astype(BF)
+        unit = tok_ref[at : at + size, :].astype(F32) * inv_ref[at : at + size, 0:1]
+        sums = sums + jnp.sum(part * unit, axis=0, keepdims=True)
+    sums_ref[...] = jnp.broadcast_to(sums, (8, TILE))
+
+
+def input_grad(gv, gg, gs, gt, w_value, w_gate, w_state, w_step, tokens, inv_rms):
+    rows, channels = gv.shape
+    width = tokens.shape[1]
+    weight = lambda k: pl.BlockSpec((TILE, k), lambda j: (j, 0))
+    return pl.pallas_call(
+        input_grad_kernel,
+        grid=(width // TILE,),
+        in_specs=[
+            whole(gv.shape), whole(gg.shape), whole(gs.shape), whole(gt.shape),
+            weight(channels), weight(channels), weight(gs.shape[1]), weight(128),
+            columns(rows), whole(inv_rms.shape),
+        ],
+        out_specs=[columns(rows), columns(rows), columns(8)],
+        out_shape=[sds((rows, width)), sds((rows, width), BF), sds((8, width))],
+        compiler_params=params(),
+        cost_estimate=cost(12),
+        name="input_grad",
+    )(gv, gg, gs, gt, w_value, w_gate, w_state, w_step, tokens, inv_rms)
+
+
+def settle_kernel(
+    cols, dps, heads, gn, gnb, joint, flat, tok, cot, gain,
+    tg_out, v_out, ext_out, flat_out,
+    mine_a, land_a, mine_b, land_b, send_a, rec_a, send_b, rec_b, tot_a, tot_b,
+    z_send, z_land, step_land, state_land, ext, acc, flat_land,
+    gn_own, gn_land, halo_land, tok_vm, cot_vm, gain_vm, local, send, recv,
+):
+    dp, row, col = here()
+    group = cols // 2
+    place = lax.rem(col, group)
+    half, wide_a = mine_a.shape
+    shard = mine_b.shape[1]
+    piece = tot_a.shape[0]
+    count, width = gn_own.shape
+    sibling = (dp, 1 - row, col)
+    mirror = (dp, row, cols - 1 - col)
+    col_peer = lambda by: (dp, row, col ^ by)
+    dp_peer = lambda by: (dp ^ by, row, col)
+    used = [0]
+    started = []
+
+    def remote(src, dst, device):
+        i = used[0]
+        used[0] += 1
+        return pltpu.make_async_remote_copy(
+            src_ref=src, dst_ref=dst, send_sem=send.at[i], recv_sem=recv.at[i],
+            device_id=device, device_id_type=pl.DeviceIdType.MESH,
+        )
+
+    def launch(src, dst, device):
+        copy = remote(src, dst, device)
+        copy.start()
+        started.append(copy)
+        return copy
+
+    def arrive(copies):
+        for copy in copies:
+            copy.wait_recv()
+
+    kept = [0]
+
+    def keep(src, dst):
+        copy = pltpu.make_async_copy(src, dst, local.at[kept[0]])
+        kept[0] += 1
+        copy.start()
+        return copy
+
+    part_a, part_b = pl.ds(shard, wide_a), pl.ds(0, shard)
+    my_rows, other_rows = pl.ds(row * half, half), pl.ds((1 - row) * half, half)
+    load_a = keep(joint.at[my_rows, part_a], mine_a)
+    load_b = keep(joint.at[my_rows, part_b], mine_b)
+    load_flat = keep(flat, acc)
+    loads = [
+        keep(gn.at[pl.ds(HALO + place * count, count), :], gn_own),
+        keep(tok, tok_vm),
+        keep(cot, cot_vm),
+        keep(gain, gain_vm),
+    ]
+    greet(
+        [sibling]
+        + [col_peer(by) for by in range(1, cols)]
+        + [dp_peer(by) for by in range(1, dps)]
+    )
+    core_a = launch(joint.at[other_rows, part_a], land_a, sibling)
+    core_b = launch(joint.at[other_rows, part_b], land_b, sibling)
+    gn_moves = [
+        launch(gnb.at[pl.ds(HALO + (place ^ by) * count, count), :], gn_land.at[by - 1], col_peer(by))
+        for by in range(1, group)
+    ]
+    halo_at = used[0]
+    used[0] += group
+    halos = [
+        pltpu.make_async_remote_copy(
+            src_ref=gnb.at[pl.ds(0, HALO), :], dst_ref=halo_land.at[j], send_sem=send.at[halo_at + j],
+            recv_sem=recv.at[halo_at + j], device_id=(dp, row, group - 1),
+            device_id_type=pl.DeviceIdType.MESH,
+        )
+        for j in range(group)
+    ]
+    for j in range(group):
+        pl.when(col == group + j)(halos[j].start)
+
+    flat_steps = [sibling]
+    by = 1
+    while by < dps:
+        flat_steps.append(dp_peer(by))
+        by *= 2
+    by = 1
+    while by < cols:
+        flat_steps.append(col_peer(by))
+        by *= 2
+    flat_moves = []
+    flat_taken = [0]
+
+    def flat_next():
+        if flat_taken[0] < len(flat_moves):
+            flat_moves[-1].wait_recv()
+            flat_moves[-1].wait_send()
+            acc[...] += flat_land[flat_taken[0]]
+            flat_taken[0] += 1
+        if len(flat_moves) < len(flat_steps):
+            at = len(flat_moves)
+            move = remote(acc, flat_land.at[at], flat_steps[at])
+            move.start()
+            flat_moves.append(move)
+
+    load_flat.wait()
+    flat_next()
+
+    def hand_out(load, core, mine, land, total, sends, recs):
+        load.wait()
+        arrive([core])
+        moves = []
+        for by in range(1, dps):
+            rows = pl.ds(pl.multiple_of((dp ^ by) * piece, 16), piece)
+            sends[by - 1] = (mine[rows, :] + land[rows, :]).astype(BF)
+            moves.append(launch(sends.at[by - 1], recs.at[by - 1], dp_peer(by)))
+        rows = pl.ds(pl.multiple_of(dp * piece, 16), piece)
+        total[...] = mine[rows, :] + land[rows, :]
+        return moves
+
+    moves_a = hand_out(load_a, core_a, mine_a, land_a, tot_a, send_a, rec_a)
+    flat_next()
+    moves_b = hand_out(load_b, core_b, mine_b, land_b, tot_b, send_b, rec_b)
+    flat_next()
+    arrive(moves_a)
+    for by in range(1, dps):
+        tot_a[...] += rec_a[by - 1].astype(F32)
+    z_send[...] = tot_a[:, 0:shard].astype(BF)
+    z_move = launch(z_send, z_land, mirror)
+    step_move = launch(tot_a.at[:, pl.ds(shard + N, 128)], step_land, mirror)
+    state_block = tot_a.at[:, pl.ds(shard, N)]
+    state_moves = [launch(state_block, state_land.at[col], col_peer(by)) for by in range(1, cols)]
+    state_land[col] = tot_a[:, shard : shard + N]
+    flat_next()
+    arrive(moves_b)
+    for by in range(1, dps):
+        tot_b[...] += rec_b[by - 1].astype(F32)
+    arrive([z_move, step_move])
+    tot_b[...] += z_land[...].astype(F32)
+    ext[:, 0:128] = tot_a[:, shard + N : shard + N + 128] + pltpu.roll(step_land[...], 128 - heads, 1)
+    out_rows = pl.ds(dp * piece, piece)
+    v_moves = [launch(tot_b, v_out.at[out_rows, :], dp_peer(by)) for by in range(1, dps)]
+    v_keep = keep(tot_b, v_out.at[out_rows, :])
+    arrive(state_moves)
+    part = col // 2
+    ext[:, 128:256] = state_land[part] + state_land[part + group]
+    e_moves = [launch(ext, ext_out.at[out_rows, :], dp_peer(by)) for by in range(1, dps)]
+    e_keep = keep(ext, ext_out.at[out_rows, :])
+    flat_next()
+    for copy in loads:
+        copy.wait()
+    arrive(gn_moves)
+    for by in range(1, group):
+        gn_own[...] += gn_land[by - 1].astype(F32)
+
+    @pl.when(col == group - 1)
+    def _():
+        for copy in halos:
+            copy.wait_recv()
+        for j in range(group):
+            gn_own[count - HALO :, :] += halo_land[j].astype(F32)
+
+    for j in range(group):
+        pl.when(col == group + j)(halos[j].wait_send)
+    flat_next()
+    step = 64
+    for at in range(0, count, step):
+        rows = slice(at, at + step)
+        values = tok_vm[rows, :].astype(F32)
+        inv = lax.rsqrt(jnp.mean(values * values, axis=-1, keepdims=True) + EPSILON)
+        unit = values * inv
+        pulled = gn_own[rows, :] * gain_vm[0:1, :]
+        mean = jnp.mean(pulled * unit, axis=-1, keepdims=True)
+        gn_own[rows, :] = cot_vm[rows, :].astype(F32) + inv * (pulled - unit * mean)
+    tg_keep = keep(gn_own, tg_out)
+    while flat_taken[0] < len(flat_steps):
+        flat_next()
+    flat_keep = keep(acc, flat_out)
+    arrive(v_moves)
+    arrive(e_moves)
+    for copy in [v_keep, e_keep, tg_keep, flat_keep]:
+        copy.wait()
+    for copy in started:
+        copy.wait_send()
+
+
+def settle(cols, dps, heads, gn, gnb, joint, flat, tokens, cotangent, gain, shard):
+    width, wide = joint.shape
+    half, wide_a = width // 2, wide - shard
+    piece = half // dps
+    count = tokens.shape[0]
+    group = cols // 2
+    any_spec = pl.BlockSpec(memory_space=pl.ANY)
+    steps = (dps.bit_length() - 1) + (cols.bit_length() - 1) + 1
+    copies = 2 + (group - 1) + group + steps + 4 * (dps - 1) + 2 + (cols - 1)
+    vmem = pltpu.VMEM
+    return pl.pallas_call(
+        partial(settle_kernel, cols, dps, heads),
+        in_specs=[any_spec] * 7,
+        out_specs=[any_spec] * 4,
+        out_shape=[
+            sds((count, width)), sds((half, shard)), sds((half, 256)), sds(flat.shape),
+        ],
+        scratch_shapes=[
+            vmem((half, wide_a), F32), vmem((half, wide_a), F32),
+            vmem((half, shard), F32), vmem((half, shard), F32),
+            vmem((dps - 1, piece, wide_a), BF), vmem((dps - 1, piece, wide_a), BF),
+            vmem((dps - 1, piece, shard), BF), vmem((dps - 1, piece, shard), BF),
+            vmem((piece, wide_a), F32), vmem((piece, shard), F32),
+            vmem((piece, shard), BF), vmem((piece, shard), BF),
+            vmem((piece, 128), F32), vmem((cols, piece, N), F32),
+            vmem((piece, 256), F32),
+            vmem(flat.shape, F32), vmem((steps,) + flat.shape, F32),
+            vmem((count, width), F32), vmem((max(group - 1, 1), count, width), BF),
+            vmem((group, HALO, width), BF),
+            vmem((count, width), BF), vmem((count, width), BF), vmem((1, width), F32),
+            pltpu.SemaphoreType.DMA((11,)),
+            pltpu.SemaphoreType.DMA((copies,)),
+            pltpu.SemaphoreType.DMA((copies,)),
+        ],
+        compiler_params=pltpu.CompilerParams(
+            collective_id=2, has_side_effects=True, vmem_limit_bytes=VMEM_LIMIT
+        ),
+        cost_estimate=cost(90),
+        name="settle",
+    )(gn, gnb, joint, flat, tokens, cotangent, gain)
+
+
 def flips(size, by):
     return [(i, i ^ by) for i in range(size)]
 
@@ -730,62 +1247,31 @@
     def ring(by):
         return [(i, (i // group) * group + (i % group + by) % group) for i in range(cols)]
 
-    def mine_first(values, axis):
-        a, b = jnp.split(values, 2, axis=axis)
-        return jnp.where(row == 0, values, jnp.concatenate([b, a], axis=axis))
-
-    def own_then_mirror(own, other):
-        return jnp.concatenate([own, other], axis=0)
-
-    tokens_p = mine_first(tokens, 1)
-    cot_p = mine_first(cotangent, 1)
-    gain_p = mine_first(norm_gain.astype(F32), 0)
-
-    def gather_tokens(values, first_rows):
-        out = jnp.zeros((first_rows + span, width), values.dtype)
-        out = lax.dynamic_update_slice_in_dim(out, values, first_rows + place * local, 0)
+    state_width = w_state.shape[1]
+    small = jnp.pad(
+        jnp.concatenate([w_state, w_step], axis=1), ((0, 0), (0, 128 - state_width - heads))
+    )
+    group_tokens, value_full, gate_full, out_full, small_full = import_all(
+        cols, dps, tokens, w_value, w_gate, w_out, small
+    )
+    from_col = lax.broadcasted_iota(jnp.int32, (cols * 128, TILE + 128), 0) // 128
+    from_lane = lax.broadcasted_iota(jnp.int32, (cols * 128, TILE + 128), 0) % 128
+    to = lax.broadcasted_iota(jnp.int32, (cols * 128, TILE + 128), 1)
+    head_to = to - TILE
+    is_state = (to < TILE) & (from_lane < state_width) & (from_col * state_width + from_lane == to)
+    is_own = (from_col == col) & (head_to < heads) & (from_lane == state_width + head_to)
+    is_mirror = (from_col == cols - 1 - col) & (head_to >= heads) & (head_to < 2 * heads)
+    is_mirror = is_mirror & (from_lane == state_width + head_to - heads)
+    pick = (is_state | ((head_to >= 0) & (is_own | is_mirror))).astype(BF)
+
+    def gather_tokens(values):
+        out = jnp.zeros((span, width), values.dtype)
+        out = lax.dynamic_update_slice_in_dim(out, values, place * local, 0)
         for by in range(1, group):
             other = lax.ppermute(values, "col", ring(by))
             at = lax.rem(place - by + group, group)
-            out = lax.dynamic_update_slice_in_dim(out, other, first_rows + at * local, 0)
+            out = lax.dynamic_update_slice_in_dim(out, other, at * local, 0)
         return out
-
-    group_tokens = gather_tokens(tokens_p, HALO)
-    halo = sum(
-        lax.ppermute(tokens_p[local - HALO :], "col", [(group - 1, group + j)]) for j in range(group)
-    )
-    group_tokens = lax.dynamic_update_slice_in_dim(group_tokens, halo, 0, 0)
-
-    def import_shard(values):
-        piece = values.shape[0] // dps
-        return collect_dp(lax.ppermute(at_rows(values, dp, piece), "col", mirror), dp)
-
-    mirror_value = import_shard(w_value)
-    value_rows = jnp.concatenate([w_value, mirror_value], axis=1)
-    value_other = swap_core(value_rows)
-    small = jnp.concatenate([w_state, w_step], axis=1)
-    small = lax.all_gather(lax.all_gather(small, "col", axis=0), "row", axis=1, tiled=True)
-    small = mine_first(small, 1)
-    state_width = w_state.shape[1]
-    state_full = jnp.transpose(small[:, :, :state_width], (1, 0, 2)).reshape(width, state_all)
-    step_own = lax.dynamic_index_in_dim(small, col, 0, keepdims=False)[:, state_width:]
-    step_mirror = lax.dynamic_index_in_dim(small, cols - 1 - col, 0, keepdims=False)[:, state_width:]
-    step_full = jnp.pad(
-        jnp.concatenate([step_own, step_mirror], axis=1), ((0, 0), (0, 128 - 2 * heads))
-    )
-    value_full = jnp.concatenate([value_rows, value_other], axis=0)
-    weights = jnp.concatenate([value_full, state_full], axis=1)
-    gate_out = import_shard(jnp.concatenate([w_gate.reshape(dps, -1, shard), w_out.reshape(dps, -1, half_width)], axis=1).reshape(-1, shard)) if shard == half_width else None
-    if gate_out is None:
-        mirror_gate, mirror_out = import_shard(w_gate), import_shard(w_out)
-    else:
-        gate_out = gate_out.reshape(dps, 2, -1, shard)
-        mirror_gate = gate_out[:, 0].reshape(half_width, shard)
-        mirror_out = gate_out[:, 1].reshape(shard, half_width)
-    gate_rows = jnp.concatenate([w_gate, mirror_gate], axis=1)
-    gate_full = jnp.concatenate([gate_rows, swap_core(gate_rows)], axis=0)
-    out_rows = jnp.concatenate([w_out, mirror_out], axis=0)
-    out_full = jnp.concatenate([out_rows, swap_core(out_rows)], axis=1)
 
     def per_channel(own_taps, own_bias):
         taps = jnp.concatenate([own_taps.astype(F32).T, own_bias.astype(F32)[None]], axis=0)
@@ -826,10 +1312,10 @@
         == lax.broadcasted_iota(jnp.int32, (channels, 128), 1)
     ).astype(BF)
 
-    rows_float = group_tokens.astype(F32)
-    inv_rms = lax.rsqrt(jnp.mean(rows_float * rows_float, axis=-1, keepdims=True) + EPSILON)
-    normed = (rows_float * inv_rms * gain_p).astype(BF)
-    raw, act, step_in, step, cum, grow, offs = project(normed, weights, taps, step_full, head_rows)
+    gain = norm_gain.astype(F32)
+    raw, act, normed, step_in, step, cum, grow, offs, inv_rms, picked = project(
+        group_tokens, gain[None], value_full, small_full, pick, taps, head_rows
+    )
     states, final_state = scan_states(act, step, cum, spread, channels)
 
     def cross(values, pairs):
@@ -838,7 +1324,7 @@
 
     early = cross(final_state, forth)
     y0 = scan_forward(act, step, cum, spread, states, channels)
-    group_cot = gather_tokens(cot_p, 0)
+    group_cot = gather_tokens(cotangent)
     graw, y, gm, stats = gate_forward(
         normed, group_cot, gate_full, out_full, y0, act, early, grow, spread, vectors
     )
@@ -862,30 +1348,30 @@
     after, first_grad = scan_grad_states(dy, act, cum, spread)
     late = cross(first_grad, back)
     branch = scatter_rows(lambda at: mm(at_rows(mixed, at, local), out_full))
-    block_out = mine_first((tokens_p.astype(F32) + branch).astype(BF), 1)
-
-    tn = (((0,), (0,)), ((), ()))
-
-    def weight_grad(left, right):
-        return lax.dot_general(left, right, tn, preferred_element_type=F32)
+    block_out = (tokens.astype(F32) + branch).astype(BF)
+
+    def halves(values, axis):
+        size = values.shape[axis] // 2
+        mine = lax.dynamic_slice_in_dim(values, row * size, size, axis)
+        return mine, lax.dynamic_slice_in_dim(values, (1 - row) * size, size, axis)
 
     def reduce_weight(values):
-        mine, other = jnp.split(values, 2, axis=0)
+        mine, other = halves(values, 0)
         kept = mine + swap_core(other)
         return reduce_dp(kept.reshape(dps, -1, values.shape[1]), dp)
 
-    def settle(own, other):
+    def settle_shards(own, other):
         total = own + lax.ppermute(other.astype(BF), "col", mirror).astype(F32)
         return collect_dp(total, dp)
 
-    grad_out = weight_grad(mixed, group_cot)
-    out_mine, out_other = jnp.split(grad_out, 2, axis=1)
+    grad_out = weight_grad(mixed, [group_cot])
+    out_mine, out_other = halves(grad_out, 1)
     out_kept = (out_mine + swap_core(out_other)).reshape(2, dps, -1, half_width)
     out_piece = reduce_dp(jnp.transpose(out_kept, (1, 0, 2, 3)), dp)
-    sum_out = settle(out_piece[0], out_piece[1])
-
-    gate_piece = reduce_weight(weight_grad(normed[HALO:], grad_gate))
-    sum_gate = settle(gate_piece[:, :shard], gate_piece[:, shard:])
+    sum_out = settle_shards(out_piece[0], out_piece[1])
+
+    gate_piece = reduce_weight(weight_grad(normed, [grad_gate]))
+    sum_gate = settle_shards(gate_piece[:, :shard], gate_piece[:, shard:])
 
     gx, gbc_near = scan_backward_near(dy, act, step, cum, spread, states, early, offs)
     ga, grad_step, gbc, head_sums = scan_backward_far(
@@ -904,41 +1390,11 @@
     state_taps = state_slice(state_vecs, place)
     gs, state_sums = conv_back(gbc_own, state_slice(raw[:, channels:], place), state_taps)
 
-    state_here = state_slice(state_full, place)
-    nt = (((1,), (1,)), ((), ()))
-
-    def back_dot(left, right):
-        return lax.dot_general(left, right, nt, preferred_element_type=F32)
-
-    grad_normed = back_dot(gv, value_full) + back_dot(gs, state_here)
-    token_part = back_dot(grad_gate, gate_full) + back_dot(grad_step, step_full)
-    grad_normed = grad_normed + jnp.pad(token_part, ((HALO, 0), (0, 0)))
-    norm_part = jnp.sum(grad_normed * (rows_float * inv_rms), axis=0)
-    halo_part = sum(
-        lax.ppermute(grad_normed[:HALO].astype(BF), "col", [(group + j, group - 1)]).astype(F32)
-        for j in range(group)
-    )
-    own_grad = scatter_rows(lambda at: at_rows(grad_normed[HALO:], at, local))
-    own_grad = own_grad + jnp.pad(halo_part, ((local - HALO, 0), (0, 0)))
-
-    joint = weight_grad(normed, jnp.concatenate([gv, gs], axis=1))
-    joint_step = weight_grad(normed[HALO:], grad_step)
-    value_piece = reduce_weight(jnp.concatenate([joint, joint_step], axis=1))
-    state_piece = jnp.zeros((half_width // dps, state_all), F32)
-    state_piece = lax.dynamic_update_slice_in_dim(
-        state_piece, value_piece[:, channels : channels + state_part], place * state_part, 1
-    )
-    state_piece = lax.dynamic_slice_in_dim(
-        butterfly(state_piece, "col"), col * state_width, state_width, axis=1
-    )
-    step_piece = value_piece[:, channels + state_part :]
-    settled = jnp.concatenate([value_piece[:, :shard], step_piece[:, :heads]], axis=1)
-    leaving = jnp.concatenate([value_piece[:, shard:channels], step_piece[:, heads : 2 * heads]], axis=1)
-    settled = settled + lax.ppermute(leaving.astype(BF), "col", mirror).astype(F32)
-    sum_joint = collect_dp(jnp.concatenate([settled, state_piece], axis=1), dp)
-    sum_value = sum_joint[:, :shard]
-    sum_step = sum_joint[:, shard : shard + heads]
-    sum_state = sum_joint[:, shard + heads :]
+    state_here, step_here = state_slice(picked, place), picked[:, TILE:]
+    grad_normed, grad_normed_low, norm_sums = input_grad(
+        gv, grad_gate, gs, grad_step, value_full, gate_full, state_here, step_here, group_tokens, inv_rms
+    )
+    joint = weight_grad(normed, [gv, jnp.pad(gs, ((0, 0), (0, N - state_part))), grad_step])
 
     wide = jnp.concatenate([value_sums[:5], mix_sums[0:1]], axis=0)
     wide_all = jnp.zeros((6, inner_channels), F32)
@@ -953,11 +1409,16 @@
     head_all = lax.dynamic_update_slice_in_dim(head_all, head_parts[:, heads:], (cols - 1 - col) * heads, 1)
     lengths = [wide_all.size, state_wide.size, head_all.size, width]
     flat = jnp.concatenate(
-        [wide_all.reshape(-1), state_wide.reshape(-1), head_all.reshape(-1), mine_first(norm_part, 0)]
+        [wide_all.reshape(-1), state_wide.reshape(-1), head_all.reshape(-1), norm_sums[0]]
     )
     flat = jnp.pad(flat, (0, -flat.size % 1024)).reshape(-1, 128)
-    for axis in ("row", "dp", "col"):
-        flat = butterfly(flat, axis)
+    tokens_grad, sum_value, extra, flat = settle(
+        cols, dps, heads, grad_normed, grad_normed_low, joint, flat, tokens, cotangent, gain[None], shard
+    )
+    sum_step = extra[:, :heads]
+    sum_state = lax.dynamic_slice_in_dim(
+        extra, 128 + lax.rem(col, cols // group) * state_width, state_width, axis=1
+    )
     flat = flat.reshape(-1)
     ends = [sum(lengths[: i + 1]) for i in range(4)]
     wide_all = flat[: ends[0]].reshape(6, inner_channels)
@@ -968,14 +1429,6 @@
     state_own = lax.dynamic_slice_in_dim(state_wide, col * state_width, state_width, axis=1)
     head_own = lax.dynamic_slice_in_dim(head_all, col * heads, heads, axis=1)
 
-    own_float = tokens_p.astype(F32)
-    own_inv = lax.rsqrt(jnp.mean(own_float * own_float, axis=-1, keepdims=True) + EPSILON)
-    unit = own_float * own_inv
-    pulled = own_grad * gain_p
-    tokens_grad = cot_p.astype(F32) + own_inv * (
-        pulled - unit * jnp.mean(pulled * unit, axis=-1, keepdims=True)
-    )
-    tokens_grad = mine_first(tokens_grad, 1)
     return (
         block_out,
         tokens_grad,

time: 780 us -> 655 us (0.84)
  Pallas kernels: 172 us -> 417 us
  local copies, waits for them, and re-layouts: 116 us -> 48.2 us
  other arithmetic: 99.3 us -> 32 us
  matrix products: 76.1 us -> 12.3 us
  starting transfers between devices: 93.8 us -> 33.5 us
  waiting for transfers between devices: 158 us -> 101 us
  blocking collectives: 51 us -> 0 us
    pallas_call x0 -> x6, Pallas kernels: none -> 242 us  [the longest x1 104 us: import_all(): pl.pallas_call(partial(import_kernel, cols, dps), in_specs=[any_spec] * 5...]
    dot_general x8 -> x0, matrix products: 64.9 us -> none  [the longest x4 39.1 us: back_dot(): return lax.dot_general(left, right, nt, preferred_element_type=F32)]
    all_gather x2 -> x0, blocking collectives: 51 us -> none  [the longest x1 48.5 us: per_device(): lax.all_gather(small, 'col', axis=0)]
    concatenate x12 -> x1, other arithmetic: 50.1 us -> 0.81 us  [per_device(): jnp.concatenate([w_state, w_step], axis=1)]
    ppermute x9 -> x2, waiting for transfers between devices: 38.6 us -> 0.01 us  [butterfly(): values = values + lax.ppermute(values, axis, flips(size, by))]
    dynamic_update_slice x15 -> x6, local copies, waits for them, and re-layouts: 27.9 us -> 0.27 us  [collect_dp(): out = lax.dynamic_update_slice_in_dim(out, other, (dp ^ by) * rows, 0)]
    ppermute x9 -> x2, starting transfers between devices: 17.3 us -> 0.01 us  [settle_shards(): total = own + lax.ppermute(other.astype(BF), 'col', mirror).astype(F32)]
    ppermute x9 -> x2, starting transfers between devices: 20.7 us -> 4.42 us  [butterfly(): values = values + lax.ppermute(values, axis, flips(size, by))]
  transfers between devices with their start and end apart: 57 -> 25, of which waited for: 24 -> 12; matrix products, arithmetic and copies ran while one was open for 33% -> 11% of each run, Pallas kernels for 17% -> 57%
where the time goes in v2:
time: 655 us; the launch traced here: 646 us
  Pallas kernels  417 us (64%)
  waiting for transfers between devices  101 us (15%)
  local copies, waits for them, and re-layouts  48.2 us (7%)
  starting transfers between devices  33.5 us (5%)
  other arithmetic  32 us (5%)
  matrix products  12.3 us (2%)
    pallas_call x1, Pallas kernels, import_all(): pl.pallas_call(partial(import_kernel, cols, dps), in_specs=[any_spec] * 5...  104 us
    pallas_call x1, Pallas kernels, settle(): pl.pallas_call(partial(settle_kernel, cols, dps, heads), in_specs=[any_sp...  85.8 us
    ppermute x6, waiting for transfers between devices, collect_dp(): other = lax.ppermute(piece, 'dp', flips(size, by))  37.8 us
    pallas_call x3, Pallas kernels, weight_grad(): pl.pallas_call(partial(weight_grad_kernel, skips, widths), grid=(height /...  33.8 us
    ppermute x6, waiting for transfers between devices, reduce_dp(): total = total + lax.ppermute(piece, 'dp', flips(size, by)).astype(F32)  30 us
    pallas_call x1, Pallas kernels, scan_backward_far(): pl.pallas_call(backward_far_kernel, grid=(tokens // Q,), in_specs=[rows,...  28.1 us
    pallas_call x1, Pallas kernels, scan_backward_near(): pl.pallas_call(backward_near_kernel, grid=(tokens // Q,), in_specs=[rows,...  25.2 us
    pallas_call x1, Pallas kernels, gate_forward(): pl.pallas_call(gate_kernel, grid=(channels // TILE,), in_specs=[whole((ro...  23.1 us
  transfers between devices with their start and end apart: 25, of which 12 were waited for; matrix products, arithmetic and copies ran while one was open for 11% of the time, Pallas kernels for 57%

profile of v2, /device:TPU:0, one launch (start us, length us, event | category | flops | bytes accessed | tf_op | source)
XLA Modules:
  0.0 645.6 jit_solution(11753857734497216826)
XLA Ops:
  1.6 3.1 collective-permute-start.1
  10.2 2.4 collective-permute-start
  13.5 2.2 fusion.13.gather_ref
  18.2 1.6 fusion.12.pick_ref
  25.4 104.0 %import_all.1 = (bf16[1040,1536]{1,0:T(8,128)(2,1)}, bf16[1536,1536]{1,0:T(8,128)(2,1)}, bf16[1536,1536]{1,0:T(8,128)(2,1)}, bf16[1536,1536]{1,0:T(8,128)(2,1)}, bf16[1536,512]{1,0:T(8,128)(2,1)}) custom-call(bf16[512,1536]{1,0:T(8,128)(2,1)} %tok.3, bf16[768,768]{1,0:T(8,128)(2,1)} %wv.1, bf16[768,768]{1,0:T(8,128)(2,1)} %wg.1, bf16[768,768]{1,0:T(8,128)(2,1)} %wo.1, ...), custom_call_target="tpu_custom_call" | custom-call | bytes 165000000 | tf_op jit(solution)/shard_map/import_all/pallas_call | solution.py:235
  132.0 22.3 %project.1 = (f32[1040,1792]{1,0:T(8,128)}, bf16[1024,1792]{1,0:T(8,128)(2,1)}, bf16[1040,1536]{1,0:T(8,128)(2,1)}, f32[1024,128]{1,0:T(8,128)}, f32[1024,128]{1...) custom-call(bf16[1040,1536]{1,0:T(8,128)(2,1)} %get-tuple-element.84, ...), custom_call_target="tpu_custom_call" | custom-call | bytes 42000000 | tf_op jit(solution)/shard_map/project/pallas_call | solution.py:330
  154.3 14.6 %scan_states.1 = (f32[9,128,1536]{2,1,0:T(8,128)}, f32[128,1536]{1,0:T(8,128)}) custom-call(bf16[1024,1792]{1,0:T(8,128)(2,1)} %get-tuple-element.90.x_ref.b_ref.c_ref, bf16[1024,1792]{1,0:T(8,128)(2,1)} %get-tuple-element.90.x_ref.b_ref.c_ref, f32[1024,128]{1,0:T(8,128)} %get-tuple-element.91.step_ref, f32[1024,128]{1,0:T(8,128)} %get-tuple-element.92.cum_ref, ...), custom_call_target="tpu_custom_call" | custom-call | bytes 18000000 | tf_op jit(solution)/shard_map/scan_states/pallas_call | solution.py:415
  168.9 4.7 collective-permute-start.4
  175.5 13.0 %scan_forward.1.y0_ref = f32[1024,1536]{1,0:T(8,128)} custom-call(bf16[1024,1792]{1,0:T(8,128)(2,1)} %get-tuple-element.90.x_ref.b_ref.c_ref, bf16[1024,1792]{1,0:T(8,128)(2,1)} %get-tuple-element.90.x_ref.b_ref.c_ref, bf16[1024,1792]{1,0:T(8,128)(2,1)} %get-tuple-element.90.x_ref.b_ref.c_ref, f32[1024,128]{1,0:T(8,128)} %get-tuple-element.91.step_ref, ...), custom_call_target="tpu_custom_call" | custom-call | bytes 39000000 | tf_op jit(solution)/shard_map/scan_forward/pallas_call | solution.py:469
  192.1 1.6 constant_dynamic-update-slice_fusion.9.cot_ref.refs_0_
  193.7 1.7 copy-done
  195.3 23.1 %gate_forward.1 = (f32[1024,1536]{1,0:T(8,128)}, f32[1024,1536]{1,0:T(8,128)}, f32[1024,1536]{1,0:T(8,128)}, f32[8,1024]{1,0:T(8,128)}) custom-call(bf16[1040,1536]{1,0:T(8,128)(2,1)} %get-tuple-element.87.normed_ref.left_ref, bf16[1024,1536]{1,0:T(8,128)(2,1)} %copy-done, bf16[1536,1536]{1,0:T(8,128)(2,1)} %get-tuple-element.88.wg_ref.g_ref, ...), custom_call_target="tpu_custom_call" | custom-call | bytes 48000000 | tf_op jit(solution)/shard_map/gate_forward/pallas_call | solution.py:767
  219.3 3.2 collective-permute-done.5
  224.2 15.9 %mix_backward.1 = (bf16[1024,1536]{1,0:T(8,128)(2,1)}, bf16[1024,1536]{1,0:T(8,128)(2,1)}, f32[1024,1536]{1,0:T(8,128)}, f32[8,1536]{1,0:T(8,128)}) custom-call(f32[1024,1536]{1,0:T(8,128)} %get-tuple-element.96.graw_ref, f32[1024,1536]{1,0:T(8,128)} %get-tuple-element.97.y_ref, f32[1024,1536]{1,0:T(8,128)} %get-tuple-element.98.gm_ref, ...), custom_call_target="tpu_custom_call" | custom-call | bytes 30000000 | tf_op jit(solution)/shard_map/mix_backward/pallas_call | solution.py:830
  240.1 10.4 %weight_grad.5 = f32[1536,1536]{1,0:T(8,128)} custom-call(bf16[1024,1536]{1,0:T(8,128)(2,1)} %get-tuple-element.100.left_ref, bf16[1024,1536]{1,0:T(8,128)(2,1)} %copy-done), custom_call_target="tpu_custom_call" | custom-call | bytes 21000000 | tf_op jit(solution)/shard_map/weight_grad/pallas_call | solution.py:907
  250.5 4.8 constant_dynamic-slice_fusion
  256.3 13.7 %scan_grad_states.1 = (f32[8,128,1536]{2,1,0:T(8,128)}, f32[128,1536]{1,0:T(8,128)}) custom-call(f32[1024,1536]{1,0:T(8,128)} %get-tuple-element.101.dy_ref, bf16[1024,1792]{1,0:T(8,128)(2,1)} %get-tuple-element.90.x_ref.b_ref.c_ref, f32[1024,128]{1,0:T(8,128)} %get-tuple-element.92.cum_ref, bf16[256,1536]{1,0:T(8,128)(2,1)} %add_convert_fusion.1.spread_ref), custom_call_target="tpu_custom_call" | custom-call | bytes 18000000 | tf_op jit(solution)/shard_map/scan_grad_states/pallas_call | solution.py:514
  271.5 10.5 %weight_grad.4 = f32[1536,1536]{1,0:T(8,128)} custom-call(bf16[1040,1536]{1,0:T(8,128)(2,1)} %get-tuple-element.87.normed_ref.left_ref, bf16[1024,1536]{1,0:T(8,128)(2,1)} %get-tuple-element.111.gg_ref.refs_0_), custom_call_target="tpu_custom_call" | custom-call | bytes 21000000 | tf_op jit(solution)/shard_map/weight_grad/pallas_call | solution.py:907
  281.9 4.8 constant_dynamic-slice_fusion.4
  288.2 25.2 %scan_backward_near.1 = (f32[1024,1536]{1,0:T(8,128)}, f32[1024,256]{1,0:T(8,128)}) custom-call(f32[1024,1536]{1,0:T(8,128)} %get-tuple-element.101.dy_ref, bf16[1024,1792]{1,0:T(8,128)(2,1)} %get-tuple-element.90.x_ref.b_ref.c_ref, bf16[1024,1792]{1,0:T(8,128)(2,1)} %get-tuple-element.90.x_ref.b_ref.c_ref, ...), custom_call_target="tpu_custom_call" | custom-call | bytes 60000000 | tf_op jit(solution)/shard_map/scan_backward_near/pallas_call | solution.py:596
  313.5 6.0 convolution_convert_fusion
  321.7 28.1 %scan_backward_far.1 = (f32[1024,1536]{1,0:T(8,128)}, bf16[1024,128]{1,0:T(8,128)(2,1)}, f32[1024,256]{1,0:T(8,128)}, f32[8,128]{1,0:T(8,128)}) custom-call(f32[1024,1536]{1,0:T(8,128)} %get-tuple-element.101.dy_ref, bf16[1024,1792]{1,0:T(8,128)(2,1)} %get-tuple-element.90.x_ref.b_ref.c_ref, f32[1024,1536]{1,0:T(8,128)} %get-tuple-element.97.y_ref, ...), custom_call_target="tpu_custom_call" | custom-call | bytes 42000000 | tf_op jit(solution)/shard_map/scan_backward_far/pallas_call | solution.py:688
  349.9 16.5 %conv_back.2 = (bf16[1040,1536]{1,0:T(8,128)(2,1)}, f32[8,1536]{1,0:T(8,128)}) custom-call(f32[1024,1536]{1,0:T(8,128)} %get-tuple-element.108.ga_ref, f32[1040,1792]{1,0:T(8,128)} %get-tuple-element.109.raw_ref, f32[8,1792]{1,0:T(8,128)} %pad_maximum_fusion.3.taps_ref), custom_call_target="tpu_custom_call" | custom-call | bytes 24000000 | tf_op jit(solution)/shard_map/conv_back/pallas_call | solution.py:877
  369.5 12.5 %collective-permute-done.8 = f32[1024,128]{1,0:T(8,128)S(1)} collective-permute-done((f32[1024,128]{1,0:T(8,128)S(1)}, f32[1024,128]{1,0:T(8,128)S(1)}, u32[]{:S(2)}, u32[]{:S(2)}) %collective-permute-start.8) | collective-permute-done | bytes 524320 | tf_op jit(solution)/shard_map/ppermute | solution.py:1388
  382.8 2.6 conv_back.3
  386.0 12.9 %weight_grad.3.joint = f32[1536,1792]{1,0:T(8,128)} custom-call(bf16[1040,1536]{1,0:T(8,128)(2,1)} %get-tuple-element.87.normed_ref.left_ref, bf16[1040,1536]{1,0:T(8,128)(2,1)} %get-tuple-element.110.gv_ref.refs_0_, bf16[1040,128]{1,0:T(8,128)(2,1)} %get-tuple-element.113.gs_ref.refs_1_, bf16[1024,128]{1,0:T(8,128)(2,1)} %get-tuple-element.114.gt_ref.refs_2_), custom_call_target="tpu_custom_call" | custom-call | bytes 21000000 | tf_op jit(solution)/shard_map/weight_grad/pallas_call | solution.py:907
  398.9 18.2 %input_grad.1 = (f32[1040,1536]{1,0:T(8,128)}, bf16[1040,1536]{1,0:T(8,128)(2,1)}, f32[8,1536]{1,0:T(8,128)}) custom-call(bf16[1040,1536]{1,0:T(8,128)(2,1)} %get-tuple-element.110.gv_ref.refs_0_, bf16[1024,1536]{1,0:T(8,128)(2,1)} %get-tuple-element.111.gg_ref.refs_0_, bf16[1040,128]{1,0:T(8,128)(2,1)} %get-tuple-element.113.gs_ref.refs_1_, ...), custom_call_target="tpu_custom_call" | custom-call | bytes 36000000 | tf_op jit(solution)/shard_map/input_grad/pallas_call | solution.py:941
  418.7 85.8 %settle.1 = (f32[512,1536]{1,0:T(8,128)}, f32[768,768]{1,0:T(8,128)}, f32[768,256]{1,0:T(8,128)}, f32[168,128]{1,0:T(8,128)}) custom-call(f32[1040,1536]{1,0:T(8,128)} %get-tuple-element.117.gn, bf16[1040,1536]{1,0:T(8,128)(2,1)} %get-tuple-element.118.gnb, f32[1536,1792]{1,0:T(8,128)} %weight_grad.3.joint, f32[168,128]{1,0:T(8,128)} %pad_bitcast_fusion.flat, ...), custom_call_target="tpu_custom_call" | custom-call | bytes 270000000 | tf_op jit(solution)/shard_map/settle/pallas_call | solution.py:1154
  507.7 4.7 dynamic-slice_add_fusion
  513.2 2.1 collective-permute-start.19
  516.1 3.3 dynamic-slice_add_fusion.1
  519.5 2.1 copy-done.2
  523.5 2.0 collective-permute-start.12
  525.5 3.4 collective-permute-done.18
  530.3 11.4 %collective-permute-done.19 = bf16[2,192,768]{2,1,0:T(8,128)(2,1)S(1)} collective-permute-done((bf16[2,192,768]{2,1,0:T(8,128)(2,1)S(1)}, bf16[2,192,768]{2,1,0:T(8,128)(2,1)S(1)}, u32[]{:S(2)}, u32[]{:S(2)}) %collective-permute-start.19) | collective-permute-done | bytes 589856 | tf_op jit(solution)/shard_map/ppermute | solution.py:1219
  541.7 5.3 collective-permute-start.6
  547.0 1.7 fusion.6
  549.4 4.9 collective-permute-done.10
  554.3 10.2 %collective-permute-done.12 = bf16[192,1536]{1,0:T(8,128)(2,1)} collective-permute-done((bf16[192,1536]{1,0:T(8,128)(2,1)}, bf16[192,1536]{1,0:T(8,128)(2,1)}, u32[]{:S(2)}, u32[]{:S(2)}) %collective-permute-start.12) | collective-permute-done | bytes 589856 | tf_op jit(solution)/shard_map/ppermute | solution.py:1219
  564.6 2.1 fusion.8
  571.0 16.7 %collective-permute-done.21 = bf16[192,768]{1,0:T(8,128)(2,1)} collective-permute-done((bf16[192,768]{1,0:T(8,128)(2,1)}, bf16[192,768]{1,0:T(8,128)(2,1)}, u32[]{:S(2)}, u32[]{:S(2)}) %collective-permute-start.21) | collective-permute-done | bytes 294944 | tf_op jit(solution)/shard_map/ppermute | solution.py:1364
  589.9 2.7 collective-permute-start.24
  593.8 6.3 add_convert_fusion
  600.1 5.5 collective-permute-done.22
  605.5 2.0 collective-permute-start.16
  607.6 23.2 %collective-permute-done.14 = f32[192,768]{1,0:T(8,128)S(1)} collective-permute-done((f32[192,768]{1,0:T(8,128)S(1)}, f32[192,768]{1,0:T(8,128)S(1)}, u32[]{:S(2)}, u32[]{:S(2)}) %collective-permute-start.14) | collective-permute-done | bytes 589856 | tf_op jit(solution)/shard_map/ppermute | solution.py:1209
  631.1 9.1 %collective-permute-done.16 = f32[192,768]{1,0:T(8,128)S(1)} collective-permute-done((f32[192,768]{1,0:T(8,128)S(1)}, f32[192,768]{1,0:T(8,128)S(1)}, u32[]{:S(2)}, u32[]{:S(2)}) %collective-permute-start.16) | collective-permute-done | bytes 589856 | tf_op jit(solution)/shard_map/ppermute | solution.py:1209
  640.3 1.7 copy.65
  (190 shorter events, 58.4 us)
Async XLA Ops:
  1.6 19.2 %collective-permute-start.1 = (f32[8,256]{1,0:T(8,128)S(1)}, f32[8,256]{1,0:T(8,128)S(1)}, u32[]{:S(2)}, u32[]{:S(2)}) collective-permute-start(f32[8,256]{1,0:T(8,128)S(1)} %dynamic_update_slice.50), channel_id=1, source_target_pairs={{0,1},{1,0},{2,3},{3,2},{4,5},{5,4},{6,7},{7,6},{8,9},{9,8},{10,11... | collective-permute-start | bytes 24584 | tf_op jit(solution)/shard_map/ppermute | solution.py:1194
  5.4 2.6 copy-start.19
  10.2 119.2 %collective-permute-start = (f32[8,768]{1,0:T(8,128)}, f32[8,768]{1,0:T(8,128)}, u32[]{:S(2)}, u32[]{:S(2)}) collective-permute-start(f32[8,768]{1,0:T(8,128)} %concatenate.66), channel_id=1, source_target_pairs={{0,3},{1,2},{2,1},{3,0},{4,7},{5,6},{6,5},{7,4},{8,11},{9,10},{10,... | collective-permute-start | bytes 73736 | tf_op jit(solution)/shard_map/ppermute | solution.py:1291
  12.6 179.5 %collective-permute-start.3 = (bf16[512,1536]{1,0:T(8,128)(2,1)}, bf16[512,1536]{1,0:T(8,128)(2,1)}, u32[]{:S(2)}, u32[]{:S(2)}) collective-permute-start(bf16[512,1536]{1,0:T(8,128)(2,1)} %cot.1), channel_id=1, source_target_pairs={{0,1},{1,0},{2,3},{3,2},{4,5},{5,4},{6,7},{7,6},{8,9},{9,8},{10,11... | collective-permute-start | bytes 4718600 | tf_op jit(solution)/shard_map/ppermute | solution.py:1271
  16.6 3.2 copy-start.15
  21.8 107.5 %collective-permute-start.2 = (f32[8,256]{1,0:T(8,128)S(1)}, f32[8,256]{1,0:T(8,128)S(1)}, u32[]{:S(2)}, u32[]{:S(2)}) collective-permute-start(f32[8,256]{1,0:T(8,128)S(1)} %add.199), channel_id=1, source_target_pairs={{0,2},{1,3},{2,0},{3,1},{4,6},{5,7},{6,4},{7,5},{8,10},{9,11},{10,... | collective-permute-start | bytes 24584 | tf_op jit(solution)/shard_map/ppermute | solution.py:1194
  24.0 106.2 %copy-start.20 = (f32[12]{0:T(128)S(1)}, f32[12]{0:T(128)}, u32[]{:S(2)}) copy-start(f32[12]{0:T(128)} %copy-done.19) | copy-start | bytes 148
  24.0 106.3 %copy-start.18 = (pred[8]{0:T(512)(128)(4,1)S(1)}, pred[8]{0:T(512)(128)(4,1)}, u32[]{:S(2)}) copy-start(pred[8]{0:T(512)(128)(4,1)} %constant.196.clone.1) | copy-start | bytes 28
  24.0 107.1 %copy-start.21 = (f32[1,12]{1,0:T(1,128)S(1)}, f32[1,12]{1,0:T(1,128)}, u32[]{:S(2)}) copy-start(f32[1,12]{1,0:T(1,128)} %get-tuple-element.175) | copy-start | bytes 148
  168.9 22.2 %collective-permute-start.4 = (f32[128,1536]{1,0:T(8,128)}, f32[128,1536]{1,0:T(8,128)S(1)}, u32[]{:S(2)}, u32[]{:S(2)}) collective-permute-start(f32[128,1536]{1,0:T(8,128)} %get-tuple-element.94), channel_id=1, source_target_pairs={{0,3},{1,2},{4,7},{5,6},{8,11},{9,10},{12,15},{13,14},{16,19},{17,... | collective-permute-start | bytes 2359304 | tf_op jit(solution)/shard_map/ppermute | solution.py:1322
  193.7 1.7 copy-start
  218.4 4.2 collective-permute-start.5
  250.5 4.9 copy-start.14
  255.3 252.3 %collective-permute-start.17 = (f32[1536,768]{1,0:T(8,128)}, f32[1536,768]{1,0:T(8,128)}, u32[]{:S(2)}, u32[]{:S(2)}) collective-permute-start(f32[1536,768]{1,0:T(8,128)} %constant_dynamic-slice_fusion), channel_id=1, source_target_pairs={{0,4},{4,0},{1,5},{5,1},{2,6},{6,2},{3,7},{7,3},{8,12},{12,8},{9,1... | collective-permute-start | bytes 14155784 | tf_op jit(solution)/shard_map/ppermute | solution.py:1224
  270.0 49.6 %collective-permute-start.7 = (f32[128,1536]{1,0:T(8,128)}, f32[128,1536]{1,0:T(8,128)}, u32[]{:S(2)}, u32[]{:S(2)}) collective-permute-start(f32[128,1536]{1,0:T(8,128)} %get-tuple-element.106), channel_id=1, source_target_pairs={{3,0},{2,1},{7,4},{6,5},{11,8},{10,9},{15,12},{14,13},{19,16},{18,... | collective-permute-start | bytes 2359304 | tf_op jit(solution)/shard_map/ppermute | solution.py:1322
  286.8 229.3 %collective-permute-start.9 = (f32[768,1536]{1,0:T(8,128)}, f32[768,1536]{1,0:T(8,128)}, u32[]{:S(2)}, u32[]{:S(2)}) collective-permute-start(f32[768,1536]{1,0:T(8,128)} %constant_dynamic-slice_fusion.4), channel_id=1, source_target_pairs={{0,4},{4,0},{1,5},{5,1},{2,6},{6,2},{3,7},{7,3},{8,12},{12,8},{9,1... | collective-permute-start | bytes 14155784 | tf_op jit(solution)/shard_map/ppermute | solution.py:1224
  288.2 25.3 %copy-start.6 = (bf16[1024,1536]{1,0:T(8,128)(2,1)S(1)}, bf16[1024,1536]{1,0:T(8,128)(2,1)}, u32[]{:S(2)}) copy-start(bf16[1024,1536]{1,0:T(8,128)(2,1)} %get-tuple-element.100.left_ref) | copy-start | bytes 9437188
  349.9 18.1 %copy-start.11 = (f32[1024,256]{1,0:T(8,128)S(1)}, f32[1024,256]{1,0:T(8,128)}, u32[]{:S(2)}) copy-start(f32[1024,256]{1,0:T(8,128)} %get-tuple-element.112) | copy-start | bytes 3145732
  368.0 13.9 %collective-permute-start.8 = (f32[1024,128]{1,0:T(8,128)S(1)}, f32[1024,128]{1,0:T(8,128)S(1)}, u32[]{:S(2)}, u32[]{:S(2)}) collective-permute-start(f32[1024,128]{1,0:T(8,128)S(1)} %constant_dynamic-slice_fusion.8), channel_id=1, source_target_pairs={{0,1},{1,0},{2,3},{3,2},{4,5},{5,4},{6,7},{7,6},{8,9},{9,8},{10,11... | collective-permute-start | bytes 1572872 | tf_op jit(solution)/shard_map/ppermute | solution.py:1388
  507.1 9.0 %slice-start = ((s8[9437184]{0:T(1024)(128)(4,1)}), s8[4194304]{0:T(1024)(128)(4,1)S(1)}, s32[]{:S(2)}) async-start(s8[9437184]{0:T(1024)(128)(4,1)} %bitcast.74), calls=%async_computation | async-start | bytes 8388608
  507.6 8.4 %slice-start.1 = ((s8[9437184]{0:T(1024)(128)(4,1)}), s8[4194304]{0:T(1024)(128)(4,1)S(1)}, s32[]{:S(2)}) async-start(s8[9437184]{0:T(1024)(128)(4,1)} %bitcast.74), calls=%async_computation.1 | async-start | bytes 8388608
  507.7 8.4 %slice-start.2 = ((s8[9437184]{0:T(1024)(128)(4,1)}), s8[1048576]{0:T(1024)(128)(4,1)S(1)}, s32[]{:S(2)}) async-start(s8[9437184]{0:T(1024)(128)(4,1)} %bitcast.74), calls=%async_computation.2 | async-start | bytes 2097152
  512.3 7.1 %copy-start.1 = (f32[1536,768]{1,0:T(8,128)}, f32[1536,768]{1,0:T(8,128)S(1)}, u32[]{:S(2)}) copy-start(f32[1536,768]{1,0:T(8,128)S(1)} %dynamic-slice_add_fusion) | copy-start | bytes 14155780
  512.5 16.3 %collective-permute-start.18 = (bf16[2,192,768]{2,1,0:T(8,128)(2,1)S(1)}, bf16[2,192,768]{2,1,0:T(8,128)(2,1)S(1)}, u32[]{:S(2)}, u32[]{:S(2)}) collective-permute-start(bf16[2,192,768]{2,1,0:T(8,128)(2,1)S(1)} %get-tuple-element.150), channel_id=1, source_target_pairs={{0,8},{8,0},{16,24},{24,16},{1,9},{9,1},{17,25},{25,17},{2,10},{10... | collective-permute-start | bytes 1769480 | tf_op jit(solution)/shard_map/ppermute | solution.py:1219
  513.2 28.6 %collective-permute-start.19 = (bf16[2,192,768]{2,1,0:T(8,128)(2,1)S(1)}, bf16[2,192,768]{2,1,0:T(8,128)(2,1)S(1)}, u32[]{:S(2)}, u32[]{:S(2)}) collective-permute-start(bf16[2,192,768]{2,1,0:T(8,128)(2,1)S(1)} %get-tuple-element.151), channel_id=1, source_target_pairs={{0,16},{8,24},{16,0},{24,8},{1,17},{9,25},{17,1},{25,9},{2,18},{10... | collective-permute-start | bytes 1769480 | tf_op jit(solution)/shard_map/ppermute | solution.py:1219
  515.3 31.7 %collective-permute-start.20 = (bf16[2,192,768]{2,1,0:T(8,128)(2,1)S(1)}, bf16[2,192,768]{2,1,0:T(8,128)(2,1)}, u32[]{:S(2)}, u32[]{:S(2)}) collective-permute-start(bf16[2,192,768]{2,1,0:T(8,128)(2,1)S(1)} %get-tuple-element.152), channel_id=1, source_target_pairs={{0,24},{8,16},{16,8},{24,0},{1,25},{9,17},{17,9},{25,1},{2,26},{10... | collective-permute-start | bytes 1769480 | tf_op jit(solution)/shard_map/ppermute | solution.py:1219
  519.5 2.1 copy-start.2
  519.5 10.6 %copy-start.12 = (f32[768,256]{1,0:T(8,128)S(1)}, f32[768,256]{1,0:T(8,128)}, u32[]{:S(2)}) copy-start(f32[768,256]{1,0:T(8,128)} %get-tuple-element.127) | copy-start | bytes 2359300
  519.5 10.8 %copy-start.16 = (f32[168,128]{1,0:T(8,128)S(1)}, f32[168,128]{1,0:T(8,128)}, u32[]{:S(2)}) copy-start(f32[168,128]{1,0:T(8,128)} %get-tuple-element.125) | copy-start | bytes 258052
  522.8 31.5 %collective-permute-start.10 = (bf16[192,1536]{1,0:T(8,128)(2,1)}, bf16[192,1536]{1,0:T(8,128)(2,1)}, u32[]{:S(2)}, u32[]{:S(2)}) collective-permute-start(bf16[192,1536]{1,0:T(8,128)(2,1)} %get-tuple-element.153), channel_id=1, source_target_pairs={{0,8},{8,0},{16,24},{24,16},{1,9},{9,1},{17,25},{25,17},{2,10},{10... | collective-permute-start | bytes 1769480 | tf_op jit(solution)/shard_map/ppermute | solution.py:1219
  523.5 41.0 %collective-permute-start.12 = (bf16[192,1536]{1,0:T(8,128)(2,1)}, bf16[192,1536]{1,0:T(8,128)(2,1)}, u32[]{:S(2)}, u32[]{:S(2)}) collective-permute-start(bf16[192,1536]{1,0:T(8,128)(2,1)} %get-tuple-element.154), channel_id=1, source_target_pairs={{0,24},{8,16},{16,8},{24,0},{1,25},{9,17},{17,9},{25,1},{2,26},{10... | collective-permute-start | bytes 1769480 | tf_op jit(solution)/shard_map/ppermute | solution.py:1219
  528.9 35.7 %collective-permute-start.11 = (bf16[192,1536]{1,0:T(8,128)(2,1)}, bf16[192,1536]{1,0:T(8,128)(2,1)}, u32[]{:S(2)}, u32[]{:S(2)}) collective-permute-start(bf16[192,1536]{1,0:T(8,128)(2,1)} %get-tuple-element.155), channel_id=1, source_target_pairs={{0,16},{8,24},{16,0},{24,8},{1,17},{9,25},{17,1},{25,9},{2,18},{10... | collective-permute-start | bytes 1769480 | tf_op jit(solution)/shard_map/ppermute | solution.py:1219
  541.7 51.4 %collective-permute-start.6 = (bf16[512,1536]{1,0:T(8,128)(2,1)}, bf16[512,1536]{1,0:T(8,128)(2,1)}, u32[]{:S(2)}, u32[]{:S(2)}) collective-permute-start(bf16[512,1536]{1,0:T(8,128)(2,1)} %convolution_convert_fusion), channel_id=1, source_target_pairs={{0,1},{1,0},{2,3},{3,2},{4,5},{5,4},{6,7},{7,6},{8,9},{9,8},{10,11... | collective-permute-start | bytes 4718600 | tf_op jit(solution)/shard_map/ppermute | solution.py:1342
  548.7 20.0 %copy-start.13 = (f32[768,256]{1,0:T(8,128)S(1)}, f32[768,256]{1,0:T(8,128)}, u32[]{:S(2)}) copy-start(f32[768,256]{1,0:T(8,128)} %get-tuple-element.127) | copy-start | bytes 2359300
  549.4 38.3 %collective-permute-start.21 = (bf16[192,768]{1,0:T(8,128)(2,1)}, bf16[192,768]{1,0:T(8,128)(2,1)}, u32[]{:S(2)}, u32[]{:S(2)}) collective-permute-start(bf16[192,768]{1,0:T(8,128)(2,1)} %fusion.31), channel_id=1, source_target_pairs={{0,3},{1,2},{2,1},{3,0},{4,7},{5,6},{6,5},{7,4},{8,11},{9,10},{10,... | collective-permute-start | bytes 884744 | tf_op jit(solution)/shard_map/ppermute | solution.py:1364
  567.4 25.3 %collective-permute-start.13 = (bf16[192,768]{1,0:T(8,128)(2,1)}, bf16[192,768]{1,0:T(8,128)(2,1)S(1)}, u32[]{:S(2)}, u32[]{:S(2)}) collective-permute-start(bf16[192,768]{1,0:T(8,128)(2,1)} %slice.262), channel_id=1, source_target_pairs={{0,3},{1,2},{2,1},{3,0},{4,7},{5,6},{6,5},{7,4},{8,11},{9,10},{10,... | collective-permute-start | bytes 884744 | tf_op jit(solution)/shard_map/ppermute | solution.py:1364
  587.9 5.9 copy-start.4
  587.9 5.9 copy-start.7
  589.1 41.8 %collective-permute-start.23 = (f32[192,768]{1,0:T(8,128)S(1)}, f32[192,768]{1,0:T(8,128)S(1)}, u32[]{:S(2)}, u32[]{:S(2)}) collective-permute-start(f32[192,768]{1,0:T(8,128)S(1)} %get-tuple-element.147), channel_id=1, source_target_pairs={{0,16},{8,24},{16,0},{24,8},{1,17},{9,25},{17,1},{25,9},{2,18},{10... | collective-permute-start | bytes 1769480 | tf_op jit(solution)/shard_map/ppermute | solution.py:1209
  589.2 16.3 %collective-permute-start.22 = (f32[192,768]{1,0:T(8,128)S(1)}, f32[192,768]{1,0:T(8,128)S(1)}, u32[]{:S(2)}, u32[]{:S(2)}) collective-permute-start(f32[192,768]{1,0:T(8,128)S(1)} %get-tuple-element.147), channel_id=1, source_target_pairs={{0,8},{8,0},{16,24},{24,16},{1,9},{9,1},{17,25},{25,17},{2,10},{10... | collective-permute-start | bytes 1769480 | tf_op jit(solution)/shard_map/ppermute | solution.py:1209
  589.9 41.1 %collective-permute-start.24 = (f32[192,768]{1,0:T(8,128)S(1)}, f32[192,768]{1,0:T(8,128)S(1)}, u32[]{:S(2)}, u32[]{:S(2)}) collective-permute-start(f32[192,768]{1,0:T(8,128)S(1)} %get-tuple-element.147), channel_id=1, source_target_pairs={{0,24},{8,16},{16,8},{24,0},{1,25},{9,17},{17,9},{25,1},{2,26},{10... | collective-permute-start | bytes 1769480 | tf_op jit(solution)/shard_map/ppermute | solution.py:1209
  592.9 38.0 %collective-permute-start.15 = (f32[192,768]{1,0:T(8,128)S(1)}, f32[192,768]{1,0:T(8,128)S(1)}, u32[]{:S(2)}, u32[]{:S(2)}) collective-permute-start(f32[192,768]{1,0:T(8,128)S(1)} %get-tuple-element.149), channel_id=1, source_target_pairs={{0,16},{8,24},{16,0},{24,8},{1,17},{9,25},{17,1},{25,9},{2,18},{10... | collective-permute-start | bytes 1769480 | tf_op jit(solution)/shard_map/ppermute | solution.py:1209
  593.1 37.8 %collective-permute-start.14 = (f32[192,768]{1,0:T(8,128)S(1)}, f32[192,768]{1,0:T(8,128)S(1)}, u32[]{:S(2)}, u32[]{:S(2)}) collective-permute-start(f32[192,768]{1,0:T(8,128)S(1)} %get-tuple-element.149), channel_id=1, source_target_pairs={{0,8},{8,0},{16,24},{24,16},{1,9},{9,1},{17,25},{25,17},{2,10},{10... | collective-permute-start | bytes 1769480 | tf_op jit(solution)/shard_map/ppermute | solution.py:1209
  605.5 34.7 %collective-permute-start.16 = (f32[192,768]{1,0:T(8,128)S(1)}, f32[192,768]{1,0:T(8,128)S(1)}, u32[]{:S(2)}, u32[]{:S(2)}) collective-permute-start(f32[192,768]{1,0:T(8,128)S(1)} %get-tuple-element.149), channel_id=1, source_target_pairs={{0,24},{8,16},{16,8},{24,0},{1,25},{9,17},{17,9},{25,1},{2,26},{10... | collective-permute-start | bytes 1769480 | tf_op jit(solution)/shard_map/ppermute | solution.py:1209
  607.6 32.7 %copy-start.5 = (f32[512,1536]{1,0:T(8,128)S(1)}, f32[512,1536]{1,0:T(8,128)}, u32[]{:S(2)}) copy-start(f32[512,1536]{1,0:T(8,128)} %get-tuple-element.208) | copy-start | bytes 9437188
  631.1 10.9 %copy-start.9 = (f32[768,768]{1,0:T(8,128)}, f32[768,768]{1,0:T(8,128)S(1)}, u32[]{:S(2)}) copy-start(f32[768,768]{1,0:T(8,128)S(1)} %constant_dynamic-update-slice_fusion) | copy-start | bytes 7077892
  640.3 2.7 copy-start.8
  640.3 3.4 copy-start.10
  (2 other events, 2.1 us)

commit v3 on v2

--- a/solution.py
+++ b/solution.py
@@ -2,6 +2,7 @@
 
 import jax
 import jax.numpy as jnp
+import numpy as np
 from jax import lax
 from jax.experimental import pallas as pl
 from jax.experimental.pallas import tpu as pltpu
@@ -83,8 +84,48 @@
     pl.semaphore_wait(barrier, len(others))
 
 
+def at_step(step):
+    return pl.when(pl.program_id(0) == step)
+
+
+def copy_to(src, dst, sems, i, device):
+    return pltpu.make_async_remote_copy(
+        src_ref=src, dst_ref=dst, send_sem=sems.at[0, i], recv_sem=sems.at[1, i],
+        device_id=device, device_id_type=pl.DeviceIdType.MESH,
+    )
+
+
+def dp_copies(dps, sems, src_of, dst_of, first=0):
+    dp, row, col = here()
+    return [
+        copy_to(src_of(dp ^ by, by - 1), dst_of(dp ^ by, by - 1), sems, first + by - 1, (dp ^ by, row, col))
+        for by in range(1, dps)
+    ]
+
+
+def dp_peers(dps):
+    dp, row, col = here()
+    return [(dp ^ by, row, col) for by in range(1, dps)]
+
+
+def mirror_of(cols):
+    dp, row, col = here()
+    return (dp, row, cols - 1 - col)
+
+
+def remote_params(collective_id):
+    return pltpu.CompilerParams(
+        dimension_semantics=("arbitrary",), vmem_limit_bytes=VMEM_LIMIT, collective_id=collective_id,
+        has_side_effects=True,
+    )
+
+
+ANY = pl.BlockSpec(memory_space=pl.ANY)
+
+
 def import_kernel(
-    cols, dps, tok, wv, wg, wo, sw, tg, vf, gf, of, sf, zeros, tok_vm, w_vm, wo_vm, s_vm, local, send, recv
+    cols, dps, tok, wv, wg, wo, sw, vec, tg, vf, gf, of, sf, vecs,
+    zeros, tok_vm, w_vm, wo_vm, s_vm, vec_vm, local, send, recv,
 ):
     dp, row, col = here()
     group = cols // 2
@@ -131,6 +172,7 @@
     src_piece, src_out = pl.ds(dp * piece, piece), pl.ds(dp * piece_out, piece_out)
 
     staged = [
+        keep(6, vec, vec_vm),
         keep(0, sw.at[src_piece, :], s_vm),
         keep(2, tok, tok_vm),
         keep(3, wv, w_vm.at[0]),
@@ -142,6 +184,7 @@
         for by in range(1, cols)
     ]
     v_cross = launch(wv.at[src_piece, :], vf.at[my_piece, other], mirror)
+    vec_cross = [launch(vec, vecs.at[col], col_peer(by)) for by in range(1, cols)]
     my_tokens = tg.at[pl.ds(HALO + place * count, count), :]
     tok_cross = [launch(tok, my_tokens, col_peer(by)) for by in range(1, group)]
     halo_src = tok.at[pl.ds(count - HALO, HALO), :]
@@ -176,6 +219,7 @@
         copy.wait()
     small_own = keep(0, s_vm, sf.at[my_piece, lanes_at(col, 128)])
     kept = [
+        keep(6, vec_vm, vecs.at[col]),
         keep(2, tok_vm, my_tokens),
         keep(3, w_vm.at[0], vf.at[my_rows, own]),
         keep(4, w_vm.at[1], gf.at[my_rows, own]),
@@ -210,6 +254,7 @@
     last += [launch(of.at[other, my_lanes], of.at[other, my_lanes], sibling)]
     arrive(last)
     arrive([v_own, g_own, o_own])
+    arrive(vec_cross)
     arrive(tok_cross)
 
     @pl.when(col >= group)
@@ -227,21 +272,22 @@
         copy.wait_send()
 
 
-def import_all(cols, dps, tokens, w_value, w_gate, w_out, small):
+def import_all(cols, dps, tokens, w_value, w_gate, w_out, small, vec):
     half, shard = w_value.shape
     count, width = tokens.shape
     any_spec = pl.BlockSpec(memory_space=pl.ANY)
-    copies = 3 + (cols - 1) + (cols // 2 - 1) + cols // 2 + 3 + 4 * (dps - 1) + 4
+    copies = 3 + 2 * (cols - 1) + (cols // 2 - 1) + cols // 2 + 3 + 4 * (dps - 1) + 4
     return pl.pallas_call(
         partial(import_kernel, cols, dps),
-        in_specs=[any_spec] * 5,
-        out_specs=[any_spec] * 5,
+        in_specs=[any_spec] * 6,
+        out_specs=[any_spec] * 6,
         out_shape=[
             sds((HALO + count * (cols // 2), width), BF),
             sds((2 * half, 2 * shard), BF),
             sds((2 * half, 2 * shard), BF),
             sds((2 * shard, 2 * half), BF),
             sds((2 * half, cols * 128), BF),
+            sds((cols,) + vec.shape, BF),
         ],
         scratch_shapes=[
             pltpu.VMEM((HALO, width), BF),
@@ -249,7 +295,8 @@
             pltpu.VMEM((2, half, shard), BF),
             pltpu.VMEM((shard, half), BF),
             pltpu.VMEM((half // dps, 128), BF),
-            pltpu.SemaphoreType.DMA((6,)),
+            pltpu.VMEM(vec.shape, BF),
+            pltpu.SemaphoreType.DMA((7,)),
             pltpu.SemaphoreType.DMA((copies,)),
             pltpu.SemaphoreType.DMA((copies,)),
         ],
@@ -258,7 +305,7 @@
         ),
         cost_estimate=cost(55),
         name="import_all",
-    )(tokens, w_value, w_gate, w_out, small)
+    )(tokens, w_value, w_gate, w_out, small, vec)
 
 
 def conv_rows(raw_ref, taps, start, size):
@@ -532,11 +579,10 @@
     )(dy, act, cum, spread)
 
 
-def backward_near_kernel(
-    dy_ref, x_ref, b_ref, c_ref, step_ref, cum_ref, spread_ref, state_ref, early_ref, offs_ref,
-    gx_ref, gbc_ref,
+def near_block(
+    at_block, here_rows, dy_ref, x_ref, b_ref, c_ref, step_ref, cum_ref, spread_ref, state_ref, early_ref,
+    offs_ref, gx_ref, gbc_ref,
 ):
-    at_block = pl.program_id(0)
     b_blk, c_blk = b_ref[...], c_ref[...]
     affinity_t = mm_nt(b_blk, c_blk)
     causal_t = iota2((Q, Q), 1) >= iota2((Q, Q), 0)
@@ -581,53 +627,20 @@
                 dh, dl = jnp.where(keep, d_high, zero), jnp.where(keep, d_low, zero)
                 left += [m_high, m_low, m_high]
                 right += [dh, dh, dl]
-            gx_ref[:, at : at + 128] = mm(jnp.concatenate(left, 1), jnp.concatenate(right, 0))
+            gx_ref[here_rows, at : at + 128] = mm(jnp.concatenate(left, 1), jnp.concatenate(right, 0))
     a_high, a_low = split2(grad_affinity_t)
-    gbc_ref[:, 0:N] = mm(jnp.concatenate([a_high, a_low], 1), jnp.concatenate([c_blk, c_blk], 0))
+    gbc_ref[here_rows, 0:N] = mm(jnp.concatenate([a_high, a_low], 1), jnp.concatenate([c_blk, c_blk], 0))
     t_high, t_low = split2(grad_affinity_t.T)
-    gbc_ref[:, N : 2 * N] = grad_c + mm(
+    gbc_ref[here_rows, N : 2 * N] = grad_c + mm(
         jnp.concatenate([t_high, t_low], 1), jnp.concatenate([b_blk, b_blk], 0)
     )
 
 
-def scan_backward_near(dy, act, step, cum, spread, states, early, offs):
-    tokens, channels = dy.shape
-    rows = pl.BlockSpec((Q, channels), lambda i: (i, 0))
-    return pl.pallas_call(
-        backward_near_kernel,
-        grid=(tokens // Q,),
-        in_specs=[
-            rows,
-            rows,
-            pl.BlockSpec((Q, N), lambda i: (i, channels // N)),
-            pl.BlockSpec((Q, N), lambda i: (i, channels // N + 1)),
-            pl.BlockSpec((Q, 128), lambda i: (i, 0)),
-            pl.BlockSpec((Q, 128), lambda i: (i, 0)),
-            whole((256, channels)),
-            pl.BlockSpec((1, N, channels), lambda i: (i, 0, 0)),
-            whole((N, channels)),
-            whole((16, 128)),
-        ],
-        out_specs=[rows, pl.BlockSpec((Q, 2 * N), lambda i: (i, 0))],
-        out_shape=[sds((tokens, channels)), sds((tokens, 2 * N))],
-        compiler_params=params(),
-        cost_estimate=cost(20),
-        name="scan_backward_near",
-    )(dy, act, act, act, step, cum, spread, states, early, offs)
-
-
-def backward_far_kernel(
-    dy_ref, x_ref, y_ref, gx_ref, b_ref, step_ref, cum_ref, stepin_ref, spread_ref, gather_ref,
-    after_ref, late_ref, state_ref, early_ref, offs_ref, head_ref, skip_ref, gbc_ref,
+def far_block(
+    blocks, at_block, here_rows, dy_ref, x_ref, y_ref, gx_ref, b_ref, step_ref, cum_ref, stepin_ref, spread_ref,
+    gather_ref, after_ref, late_ref, state_ref, early_ref, offs_ref, head_ref, skip_ref, gbc_ref,
     ga_ref, gstep_ref, gbc_out_ref, sums_ref,
 ):
-    blocks = pl.num_programs(0)
-    at_block = pl.program_id(0)
-
-    @pl.when(at_block == 0)
-    def _():
-        sums_ref[...] = jnp.zeros_like(sums_ref)
-
     b_blk = b_ref[...]
     b2 = jnp.concatenate([b_blk, b_blk], 1)
     cum, step = cum_ref[...], step_ref[...]
@@ -640,7 +653,7 @@
     row_dots = jnp.zeros((Q, 128), F32)
     col_dots = jnp.zeros((Q, 128), F32)
     last_add = jnp.zeros((8, 128), F32)
-    grad_b = gbc_ref[:, 0:N]
+    grad_b = gbc_ref[here_rows, 0:N]
     for start in range(0, x_ref.shape[1], TILE):
         lanes = slice(start, start + TILE)
         spread = spread_ref[:, lanes]
@@ -655,7 +668,7 @@
         t_high, t_low = split2(touch)
         last_add = last_add + mm(jnp.concatenate([t_high, t_low], 1), gather2)
         s_high, s_low = split2(d_state)
-        gx = gx_ref[:, lanes] + expand(tail, spread) * mm(b2, jnp.concatenate([s_high, s_low], 0))
+        gx = gx_ref[here_rows, lanes] + expand(tail, spread) * mm(b2, jnp.concatenate([s_high, s_low], 0))
         w_high, w_low = split2(expand(tail_step, spread) * x_quad)
         grad_b = grad_b + mm_nt(
             jnp.concatenate([w_high, w_low, w_high], 1), jnp.concatenate([s_high, s_high, s_low], 1)
@@ -675,50 +688,168 @@
     sums_ref[0:1, :] += jnp.sum(grad_rate * step, axis=0, keepdims=True)
     sums_ref[1:2, :] += jnp.sum(grad_raw, axis=0, keepdims=True)
     gbc_out_ref[:, 0:N] = grad_b
-    gbc_out_ref[:, N : 2 * N] = gbc_ref[:, N : 2 * N]
-
-
-def scan_backward_far(
-    dy, act, y, gx, step, cum, step_in, spread, gather, after, late, states, early, offs, head_rows, skip, gbc
+    gbc_out_ref[:, N : 2 * N] = gbc_ref[here_rows, N : 2 * N]
+
+
+def backward_kernel(
+    cols, dps,
+    dy_ref, x_ref, y_ref, b_ref, c_ref, step_ref, cum_ref, stepin_ref, spread_ref, gather_ref, after_ref,
+    state_ref, early_ref, offs_ref, head_ref, skip_ref, o_low, o_full, g_low, g_full, late_ref, parts,
+    ga_ref, gstep_ref, gbc_out_ref, sums_ref, o_total_ref, g_own_ref, g_cross_ref, branch_in,
+    gx_ref, gbc_ref, o_own, o_land, o_cross, o_cross_land, g_own, g_land, sems, local,
+):
+    step_at = pl.program_id(0)
+    blocks = pl.num_programs(0) // 2
+    at_block = lax.rem(step_at, blocks)
+    here_rows = pl.ds(pl.multiple_of(at_block * Q, Q), Q)
+    dp, row, col = here()
+    group = cols // 2
+    shard = g_own_ref.shape[1]
+    others = dps - 1
+    own, other = pl.ds(0, shard), pl.ds(shard, shard)
+
+    def o_moves():
+        return dp_copies(dps, sems, lambda to, i: o_low.at[:, to], lambda to, i: o_land.at[i])
+
+    def g_moves():
+        return dp_copies(dps, sems, lambda to, i: g_low.at[to], lambda to, i: g_land.at[i], others)
+
+    def cross_move():
+        return copy_to(o_cross, o_cross_land, sems, 2 * others, mirror_of(cols))
+
+    def part_moves():
+        return [
+            copy_to(
+                parts.at[by - 1], branch_in.at[by - 1], sems, 2 * others + by, (dp, row, col ^ by)
+            )
+            for by in range(1, group)
+        ]
+
+    load_o = pltpu.make_async_copy(o_full.at[:, dp], o_own, local.at[0])
+    load_g = pltpu.make_async_copy(g_full.at[dp], g_own, local.at[1])
+
+    @at_step(0)
+    def _():
+        greet(dp_peers(dps) + [mirror_of(cols)] + [(dp, row, col ^ by) for by in range(1, group)])
+        for move in o_moves() + part_moves():
+            move.start()
+        load_o.start()
+        load_g.start()
+
+        sums_ref[...] = jnp.zeros_like(sums_ref)
+
+    @pl.when(step_at < blocks)
+    def _():
+        near_block(
+            at_block, here_rows, dy_ref, x_ref, b_ref, c_ref, step_ref, cum_ref, spread_ref, state_ref,
+            early_ref, offs_ref, gx_ref, gbc_ref,
+        )
+
+    @pl.when(step_at == blocks)
+    def _():
+        for move in o_moves():
+            move.wait_recv()
+        for move in g_moves():
+            move.start()
+        load_o.wait()
+        for i in range(others):
+            o_own[...] += o_land[i].astype(F32)
+        o_cross[...] = o_own[1].astype(BF)
+        cross_move().start()
+
+    @pl.when(step_at >= blocks)
+    def _():
+        far_block(
+            blocks, at_block, here_rows, dy_ref, x_ref, y_ref, gx_ref, b_ref, step_ref, cum_ref, stepin_ref,
+            spread_ref, gather_ref, after_ref, late_ref, state_ref, early_ref, offs_ref, head_ref, skip_ref,
+            gbc_ref, ga_ref, gstep_ref, gbc_out_ref, sums_ref,
+        )
+
+    @at_step(2 * blocks - 1)
+    def _():
+        cross_move().wait()
+        o_total_ref[...] = o_own[0] + o_cross_land[...].astype(F32)
+        load_g.wait()
+        for move in g_moves():
+            move.wait()
+        for i in range(others):
+            g_own[...] += g_land[i].astype(F32)
+        g_own_ref[...] = g_own[:, :shard]
+        g_cross_ref[...] = g_own[:, shard:].astype(BF)
+        for move in part_moves():
+            move.wait()
+        for move in o_moves():
+            move.wait_send()
+
+
+def scan_backward(
+    cols, dps, dy, act, y, step, cum, step_in, spread, gather, after, states, early, offs, head_rows, skip,
+    o_low, o_full, g_low, g_full, late, parts,
 ):
     tokens, channels = dy.shape
-    rows = pl.BlockSpec((Q, channels), lambda i: (i, 0))
-    heads = pl.BlockSpec((Q, 128), lambda i: (i, 0))
-    pairs = pl.BlockSpec((Q, 2 * N), lambda i: (i, 0))
+    blocks, group, shard = tokens // Q, cols // 2, channels // 2
+    piece, half = o_low.shape[2:]
+    piece_g = g_low.shape[1]
+    block = lambda i: lax.rem(i, blocks)
+    second = lambda i: jnp.maximum(i - blocks, 0)
+    rows = lambda at, width: pl.BlockSpec((Q, width), lambda i: (at(i), 0))
+    vmem = pltpu.VMEM
     return pl.pallas_call(
-        backward_far_kernel,
-        grid=(tokens // Q,),
+        partial(backward_kernel, cols, dps),
+        grid=(2 * blocks,),
         in_specs=[
-            rows,
-            rows,
-            rows,
-            rows,
-            pl.BlockSpec((Q, N), lambda i: (i, channels // N)),
-            heads,
-            heads,
-            heads,
-            whole((256, channels)),
-            whole((channels, 128)),
-            pl.BlockSpec((1, N, channels), lambda i: (i, 0, 0)),
-            whole((N, channels)),
-            pl.BlockSpec((1, N, channels), lambda i: (i + 1, 0, 0)),
-            whole((N, channels)),
+            rows(block, channels),
+            rows(block, channels),
+            rows(second, channels),
+            pl.BlockSpec((Q, N), lambda i: (block(i), channels // N)),
+            pl.BlockSpec((Q, N), lambda i: (block(i), channels // N + 1)),
+            rows(block, 128),
+            rows(block, 128),
+            rows(second, 128),
+            whole(spread.shape),
+            whole(gather.shape),
+            pl.BlockSpec((1, N, channels), lambda i: (second(i), 0, 0)),
+            pl.BlockSpec((1, N, channels), lambda i: (block(i) + lax.div(i, blocks), 0, 0)),
+            whole(early.shape),
             whole((16, 128)),
             whole((8, 128)),
             whole((8, channels)),
-            pairs,
-        ],
-        out_specs=[rows, heads, pairs, whole((8, 128))],
+        ] + [ANY] * 4 + [whole(late.shape), ANY],
+        out_specs=[
+            rows(second, channels),
+            rows(second, 128),
+            rows(second, 2 * N),
+            whole((8, 128)),
+            whole((piece, half)),
+            whole((piece_g, shard)),
+            whole((piece_g, shard)),
+            ANY,
+        ],
         out_shape=[
             sds((tokens, channels)),
             sds((tokens, 128), BF),
             sds((tokens, 2 * N)),
             sds((8, 128)),
-        ],
-        compiler_params=params(),
-        cost_estimate=cost(14),
-        name="scan_backward_far",
-    )(dy, act, y, gx, act, step, cum, step_in, spread, gather, after, late, states, early, offs, head_rows, skip, gbc)
+            sds((piece, half)),
+            sds((piece_g, shard)),
+            sds((piece_g, shard), BF),
+            sds(parts.shape, BF),
+        ],
+        scratch_shapes=[
+            vmem((tokens, channels), F32), vmem((tokens, 2 * N), F32),
+            vmem((2, piece, half), F32), vmem((dps - 1, 2, piece, half), BF),
+            vmem((piece, half), BF), vmem((piece, half), BF),
+            vmem((piece_g, channels), F32), vmem((dps - 1, piece_g, channels), BF),
+            pltpu.SemaphoreType.DMA((2, 2 * (dps - 1) + group)),
+            pltpu.SemaphoreType.DMA((2,)),
+        ],
+        compiler_params=remote_params(3),
+        cost_estimate=cost(55),
+        name="scan_backward",
+    )(
+        dy, act, y, act, act, step, cum, step_in, spread, gather, after, states, early, offs, head_rows, skip,
+        o_low, o_full, g_low, g_full, late, parts,
+    )
 
 
 def gate_kernel(
@@ -845,7 +976,7 @@
     )(graw, y, gm, act, stats, vectors)
 
 
-def conv_back_kernel(ga_ref, raw_ref, taps_ref, gv_ref, sums_ref, g_pad):
+def conv_back_tile(ga_ref, raw_ref, taps_ref, gv_ref, sums_ref, g_pad):
     tokens, width = ga_ref.shape
     taps = taps_ref[...]
     g_pad[0:HALO, :] = jnp.zeros((HALO, width), F32)
@@ -871,52 +1002,45 @@
         sums_ref[k : k + 1, :] = sums[k]
 
 
-def conv_back(ga, raw, taps):
-    tokens, channels = ga.shape
-    width = min(channels, TILE)
-    return pl.pallas_call(
-        conv_back_kernel,
-        grid=(channels // width,),
-        in_specs=[columns(tokens, width), columns(tokens + HALO, width), columns(8, width)],
-        out_specs=[columns(tokens + HALO, width), columns(8, width)],
-        out_shape=[sds((tokens + HALO, channels), BF), sds((8, channels))],
-        scratch_shapes=[pltpu.VMEM((tokens + 2 * HALO, width), F32)],
-        compiler_params=params(),
-        cost_estimate=cost(8 * channels / 1536),
-        name="conv_back",
-    )(ga, raw, taps)
-
-
 def mm_tn(a, b):
     return lax.dot_general(a, b, (((0,), (0,)), ((), ())), preferred_element_type=F32)
 
 
-def weight_grad_kernel(skips, widths, left_ref, *refs):
-    rights, out_ref = refs[:-1], refs[-1]
-    rows = left_ref.shape[0]
+def weight_grad_kernel(skips, widths, outs, *refs):
+    out_ref = refs[-outs]
+    sources = len(skips)
+    lefts, rights = refs[:sources], refs[sources:-outs]
     at = 0
-    for skip, width, right in zip(skips, widths, rights):
-        out_ref[:, at : at + width] = mm_tn(left_ref[skip:rows, :], right[...])
+    for i, width in enumerate(widths):
+        total = None
+        for source in range(sources):
+            left, right = lefts[source], rights[source * len(widths) + i]
+            part = mm_tn(left[skips[source][i] :, :], right[...])
+            total = part if total is None else total + part
+        out_ref[:, at : at + width] = total
+        if outs > 1:
+            refs[-1][:, at : at + width] = total.astype(BF)
         at += width
 
 
-def weight_grad(left, rights):
-    rows, height = left.shape
-    widths = [right.shape[1] for right in rights]
-    skips = [rows - right.shape[0] for right in rights]
+def weight_grad(lefts, rights, low=False):
+    height = lefts[0].shape[1]
+    widths = [right.shape[1] for right in rights[0]]
+    skips = [[left.shape[0] - r.shape[0] for r in group] for left, group in zip(lefts, rights)]
+    flat = [r for group in rights for r in group]
     return pl.pallas_call(
-        partial(weight_grad_kernel, skips, widths),
+        partial(weight_grad_kernel, skips, widths, 1 + low),
         grid=(height // TILE,),
-        in_specs=[columns(rows)] + [whole(right.shape) for right in rights],
-        out_specs=pl.BlockSpec((TILE, sum(widths)), lambda j: (j, 0)),
-        out_shape=sds((height, sum(widths))),
+        in_specs=[columns(left.shape[0]) for left in lefts] + [whole(r.shape) for r in flat],
+        out_specs=[pl.BlockSpec((TILE, sum(widths)), lambda j: (j, 0))] * (1 + low),
+        out_shape=[sds((height, sum(widths))), sds((height, sum(widths)), BF)][: 1 + low],
         compiler_params=params(),
-        cost_estimate=cost(7),
+        cost_estimate=cost(8),
         name="weight_grad",
-    )(left, *rights)
-
-
-def input_grad_kernel(
+    )(*lefts, *flat)
+
+
+def input_grad_tile(
     gv_ref, gg_ref, gs_ref, gt_ref, v_ref, g_ref, s_ref, t_ref, tok_ref, inv_ref, out_ref, low_ref, sums_ref
 ):
     rows = gv_ref.shape[0]
@@ -934,30 +1058,209 @@
     sums_ref[...] = jnp.broadcast_to(sums, (8, TILE))
 
 
-def input_grad(gv, gg, gs, gt, w_value, w_gate, w_state, w_step, tokens, inv_rms):
-    rows, channels = gv.shape
-    width = tokens.shape[1]
-    weight = lambda k: pl.BlockSpec((TILE, k), lambda j: (j, 0))
+def finish_kernel(
+    cols, dps, part, whole_state,
+    ga_ref, raw_ref, taps_ref, gg_ref, gt_ref, v_ref, g_ref, picked_ref, tok_ref, inv_ref, g_own_ref,
+    o_total, g_cross, gbc, normed, gt_hbm,
+    sums_ref, gn_ref, low_ref, norm_ref, joint_ref, o_out, g_out,
+    gv_vm, gv_sib, gs_vm, gs_sib, gt_sib, bc_own, bc_land, g_pad,
+    raw_part, taps_part, sums_part, g_pad_part, n_own, n_sib, o_vm, g_vm, g_land, sems, local,
+):
+    step = pl.program_id(0)
+    conv_steps = gv_vm.shape[1] // TILE
+    input_steps = 2 * n_own.shape[1] // TILE
+    dp, row, col = here()
+    group = cols // 2
+    place = lax.rem(col, group)
+    sibling = (dp, 1 - row, col)
+    peers = [(dp, row, col ^ by) for by in range(1, group)]
+    half = n_own.shape[1]
+    piece = o_total.shape[0]
+    span = gs_vm.shape[1]
+    others = dps - 1
+    out_rows = pl.ds(dp * piece, piece)
+    g_rows = pl.ds(dp * g_vm.shape[0], g_vm.shape[0])
+
+    def part_at(at):
+        return pl.ds(0, span) if whole_state else lanes_at(at, span)
+
+    def o_moves():
+        return dp_copies(dps, sems, lambda to, i: o_total, lambda to, i: o_out.at[out_rows, :])
+
+    def g_moves():
+        return dp_copies(dps, sems, lambda to, i: g_vm, lambda to, i: g_out.at[g_rows, :], others)
+
+    first = 2 * others
+    g_move = lambda: copy_to(g_cross, g_land, sems, first, mirror_of(cols))
+    n_move = lambda: copy_to(normed.at[:, lanes_at(1 - row, half)], n_sib, sems, first + 1, sibling)
+    t_move = lambda: copy_to(gt_hbm, gt_sib, sems, first + 2, sibling)
+    s_move = lambda: copy_to(gs_vm, gs_sib, sems, first + 3, sibling)
+
+    def bc_moves():
+        return [
+            copy_to(gbc.at[:, part_at(place ^ by)], bc_land.at[by - 1], sems, first + 3 + by, peers[by - 1])
+            for by in range(1, group)
+        ]
+
+    def v_move(tile):
+        lanes = lanes_at(tile, TILE)
+        return copy_to(gv_vm.at[:, lanes], gv_sib.at[:, lanes], sems, first + 3 + group + tile, sibling)
+
+    load_bc = pltpu.make_async_copy(gbc.at[:, part_at(place)], bc_own, local.at[0])
+    load_n = pltpu.make_async_copy(normed.at[:, lanes_at(row, half)], n_own, local.at[1])
+    load_o = pltpu.make_async_copy(o_total, o_vm, local.at[2])
+    store_o = pltpu.make_async_copy(o_vm, o_out.at[out_rows, :], local.at[3])
+    store_g = pltpu.make_async_copy(g_vm, g_out.at[g_rows, :], local.at[4])
+
+    @at_step(0)
+    def _():
+        load_o.start()
+        load_bc.start()
+        load_n.start()
+        greet([sibling, mirror_of(cols)] + peers + dp_peers(dps))
+        for move in bc_moves() + [g_move()] + o_moves() + [t_move(), n_move()]:
+            move.start()
+        load_o.wait()
+        store_o.start()
+
+    @pl.when(step < conv_steps)
+    def _():
+        conv_back_tile(
+            ga_ref, raw_ref, taps_ref, gv_vm.at[:, lanes_at(step, TILE)], sums_ref, g_pad
+        )
+        v_move(step).start()
+
+    @pl.when(step == conv_steps)
+    def _():
+        load_bc.wait()
+        for move in bc_moves():
+            move.wait_recv()
+        for i in range(group - 1):
+            bc_own[...] += bc_land[i]
+        if whole_state:
+            lane = iota2(bc_own.shape, 1)
+            mine = (lane >= place * part) & (lane < place * part + part)
+            bc_own[...] = jnp.where(mine, bc_own[...], 0.0)
+        lanes = part_at(place)
+        sums_ref[...] = jnp.zeros_like(sums_ref)
+        raw_part[...] = raw_ref[:, lanes]
+        taps_part[...] = taps_ref[:, lanes]
+        conv_back_tile(bc_own, raw_part, taps_part, gs_vm, sums_part, g_pad_part)
+        sums_ref[:, 0:span] = sums_part[...]
+        s_move().start()
+        g_move().wait_recv()
+        g_vm[...] = g_own_ref[...] + g_land[...].astype(F32)
+        for move in g_moves():
+            move.start()
+        store_g.start()
+
+    @pl.when((step > conv_steps) & (step <= conv_steps + input_steps))
+    def _():
+        input_grad_tile(
+            gv_vm, gg_ref, gs_vm, gt_ref, v_ref, g_ref, picked_ref.at[:, part_at(place)],
+            picked_ref.at[:, pl.ds(TILE, 128)], tok_ref, inv_ref, gn_ref, low_ref, norm_ref,
+        )
+
+    @pl.when(step == conv_steps + input_steps + 1)
+    def _():
+        load_n.wait()
+        for move in [n_move(), t_move(), s_move()]:
+            move.wait_recv()
+        for tile in range(conv_steps):
+            v_move(tile).wait_recv()
+
+    @pl.when(step > conv_steps + input_steps)
+    def _():
+        lanes = lanes_at(step - conv_steps - input_steps - 1, TILE)
+        channels = gv_vm.shape[1]
+        left, left_sib = n_own[:, lanes], n_sib[:, lanes]
+        joint_ref[:, 0:channels] = mm_tn(left, gv_vm[...]) + mm_tn(left_sib, gv_sib[...])
+        joint_ref[:, channels : channels + span] = mm_tn(left, gs_vm[...]) + mm_tn(left_sib, gs_sib[...])
+        joint_ref[:, channels + span :] = mm_tn(left[HALO:, :], gt_ref[...]) + mm_tn(left_sib[HALO:, :], gt_sib[...])
+
+    @at_step(pl.num_programs(0) - 1)
+    def _():
+        store_o.wait()
+        store_g.wait()
+        for move in o_moves() + g_moves():
+            move.wait()
+        for move in bc_moves() + [g_move(), n_move(), t_move(), s_move()]:
+            move.wait_send()
+        for tile in range(conv_steps):
+            v_move(tile).wait_send()
+
+
+def finish(
+    cols, dps, part, ga, raw, taps, gg, gt, w_value, w_gate, picked, tokens_in, inv_rms, g_own, o_total, g_cross,
+    gbc, normed,
+):
+    tokens, channels = ga.shape
+    rows, width = normed.shape
+    half = width // 2
+    whole_state = part % 128 != 0
+    span = 2 * N if whole_state else part
+    group = cols // 2
+    conv_steps, input_steps, weight_steps = channels // TILE, width // TILE, half // TILE
+    piece = o_total.shape[0]
+    joint_width = channels + span + 128
+
+    def clamp(first, count):
+        return lambda i: jnp.clip(i - first, 0, count - 1)
+
+    conv, input_at = clamp(0, conv_steps), clamp(conv_steps + 1, input_steps)
+    both = clamp(0, conv_steps + 1)
+    weight_at = clamp(conv_steps + 1 + input_steps, weight_steps)
+    lanes = lambda at, count: pl.BlockSpec((count, TILE), lambda i: (0, at(i)))
+    slab = lambda at, size: pl.BlockSpec((TILE, size), lambda i: (at(i), 0))
+    vmem = pltpu.VMEM
+    copies = 2 * (dps - 1) + 3 + group + conv_steps
     return pl.pallas_call(
-        input_grad_kernel,
-        grid=(width // TILE,),
+        partial(finish_kernel, cols, dps, part, whole_state),
+        grid=(conv_steps + 1 + input_steps + weight_steps,),
         in_specs=[
-            whole(gv.shape), whole(gg.shape), whole(gs.shape), whole(gt.shape),
-            weight(channels), weight(channels), weight(gs.shape[1]), weight(128),
-            columns(rows), whole(inv_rms.shape),
-        ],
-        out_specs=[columns(rows), columns(rows), columns(8)],
-        out_shape=[sds((rows, width)), sds((rows, width), BF), sds((8, width))],
-        compiler_params=params(),
-        cost_estimate=cost(12),
-        name="input_grad",
-    )(gv, gg, gs, gt, w_value, w_gate, w_state, w_step, tokens, inv_rms)
+            lanes(conv, tokens),
+            lanes(both, rows),
+            lanes(both, 8),
+            whole(gg.shape),
+            whole(gt.shape),
+            slab(input_at, channels),
+            slab(input_at, channels),
+            slab(input_at, TILE + 128),
+            lanes(input_at, rows),
+            whole(inv_rms.shape),
+            whole(g_own.shape),
+        ] + [ANY] * 5,
+        out_specs=[
+            lanes(both, 8), lanes(input_at, rows), lanes(input_at, rows), lanes(input_at, 8),
+            slab(weight_at, joint_width), ANY, ANY,
+        ],
+        out_shape=[
+            sds((8, channels + TILE)), sds((rows, width)), sds((rows, width), BF), sds((8, width)),
+            sds((half, joint_width)), sds((dps * piece, o_total.shape[1])),
+            sds((dps * g_own.shape[0], g_own.shape[1])),
+        ],
+        scratch_shapes=[
+            vmem((rows, channels), BF), vmem((rows, channels), BF), vmem((rows, span), BF), vmem((rows, span), BF),
+            vmem((tokens, 128), BF), vmem((tokens, span), F32), vmem((max(group - 1, 1), tokens, span), F32),
+            vmem((tokens + 2 * HALO, TILE), F32), vmem((rows, span), F32), vmem((8, span), F32),
+            vmem((8, span), F32), vmem((tokens + 2 * HALO, span), F32),
+            vmem((rows, half), BF), vmem((rows, half), BF),
+            vmem(o_total.shape, F32), vmem(g_own.shape, F32), vmem(g_own.shape, BF),
+            pltpu.SemaphoreType.DMA((2, copies)),
+            pltpu.SemaphoreType.DMA((5,)),
+        ],
+        compiler_params=remote_params(5),
+        cost_estimate=cost(55),
+        name="finish",
+    )(
+        ga, raw, taps, gg, gt, w_value, w_gate, picked, tokens_in, inv_rms, g_own, o_total, g_cross, gbc, normed, gt,
+    )
 
 
 def settle_kernel(
-    cols, dps, heads, gn, gnb, joint, flat, tok, cot, gain,
+    cols, dps, heads, span, gn, gnb, joint, flat, tok, cot, gain,
     tg_out, v_out, ext_out, flat_out,
-    mine_a, land_a, mine_b, land_b, send_a, rec_a, send_b, rec_b, tot_a, tot_b,
+    mine_a, mine_b, send_a, rec_a, send_b, rec_b, tot_a, tot_b,
     z_send, z_land, step_land, state_land, ext, acc, flat_land,
     gn_own, gn_land, halo_land, tok_vm, cot_vm, gain_vm, local, send, recv,
 ):
@@ -1002,9 +1305,8 @@
         return copy
 
     part_a, part_b = pl.ds(shard, wide_a), pl.ds(0, shard)
-    my_rows, other_rows = pl.ds(row * half, half), pl.ds((1 - row) * half, half)
-    load_a = keep(joint.at[my_rows, part_a], mine_a)
-    load_b = keep(joint.at[my_rows, part_b], mine_b)
+    load_a = keep(joint.at[:, part_a], mine_a)
+    load_b = keep(joint.at[:, part_b], mine_b)
     load_flat = keep(flat, acc)
     loads = [
         keep(gn.at[pl.ds(HALO + place * count, count), :], gn_own),
@@ -1017,8 +1319,6 @@
         + [col_peer(by) for by in range(1, cols)]
         + [dp_peer(by) for by in range(1, dps)]
     )
-    core_a = launch(joint.at[other_rows, part_a], land_a, sibling)
-    core_b = launch(joint.at[other_rows, part_b], land_b, sibling)
     gn_moves = [
         launch(gnb.at[pl.ds(HALO + (place ^ by) * count, count), :], gn_land.at[by - 1], col_peer(by))
         for by in range(1, group)
@@ -1063,44 +1363,45 @@
     load_flat.wait()
     flat_next()
 
-    def hand_out(load, core, mine, land, total, sends, recs):
+    def hand_out(load, mine, total, sends, recs):
         load.wait()
-        arrive([core])
         moves = []
         for by in range(1, dps):
             rows = pl.ds(pl.multiple_of((dp ^ by) * piece, 16), piece)
-            sends[by - 1] = (mine[rows, :] + land[rows, :]).astype(BF)
+            sends[by - 1] = mine[rows, :].astype(BF)
             moves.append(launch(sends.at[by - 1], recs.at[by - 1], dp_peer(by)))
-        rows = pl.ds(pl.multiple_of(dp * piece, 16), piece)
-        total[...] = mine[rows, :] + land[rows, :]
+        total[...] = mine[pl.ds(pl.multiple_of(dp * piece, 16), piece), :]
         return moves
 
-    moves_a = hand_out(load_a, core_a, mine_a, land_a, tot_a, send_a, rec_a)
+    moves_a = hand_out(load_a, mine_a, tot_a, send_a, rec_a)
     flat_next()
-    moves_b = hand_out(load_b, core_b, mine_b, land_b, tot_b, send_b, rec_b)
+    moves_b = hand_out(load_b, mine_b, tot_b, send_b, rec_b)
     flat_next()
     arrive(moves_a)
     for by in range(1, dps):
         tot_a[...] += rec_a[by - 1].astype(F32)
     z_send[...] = tot_a[:, 0:shard].astype(BF)
     z_move = launch(z_send, z_land, mirror)
-    step_move = launch(tot_a.at[:, pl.ds(shard + N, 128)], step_land, mirror)
-    state_block = tot_a.at[:, pl.ds(shard, N)]
+    step_move = launch(tot_a.at[:, pl.ds(shard + span, 128)], step_land, mirror)
+    state_block = tot_a.at[:, pl.ds(shard, span)]
     state_moves = [launch(state_block, state_land.at[col], col_peer(by)) for by in range(1, cols)]
-    state_land[col] = tot_a[:, shard : shard + N]
+    state_land[col] = tot_a[:, shard : shard + span]
     flat_next()
     arrive(moves_b)
     for by in range(1, dps):
         tot_b[...] += rec_b[by - 1].astype(F32)
     arrive([z_move, step_move])
     tot_b[...] += z_land[...].astype(F32)
-    ext[:, 0:128] = tot_a[:, shard + N : shard + N + 128] + pltpu.roll(step_land[...], 128 - heads, 1)
+    ext[:, 0:128] = tot_a[:, shard + span : shard + span + 128] + pltpu.roll(step_land[...], 128 - heads, 1)
     out_rows = pl.ds(dp * piece, piece)
     v_moves = [launch(tot_b, v_out.at[out_rows, :], dp_peer(by)) for by in range(1, dps)]
     v_keep = keep(tot_b, v_out.at[out_rows, :])
     arrive(state_moves)
-    part = col // 2
-    ext[:, 128:256] = state_land[part] + state_land[part + group]
+    if span == 2 * N:
+        ext[:, 128:] = sum(state_land[i] for i in range(cols))
+    else:
+        part = col // 2
+        ext[:, 128:] = state_land[part] + state_land[part + group]
     e_moves = [launch(ext, ext_out.at[out_rows, :], dp_peer(by)) for by in range(1, dps)]
     e_keep = keep(ext, ext_out.at[out_rows, :])
     flat_next()
@@ -1141,32 +1442,31 @@
         copy.wait_send()
 
 
-def settle(cols, dps, heads, gn, gnb, joint, flat, tokens, cotangent, gain, shard):
-    width, wide = joint.shape
-    half, wide_a = width // 2, wide - shard
+def settle(cols, dps, heads, span, gn, gnb, joint, flat, tokens, cotangent, gain, shard):
+    half, wide = joint.shape
+    width, wide_a = 2 * half, wide - shard
     piece = half // dps
     count = tokens.shape[0]
     group = cols // 2
     any_spec = pl.BlockSpec(memory_space=pl.ANY)
     steps = (dps.bit_length() - 1) + (cols.bit_length() - 1) + 1
-    copies = 2 + (group - 1) + group + steps + 4 * (dps - 1) + 2 + (cols - 1)
+    copies = (group - 1) + group + steps + 4 * (dps - 1) + 2 + (cols - 1)
     vmem = pltpu.VMEM
     return pl.pallas_call(
-        partial(settle_kernel, cols, dps, heads),
+        partial(settle_kernel, cols, dps, heads, span),
         in_specs=[any_spec] * 7,
         out_specs=[any_spec] * 4,
         out_shape=[
-            sds((count, width)), sds((half, shard)), sds((half, 256)), sds(flat.shape),
+            sds((count, width)), sds((half, shard)), sds((half, 128 + span)), sds(flat.shape),
         ],
         scratch_shapes=[
-            vmem((half, wide_a), F32), vmem((half, wide_a), F32),
-            vmem((half, shard), F32), vmem((half, shard), F32),
+            vmem((half, wide_a), F32), vmem((half, shard), F32),
             vmem((dps - 1, piece, wide_a), BF), vmem((dps - 1, piece, wide_a), BF),
             vmem((dps - 1, piece, shard), BF), vmem((dps - 1, piece, shard), BF),
             vmem((piece, wide_a), F32), vmem((piece, shard), F32),
             vmem((piece, shard), BF), vmem((piece, shard), BF),
-            vmem((piece, 128), F32), vmem((cols, piece, N), F32),
-            vmem((piece, 256), F32),
+            vmem((piece, 128), F32), vmem((cols, piece, span), F32),
+            vmem((piece, 128 + span), F32),
             vmem(flat.shape, F32), vmem((steps,) + flat.shape, F32),
             vmem((count, width), F32), vmem((max(group - 1, 1), count, width), BF),
             vmem((group, HALO, width), BF),
@@ -1209,15 +1509,6 @@
         other = lax.ppermute(piece, "dp", flips(size, by))
         out = lax.dynamic_update_slice_in_dim(out, other, (dp ^ by) * rows, 0)
     return out
-
-
-def reduce_dp(values, dp):
-    size = lax.axis_size("dp")
-    total = lax.dynamic_index_in_dim(values, dp, 0, keepdims=False)
-    for by in range(1, size):
-        piece = lax.dynamic_index_in_dim(values, dp ^ by, 0, keepdims=False).astype(BF)
-        total = total + lax.ppermute(piece, "dp", flips(size, by)).astype(F32)
-    return total
 
 
 def swap_core(values):
@@ -1251,9 +1542,21 @@
     small = jnp.pad(
         jnp.concatenate([w_state, w_step], axis=1), ((0, 0), (0, 128 - state_width - heads))
     )
-    group_tokens, value_full, gate_full, out_full, small_full = import_all(
-        cols, dps, tokens, w_value, w_gate, w_out, small
-    )
+    heads_row = jnp.pad(
+        jnp.concatenate([d_skip, a_log, dt_bias]), (0, shard - 3 * heads)
+    )[None]
+    state_rows = jnp.concatenate([conv_state.T, bias_state[None]], axis=0)
+    vec = jnp.concatenate(
+        [
+            conv_value.T, bias_value[None], mix_gain[None], heads_row, jnp.zeros((1, shard), BF),
+            jnp.pad(state_rows, ((0, 3), (0, shard - state_width))),
+        ],
+        axis=0,
+    )
+    group_tokens, value_full, gate_full, out_full, small_full, vecs = import_all(
+        cols, dps, tokens, w_value, w_gate, w_out, small, vec
+    )
+    cotangent, group_tokens = lax.optimization_barrier((cotangent, group_tokens))
     from_col = lax.broadcasted_iota(jnp.int32, (cols * 128, TILE + 128), 0) // 128
     from_lane = lax.broadcasted_iota(jnp.int32, (cols * 128, TILE + 128), 0) % 128
     to = lax.broadcasted_iota(jnp.int32, (cols * 128, TILE + 128), 1)
@@ -1273,44 +1576,32 @@
             out = lax.dynamic_update_slice_in_dim(out, other, at * local, 0)
         return out
 
-    def per_channel(own_taps, own_bias):
-        taps = jnp.concatenate([own_taps.astype(F32).T, own_bias.astype(F32)[None]], axis=0)
-        return jnp.pad(taps, ((0, 3), (0, 0)))
-
-    packed = jnp.concatenate(
+    vecs = vecs.astype(F32)
+    both = jnp.concatenate(
         [
-            per_channel(conv_value, bias_value)[:5],
-            mix_gain.astype(F32)[None],
-            jnp.repeat(d_skip.astype(F32), HEAD)[None],
-            jnp.pad(
-                jnp.concatenate([a_log.astype(F32), dt_bias.astype(F32)]), (0, shard - 2 * heads)
-            )[None],
-        ],
-        axis=0,
-    )
-    packed_both = jnp.concatenate([packed, lax.ppermute(packed, "col", mirror)], axis=1)
-    state_vec = per_channel(conv_state, bias_state)
-    state_vecs = jnp.zeros((8, state_all), F32)
-    state_vecs = lax.dynamic_update_slice_in_dim(state_vecs, state_vec, col * state_width, 1)
-    state_vecs = butterfly(state_vecs, "col")
-    value_taps = jnp.concatenate([packed_both[:5], jnp.zeros((3, channels), F32)], axis=0)
-    taps = jnp.concatenate([value_taps, state_vecs], axis=1)
+            lax.dynamic_index_in_dim(vecs, col, 0, keepdims=False),
+            lax.dynamic_index_in_dim(vecs, cols - 1 - col, 0, keepdims=False),
+        ],
+        axis=1,
+    )
+    state_vecs = jnp.transpose(vecs[:, 8:16, :state_width], (1, 0, 2)).reshape(8, state_all)
+    taps = jnp.concatenate([both[0:8], state_vecs], axis=1)
+
+    def both_heads(at):
+        return jnp.concatenate(
+            [both[6, at * heads : (at + 1) * heads], both[6, shard + at * heads : shard + (at + 1) * heads]]
+        )
+
+    skip_both, a_both, dt_both = both_heads(0), both_heads(1), both_heads(2)
     vectors = jnp.concatenate(
-        [packed_both[6:7], packed_both[5:6], jnp.zeros((6, channels), F32)], axis=0
-    )
-    head_own, head_mirror = packed_both[7, :shard], packed_both[7, shard:]
-    a_both = jnp.concatenate([head_own[:heads], head_mirror[:heads]])
-    dt_both = jnp.concatenate([head_own[heads : 2 * heads], head_mirror[heads : 2 * heads]])
+        [jnp.repeat(skip_both, HEAD)[None], both[5:6], jnp.zeros((6, channels), F32)], axis=0
+    )
     rate = -jnp.exp(a_both)
-    head_rows = jnp.zeros((8, 128), F32)
-    head_rows = head_rows.at[0, : 2 * heads].set(dt_both).at[1, : 2 * heads].set(rate)
-    head_of = lax.broadcasted_iota(jnp.int32, (128, channels), 1) // HEAD
-    spread_one = (head_of == lax.broadcasted_iota(jnp.int32, (128, channels), 0)).astype(BF)
-    spread = jnp.concatenate([spread_one, spread_one], axis=0)
-    gather = (
-        lax.broadcasted_iota(jnp.int32, (channels, 128), 0) // HEAD
-        == lax.broadcasted_iota(jnp.int32, (channels, 128), 1)
-    ).astype(BF)
+    head_rows = jnp.pad(jnp.stack([dt_both, rate]), ((0, 6), (0, 128 - 2 * heads)))
+    head_of = np.arange(channels) // HEAD
+    one_hot = (np.arange(128)[:, None] == head_of[None, :]).astype(np.float32)
+    spread = jnp.asarray(np.concatenate([one_hot, one_hot], axis=0), BF)
+    gather = jnp.asarray(one_hot.T, BF)
 
     gain = norm_gain.astype(F32)
     raw, act, normed, step_in, step, cum, grow, offs, inv_rms, picked = project(
@@ -1335,73 +1626,46 @@
     stats_pad = jnp.pad(stats, ((0, 120), (0, 0)))
     mixed, grad_gate, dy, mix_sums = mix_backward(inner_channels, graw, y, gm, act, stats_pad, vectors)
 
-    def scatter_rows(make):
-        parts = []
-        for by in range(1, group):
-            part = make(lax.rem(place + by, group)).astype(BF)
-            parts.append(lax.ppermute(part, "col", ring(by)))
-        total = make(place)
-        for part in parts:
-            total = total + part.astype(F32)
-        return total
-
     after, first_grad = scan_grad_states(dy, act, cum, spread)
     late = cross(first_grad, back)
-    branch = scatter_rows(lambda at: mm(at_rows(mixed, at, local), out_full))
-    block_out = (tokens.astype(F32) + branch).astype(BF)
-
-    def halves(values, axis):
-        size = values.shape[axis] // 2
-        mine = lax.dynamic_slice_in_dim(values, row * size, size, axis)
-        return mine, lax.dynamic_slice_in_dim(values, (1 - row) * size, size, axis)
-
-    def reduce_weight(values):
-        mine, other = halves(values, 0)
-        kept = mine + swap_core(other)
-        return reduce_dp(kept.reshape(dps, -1, values.shape[1]), dp)
-
-    def settle_shards(own, other):
-        total = own + lax.ppermute(other.astype(BF), "col", mirror).astype(F32)
-        return collect_dp(total, dp)
-
-    grad_out = weight_grad(mixed, [group_cot])
-    out_mine, out_other = halves(grad_out, 1)
-    out_kept = (out_mine + swap_core(out_other)).reshape(2, dps, -1, half_width)
-    out_piece = reduce_dp(jnp.transpose(out_kept, (1, 0, 2, 3)), dp)
-    sum_out = settle_shards(out_piece[0], out_piece[1])
-
-    gate_piece = reduce_weight(weight_grad(normed, [grad_gate]))
-    sum_gate = settle_shards(gate_piece[:, :shard], gate_piece[:, shard:])
-
-    gx, gbc_near = scan_backward_near(dy, act, step, cum, spread, states, early, offs)
-    ga, grad_step, gbc, head_sums = scan_backward_far(
-        dy, act, y, gx, step, cum, step_in, spread, gather, after, late, states, early, offs,
-        head_rows, vectors, gbc_near,
-    )
+    branch_rows = lambda at: mm(at_rows(mixed, at, local), out_full)
+    parts = jnp.stack([branch_rows(place ^ by).astype(BF) for by in range(1, group)])
+    branch = branch_rows(place)
+
+    def my_half(values):
+        mine = lax.dynamic_slice_in_dim(values, row * half_width, half_width, 1)
+        return [mine, swap_core(lax.dynamic_slice_in_dim(values, (1 - row) * half_width, half_width, 1))]
+
+    out_full_sum, out_low = weight_grad(
+        [mixed, swap_core(mixed)], [[half] for half in my_half(group_cot)], low=True
+    )
+    normed_halves = my_half(normed)
+    gate_full_sum, gate_low = weight_grad(normed_halves, [[grad_gate], [swap_core(grad_gate)]], low=True)
+    by_out = (2, dps, shard // dps, half_width)
+    by_gate = (dps, half_width // dps, channels)
+    ga, grad_step, gbc, head_sums, out_total, gate_own, gate_cross, branch_in = scan_backward(
+        cols, dps, dy, act, y, step, cum, step_in, spread, gather, after, states, early, offs, head_rows, vectors,
+        out_low.reshape(by_out), out_full_sum.reshape(by_out), gate_low.reshape(by_gate),
+        gate_full_sum.reshape(by_gate), late, parts,
+    )
+    block_out = (tokens.astype(F32) + branch + jnp.sum(branch_in.astype(F32), axis=0)).astype(BF)
     state_part = state_all // group
 
-    def state_slice(values, at):
-        return lax.dynamic_slice_in_dim(values, at * state_part, state_part, axis=1)
-
-    gbc_own = state_slice(gbc, place)
-    for by in range(1, group):
-        gbc_own = gbc_own + lax.ppermute(state_slice(gbc, lax.rem(place + by, group)), "col", ring(by))
-    gv, value_sums = conv_back(ga, raw, taps)
-    state_taps = state_slice(state_vecs, place)
-    gs, state_sums = conv_back(gbc_own, state_slice(raw[:, channels:], place), state_taps)
-
-    state_here, step_here = state_slice(picked, place), picked[:, TILE:]
-    grad_normed, grad_normed_low, norm_sums = input_grad(
-        gv, grad_gate, gs, grad_step, value_full, gate_full, state_here, step_here, group_tokens, inv_rms
-    )
-    joint = weight_grad(normed, [gv, jnp.pad(gs, ((0, 0), (0, N - state_part))), grad_step])
-
-    wide = jnp.concatenate([value_sums[:5], mix_sums[0:1]], axis=0)
+    value_sums, grad_normed, grad_normed_low, norm_sums, joint, sum_out, sum_gate = finish(
+        cols, dps, state_part, ga, raw, taps, grad_gate, grad_step, value_full, gate_full, picked, group_tokens,
+        inv_rms, gate_own, out_total, gate_cross, gbc, normed,
+    )
+    whole_state = state_part % 128 != 0
+    span = state_all if whole_state else state_part
+
+    wide = jnp.concatenate([value_sums[:5, :channels], mix_sums[0:1]], axis=0)
     wide_all = jnp.zeros((6, inner_channels), F32)
     wide_all = lax.dynamic_update_slice_in_dim(wide_all, wide[:, :shard], col * shard, 1)
     wide_all = lax.dynamic_update_slice_in_dim(wide_all, wide[:, shard:], (cols - 1 - col) * shard, 1)
     state_wide = jnp.zeros((5, state_all), F32)
-    state_wide = lax.dynamic_update_slice_in_dim(state_wide, state_sums[:5], place * state_part, 1)
+    state_wide = lax.dynamic_update_slice_in_dim(
+        state_wide, value_sums[:5, channels : channels + span], 0 if whole_state else place * state_part, 1
+    )
     skip_heads = jnp.sum(mix_sums[1].reshape(2 * heads, HEAD), axis=1)
     head_parts = jnp.stack([head_sums[0, : 2 * heads] * rate, skip_heads, head_sums[1, : 2 * heads]])
     head_all = jnp.zeros((3, heads * cols), F32)
@@ -1413,11 +1677,11 @@
     )
     flat = jnp.pad(flat, (0, -flat.size % 1024)).reshape(-1, 128)
     tokens_grad, sum_value, extra, flat = settle(
-        cols, dps, heads, grad_normed, grad_normed_low, joint, flat, tokens, cotangent, gain[None], shard
+        cols, dps, heads, span, grad_normed, grad_normed_low, joint, flat, tokens, cotangent, gain[None], shard
     )
     sum_step = extra[:, :heads]
     sum_state = lax.dynamic_slice_in_dim(
-        extra, 128 + lax.rem(col, cols // group) * state_width, state_width, axis=1
+        extra, 128 + (col if whole_state else lax.rem(col, cols // group)) * state_width, state_width, axis=1
     )
     flat = flat.reshape(-1)
     ends = [sum(lengths[: i + 1]) for i in range(4)]

time: 655 us -> 552 us (0.84)
  waiting for transfers between devices: 101 us -> 20.5 us
  other arithmetic: 32 us -> 10.7 us
  Pallas kernels: 417 us -> 432 us
  starting transfers between devices: 33.5 us -> 25.6 us
  local copies, waits for them, and re-layouts: 48.2 us -> 41 us
    ppermute x19 -> x0, waiting for transfers between devices: 97 us -> none  [the longest x6 37.8 us: collect_dp(): other = lax.ppermute(piece, 'dp', flips(size, by))]
    ppermute x19 -> x0, starting transfers between devices: 26 us -> none  [the longest x6 7.43 us: reduce_dp(): total = total + lax.ppermute(piece, 'dp', flips(size, by)).astype(F32)]
    ppermute x1, starting transfers between devices: 0.07 us -> 17.7 us  [per_device(): stats = stats + lax.ppermute(stats, 'col', flips(cols, by))]
    ppermute x2, waiting for transfers between devices: 1.05 us -> 18.3 us  [cross(): moved = lax.ppermute(values, 'col', pairs)]
    pallas_call x10 -> x6, Pallas kernels: 314 us -> 330 us  [the longest x1 89.7 us: import_all(): pl.pallas_call(partial(import_kernel, cols, dps), in_specs=[any_spec] * 6...]
    add x6 -> x0, other arithmetic: 12.6 us -> none  [the longest x1 4.66 us: per_device(): out_kept = (out_mine + swap_core(out_other)).reshape(2, dps, -1, half_width)]
    unnamed x56 -> x30, local copies, waits for them, and re-layouts: 12.5 us -> 15.7 us
  transfers between devices with their start and end apart: 25 -> 8, of which waited for: 12 -> 3; matrix products, arithmetic and copies ran while one was open for 11% -> 4% of each run, Pallas kernels for 57% -> 14%
where the time goes in v3:
time: 552 us; the launch traced here: 545 us
  Pallas kernels  432 us (78%)
  local copies, waits for them, and re-layouts  41 us (7%)
  starting transfers between devices  25.6 us (5%)
  waiting for transfers between devices  20.5 us (4%)
  matrix products  13.3 us (2%)
  other arithmetic  10.7 us (2%)
    pallas_call x1, Pallas kernels, import_all(): pl.pallas_call(partial(import_kernel, cols, dps), in_specs=[any_spec] * 6...  89.7 us
    pallas_call x1, Pallas kernels, settle(): pl.pallas_call(partial(settle_kernel, cols, dps, heads, span), in_specs=[...  83.3 us
    pallas_call x1, Pallas kernels, scan_backward(): pl.pallas_call(partial(backward_kernel, cols, dps), grid=(2 * blocks,), i...  76.4 us
    pallas_call x1, Pallas kernels, finish(): pl.pallas_call(partial(finish_kernel, cols, dps, part, whole_state), grid...  59.1 us
    pallas_call x1, Pallas kernels, gate_forward(): pl.pallas_call(gate_kernel, grid=(channels // TILE,), in_specs=[whole((ro...  23 us
    pallas_call x1, Pallas kernels, project(): pl.pallas_call(project_kernel, grid=(total // TILE,), in_specs=[whole((ro...  22.3 us
    pallas_call x2, Pallas kernels, weight_grad(): pl.pallas_call(partial(weight_grad_kernel, skips, widths, 1 + low), grid=...  21.1 us
    ppermute x2, waiting for transfers between devices, cross(): moved = lax.ppermute(values, 'col', pairs)  18.3 us
  transfers between devices with their start and end apart: 8, of which 3 were waited for; matrix products, arithmetic and copies ran while one was open for 4% of the time, Pallas kernels for 14%

profile of v3, /device:TPU:0, one launch (start us, length us, event | category | flops | bytes accessed | tf_op | source)
XLA Modules:
  0.0 544.8 jit_solution(4229013060581192175)
XLA Ops:
  0.6 1.1 copy.34
  1.7 1.0 copy.35
  6.4 1.9 concatenate.53.vec
  8.4 89.7 %import_all.1 = (bf16[1040,1536]{1,0:T(8,128)(2,1)}, bf16[1536,1536]{1,0:T(8,128)(2,1)}, bf16[1536,1536]{1,0:T(8,128)(2,1)}, bf16[1536,1536]{1,0:T(8,128)(2,1)},...) custom-call(bf16[512,1536]{1,0:T(8,128)(2,1)} %tok.3, bf16[768,768]{1,0:T(8,128)(2,1)} %wv.1, ...), custom_call_target="tpu_custom_call" | custom-call | bytes 165000000 | tf_op jit(solution)/shard_map/import_all/pallas_call | solution.py:280
  98.2 0.9 convert_element_type.31
  102.3 1.6 fusion.8.pick_ref
  103.9 22.3 %project.1 = (f32[1040,1792]{1,0:T(8,128)}, bf16[1024,1792]{1,0:T(8,128)(2,1)}, bf16[1040,1536]{1,0:T(8,128)(2,1)}, f32[1024,128]{1,0:T(8,128)}, f32[1024,128]{1...) custom-call(bf16[1040,1536]{1,0:T(8,128)(2,1)} %get-tuple-element.70, ...), custom_call_target="tpu_custom_call" | custom-call | bytes 42000000 | tf_op jit(solution)/shard_map/project/pallas_call | solution.py:377
  126.2 14.6 %scan_states.1 = (f32[9,128,1536]{2,1,0:T(8,128)}, f32[128,1536]{1,0:T(8,128)}) custom-call(bf16[1024,1792]{1,0:T(8,128)(2,1)} %get-tuple-element.78.x_ref.b_ref.c_ref, bf16[1024,1792]{1,0:T(8,128)(2,1)} %get-tuple-element.78.x_ref.b_ref.c_ref, f32[1024,128]{1,0:T(8,128)} %get-tuple-element.79.step_ref, f32[1024,128]{1,0:T(8,128)} %get-tuple-element.80.cum_ref, ...), custom_call_target="tpu_custom_call" | custom-call | bytes 18000000 | tf_op jit(solution)/shard_map/scan_states/pallas_call | solution.py:462
  140.8 5.7 %collective-permute-start.1 = (f32[128,1536]{1,0:T(8,128)}, f32[128,1536]{1,0:T(8,128)}, u32[]{:S(2)}, u32[]{:S(2)}) collective-permute-start(f32[128,1536]{1,0:T(8,128)} %get-tuple-element.82), channel_id=1, source_target_pairs={{0,3},{1,2},{4,7},{5,6},{8,11},{9,10},{12,15},{13,14},{16,19},{17,... | collective-permute-start | bytes 2359304 | tf_op jit(solution)/shard_map/ppermute | solution.py:1613
  146.5 13.0 %scan_forward.1.y0_ref = f32[1024,1536]{1,0:T(8,128)} custom-call(bf16[1024,1792]{1,0:T(8,128)(2,1)} %get-tuple-element.78.x_ref.b_ref.c_ref, bf16[1024,1792]{1,0:T(8,128)(2,1)} %get-tuple-element.78.x_ref.b_ref.c_ref, bf16[1024,1792]{1,0:T(8,128)(2,1)} %get-tuple-element.78.x_ref.b_ref.c_ref, f32[1024,128]{1,0:T(8,128)} %get-tuple-element.79.step_ref, ...), custom_call_target="tpu_custom_call" | custom-call | bytes 39000000 | tf_op jit(solution)/shard_map/scan_forward/pallas_call | solution.py:516
  159.9 3.0 collective-permute-done.1
  162.8 1.2 fusion.52
  164.0 1.0 pad_maximum_fusion.early_ref
  165.2 1.7 copy-done.1
  166.8 23.0 %gate_forward.1 = (f32[1024,1536]{1,0:T(8,128)}, f32[1024,1536]{1,0:T(8,128)}, f32[1024,1536]{1,0:T(8,128)}, f32[8,1024]{1,0:T(8,128)}) custom-call(bf16[1040,1536]{1,0:T(8,128)(2,1)} %get-tuple-element.74.normed_ref.normed, bf16[1024,1536]{1,0:T(8,128)(2,1)} %copy-done.1, bf16[1536,1536]{1,0:T(8,128)(2,1)} %get-tuple-element.76.wg_ref.g_ref, ...), custom_call_target="tpu_custom_call" | custom-call | bytes 48000000 | tf_op jit(solution)/shard_map/gate_forward/pallas_call | solution.py:898
  189.9 17.7 %collective-permute-start.2 = (f32[8,1024]{1,0:T(8,128)}, f32[8,1024]{1,0:T(8,128)S(1)}, u32[]{:S(2)}, u32[]{:S(2)}) collective-permute-start(f32[8,1024]{1,0:T(8,128)} %get-tuple-element.87), channel_id=1, source_target_pairs={{0,1},{1,0},{2,3},{3,2},{4,5},{5,4},{6,7},{7,6},{8,9},{9,8},{10,11... | collective-permute-start | bytes 98312 | tf_op jit(solution)/shard_map/ppermute | solution.py:1624
  207.5 2.1 collective-permute-done.2
  210.4 0.8 pad.28.stats_ref
  211.3 16.0 %mix_backward.1 = (bf16[1024,1536]{1,0:T(8,128)(2,1)}, bf16[1024,1536]{1,0:T(8,128)(2,1)}, f32[1024,1536]{1,0:T(8,128)}, f32[8,1536]{1,0:T(8,128)}) custom-call(f32[1024,1536]{1,0:T(8,128)} %get-tuple-element.84.graw_ref, f32[1024,1536]{1,0:T(8,128)} %get-tuple-element.85.y_ref, f32[1024,1536]{1,0:T(8,128)} %get-tuple-element.86.gm_ref, ...), custom_call_target="tpu_custom_call" | custom-call | bytes 30000000 | tf_op jit(solution)/shard_map/mix_backward/pallas_call | solution.py:961
  227.8 1.9 constant_dynamic-slice_fusion.3
  229.8 1.1 copy-done.2
  230.9 1.9 constant_dynamic-slice_fusion.5
  232.8 13.8 %scan_grad_states.1 = (f32[8,128,1536]{2,1,0:T(8,128)}, f32[128,1536]{1,0:T(8,128)}) custom-call(f32[1024,1536]{1,0:T(8,128)} %get-tuple-element.89.dy_ref, bf16[1024,1792]{1,0:T(8,128)(2,1)} %get-tuple-element.78.x_ref.b_ref.c_ref, f32[1024,128]{1,0:T(8,128)} %get-tuple-element.80.cum_ref, bf16[256,1536]{1,0:T(8,128)(2,1)} %constant.107.clone.spread_ref), custom_call_target="tpu_custom_call" | custom-call | bytes 18000000 | tf_op jit(solution)/shard_map/scan_grad_states/pallas_call | solution.py:561
  246.6 1.5 collective-permute-start.7
  248.1 0.9 slice_reduce_fusion.1
  249.2 6.1 %fusion.2.parts = bf16[1,512,1536]{2,1,0:T(8,128)(2,1)} fusion(bf16[1536,1536]{1,0:T(8,128)(2,1)} %get-tuple-element.77.wo_ref, bf16[1024,1536]{1,0:T(8,128)(2,1)S(1)} %copy-done.6, s32[]{:T(128)S(6)} %select_n.76), kind=kOutput, calls=%fused_computation.4 | convolution fusion | flops 2416705536 | bytes 7864324 | tf_op jit(solution)/shard_map/dot_general | solution.py:24
  255.2 15.4 %collective-permute-done.7 = f32[128,1536]{1,0:T(8,128)} collective-permute-done((f32[128,1536]{1,0:T(8,128)}, f32[128,1536]{1,0:T(8,128)}, u32[]{:S(2)}, u32[]{:S(2)}) %collective-permute-start.7) | collective-permute-done | bytes 786464 | tf_op jit(solution)/shard_map/ppermute | solution.py:1613
  270.6 1.2 fusion.51
  271.8 1.0 pad_maximum_fusion.1.late_ref
  272.8 10.3 %weight_grad.3 = (f32[768,1536]{1,0:T(8,128)}, bf16[768,1536]{1,0:T(8,128)(2,1)}) custom-call(bf16[1040,768]{1,0:T(8,128)(2,1)} %get-tuple-element.141.refs_0_, bf16[1040,768]{1,0:T(8,128)(2,1)} %collective-permute-done.5.refs_1_, bf16[1024,1536]{1,0:T(8,128)(2,1)} %get-tuple-element.95.refs_2_.gg_ref, bf16[1024,1536]{1,0:T(8,128)(2,1)} %collective-permute-done.6.refs_3_), custom_call_target="tpu_custom_call" | custom-call | bytes 24000000 | tf_op jit(solution)/shard_map/weight_grad/pallas_call | solution.py:1031
  283.1 10.8 %weight_grad.2 = (f32[1536,768]{1,0:T(8,128)}, bf16[1536,768]{1,0:T(8,128)(2,1)}) custom-call(bf16[1024,1536]{1,0:T(8,128)(2,1)} %get-tuple-element.88.refs_0_, bf16[1024,1536]{1,0:T(8,128)(2,1)} %collective-permute-done.3.refs_1_, bf16[1024,768]{1,0:T(8,128)(2,1)} %get-tuple-element.143.refs_2_, bf16[1024,768]{1,0:T(8,128)(2,1)} %collective-permute-done.4.refs_3_), custom_call_target="tpu_custom_call" | custom-call | bytes 24000000 | tf_op jit(solution)/shard_map/weight_grad/pallas_call | solution.py:1031
  293.9 76.4 %scan_backward.1 = (f32[1024,1536]{1,0:T(8,128)}, bf16[1024,128]{1,0:T(8,128)(2,1)}, f32[1024,256]{1,0:T(8,128)}, f32[8,128]{1,0:T(8,128)}, f32[192,768]{1,0:T(8...) custom-call(f32[1024,1536]{1,0:T(8,128)} %get-tuple-element.89.dy_ref, ...), custom_call_target="tpu_custom_call" | custom-call | bytes 165000000 | tf_op jit(solution)/shard_map/scan_backward/pallas_call | solution.py:797
  370.4 0.8 slice_multiply_fusion
  371.7 59.1 %finish.1 = (f32[8,1792]{1,0:T(8,128)}, f32[1040,1536]{1,0:T(8,128)}, bf16[1040,1536]{1,0:T(8,128)(2,1)}, f32[8,1536]{1,0:T(8,128)}, f32[768,1792]{1,0:T(8,128)}...) custom-call(f32[1024,1536]{1,0:T(8,128)} %get-tuple-element.100.ga_ref, f32[1040,1792]{1,0:T(8,128)} %get-tuple-element.101.raw_ref, ...), custom_call_target="tpu_custom_call" | custom-call | bytes 165000000 | tf_op jit(solution)/shard_map/finish/pallas_call | solution.py:1217
  434.0 83.3 %settle.1 = (f32[512,1536]{1,0:T(8,128)}, f32[768,768]{1,0:T(8,128)}, f32[768,256]{1,0:T(8,128)}, f32[168,128]{1,0:T(8,128)}) custom-call(f32[1040,1536]{1,0:T(8,128)} %get-tuple-element.109.gn, bf16[1040,1536]{1,0:T(8,128)(2,1)} %get-tuple-element.110.gnb, f32[768,1792]{1,0:T(8,128)} %get-tuple-element.111.joint, f32[168,128]{1,0:T(8,128)} %pad_bitcast_fusion.flat, ...), custom_call_target="tpu_custom_call" | custom-call | bytes 270000000 | tf_op jit(solution)/shard_map/settle/pallas_call | solution.py:1455
  517.4 0.9 slice.139
  520.8 1.4 slice.165
  522.2 1.0 slice.138
  523.2 1.2 constant_dynamic-slice_fusion.2
  524.4 0.8 copy.37
  527.3 7.3 %fusion.1 = bf16[512,1536]{1,0:T(8,128)(2,1)} fusion(bf16[1536,1536]{1,0:T(8,128)(2,1)} %get-tuple-element.77.wo_ref, bf16[512,1536]{1,0:T(8,128)(2,1)S(1)} %copy-done.4, bf16[1,512,1536]{2,1,0:T(8,128)(2,1)} %get-tuple-element.99, bf16[1024,1536]{1,0:T(8,128)(2,1)} %get-tuple-element.88.refs_0_, s32[]{:T(128)S(6)} %select_n.72), kind=kOutput, calls=%fused_computation.2 | convolution fusion | flops 2419851264 | bytes 11010052 | tf_op jit(solution)/shard_map/dot_general | solution.py:24
  535.3 1.7 copy.50
  536.9 1.1 copy-done.8
  538.1 1.4 copy.51
  539.5 1.1 copy-done.9
  540.6 1.4 copy.52
  542.0 1.1 copy-done.7
  543.1 1.4 copy.53
  (93 shorter events, 18.1 us)
Async XLA Ops:
  1.7 96.3 %copy-start.3 = (bf16[512,1536]{1,0:T(8,128)(2,1)S(1)}, bf16[512,1536]{1,0:T(8,128)(2,1)}, u32[]{:S(2)}) copy-start(bf16[512,1536]{1,0:T(8,128)(2,1)} %cot) | copy-start | bytes 4718596
  8.4 93.4 %copy-start.10 = (bf16[1536]{0:T(1024)(128)(2,1)S(1)}, bf16[1536]{0:T(1024)(128)(2,1)}, u32[]{:S(2)}) copy-start(bf16[1536]{0:T(1024)(128)(2,1)} %param.19) | copy-start | bytes 9220
  98.0 66.9 %collective-permute-start = (bf16[512,1536]{1,0:T(8,128)(2,1)S(1)}, bf16[512,1536]{1,0:T(8,128)(2,1)S(1)}, u32[]{:S(2)}, u32[]{:S(2)}) collective-permute-start(bf16[512,1536]{1,0:T(8,128)(2,1)S(1)} %copy-done.3), channel_id=1, source_target_pairs={{0,1},{1,0},{2,3},{3,2},{4,5},{5,4},{6,7},{7,6},{8,9},{9,8},{10,11... | collective-permute-start | bytes 4718600 | tf_op jit(solution)/shard_map/ppermute | solution.py:1574
  140.8 22.0 %collective-permute-start.1 = (f32[128,1536]{1,0:T(8,128)}, f32[128,1536]{1,0:T(8,128)}, u32[]{:S(2)}, u32[]{:S(2)}) collective-permute-start(f32[128,1536]{1,0:T(8,128)} %get-tuple-element.82), channel_id=1, source_target_pairs={{0,3},{1,2},{4,7},{5,6},{8,11},{9,10},{12,15},{13,14},{16,19},{17,... | collective-permute-start | bytes 2359304 | tf_op jit(solution)/shard_map/ppermute | solution.py:1613
  165.2 1.7 copy-start.1
  189.9 19.8 %collective-permute-start.2 = (f32[8,1024]{1,0:T(8,128)}, f32[8,1024]{1,0:T(8,128)S(1)}, u32[]{:S(2)}, u32[]{:S(2)}) collective-permute-start(f32[8,1024]{1,0:T(8,128)} %get-tuple-element.87), channel_id=1, source_target_pairs={{0,1},{1,0},{2,3},{3,2},{4,5},{5,4},{6,7},{7,6},{8,9},{9,8},{10,11... | collective-permute-start | bytes 98312 | tf_op jit(solution)/shard_map/ppermute | solution.py:1624
  211.3 16.5 %copy-start = (bf16[1040,1536]{1,0:T(8,128)(2,1)S(1)}, bf16[1040,1536]{1,0:T(8,128)(2,1)}, u32[]{:S(2)}) copy-start(bf16[1040,1536]{1,0:T(8,128)(2,1)} %get-tuple-element.74.normed_ref.normed) | copy-start | bytes 9584644
  227.3 45.5 %collective-permute-start.6 = (bf16[1024,1536]{1,0:T(8,128)(2,1)}, bf16[1024,1536]{1,0:T(8,128)(2,1)}, u32[]{:S(2)}, u32[]{:S(2)}) collective-permute-start(bf16[1024,1536]{1,0:T(8,128)(2,1)} %get-tuple-element.95.refs_2_.gg_ref), channel_id=1, source_target_pairs={{0,4},{4,0},{1,5},{5,1},{2,6},{6,2},{3,7},{7,3},{8,12},{12,8},{9,1... | collective-permute-start | bytes 9437192 | tf_op jit(solution)/shard_map/ppermute | solution.py:1515
  227.3 55.8 %collective-permute-start.3 = (bf16[1024,1536]{1,0:T(8,128)(2,1)}, bf16[1024,1536]{1,0:T(8,128)(2,1)}, u32[]{:S(2)}, u32[]{:S(2)}) collective-permute-start(bf16[1024,1536]{1,0:T(8,128)(2,1)} %get-tuple-element.88.refs_0_), channel_id=1, source_target_pairs={{0,4},{4,0},{1,5},{5,1},{2,6},{6,2},{3,7},{7,3},{8,12},{12,8},{9,1... | collective-permute-start | bytes 9437192 | tf_op jit(solution)/shard_map/ppermute | solution.py:1515
  227.8 3.0 copy-start.2
  229.7 43.1 %collective-permute-start.5 = (bf16[1040,768]{1,0:T(8,128)(2,1)}, bf16[1040,768]{1,0:T(8,128)(2,1)}, u32[]{:S(2)}, u32[]{:S(2)}) collective-permute-start(bf16[1040,768]{1,0:T(8,128)(2,1)} %get-tuple-element.140), channel_id=1, source_target_pairs={{0,4},{4,0},{1,5},{5,1},{2,6},{6,2},{3,7},{7,3},{8,12},{12,8},{9,1... | collective-permute-start | bytes 4792328 | tf_op jit(solution)/shard_map/ppermute | solution.py:1515
  232.7 50.4 %collective-permute-start.4 = (bf16[1024,768]{1,0:T(8,128)(2,1)}, bf16[1024,768]{1,0:T(8,128)(2,1)}, u32[]{:S(2)}, u32[]{:S(2)}) collective-permute-start(bf16[1024,768]{1,0:T(8,128)(2,1)} %get-tuple-element.142), channel_id=1, source_target_pairs={{0,4},{4,0},{1,5},{5,1},{2,6},{6,2},{3,7},{7,3},{8,12},{12,8},{9,1... | collective-permute-start | bytes 4718600 | tf_op jit(solution)/shard_map/ppermute | solution.py:1515
  232.8 16.4 %copy-start.6 = (bf16[1024,1536]{1,0:T(8,128)(2,1)S(1)}, bf16[1024,1536]{1,0:T(8,128)(2,1)}, u32[]{:S(2)}) copy-start(bf16[1024,1536]{1,0:T(8,128)(2,1)} %get-tuple-element.88.refs_0_) | copy-start | bytes 9437188
  246.6 24.0 %collective-permute-start.7 = (f32[128,1536]{1,0:T(8,128)}, f32[128,1536]{1,0:T(8,128)}, u32[]{:S(2)}, u32[]{:S(2)}) collective-permute-start(f32[128,1536]{1,0:T(8,128)} %get-tuple-element.98), channel_id=1, source_target_pairs={{3,0},{2,1},{7,4},{6,5},{11,8},{10,9},{15,12},{14,13},{19,16},{18,... | collective-permute-start | bytes 2359304 | tf_op jit(solution)/shard_map/ppermute | solution.py:1613
  434.0 93.3 %copy-start.4 = (bf16[512,1536]{1,0:T(8,128)(2,1)S(1)}, bf16[512,1536]{1,0:T(8,128)(2,1)}, u32[]{:S(2)}) copy-start(bf16[512,1536]{1,0:T(8,128)(2,1)} %tok.3) | copy-start | bytes 4718596
  527.3 8.0 %copy-start.5 = (f32[512,1536]{1,0:T(8,128)S(1)}, f32[512,1536]{1,0:T(8,128)}, u32[]{:S(2)}) copy-start(f32[512,1536]{1,0:T(8,128)} %get-tuple-element.199) | copy-start | bytes 9437188
  535.2 2.8 copy-start.8
  538.1 2.5 copy-start.9
  540.6 2.5 copy-start.7

commit v4 on v3

--- a/solution.py
+++ b/solution.py
@@ -124,15 +124,14 @@
 
 
 def import_kernel(
-    cols, dps, tok, wv, wg, wo, sw, vec, tg, vf, gf, of, sf, vecs,
-    zeros, tok_vm, w_vm, wo_vm, s_vm, vec_vm, local, send, recv,
+    cols, dps, tok, wv, sw, vec, tg, vf, sf, vecs, zeros, tok_vm, w_vm, s_vm, vec_vm, local, send, recv,
 ):
     dp, row, col = here()
     group = cols // 2
     place = lax.rem(col, group)
     half, shard = wv.shape
     count = tok.shape[0]
-    piece, piece_out = half // dps, wo.shape[0] // dps
+    piece = half // dps
     sibling = (dp, 1 - row, col)
     mirror = (dp, row, cols - 1 - col)
     col_peer = lambda by: (dp, row, col ^ by)
@@ -166,18 +165,14 @@
 
     my_rows = pl.ds(row * half, half)
     my_piece = pl.ds(row * half + dp * piece, piece)
-    out_piece = pl.ds(shard + dp * piece_out, piece_out)
-    my_lanes = lanes_at(row, half)
     own, other = pl.ds(0, shard), pl.ds(shard, shard)
-    src_piece, src_out = pl.ds(dp * piece, piece), pl.ds(dp * piece_out, piece_out)
+    src_piece = pl.ds(dp * piece, piece)
 
     staged = [
         keep(6, vec, vec_vm),
         keep(0, sw.at[src_piece, :], s_vm),
         keep(2, tok, tok_vm),
-        keep(3, wv, w_vm.at[0]),
-        keep(4, wg, w_vm.at[1]),
-        keep(5, wo, wo_vm),
+        keep(3, wv, w_vm),
     ]
     s_cross = [
         launch(sw.at[src_piece, :], sf.at[my_piece, lanes_at(col, 128)], col_peer(by))
@@ -213,17 +208,13 @@
         clear.wait()
 
     v_own = launch(wv, vf.at[my_rows, own], sibling)
-    g_own = launch(wg, gf.at[my_rows, own], sibling)
-    o_own = launch(wo, of.at[own, my_lanes], sibling)
     for copy in staged:
         copy.wait()
     small_own = keep(0, s_vm, sf.at[my_piece, lanes_at(col, 128)])
     kept = [
         keep(6, vec_vm, vecs.at[col]),
         keep(2, tok_vm, my_tokens),
-        keep(3, w_vm.at[0], vf.at[my_rows, own]),
-        keep(4, w_vm.at[1], gf.at[my_rows, own]),
-        keep(5, wo_vm, of.at[own, my_lanes]),
+        keep(3, w_vm, vf.at[my_rows, own]),
     ]
 
     def spread_out(ref):
@@ -237,23 +228,13 @@
     small_own.wait()
     s_dp = spread_out(sf.at[my_piece, :])
     arrive([v_cross])
-    g_cross = launch(wg.at[src_piece, :], gf.at[my_piece, other], mirror)
     v_dp = spread_out(vf.at[my_piece, other])
-    arrive([g_cross])
-    o_cross = launch(wo.at[src_out, :], of.at[out_piece, my_lanes], mirror)
-    g_dp = spread_out(gf.at[my_piece, other])
     arrive(s_dp)
     last = [launch(sf.at[my_rows, :], sf.at[my_rows, :], sibling)]
     arrive(v_dp)
     last += [launch(vf.at[my_rows, other], vf.at[my_rows, other], sibling)]
-    arrive([o_cross])
-    o_dp = spread_out(of.at[out_piece, my_lanes])
-    arrive(g_dp)
-    last += [launch(gf.at[my_rows, other], gf.at[my_rows, other], sibling)]
-    arrive(o_dp)
-    last += [launch(of.at[other, my_lanes], of.at[other, my_lanes], sibling)]
     arrive(last)
-    arrive([v_own, g_own, o_own])
+    arrive([v_own])
     arrive(vec_cross)
     arrive(tok_cross)
 
@@ -272,28 +253,25 @@
         copy.wait_send()
 
 
-def import_all(cols, dps, tokens, w_value, w_gate, w_out, small, vec):
+def import_all(cols, dps, tokens, w_value, small, vec):
     half, shard = w_value.shape
     count, width = tokens.shape
     any_spec = pl.BlockSpec(memory_space=pl.ANY)
-    copies = 3 + 2 * (cols - 1) + (cols // 2 - 1) + cols // 2 + 3 + 4 * (dps - 1) + 4
+    copies = 1 + 2 * (cols - 1) + (cols // 2 - 1) + cols // 2 + 1 + 2 * (dps - 1) + 2
     return pl.pallas_call(
         partial(import_kernel, cols, dps),
-        in_specs=[any_spec] * 6,
-        out_specs=[any_spec] * 6,
+        in_specs=[any_spec] * 4,
+        out_specs=[any_spec] * 4,
         out_shape=[
             sds((HALO + count * (cols // 2), width), BF),
             sds((2 * half, 2 * shard), BF),
-            sds((2 * half, 2 * shard), BF),
-            sds((2 * shard, 2 * half), BF),
             sds((2 * half, cols * 128), BF),
             sds((cols,) + vec.shape, BF),
         ],
         scratch_shapes=[
             pltpu.VMEM((HALO, width), BF),
             pltpu.VMEM((count, width), BF),
-            pltpu.VMEM((2, half, shard), BF),
-            pltpu.VMEM((shard, half), BF),
+            pltpu.VMEM((half, shard), BF),
             pltpu.VMEM((half // dps, 128), BF),
             pltpu.VMEM(vec.shape, BF),
             pltpu.SemaphoreType.DMA((7,)),
@@ -303,9 +281,9 @@
         compiler_params=pltpu.CompilerParams(
             collective_id=1, has_side_effects=True, vmem_limit_bytes=VMEM_LIMIT
         ),
-        cost_estimate=cost(55),
+        cost_estimate=cost(45),
         name="import_all",
-    )(tokens, w_value, w_gate, w_out, small, vec)
+    )(tokens, w_value, small, vec)
 
 
 def conv_rows(raw_ref, taps, start, size):
@@ -315,105 +293,54 @@
     return total
 
 
-def project_kernel(
-    tok_ref, gain_ref, w_ref, small_ref, pick_ref, taps_ref, head_ref,
-    raw_ref, act_ref, normed_ref, stepin_ref, step_ref, cum_ref, grow_ref, offs_ref, inv_ref, picked_ref,
+def normalize(tok_ref, gain_ref, normed_ref, inv_ref):
+    tokens = tok_ref.shape[0] - HALO
+    for at in [0] + list(range(HALO, HALO + tokens, Q)):
+        size = HALO if at == 0 else Q
+        values = tok_ref[at : at + size, :].astype(F32)
+        inv = lax.rsqrt(jnp.mean(values * values, axis=-1, keepdims=True) + EPSILON)
+        normed_ref[at : at + size, :] = (values * inv * gain_ref[0:1, :]).astype(BF)
+        inv_ref[at : at + size, :] = jnp.broadcast_to(inv, (size, 128))
+
+
+def project_steps(
+    small_ref, pick_ref, head_ref, normed_ref, raw_ref, stepin_ref, step_ref, cum_ref, grow_ref, offs_ref,
+    picked_ref,
 ):
+    tokens = step_ref.shape[0]
+    picked = mm(small_ref[...], pick_ref[...]).astype(BF)
+    picked_ref[...] = picked
+    raw_ref[...] = mm(normed_ref[...], picked[:, :TILE])
+    step_in = mm(normed_ref[HALO:, :], picked[:, TILE:]) + head_ref[0:1, :]
+    small = jnp.exp(-jnp.abs(step_in))
+    plus = 1.0 + small
+    safe = jnp.where(plus == 1.0, 1.0, plus - 1.0)
+    log_part = jnp.where(plus == 1.0, small, jnp.log(plus) * (small / safe))
+    step = jnp.maximum(step_in, 0.0) + log_part
+    stepin_ref[...] = step_in
+    step_ref[...] = step
+    falls = step * head_ref[1:2, :]
+    lower = (iota2((Q, Q), 0) >= iota2((Q, Q), 1)).astype(F32)
+    before = jnp.zeros((1, 128), F32)
+    offs_ref[...] = jnp.zeros_like(offs_ref)
+    for b in range(tokens // Q):
+        rows = slice(b * Q, b * Q + Q)
+        cum = mm_exact(lower, falls[rows, :])
+        cum_ref[rows, :] = cum
+        high, low = split2(jnp.exp(cum + before))
+        grow_ref[rows, 0:128] = high
+        grow_ref[rows, 128:256] = low
+        before = before + cum[Q - 1 : Q, :]
+        offs_ref[b + 1 : b + 2, :] = before
+
+
+def activate(raw_ref, taps, act_ref, copy_ref):
     tokens = act_ref.shape[0]
-    at_tile = pl.program_id(0)
-    last = pl.num_programs(0) - 1
-
-    @pl.when(at_tile == 0)
-    def _():
-        for at in [0] + list(range(HALO, HALO + tokens, Q)):
-            size = HALO if at == 0 else Q
-            values = tok_ref[at : at + size, :].astype(F32)
-            inv = lax.rsqrt(jnp.mean(values * values, axis=-1, keepdims=True) + EPSILON)
-            normed_ref[at : at + size, :] = (values * inv * gain_ref[0:1, :]).astype(BF)
-            inv_ref[at : at + size, :] = jnp.broadcast_to(inv, (size, 128))
-
-    @pl.when(at_tile < last)
-    def _():
-        raw_ref[...] = mm(normed_ref[...], w_ref[...])
-
-    @pl.when(at_tile == last)
-    def _():
-        picked = mm(small_ref[...], pick_ref[...]).astype(BF)
-        picked_ref[...] = picked
-        raw_ref[...] = mm(normed_ref[...], picked[:, :TILE])
-        step_in = mm(normed_ref[HALO:, :], picked[:, TILE:]) + head_ref[0:1, :]
-        small = jnp.exp(-jnp.abs(step_in))
-        plus = 1.0 + small
-        safe = jnp.where(plus == 1.0, 1.0, plus - 1.0)
-        log_part = jnp.where(plus == 1.0, small, jnp.log(plus) * (small / safe))
-        step = jnp.maximum(step_in, 0.0) + log_part
-        stepin_ref[...] = step_in
-        step_ref[...] = step
-        falls = step * head_ref[1:2, :]
-        lower = (iota2((Q, Q), 0) >= iota2((Q, Q), 1)).astype(F32)
-        before = jnp.zeros((1, 128), F32)
-        offs_ref[...] = jnp.zeros_like(offs_ref)
-        for b in range(tokens // Q):
-            rows = slice(b * Q, b * Q + Q)
-            cum = mm_exact(lower, falls[rows, :])
-            cum_ref[rows, :] = cum
-            high, low = split2(jnp.exp(cum + before))
-            grow_ref[rows, 0:128] = high
-            grow_ref[rows, 128:256] = low
-            before = before + cum[Q - 1 : Q, :]
-            offs_ref[b + 1 : b + 2, :] = before
-
-    taps = taps_ref[...]
     for at in range(0, tokens, Q):
         pre = conv_rows(raw_ref, taps, at, Q)
-        act_ref[at : at + Q, :] = (pre * sigmoid(pre)).astype(BF)
-
-
-def project(group_tokens, gain, weights, small, pick, taps, head_rows):
-    rows, width = group_tokens.shape
-    tokens = rows - HALO
-    total = weights.shape[1] + TILE
-    last = weights.shape[1] // TILE - 1
-    return pl.pallas_call(
-        project_kernel,
-        grid=(total // TILE,),
-        in_specs=[
-            whole((rows, width)),
-            whole((1, width)),
-            pl.BlockSpec((width, TILE), lambda j: (0, jnp.minimum(j, last))),
-            whole(small.shape),
-            whole(pick.shape),
-            columns(8),
-            whole((8, 128)),
-        ],
-        out_specs=[
-            columns(rows),
-            columns(tokens),
-            whole((rows, width)),
-            whole((tokens, 128)),
-            whole((tokens, 128)),
-            whole((tokens, 128)),
-            whole((tokens, 256)),
-            whole((16, 128)),
-            whole((rows, 128)),
-            whole((width, TILE + 128)),
-        ],
-        out_shape=[
-            sds((rows, total)),
-            sds((tokens, total), BF),
-            sds((rows, width), BF),
-            sds((tokens, 128)),
-            sds((tokens, 128)),
-            sds((tokens, 128)),
-            sds((tokens, 256), BF),
-            sds((16, 128)),
-            sds((rows, 128)),
-            sds((width, TILE + 128), BF),
-        ],
-        compiler_params=params(),
-        cost_estimate=cost(14),
-        name="project",
-    )(group_tokens, gain, weights, small, pick, taps, head_rows)
+        act = (pre * sigmoid(pre)).astype(BF)
+        act_ref[at : at + Q, :] = act
+        copy_ref[at : at + Q, :] = act
 
 
 def expand(per_head, spread):
@@ -425,63 +352,23 @@
     return values.astype(F32).T.astype(BF)
 
 
-def states_kernel(x_ref, b_ref, step_ref, cum_ref, spread_ref, states_ref, final_ref, held):
-    at = pl.program_id(0)
-    last = pl.num_programs(0) - 1
-
-    @pl.when(at == 0)
-    def _():
-        held[...] = jnp.zeros_like(held)
-
-    states_ref[0] = held[...]
-
-    @pl.when(at == last)
-    def _():
-        final_ref[...] = held[...]
-
-    @pl.when(at < last)
-    def _():
-        cum = cum_ref[...]
-        end = cum[Q - 1 : Q, :]
-        tail = jnp.exp(end - cum) * step_ref[...]
-        fall = jnp.broadcast_to(jnp.exp(end), (8, 128))
-        b_t = transpose_bf(b_ref[...])
-        b_t2 = jnp.concatenate([b_t, b_t], 1)
-        for start in range(0, x_ref.shape[1], TILE):
-            lanes = slice(start, start + TILE)
-            spread = spread_ref[:, lanes]
-            scaled = expand(tail, spread) * x_ref[:, lanes].astype(F32)
-            high, low = split2(scaled)
-            fresh = mm(b_t2, jnp.concatenate([high, low], 0))
-            held[:, lanes] = held[:, lanes] * expand(fall, spread)[0:1, :] + fresh
-
-
-def scan_states(act, step, cum, spread, channels):
-    blocks = act.shape[0] // Q
-    clamp = lambda i: jnp.minimum(i, blocks - 1)
-    return pl.pallas_call(
-        states_kernel,
-        grid=(blocks + 1,),
-        in_specs=[
-            pl.BlockSpec((Q, channels), lambda i: (clamp(i), 0)),
-            pl.BlockSpec((Q, N), lambda i: (clamp(i), channels // N)),
-            pl.BlockSpec((Q, 128), lambda i: (clamp(i), 0)),
-            pl.BlockSpec((Q, 128), lambda i: (clamp(i), 0)),
-            whole((256, channels)),
-        ],
-        out_specs=[
-            pl.BlockSpec((1, N, channels), lambda i: (i, 0, 0)),
-            whole((N, channels)),
-        ],
-        out_shape=[sds((blocks + 1, N, channels)), sds((N, channels))],
-        scratch_shapes=[pltpu.VMEM((N, channels), F32)],
-        compiler_params=params(),
-        cost_estimate=cost(6),
-        name="scan_states",
-    )(act, act, step, cum, spread)
-
-
-def forward_kernel(x_ref, b_ref, c_ref, step_ref, cum_ref, spread_ref, state_ref, y_ref):
+def state_block(x_ref, b_ref, step_ref, cum_ref, spread_ref, held):
+    cum = cum_ref[...]
+    end = cum[Q - 1 : Q, :]
+    tail = jnp.exp(end - cum) * step_ref[...]
+    fall = jnp.broadcast_to(jnp.exp(end), (8, 128))
+    b_t = transpose_bf(b_ref[...])
+    b_t2 = jnp.concatenate([b_t, b_t], 1)
+    for start in range(0, x_ref.shape[1], TILE):
+        lanes = slice(start, start + TILE)
+        spread = spread_ref[:, lanes]
+        scaled = expand(tail, spread) * x_ref[:, lanes].astype(F32)
+        high, low = split2(scaled)
+        fresh = mm(b_t2, jnp.concatenate([high, low], 0))
+        held[:, lanes] = held[:, lanes] * expand(fall, spread)[0:1, :] + fresh
+
+
+def forward_block(x_ref, b_ref, c_ref, step_ref, cum_ref, spread_ref, state_ref, y_ref):
     b_blk, c_blk = b_ref[...], c_ref[...]
     affinity = mm_nt(c_blk, b_blk)
     causal = iota2((Q, Q), 0) >= iota2((Q, Q), 1)
@@ -511,72 +398,329 @@
             y_ref[:, at : at + 128] = intra + reached[:, pair * 128 : pair * 128 + 128]
 
 
-def scan_forward(act, step, cum, spread, states, channels):
-    tokens = act.shape[0]
+def forward_all_kernel(
+    cols, dps,
+    tok_ref, gain_ref, w_ref, small_ref, pick_ref, taps_ref, head_ref, spread_ref, cot, wg, wo,
+    raw_ref, act_ref, normed_ref, stepin_ref, step_ref, cum_ref, grow_ref, offs_ref, inv_ref, picked_ref,
+    states_ref, y_ref, graw_ref, gm_ref, early_ref, cot_out, gf, of,
+    act_vm, states_vm, held, early_land, cot_vm, g_tiles, o_tiles, wg_vm, wo_vm, sems, local,
+):
+    step = pl.program_id(0)
+    tokens, channels = states_vm.shape[0] * Q, held.shape[1]
+    blocks = states_vm.shape[0]
+    tiles = channels // TILE
+    scan_at = tiles + 1
+    out_at = scan_at + blocks
+    gate_at = out_at + blocks
+    dp, row, col = here()
+    group = cols // 2
+    place = lax.rem(col, group)
+    half, shard = wg.shape
+    count = cot.shape[0]
+    others = dps - 1
+    piece, piece_out = half // dps, wo.shape[0] // dps
+    sibling, mirror = (dp, 1 - row, col), mirror_of(cols)
+    peers = [(dp, row, col ^ by) for by in range(1, group)]
+    my_rows = pl.ds(row * half, half)
+    my_piece = pl.ds(row * half + dp * piece, piece)
+    out_piece = pl.ds(shard + dp * piece_out, piece_out)
+    my_lanes = lanes_at(row, half)
+    own, other = pl.ds(0, shard), pl.ds(shard, shard)
+    src_piece, src_out = pl.ds(dp * piece, piece), pl.ds(dp * piece_out, piece_out)
+    my_cot = cot_vm.at[pl.ds(place * count, count), :]
+
+    g_cross = lambda: copy_to(wg.at[src_piece, :], gf.at[my_piece, other], sems, 0, mirror)
+    o_cross = lambda: copy_to(wo.at[src_out, :], of.at[out_piece, my_lanes], sems, 1, mirror)
+    g_own = lambda: copy_to(wg, gf.at[my_rows, own], sems, 2, sibling)
+    o_own = lambda: copy_to(wo, of.at[own, my_lanes], sems, 3, sibling)
+    g_rest = lambda: copy_to(gf.at[my_rows, other], gf.at[my_rows, other], sems, 4, sibling)
+    o_rest = lambda: copy_to(of.at[other, my_lanes], of.at[other, my_lanes], sems, 5, sibling)
+    early_moves = lambda: [
+        copy_to(held.at[:, own], early_land.at[:, other], sems, 6, mirror),
+        copy_to(held.at[:, other], early_land.at[:, own], sems, 7, mirror),
+    ]
+    cot_moves = lambda: [copy_to(cot, my_cot, sems, 8 + i, peer) for i, peer in enumerate(peers)]
+    first = 8 + group - 1
+
+    def g_dp():
+        ref = gf.at[my_piece, other]
+        return dp_copies(dps, sems, lambda to, i: ref, lambda to, i: ref, first)
+
+    def o_dp():
+        ref = of.at[out_piece, my_lanes]
+        return dp_copies(dps, sems, lambda to, i: ref, lambda to, i: ref, first + others)
+
+    load_cot = pltpu.make_async_copy(cot, my_cot, local.at[0])
+    load_g = pltpu.make_async_copy(wg, wg_vm, local.at[1])
+    load_o = pltpu.make_async_copy(wo, wo_vm, local.at[2])
+    store_g = pltpu.make_async_copy(wg_vm, gf.at[my_rows, own], local.at[1])
+    store_o = pltpu.make_async_copy(wo_vm, of.at[own, my_lanes], local.at[2])
+    store_cot = pltpu.make_async_copy(cot_vm, cot_out, local.at[0])
+
+    def g_tile(at):
+        return pltpu.make_async_copy(gf.at[:, lanes_at(at, TILE)], g_tiles.at[lax.rem(at, 2)], local.at[3])
+
+    def o_tile(at):
+        rows = pl.ds(pl.multiple_of(at * TILE, TILE), TILE)
+        return pltpu.make_async_copy(of.at[rows, :], o_tiles.at[lax.rem(at, 2)], local.at[4])
+
+    @at_step(0)
+    def _():
+        load_cot.start()
+        load_g.start()
+        load_o.start()
+        greet([sibling, mirror] + peers + dp_peers(dps))
+        for move in [g_cross(), o_cross(), g_own(), o_own()]:
+            move.start()
+        normalize(tok_ref, gain_ref, normed_ref, inv_ref)
+
+    @at_step(1)
+    def _():
+        load_g.wait()
+        store_g.start()
+        load_o.wait()
+        store_o.start()
+
+    @at_step(tiles - 2)
+    def _():
+        for move in cot_moves():
+            move.start()
+
+    @at_step(scan_at + 2)
+    def _():
+        g_cross().wait_recv()
+        for move in g_dp():
+            move.start()
+
+    @at_step(out_at)
+    def _():
+        o_cross().wait_recv()
+        for move in o_dp():
+            move.start()
+
+    @at_step(out_at + blocks // 2)
+    def _():
+        for move in g_dp():
+            move.wait_recv()
+        g_rest().start()
+
+    @at_step(gate_at + tiles // 2)
+    def _():
+        for move in o_dp():
+            move.wait_recv()
+        o_rest().start()
+
+    @at_step(out_at)
+    def _():
+        @pl.when(col < group)
+        def _():
+            for move in early_moves():
+                move.start()
+
+    @pl.when(step < tiles)
+    def _():
+        raw_ref[...] = mm(normed_ref[...], w_ref[...])
+
+    @pl.when(step == tiles)
+    def _():
+        project_steps(
+            small_ref, pick_ref, head_ref, normed_ref, raw_ref, stepin_ref, step_ref, cum_ref, grow_ref, offs_ref,
+            picked_ref,
+        )
+
+    @pl.when(step <= tiles)
+    def _():
+        activate(raw_ref, taps_ref[...], act_ref, act_vm.at[:, lanes_at(step, TILE)])
+
+    def block_refs(at):
+        rows = pl.ds(pl.multiple_of(at * Q, Q), Q)
+        return (
+            act_vm.at[rows, pl.ds(0, channels)], act_vm.at[rows, pl.ds(channels, N)],
+            act_vm.at[rows, pl.ds(channels + N, N)], step_ref.at[rows, :], cum_ref.at[rows, :],
+        )
+
+    @pl.when(step == scan_at)
+    def _():
+        held[...] = jnp.zeros_like(held)
+
+    @pl.when((step >= scan_at) & (step < out_at))
+    def _():
+        x_blk, b_blk, _, step_blk, cum_blk = block_refs(step - scan_at)
+        states_ref[0] = held[...]
+        states_vm[step - scan_at] = held[...]
+        state_block(x_blk, b_blk, step_blk, cum_blk, spread_ref, held)
+
+    @pl.when(step == out_at)
+    def _():
+        states_ref[0] = held[...]
+
+    @pl.when((step >= out_at) & (step < gate_at))
+    def _():
+        x_blk, b_blk, c_blk, step_blk, cum_blk = block_refs(step - out_at)
+        forward_block(
+            x_blk, b_blk, c_blk, step_blk, cum_blk, spread_ref, states_vm.at[pl.ds(step - out_at, 1)], y_ref
+        )
+
+    @pl.when(step == gate_at)
+    def _():
+        for move in [g_own(), g_rest()]:
+            move.wait_recv()
+        store_g.wait()
+        g_tile(0).start()
+
+    @pl.when((step >= gate_at) & (step < gate_at + tiles))
+    def _():
+        at = step - gate_at
+        g_tile(at).wait()
+
+        @pl.when(at < tiles - 1)
+        def _():
+            g_tile(at + 1).start()
+
+        graw_ref[...] = mm(normed_ref[HALO:, :], g_tiles[lax.rem(at, 2)])
+
+    @pl.when(step == gate_at + tiles)
+    def _():
+        for move in [o_own(), o_rest()] + cot_moves():
+            move.wait_recv()
+        store_o.wait()
+        load_cot.wait()
+        store_cot.start()
+        o_tile(0).start()
+
+    @pl.when(step >= gate_at + tiles)
+    def _():
+        at = step - gate_at - tiles
+        o_tile(at).wait()
+
+        @pl.when(at < tiles - 1)
+        def _():
+            o_tile(at + 1).start()
+
+        gm_ref[...] = mm_nt(cot_vm[...], o_tiles[lax.rem(at, 2)])
+
+    @at_step(pl.num_programs(0) - 1)
+    def _():
+        store_cot.wait()
+        for move in [g_cross(), o_cross(), g_own(), o_own(), g_rest(), o_rest()] + cot_moves() + g_dp() + o_dp():
+            move.wait_send()
+
+        @pl.when(col < group)
+        def _():
+            for move in early_moves():
+                move.wait_send()
+            early_ref[...] = jnp.zeros_like(early_ref)
+
+        @pl.when(col >= group)
+        def _():
+            for move in early_moves():
+                move.wait_recv()
+            early_ref[...] = early_land[...]
+
+
+def forward_all(cols, dps, group_tokens, gain, weights, small, pick, taps, head_rows, spread, cotangent, w_gate, w_out):
+    rows, width = group_tokens.shape
+    tokens = rows - HALO
+    channels = weights.shape[1]
+    total = channels + TILE
+    blocks, tiles = tokens // Q, channels // TILE
+    half, shard = w_gate.shape
+    scan_at = tiles + 1
+    out_at = scan_at + blocks
+    gate_at = out_at + blocks
+
+    def clamp(first, count):
+        return lambda i: jnp.clip(i - first, 0, count - 1)
+
+    lanes = lambda at, count: pl.BlockSpec((count, TILE), lambda i: (0, at(i)))
+    both, value_at = clamp(0, tiles + 1), clamp(0, tiles)
+    state_at, y_at = clamp(scan_at, blocks + 1), clamp(out_at, blocks)
+    raw_tile, gm_tile = clamp(gate_at, tiles), clamp(gate_at + tiles, tiles)
+    vmem = pltpu.VMEM
     return pl.pallas_call(
-        forward_kernel,
-        grid=(tokens // Q,),
+        partial(forward_all_kernel, cols, dps),
+        grid=(gate_at + 2 * tiles,),
         in_specs=[
-            pl.BlockSpec((Q, channels), lambda i: (i, 0)),
-            pl.BlockSpec((Q, N), lambda i: (i, channels // N)),
-            pl.BlockSpec((Q, N), lambda i: (i, channels // N + 1)),
-            pl.BlockSpec((Q, 128), lambda i: (i, 0)),
-            pl.BlockSpec((Q, 128), lambda i: (i, 0)),
-            whole((256, channels)),
-            pl.BlockSpec((1, N, channels), lambda i: (i, 0, 0)),
+            whole((rows, width)),
+            whole((1, width)),
+            lanes(value_at, width),
+            whole(small.shape),
+            whole(pick.shape),
+            lanes(both, 8),
+            whole((8, 128)),
+            whole(spread.shape),
+            ANY, ANY, ANY,
         ],
-        out_specs=pl.BlockSpec((Q, channels), lambda i: (i, 0)),
-        out_shape=sds((tokens, channels)),
-        compiler_params=params(),
-        cost_estimate=cost(13),
-        name="scan_forward",
-    )(act, act, act, step, cum, spread, states)
-
-
-def grad_states_kernel(dy_ref, c_ref, cum_ref, spread_ref, after_ref, first_ref, held):
-    at = pl.program_id(0)
-
-    @pl.when(at == 0)
-    def _():
-        held[...] = jnp.zeros_like(held)
-
+        out_specs=[
+            lanes(both, rows),
+            lanes(both, tokens),
+            whole((rows, width)),
+            whole((tokens, 128)),
+            whole((tokens, 128)),
+            whole((tokens, 128)),
+            whole((tokens, 256)),
+            whole((16, 128)),
+            whole((rows, 128)),
+            whole((width, TILE + 128)),
+            pl.BlockSpec((1, N, channels), lambda i: (state_at(i), 0, 0)),
+            pl.BlockSpec((Q, channels), lambda i: (y_at(i), 0)),
+            lanes(raw_tile, tokens),
+            lanes(gm_tile, tokens),
+            whole((N, channels)),
+            ANY, ANY, ANY,
+        ],
+        out_shape=[
+            sds((rows, total)),
+            sds((tokens, total), BF),
+            sds((rows, width), BF),
+            sds((tokens, 128)),
+            sds((tokens, 128)),
+            sds((tokens, 128)),
+            sds((tokens, 256), BF),
+            sds((16, 128)),
+            sds((rows, 128)),
+            sds((width, TILE + 128), BF),
+            sds((blocks + 1, N, channels)),
+            sds((tokens, channels)),
+            sds((tokens, channels)),
+            sds((tokens, channels)),
+            sds((N, channels)),
+            sds((tokens, width), BF),
+            sds((width, channels), BF),
+            sds((channels, width), BF),
+        ],
+        scratch_shapes=[
+            vmem((tokens, total), BF),
+            vmem((blocks, N, channels), F32),
+            vmem((N, channels), F32),
+            vmem((N, channels), F32),
+            vmem((tokens, width), BF),
+            vmem((2, width, TILE), BF),
+            vmem((2, TILE, width), BF),
+            vmem((half, shard), BF),
+            vmem((shard, half), BF),
+            pltpu.SemaphoreType.DMA((2, 7 + cols // 2 + 2 * (dps - 1))),
+            pltpu.SemaphoreType.DMA((5,)),
+        ],
+        compiler_params=remote_params(4),
+        cost_estimate=cost(70),
+        name="forward_all",
+    )(group_tokens, gain, weights, small, pick, taps, head_rows, spread, cotangent, w_gate, w_out)
+
+
+def grad_state_block(dy_tiles, c_ref, cum_ref, spread_ref, after_ref, held):
     after_ref[0] = held[...]
     cum = cum_ref[...]
     growth = jnp.exp(cum)
     fall = jnp.broadcast_to(growth[Q - 1 : Q, :], (8, 128))
     c_t = transpose_bf(c_ref[...])
     c_t2 = jnp.concatenate([c_t, c_t], 1)
-    for start in range(0, dy_ref.shape[1], TILE):
-        lanes = slice(start, start + TILE)
+    for tile in range(held.shape[1] // TILE):
+        lanes = slice(tile * TILE, tile * TILE + TILE)
         spread = spread_ref[:, lanes]
-        high, low = split2(dy_ref[:, lanes] * expand(growth, spread))
+        high, low = split2(dy_tiles[tile] * expand(growth, spread))
         direct = mm(c_t2, jnp.concatenate([high, low], 0))
         held[:, lanes] = held[:, lanes] * expand(fall, spread)[0:1, :] + direct
-    first_ref[...] = held[...]
-
-
-def scan_grad_states(dy, act, cum, spread):
-    tokens, channels = dy.shape
-    blocks = tokens // Q
-    return pl.pallas_call(
-        grad_states_kernel,
-        grid=(blocks,),
-        in_specs=[
-            pl.BlockSpec((Q, channels), lambda i: (blocks - 1 - i, 0)),
-            pl.BlockSpec((Q, N), lambda i: (blocks - 1 - i, channels // N + 1)),
-            pl.BlockSpec((Q, 128), lambda i: (blocks - 1 - i, 0)),
-            whole((256, channels)),
-        ],
-        out_specs=[
-            pl.BlockSpec((1, N, channels), lambda i: (blocks - 1 - i, 0, 0)),
-            whole((N, channels)),
-        ],
-        out_shape=[sds((blocks, N, channels)), sds((N, channels))],
-        scratch_shapes=[pltpu.VMEM((N, channels), F32)],
-        compiler_params=params(),
-        cost_estimate=cost(6),
-        name="scan_grad_states",
-    )(dy, act, cum, spread)
 
 
 def near_block(
@@ -691,22 +835,41 @@
     gbc_out_ref[:, N : 2 * N] = gbc_ref[here_rows, N : 2 * N]
 
 
+WEIGHT_TILE = 384
+
+
+def mm_tn(a, b):
+    return lax.dot_general(a, b, (((0,), (0,)), ((), ())), preferred_element_type=F32)
+
+
 def backward_kernel(
     cols, dps,
     dy_ref, x_ref, y_ref, b_ref, c_ref, step_ref, cum_ref, stepin_ref, spread_ref, gather_ref, after_ref,
-    state_ref, early_ref, offs_ref, head_ref, skip_ref, o_low, o_full, g_low, g_full, late_ref, parts,
-    ga_ref, gstep_ref, gbc_out_ref, sums_ref, o_total_ref, g_own_ref, g_cross_ref, branch_in,
-    gx_ref, gbc_ref, o_own, o_land, o_cross, o_cross_land, g_own, g_land, sems, local,
+    state_ref, early_ref, offs_ref, head_ref, skip_ref, mixed_ref, of_ref, gg_ref,
+    first_grad, mixed_hbm, gg_hbm, cot, normed,
+    ga_ref, gstep_ref, gbc_out_ref, sums_ref, o_total_ref, g_own_ref, g_cross_ref, branch_ref, branch_in,
+    mixed_sib, gg_sib,
+    gx_ref, gbc_ref, late_ref, o_low, o_own, o_land, o_cross, o_cross_land, g_low, g_own, g_land, parts,
+    c_own, c_sib, n_own, n_sib, m_tiles, gg_tiles, sems, local,
 ):
     step_at = pl.program_id(0)
-    blocks = pl.num_programs(0) // 2
-    at_block = lax.rem(step_at, blocks)
-    here_rows = pl.ds(pl.multiple_of(at_block * Q, Q), Q)
+    blocks = gx_ref.shape[0] // Q
     dp, row, col = here()
     group = cols // 2
-    shard = g_own_ref.shape[1]
+    place = lax.rem(col, group)
+    shard, channels = g_own_ref.shape[1], gx_ref.shape[1]
+    half = c_own.shape[1]
+    count = branch_ref.shape[0]
     others = dps - 1
     own, other = pl.ds(0, shard), pl.ds(shard, shard)
+    sibling, mirror = (dp, 1 - row, col), mirror_of(cols)
+    peers = [(dp, row, col ^ by) for by in range(1, group)]
+    out_steps, o_steps, g_steps = 2 * half // TILE, channels // WEIGHT_TILE, channels // TILE
+    o_at = out_steps
+    g_at = o_at + o_steps
+    near_at = g_at + g_steps
+    far_at = near_at + blocks
+    last = far_at + blocks - 1
 
     def o_moves():
         return dp_copies(dps, sems, lambda to, i: o_low.at[:, to], lambda to, i: o_land.at[i])
@@ -714,50 +877,147 @@
     def g_moves():
         return dp_copies(dps, sems, lambda to, i: g_low.at[to], lambda to, i: g_land.at[i], others)
 
-    def cross_move():
-        return copy_to(o_cross, o_cross_land, sems, 2 * others, mirror_of(cols))
-
-    def part_moves():
-        return [
-            copy_to(
-                parts.at[by - 1], branch_in.at[by - 1], sems, 2 * others + by, (dp, row, col ^ by)
-            )
-            for by in range(1, group)
-        ]
-
-    load_o = pltpu.make_async_copy(o_full.at[:, dp], o_own, local.at[0])
-    load_g = pltpu.make_async_copy(g_full.at[dp], g_own, local.at[1])
+    at = 2 * others
+    cross_move = lambda: copy_to(o_cross, o_cross_land, sems, at, mirror)
+    late_moves = lambda: [
+        copy_to(first_grad.at[:, own], late_ref.at[:, other], sems, at + 1, mirror),
+        copy_to(first_grad.at[:, other], late_ref.at[:, own], sems, at + 2, mirror),
+    ]
+    core_moves = lambda: [
+        copy_to(cot.at[:, lanes_at(1 - row, half)], c_sib, sems, at + 3, sibling),
+        copy_to(mixed_hbm, mixed_sib, sems, at + 4, sibling),
+        copy_to(normed.at[:, lanes_at(1 - row, half)], n_sib, sems, at + 5, sibling),
+        copy_to(gg_hbm, gg_sib, sems, at + 6, sibling),
+    ]
+    part_moves = lambda: [
+        copy_to(parts.at[i], branch_in.at[i], sems, at + 7 + i, peer) for i, peer in enumerate(peers)
+    ]
+    load_c = pltpu.make_async_copy(cot.at[:, lanes_at(row, half)], c_own, local.at[0])
+    load_n = pltpu.make_async_copy(normed.at[:, lanes_at(row, half)], n_own, local.at[1])
+
+    def m_tile(tile):
+        lanes = lanes_at(tile, WEIGHT_TILE)
+        return pltpu.make_async_copy(mixed_sib.at[:, lanes], m_tiles.at[lax.rem(tile, 2)], local.at[2])
+
+    def gg_tile(tile):
+        lanes = lanes_at(tile, TILE)
+        return pltpu.make_async_copy(gg_sib.at[:, lanes], gg_tiles.at[lax.rem(tile, 2)], local.at[3])
 
     @at_step(0)
     def _():
-        greet(dp_peers(dps) + [mirror_of(cols)] + [(dp, row, col ^ by) for by in range(1, group)])
-        for move in o_moves() + part_moves():
+        load_c.start()
+        load_n.start()
+        greet([sibling, mirror] + peers + dp_peers(dps))
+        for move in core_moves():
             move.start()
-        load_o.start()
-        load_g.start()
+
+        @pl.when(col >= group)
+        def _():
+            for move in late_moves():
+                move.start()
+            late_ref[...] = jnp.zeros_like(late_ref)
 
         sums_ref[...] = jnp.zeros_like(sums_ref)
 
-    @pl.when(step_at < blocks)
+    @pl.when(step_at < o_at)
+    def _():
+        rows = lambda index: pl.ds(pl.multiple_of(index * count, 128), count)
+        branch_ref[...] = mm(mixed_ref[rows(place), :], of_ref[...])
+        for by in range(1, group):
+            parts[by - 1, :, lanes_at(step_at, TILE)] = mm(mixed_ref[rows(place ^ by), :], of_ref[...]).astype(BF)
+
+    @pl.when(step_at == o_at)
+    def _():
+        load_c.wait()
+        for move in core_moves()[:2]:
+            move.wait_recv()
+        m_tile(0).start()
+
+    @pl.when((step_at >= o_at) & (step_at < g_at))
+    def _():
+        tile = step_at - o_at
+        m_tile(tile).wait()
+
+        @pl.when(tile < o_steps - 1)
+        def _():
+            m_tile(tile + 1).start()
+
+        total = mm_tn(mixed_ref[:, lanes_at(tile, WEIGHT_TILE)], c_own[...])
+        total = total + mm_tn(m_tiles[lax.rem(tile, 2)], c_sib[...])
+        piece = o_own.shape[1]
+        per, each = WEIGHT_TILE // piece, shard // WEIGHT_TILE
+        which, inside = lax.div(tile, each), lax.rem(tile, each)
+        for p in range(per):
+            part = total[p * piece : p * piece + piece, :]
+            o_low[which, inside * per + p] = part.astype(BF)
+
+            @pl.when(dp == inside * per + p)
+            def _():
+                o_own[which] = part
+
+    @pl.when(step_at == g_at)
+    def _():
+        for move in o_moves():
+            move.start()
+        load_n.wait()
+        for move in core_moves()[2:]:
+            move.wait_recv()
+        gg_tile(0).start()
+
+    @pl.when((step_at >= g_at) & (step_at < near_at))
+    def _():
+        tile = step_at - g_at
+        gg_tile(tile).wait()
+
+        @pl.when(tile < g_steps - 1)
+        def _():
+            gg_tile(tile + 1).start()
+
+        lanes = lanes_at(tile, TILE)
+        total = mm_tn(n_own[HALO:, :], gg_ref[...]) + mm_tn(n_sib[HALO:, :], gg_tiles[lax.rem(tile, 2)])
+        piece = g_own.shape[0]
+        for p in range(dps):
+            part = total[p * piece : p * piece + piece, :]
+            g_low[p, :, lanes] = part.astype(BF)
+
+            @pl.when(dp == p)
+            def _():
+                g_own[:, lanes] = part
+
+    at_block = lax.rem(jnp.maximum(step_at - near_at, 0), blocks)
+    here_rows = pl.ds(pl.multiple_of(at_block * Q, Q), Q)
+
+    @pl.when((step_at >= near_at) & (step_at < far_at))
     def _():
         near_block(
             at_block, here_rows, dy_ref, x_ref, b_ref, c_ref, step_ref, cum_ref, spread_ref, state_ref,
             early_ref, offs_ref, gx_ref, gbc_ref,
         )
 
-    @pl.when(step_at == blocks)
+    @pl.when(step_at == near_at + 2)
+    def _():
+        for move in part_moves():
+            move.start()
+
+    @pl.when(step_at == near_at + blocks // 2)
     def _():
         for move in o_moves():
             move.wait_recv()
         for move in g_moves():
             move.start()
-        load_o.wait()
         for i in range(others):
             o_own[...] += o_land[i].astype(F32)
         o_cross[...] = o_own[1].astype(BF)
         cross_move().start()
 
-    @pl.when(step_at >= blocks)
+    @pl.when(step_at == far_at)
+    def _():
+        @pl.when(col < group)
+        def _():
+            for move in late_moves():
+                move.wait_recv()
+
+    @pl.when(step_at >= far_at)
     def _():
         far_block(
             blocks, at_block, here_rows, dy_ref, x_ref, y_ref, gx_ref, b_ref, step_ref, cum_ref, stepin_ref,
@@ -765,11 +1025,10 @@
             gbc_ref, ga_ref, gstep_ref, gbc_out_ref, sums_ref,
         )
 
-    @at_step(2 * blocks - 1)
+    @at_step(last)
     def _():
         cross_move().wait()
         o_total_ref[...] = o_own[0] + o_cross_land[...].astype(F32)
-        load_g.wait()
         for move in g_moves():
             move.wait()
         for i in range(others):
@@ -778,25 +1037,44 @@
         g_cross_ref[...] = g_own[:, shard:].astype(BF)
         for move in part_moves():
             move.wait()
-        for move in o_moves():
+        for move in o_moves() + core_moves():
             move.wait_send()
+
+        @pl.when(col >= group)
+        def _():
+            for move in late_moves():
+                move.wait_send()
 
 
 def scan_backward(
     cols, dps, dy, act, y, step, cum, step_in, spread, gather, after, states, early, offs, head_rows, skip,
-    o_low, o_full, g_low, g_full, late, parts,
+    mixed, w_out, gg, first_grad, cot, normed,
 ):
     tokens, channels = dy.shape
+    rows_n, width = normed.shape
+    half = width // 2
     blocks, group, shard = tokens // Q, cols // 2, channels // 2
-    piece, half = o_low.shape[2:]
-    piece_g = g_low.shape[1]
-    block = lambda i: lax.rem(i, blocks)
-    second = lambda i: jnp.maximum(i - blocks, 0)
-    rows = lambda at, width: pl.BlockSpec((Q, width), lambda i: (at(i), 0))
+    count = tokens // group
+    piece_o, piece_g = shard // dps, half // dps
+    out_steps, o_steps, g_steps = width // TILE, channels // WEIGHT_TILE, channels // TILE
+    g_at = out_steps + o_steps
+    near_at = g_at + g_steps
+    far_at = near_at + blocks
+
+    def clamp(first, size):
+        return lambda i: jnp.clip(i - first, 0, size - 1)
+
+    block = lambda i: jnp.where(i < near_at, 0, lax.rem(jnp.maximum(i - near_at, 0), blocks))
+    second = clamp(far_at, blocks)
+    state_at = lambda i: block(i) + jnp.where(i < far_at, 0, 1)
+    rows = lambda at, size: pl.BlockSpec((Q, size), lambda i: (at(i), 0))
+    lanes = lambda at, size: pl.BlockSpec((size, TILE), lambda i: (0, at(i)))
+    once = lambda shape: pl.BlockSpec(shape, lambda *_: (0,) * len(shape), pipeline_mode=pl.Buffered(1))
     vmem = pltpu.VMEM
+    dma = pltpu.SemaphoreType.DMA
     return pl.pallas_call(
         partial(backward_kernel, cols, dps),
-        grid=(2 * blocks,),
+        grid=(far_at + blocks,),
         in_specs=[
             rows(block, channels),
             rows(block, channels),
@@ -806,174 +1084,210 @@
             rows(block, 128),
             rows(block, 128),
             rows(second, 128),
-            whole(spread.shape),
-            whole(gather.shape),
+            once(spread.shape),
+            once(gather.shape),
             pl.BlockSpec((1, N, channels), lambda i: (second(i), 0, 0)),
-            pl.BlockSpec((1, N, channels), lambda i: (block(i) + lax.div(i, blocks), 0, 0)),
-            whole(early.shape),
-            whole((16, 128)),
-            whole((8, 128)),
-            whole((8, channels)),
-        ] + [ANY] * 4 + [whole(late.shape), ANY],
+            pl.BlockSpec((1, N, channels), lambda i: (state_at(i), 0, 0)),
+            once(early.shape),
+            once((16, 128)),
+            once((8, 128)),
+            once((8, channels)),
+            once(mixed.shape),
+            lanes(clamp(0, out_steps), channels),
+            lanes(clamp(g_at, g_steps), tokens),
+        ] + [ANY] * 5,
         out_specs=[
             rows(second, channels),
             rows(second, 128),
             rows(second, 2 * N),
             whole((8, 128)),
-            whole((piece, half)),
+            whole((piece_o, half)),
             whole((piece_g, shard)),
             whole((piece_g, shard)),
-            ANY,
+            lanes(clamp(0, out_steps), count),
+            ANY, ANY, ANY,
         ],
         out_shape=[
             sds((tokens, channels)),
             sds((tokens, 128), BF),
             sds((tokens, 2 * N)),
             sds((8, 128)),
-            sds((piece, half)),
+            sds((piece_o, half)),
             sds((piece_g, shard)),
             sds((piece_g, shard), BF),
-            sds(parts.shape, BF),
+            sds((count, width)),
+            sds((max(group - 1, 1), count, width), BF),
+            sds(mixed.shape, BF),
+            sds(gg.shape, BF),
         ],
         scratch_shapes=[
-            vmem((tokens, channels), F32), vmem((tokens, 2 * N), F32),
-            vmem((2, piece, half), F32), vmem((dps - 1, 2, piece, half), BF),
-            vmem((piece, half), BF), vmem((piece, half), BF),
-            vmem((piece_g, channels), F32), vmem((dps - 1, piece_g, channels), BF),
-            pltpu.SemaphoreType.DMA((2, 2 * (dps - 1) + group)),
-            pltpu.SemaphoreType.DMA((2,)),
+            vmem((tokens, channels), F32), vmem((tokens, 2 * N), F32), vmem((N, channels), F32),
+            vmem((2, dps, piece_o, half), BF), vmem((2, piece_o, half), F32),
+            vmem((dps - 1, 2, piece_o, half), BF), vmem((piece_o, half), BF), vmem((piece_o, half), BF),
+            vmem((dps, piece_g, channels), BF), vmem((piece_g, channels), F32),
+            vmem((dps - 1, piece_g, channels), BF),
+            vmem((max(group - 1, 1), count, width), BF),
+            vmem((tokens, half), BF), vmem((tokens, half), BF),
+            vmem((rows_n, half), BF), vmem((rows_n, half), BF),
+            vmem((2, tokens, WEIGHT_TILE), BF), vmem((2, tokens, TILE), BF),
+            dma((2, 2 * (dps - 1) + 6 + group)),
+            dma((4,)),
         ],
         compiler_params=remote_params(3),
-        cost_estimate=cost(55),
+        cost_estimate=cost(80),
         name="scan_backward",
     )(
         dy, act, y, act, act, step, cum, step_in, spread, gather, after, states, early, offs, head_rows, skip,
-        o_low, o_full, g_low, g_full, late, parts,
+        mixed, w_out, gg, first_grad, mixed, gg, cot, normed,
     )
 
 
 def gate_kernel(
-    normed_ref, cot_ref, wg_ref, wo_ref, y0_ref, x_ref, early_ref, c_ref, grow_ref, spread_ref, vec_ref,
-    graw_ref, y_ref, gm_ref, stats_ref, squares, inners,
+    cols, inner_channels,
+    y0_ref, graw_ref, gm_ref, x_ref, early_ref, c_ref, grow_ref, spread_ref, vec_ref,
+    cum_ref, c_block_ref, spread_all_ref,
+    y_ref, mixed_ref, gg_ref, dy_ref, sums_ref, after_ref, first_ref,
+    y_vm, graw_vm, gm_vm, squares, inners, stats, stats_land, stats_col, held, sems,
 ):
-    at = pl.program_id(0)
-    tokens = cot_ref.shape[0]
-
-    @pl.when(at == 0)
-    def _():
+    step = pl.program_id(0)
+    tiles = y_vm.shape[0]
+    tokens = y0_ref.shape[0]
+    dp, row, col = here()
+    group = cols // 2
+    peers = [(dp, row, col ^ by) for by in range(1, group)]
+    gain = vec_ref[1:2, :]
+    nt = (((1,), (1,)), ((), ()))
+    moves = lambda: [copy_to(stats, stats_land.at[i], sems, i, peer) for i, peer in enumerate(peers)]
+
+    @at_step(0)
+    def _():
+        greet(peers)
         squares[...] = jnp.zeros_like(squares)
         inners[...] = jnp.zeros_like(inners)
 
-    graw_ref[...] = mm(normed_ref[HALO:, :], wg_ref[...])
-    gm_ref[...] = mm_nt(cot_ref[...], wo_ref[...])
-    s_high, s_low = split2(early_ref[...])
-    s2 = jnp.concatenate([s_high, s_low], 0)
-    spread = spread_ref[...]
-    skip, gain = vec_ref[0:1, :], vec_ref[1:2, :]
-    for row in range(0, tokens, Q):
-        rows = slice(row, row + Q)
-        c_blk = c_ref[rows, :]
-        carried = mm(jnp.concatenate([c_blk, c_blk], 1), s2) * mm(grow_ref[rows, :], spread)
-        y = y0_ref[rows, :] + carried + skip * x_ref[rows, :].astype(F32)
-        y_ref[rows, :] = y
-        raw = graw_ref[rows, :]
-        gated = y * raw * sigmoid(raw)
-        square = gated * gated
-        inner = gm_ref[rows, :] * gain * gated
-        squares[rows, :] += square[:, 0:128] + square[:, 128:256]
-        inners[rows, :] += inner[:, 0:128] + inner[:, 128:256]
-
-    @pl.when(at == pl.num_programs(0) - 1)
+    @pl.when(step < tiles)
+    def _():
+        s_high, s_low = split2(early_ref[...])
+        s2 = jnp.concatenate([s_high, s_low], 0)
+        spread = spread_ref[...]
+        skip = vec_ref[0:1, :]
+        for at in range(0, tokens, Q):
+            rows = slice(at, at + Q)
+            c_blk = c_ref[rows, :]
+            carried = mm(jnp.concatenate([c_blk, c_blk], 1), s2) * mm(grow_ref[rows, :], spread)
+            y = y0_ref[rows, :] + carried + skip * x_ref[rows, :].astype(F32)
+            raw, gm = graw_ref[rows, :], gm_ref[rows, :]
+            y_ref[rows, :] = y
+            y_vm[step, rows, :] = y
+            graw_vm[step, rows, :] = raw
+            gm_vm[step, rows, :] = gm
+            gated = y * raw * sigmoid(raw)
+            square = gated * gated
+            inner = gm * gain * gated
+            squares[rows, :] += square[:, 0:128] + square[:, 128:256]
+            inners[rows, :] += inner[:, 0:128] + inner[:, 128:256]
+
+    @at_step(tiles - 1)
     def _():
         ones = jnp.ones((8, 128), F32)
-        nt = (((1,), (1,)), ((), ()))
         square_row = lax.dot_general(ones, squares[...], nt, precision=HIGHEST, preferred_element_type=F32)
         inner_row = lax.dot_general(ones, inners[...], nt, precision=HIGHEST, preferred_element_type=F32)
-        stats_ref[...] = jnp.where(iota2(square_row.shape, 0) == 0, square_row, inner_row)
-
-
-def gate_forward(normed, cot, w_gate, w_out, y0, act, early, grow, spread, vectors):
-    rows, width = normed.shape
+        stats[...] = jnp.where(iota2(square_row.shape, 0) == 0, square_row, inner_row)
+        for move in moves():
+            move.start()
+        for move in moves():
+            move.wait_recv()
+        total = stats[...]
+        for i in range(group - 1):
+            total = total + stats_land[i]
+        wide = jnp.concatenate([total, jnp.zeros((120, tokens), F32)], 0)
+        stats_col[...] = wide.T
+
+    @pl.when((step >= tiles) & (step < 2 * tiles))
+    def _():
+        tile = step - tiles
+        gain_sum = jnp.zeros((1, TILE), F32)
+        skip_sum = jnp.zeros((1, TILE), F32)
+        for at in range(0, tokens, Q):
+            rows = slice(at, at + Q)
+            inv = lax.rsqrt(stats_col[rows, 0:1] * (1.0 / inner_channels) + EPSILON)
+            pull = inv * inv * inv * (stats_col[rows, 1:2] * (1.0 / inner_channels))
+            raw, y, gm = graw_vm[tile, rows, :], y_vm[tile, rows, :], gm_vm[tile, rows, :]
+            sig = sigmoid(raw)
+            act = raw * sig
+            gated = y * act
+            unit = gated * inv
+            mixed_ref[rows, :] = (unit * gain).astype(BF)
+            gain_sum = gain_sum + jnp.sum(gm * unit, axis=0, keepdims=True)
+            grad_gated = inv * (gm * gain) - gated * pull
+            dy = grad_gated * act
+            dy_ref[rows, :] = dy
+            y_vm[tile, rows, :] = dy
+            gg_ref[rows, :] = (grad_gated * y * (sig * (1.0 + raw * (1.0 - sig)))).astype(BF)
+            skip_sum = skip_sum + jnp.sum(dy * x_ref[rows, :].astype(F32), axis=0, keepdims=True)
+        sums_ref[...] = jnp.zeros_like(sums_ref)
+        sums_ref[0:1, :] = gain_sum
+        sums_ref[1:2, :] = skip_sum
+
+    @pl.when(step == 2 * tiles)
+    def _():
+        for move in moves():
+            move.wait_send()
+        held[...] = jnp.zeros_like(held)
+
+    @pl.when(step >= 2 * tiles)
+    def _():
+        at = pl.num_programs(0) - 1 - step
+        rows = pl.ds(pl.multiple_of(at * Q, Q), Q)
+        grad_state_block(y_vm.at[:, rows, :], c_block_ref, cum_ref, spread_all_ref, after_ref, held)
+        first_ref[...] = held[...]
+
+
+def gate_and_mix(cols, inner_channels, y0, graw, gm, act, early, grow, spread, vectors, cum):
     tokens, channels = y0.shape
+    blocks = tokens // Q
+    tiles, group = channels // TILE, cols // 2
+    first = lambda i: jnp.minimum(i, tiles - 1)
+    second = lambda i: jnp.clip(i - tiles, 0, tiles - 1)
+    either = lambda i: jnp.where(i < 2 * tiles, lax.rem(i, tiles), tiles - 1)
+    third = lambda i: blocks - 1 - jnp.maximum(i - 2 * tiles, 0)
+    lanes = lambda at, count: pl.BlockSpec((count, TILE), lambda i: (0, at(i)))
+    vmem = pltpu.VMEM
     return pl.pallas_call(
-        gate_kernel,
-        grid=(channels // TILE,),
+        partial(gate_kernel, cols, inner_channels),
+        grid=(2 * tiles + blocks,),
         in_specs=[
-            whole((rows, width)),
-            whole((tokens, width)),
-            columns(width),
-            pl.BlockSpec((TILE, width), lambda j: (j, 0)),
-            columns(tokens),
-            columns(tokens),
-            columns(N),
-            pl.BlockSpec((tokens, N), lambda j: (0, channels // N + 1)),
+            lanes(first, tokens), lanes(first, tokens), lanes(first, tokens), lanes(either, tokens),
+            lanes(first, N),
+            pl.BlockSpec((tokens, N), lambda i: (0, channels // N + 1)),
             whole((tokens, 256)),
-            columns(256),
-            columns(8),
+            lanes(first, 256),
+            lanes(either, 8),
+            pl.BlockSpec((Q, 128), lambda i: (third(i), 0)),
+            pl.BlockSpec((Q, N), lambda i: (third(i), channels // N + 1)),
+            whole((256, channels)),
         ],
-        out_specs=[columns(tokens), columns(tokens), columns(tokens), whole((8, tokens))],
-        out_shape=[sds((tokens, channels))] * 3 + [sds((8, tokens))],
-        scratch_shapes=[pltpu.VMEM((tokens, 128), F32), pltpu.VMEM((tokens, 128), F32)],
-        compiler_params=params(),
-        cost_estimate=cost(16),
-        name="gate_forward",
-    )(normed, cot, w_gate, w_out, y0, act, early, act, grow, spread, vectors)
-
-
-def mix_kernel(
-    inner_channels, graw_ref, y_ref, gm_ref, x_ref, stats_ref, vec_ref,
-    mixed_ref, gg_ref, dy_ref, sums_ref, stats_col,
-):
-    tokens = y_ref.shape[0]
-
-    @pl.when(pl.program_id(0) == 0)
-    def _():
-        stats_col[...] = stats_ref[...].T
-
-    gain = vec_ref[1:2, :]
-    gain_sum = jnp.zeros((1, TILE), F32)
-    skip_sum = jnp.zeros((1, TILE), F32)
-    for row in range(0, tokens, Q):
-        rows = slice(row, row + Q)
-        inv = lax.rsqrt(stats_col[rows, 0:1] * (1.0 / inner_channels) + EPSILON)
-        pull = inv * inv * inv * (stats_col[rows, 1:2] * (1.0 / inner_channels))
-        raw = graw_ref[rows, :]
-        y = y_ref[rows, :]
-        gm = gm_ref[rows, :]
-        sig = sigmoid(raw)
-        act = raw * sig
-        gated = y * act
-        unit = gated * inv
-        mixed_ref[rows, :] = (unit * gain).astype(BF)
-        gain_sum = gain_sum + jnp.sum(gm * unit, axis=0, keepdims=True)
-        grad_gated = inv * (gm * gain) - gated * pull
-        dy = grad_gated * act
-        dy_ref[rows, :] = dy
-        gg_ref[rows, :] = (grad_gated * y * (sig * (1.0 + raw * (1.0 - sig)))).astype(BF)
-        skip_sum = skip_sum + jnp.sum(dy * x_ref[rows, :].astype(F32), axis=0, keepdims=True)
-    sums_ref[...] = jnp.zeros_like(sums_ref)
-    sums_ref[0:1, :] = gain_sum
-    sums_ref[1:2, :] = skip_sum
-
-
-def mix_backward(inner_channels, graw, y, gm, act, stats, vectors):
-    tokens, channels = y.shape
-    return pl.pallas_call(
-        partial(mix_kernel, inner_channels),
-        grid=(channels // TILE,),
-        in_specs=[columns(tokens)] * 4 + [whole((128, tokens)), columns(8)],
-        out_specs=[columns(tokens)] * 3 + [columns(8)],
+        out_specs=[
+            lanes(first, tokens), lanes(second, tokens), lanes(second, tokens), lanes(second, tokens),
+            lanes(second, 8),
+            pl.BlockSpec((1, N, channels), lambda i: (third(i), 0, 0)),
+            whole((N, channels)),
+        ],
         out_shape=[
-            sds((tokens, channels), BF),
-            sds((tokens, channels), BF),
-            sds((tokens, channels)),
-            sds((8, channels)),
+            sds((tokens, channels)), sds((tokens, channels), BF), sds((tokens, channels), BF),
+            sds((tokens, channels)), sds((8, channels)), sds((blocks, N, channels)), sds((N, channels)),
         ],
-        scratch_shapes=[pltpu.VMEM((tokens, 128), F32)],
-        compiler_params=params(),
-        cost_estimate=cost(10),
-        name="mix_backward",
-    )(graw, y, gm, act, stats, vectors)
+        scratch_shapes=[
+            vmem((tiles, tokens, TILE), F32), vmem((tiles, tokens, TILE), F32), vmem((tiles, tokens, TILE), F32),
+            vmem((tokens, 128), F32), vmem((tokens, 128), F32),
+            vmem((8, tokens), F32), vmem((max(group - 1, 1), 8, tokens), F32), vmem((tokens, 128), F32),
+            vmem((N, channels), F32),
+            pltpu.SemaphoreType.DMA((2, max(group - 1, 1))),
+        ],
+        compiler_params=remote_params(6),
+        cost_estimate=cost(40),
+        name="gate_and_mix",
+    )(y0, graw, gm, act, early, act, grow, spread, vectors, cum, act, spread)
 
 
 def conv_back_tile(ga_ref, raw_ref, taps_ref, gv_ref, sums_ref, g_pad):
@@ -1000,44 +1314,6 @@
     sums_ref[...] = jnp.zeros_like(sums_ref)
     for k in range(5):
         sums_ref[k : k + 1, :] = sums[k]
-
-
-def mm_tn(a, b):
-    return lax.dot_general(a, b, (((0,), (0,)), ((), ())), preferred_element_type=F32)
-
-
-def weight_grad_kernel(skips, widths, outs, *refs):
-    out_ref = refs[-outs]
-    sources = len(skips)
-    lefts, rights = refs[:sources], refs[sources:-outs]
-    at = 0
-    for i, width in enumerate(widths):
-        total = None
-        for source in range(sources):
-            left, right = lefts[source], rights[source * len(widths) + i]
-            part = mm_tn(left[skips[source][i] :, :], right[...])
-            total = part if total is None else total + part
-        out_ref[:, at : at + width] = total
-        if outs > 1:
-            refs[-1][:, at : at + width] = total.astype(BF)
-        at += width
-
-
-def weight_grad(lefts, rights, low=False):
-    height = lefts[0].shape[1]
-    widths = [right.shape[1] for right in rights[0]]
-    skips = [[left.shape[0] - r.shape[0] for r in group] for left, group in zip(lefts, rights)]
-    flat = [r for group in rights for r in group]
-    return pl.pallas_call(
-        partial(weight_grad_kernel, skips, widths, 1 + low),
-        grid=(height // TILE,),
-        in_specs=[columns(left.shape[0]) for left in lefts] + [whole(r.shape) for r in flat],
-        out_specs=[pl.BlockSpec((TILE, sum(widths)), lambda j: (j, 0))] * (1 + low),
-        out_shape=[sds((height, sum(widths))), sds((height, sum(widths)), BF)][: 1 + low],
-        compiler_params=params(),
-        cost_estimate=cost(8),
-        name="weight_grad",
-    )(*lefts, *flat)
 
 
 def input_grad_tile(
@@ -1553,10 +1829,7 @@
         ],
         axis=0,
     )
-    group_tokens, value_full, gate_full, out_full, small_full, vecs = import_all(
-        cols, dps, tokens, w_value, w_gate, w_out, small, vec
-    )
-    cotangent, group_tokens = lax.optimization_barrier((cotangent, group_tokens))
+    group_tokens, value_full, small_full, vecs = import_all(cols, dps, tokens, w_value, small, vec)
     from_col = lax.broadcasted_iota(jnp.int32, (cols * 128, TILE + 128), 0) // 128
     from_lane = lax.broadcasted_iota(jnp.int32, (cols * 128, TILE + 128), 0) % 128
     to = lax.broadcasted_iota(jnp.int32, (cols * 128, TILE + 128), 1)
@@ -1567,15 +1840,6 @@
     is_mirror = is_mirror & (from_lane == state_width + head_to - heads)
     pick = (is_state | ((head_to >= 0) & (is_own | is_mirror))).astype(BF)
 
-    def gather_tokens(values):
-        out = jnp.zeros((span, width), values.dtype)
-        out = lax.dynamic_update_slice_in_dim(out, values, place * local, 0)
-        for by in range(1, group):
-            other = lax.ppermute(values, "col", ring(by))
-            at = lax.rem(place - by + group, group)
-            out = lax.dynamic_update_slice_in_dim(out, other, at * local, 0)
-        return out
-
     vecs = vecs.astype(F32)
     both = jnp.concatenate(
         [
@@ -1604,49 +1868,21 @@
     gather = jnp.asarray(one_hot.T, BF)
 
     gain = norm_gain.astype(F32)
-    raw, act, normed, step_in, step, cum, grow, offs, inv_rms, picked = project(
-        group_tokens, gain[None], value_full, small_full, pick, taps, head_rows
-    )
-    states, final_state = scan_states(act, step, cum, spread, channels)
-
-    def cross(values, pairs):
-        moved = lax.ppermute(values, "col", pairs)
-        return jnp.concatenate([moved[:, shard:], moved[:, :shard]], axis=1)
-
-    early = cross(final_state, forth)
-    y0 = scan_forward(act, step, cum, spread, states, channels)
-    group_cot = gather_tokens(cotangent)
-    graw, y, gm, stats = gate_forward(
-        normed, group_cot, gate_full, out_full, y0, act, early, grow, spread, vectors
-    )
-    by = 1
-    while by < group:
-        stats = stats + lax.ppermute(stats, "col", flips(cols, by))
-        by *= 2
-    stats_pad = jnp.pad(stats, ((0, 120), (0, 0)))
-    mixed, grad_gate, dy, mix_sums = mix_backward(inner_channels, graw, y, gm, act, stats_pad, vectors)
-
-    after, first_grad = scan_grad_states(dy, act, cum, spread)
-    late = cross(first_grad, back)
-    branch_rows = lambda at: mm(at_rows(mixed, at, local), out_full)
-    parts = jnp.stack([branch_rows(place ^ by).astype(BF) for by in range(1, group)])
-    branch = branch_rows(place)
-
-    def my_half(values):
-        mine = lax.dynamic_slice_in_dim(values, row * half_width, half_width, 1)
-        return [mine, swap_core(lax.dynamic_slice_in_dim(values, (1 - row) * half_width, half_width, 1))]
-
-    out_full_sum, out_low = weight_grad(
-        [mixed, swap_core(mixed)], [[half] for half in my_half(group_cot)], low=True
-    )
-    normed_halves = my_half(normed)
-    gate_full_sum, gate_low = weight_grad(normed_halves, [[grad_gate], [swap_core(grad_gate)]], low=True)
-    by_out = (2, dps, shard // dps, half_width)
-    by_gate = (dps, half_width // dps, channels)
-    ga, grad_step, gbc, head_sums, out_total, gate_own, gate_cross, branch_in = scan_backward(
+    (
+        raw, act, normed, step_in, step, cum, grow, offs, inv_rms, picked, states, y0, graw, gm, early,
+        group_cot, gate_full, out_full,
+    ) = forward_all(
+        cols, dps, group_tokens, gain[None], value_full, small_full, pick, taps, head_rows, spread, cotangent,
+        w_gate, w_out,
+    )
+    y, mixed, grad_gate, dy, mix_sums, after, first_grad = gate_and_mix(
+        cols, inner_channels, y0, graw, gm, act, early, grow, spread, vectors, cum
+    )
+    (
+        ga, grad_step, gbc, head_sums, out_total, gate_own, gate_cross, branch, branch_in, _, _,
+    ) = scan_backward(
         cols, dps, dy, act, y, step, cum, step_in, spread, gather, after, states, early, offs, head_rows, vectors,
-        out_low.reshape(by_out), out_full_sum.reshape(by_out), gate_low.reshape(by_gate),
-        gate_full_sum.reshape(by_gate), late, parts,
+        mixed, out_full, grad_gate, first_grad, group_cot, normed,
     )
     block_out = (tokens.astype(F32) + branch + jnp.sum(branch_in.astype(F32), axis=0)).astype(BF)
     state_part = state_all // group

time: 552 us -> 461 us (0.84)
  starting transfers between devices: 25.6 us -> 0 us
  waiting for transfers between devices: 20.5 us -> 0 us
  Pallas kernels: 432 us -> 413 us
  matrix products: 13.3 us -> 0 us
  local copies, waits for them, and re-layouts: 41 us -> 30.8 us
    ppermute x8 -> x0, starting transfers between devices: 25.6 us -> none  [the longest x1 17.7 us: per_device(): stats = stats + lax.ppermute(stats, 'col', flips(cols, by))]
    pallas_call x10 -> x4, Pallas kernels: 290 us -> 267 us  [the longest x1 88.9 us: scan_backward(): pl.pallas_call(partial(backward_kernel, cols, dps), grid=(far_at + blocks...]
    ppermute x8 -> x0, waiting for transfers between devices: 20.5 us -> none  [the longest x2 18.3 us: cross(): moved = lax.ppermute(values, 'col', pairs)]
    dot_general x2 -> x0, matrix products: 13.3 us -> none  [mm(): lax.dot_general(a, b, (((1,), (0,)), ((), ())), preferred_element_type=F32)]
    unnamed x30 -> x22, local copies, waits for them, and re-layouts: 15.7 us -> 12.8 us
  transfers between devices with their start and end apart: 8 -> 0, of which waited for: 3 -> 0; matrix products, arithmetic and copies ran while one was open for 4% -> 0% of each run, Pallas kernels for 14% -> 0%
where the time goes in v4:
time: 461 us; the launch traced here: 457 us
  Pallas kernels  413 us (90%)
  local copies, waits for them, and re-layouts  30.8 us (7%)
  other arithmetic  11.8 us (3%)
    pallas_call x1, Pallas kernels, scan_backward(): pl.pallas_call(partial(backward_kernel, cols, dps), grid=(far_at + blocks...  88.9 us
    pallas_call x1, Pallas kernels, settle(): pl.pallas_call(partial(settle_kernel, cols, dps, heads, span), in_specs=[...  84.2 us
    pallas_call x1, Pallas kernels, forward_all(): pl.pallas_call(partial(forward_all_kernel, cols, dps), grid=(gate_at + 2...  76.4 us
    pallas_call x1, Pallas kernels, finish(): pl.pallas_call(partial(finish_kernel, cols, dps, part, whole_state), grid...  62.1 us
    pallas_call x1, Pallas kernels, import_all(): pl.pallas_call(partial(import_kernel, cols, dps), in_specs=[any_spec] * 4...  51.6 us
    pallas_call x1, Pallas kernels, gate_and_mix(): pl.pallas_call(partial(gate_kernel, cols, inner_channels), grid=(2 * tile...  50.2 us
    unnamed x22, local copies, waits for them, and re-layouts  12.8 us

profile of v4, /device:TPU:0, one launch (start us, length us, event | category | flops | bytes accessed | tf_op | source)
XLA Modules:
  0.0 457.2 jit_solution(11070685594695134848)
XLA Ops:
  0.7 1.1 copy.34
  1.7 0.9 copy.35
  2.6 0.8 fusion.15.sw
  3.5 0.7 fusion.28
  4.2 0.8 fusion.37
  4.9 0.7 broadcast_in_dim.36
  5.6 0.7 broadcast_in_dim.37
  6.3 1.9 concatenate.47.vec
  8.2 51.6 %import_all.1 = (bf16[1040,1536]{1,0:T(8,128)(2,1)}, bf16[1536,1536]{1,0:T(8,128)(2,1)}, bf16[1536,512]{1,0:T(8,128)(2,1)}, bf16[4,16,768]{2,1,0:T(8,128)(2,1)}) custom-call(bf16[512,1536]{1,0:T(8,128)(2,1)} %tok.3, bf16[768,768]{1,0:T(8,128)(2,1)} %wv.1, bf16[768,128]{1,0:T(8,128)(2,1)} %fusion.15.sw, bf16[16,768]{1,0:T(8,128)(2,1)} %concatenate.47.vec), custom_call_target="tpu_custom_call" | custom-call | bytes 135000000 | tf_op jit(solution)/shard_map/import_all/pallas_call | solution.py:261
  59.8 0.9 convert_element_type.26
  61.0 0.6 select_maximum_fusion.1.head_ref
  61.9 0.7 fusion.18
  62.7 0.6 pad_maximum_fusion.taps_ref
  63.4 1.6 fusion.4.pick_ref
  65.0 0.6 reshape.106.gain_ref.gain
  65.6 76.4 %forward_all.1 = (f32[1040,1792]{1,0:T(8,128)}, bf16[1024,1792]{1,0:T(8,128)(2,1)}, bf16[1040,1536]{1,0:T(8,128)(2,1)}, f32[1024,128]{1,0:T(8,128)}, f32[1024,12...) custom-call(bf16[1040,1536]{1,0:T(8,128)(2,1)} %get-tuple-element.65, ...), custom_call_target="tpu_custom_call" | custom-call | bytes 210000000 | tf_op jit(solution)/shard_map/forward_all/pallas_call | solution.py:640
  142.0 50.2 %gate_and_mix.1 = (f32[1024,1536]{1,0:T(8,128)}, bf16[1024,1536]{1,0:T(8,128)(2,1)}, bf16[1024,1536]{1,0:T(8,128)(2,1)}, f32[1024,1536]{1,0:T(8,128)}, f32[8,153...) custom-call(f32[1024,1536]{1,0:T(8,128)} %get-tuple-element.69.y0_ref, ...), custom_call_target="tpu_custom_call" | custom-call | bytes 120000000 | tf_op jit(solution)/shard_map/gate_and_mix/pallas_call | solution.py:1256
  192.3 88.9 %scan_backward.1 = (f32[1024,1536]{1,0:T(8,128)}, bf16[1024,128]{1,0:T(8,128)(2,1)}, f32[1024,256]{1,0:T(8,128)}, f32[8,128]{1,0:T(8,128)}, f32[192,768]{1,0:T(8...) custom-call(f32[1024,1536]{1,0:T(8,128)} %get-tuple-element.76.dy_re, ...), custom_call_target="tpu_custom_call" | custom-call | bytes 240000000 | tf_op jit(solution)/shard_map/scan_backward/pallas_call | solution.py:1075
  281.1 0.8 slice_multiply_fusion
  282.0 0.9 slice_reduce_fusion.1
  283.3 0.2 dynamic_update_slice.19
  283.6 62.1 %finish.1 = (f32[8,1792]{1,0:T(8,128)}, f32[1040,1536]{1,0:T(8,128)}, bf16[1040,1536]{1,0:T(8,128)(2,1)}, f32[8,1536]{1,0:T(8,128)}, f32[768,1792]{1,0:T(8,128)}...) custom-call(f32[1024,1536]{1,0:T(8,128)} %get-tuple-element.91.ga_ref, f32[1040,1792]{1,0:T(8,128)} %get-tuple-element.92.raw_ref, ...), custom_call_target="tpu_custom_call" | custom-call | bytes 165000000 | tf_op jit(solution)/shard_map/finish/pallas_call | solution.py:1493
  345.7 0.8 slice.110
  346.6 0.7 slice_dynamic-update-slice_fusion
  347.3 0.8 slice_reduce_fusion
  348.2 0.6 pad_bitcast_fusion.flat
  348.8 84.2 %settle.1 = (f32[512,1536]{1,0:T(8,128)}, f32[768,768]{1,0:T(8,128)}, f32[768,256]{1,0:T(8,128)}, f32[168,128]{1,0:T(8,128)}) custom-call(f32[1040,1536]{1,0:T(8,128)} %get-tuple-element.101.gn, bf16[1040,1536]{1,0:T(8,128)(2,1)} %get-tuple-element.102.gnb, f32[768,1792]{1,0:T(8,128)} %get-tuple-element.103.joint, f32[168,128]{1,0:T(8,128)} %pad_bitcast_fusion.flat, ...), custom_call_target="tpu_custom_call" | custom-call | bytes 270000000 | tf_op jit(solution)/shard_map/settle/pallas_call | solution.py:1731
  433.0 1.3 constant_dynamic-slice_fusion.2
  434.3 0.8 copy.37
  435.1 1.0 slice.122
  436.2 0.8 copy.38
  436.9 0.9 slice.123
  437.8 0.6 dynamic-slice_bitcast_fusion.2
  438.4 0.7 dynamic-slice_reduce_fusion
  439.1 0.7 slice.126
  439.9 0.6 slice_bitcast_fusion.1
  440.5 0.5 slice_bitcast_fusion.9
  441.0 0.7 slice.146
  441.8 0.5 slice_bitcast_fusion.6
  442.4 1.4 slice.145
  443.7 3.8 fusion
  447.6 1.7 copy.48
  449.2 1.1 copy-done.3
  450.4 1.4 copy.49
  451.8 1.1 copy-done.4
  452.9 1.4 copy.50
  454.3 1.1 copy-done.2
  455.4 1.4 copy.51
  (51 shorter events, 1.6 us)
Async XLA Ops:
  0.6 64.4 %copy-start.6 = (bf16[1536]{0:T(1024)(128)(2,1)S(1)}, bf16[1536]{0:T(1024)(128)(2,1)}, u32[]{:S(2)}) copy-start(bf16[1536]{0:T(1024)(128)(2,1)} %param.19) | copy-start | bytes 9220
  348.8 94.9 %copy-start.5 = (bf16[1,512,1536]{2,1,0:T(8,128)(2,1)S(1)}, bf16[1,512,1536]{2,1,0:T(8,128)(2,1)}, u32[]{:S(2)}) copy-start(bf16[1,512,1536]{2,1,0:T(8,128)(2,1)} %get-tuple-element.90) | copy-start | bytes 4718596
  433.0 10.7 %copy-start = (bf16[512,1536]{1,0:T(8,128)(2,1)S(1)}, bf16[512,1536]{1,0:T(8,128)(2,1)}, u32[]{:S(2)}) copy-start(bf16[512,1536]{1,0:T(8,128)(2,1)} %tok.3) | copy-start | bytes 4718596
  443.7 3.8 copy-start.1
  447.5 2.8 copy-start.3
  450.4 2.5 copy-start.4
  452.9 2.5 copy-start.2

commit v5 on v4

--- a/solution.py
+++ b/solution.py
@@ -15,6 +15,7 @@
 Q = 128
 HEAD = 64
 HALO = 16
+ROWS = 64
 TILE = 256
 HIGHEST = lax.Precision.HIGHEST
 VMEM_LIMIT = 56 * 2**20
@@ -101,6 +102,23 @@
         copy_to(src_of(dp ^ by, by - 1), dst_of(dp ^ by, by - 1), sems, first + by - 1, (dp ^ by, row, col))
         for by in range(1, dps)
     ]
+
+
+def hand_out(dps, sems, first, src, out):
+    dp, row, col = here()
+    piece, lanes = src.shape
+    rows = lambda d: pl.ds(d * piece, piece)
+    if dps != 4:
+        return dp_copies(dps, sems, lambda to, i: src, lambda to, i: out.at[rows(dp), :], first), []
+    left, right = pl.ds(0, lanes // 2), pl.ds(lanes // 2, lanes // 2)
+    near = [
+        copy_to(src, out.at[rows(dp), :], sems, first + i, (dp ^ by, row, col)) for i, by in enumerate((1, 2))
+    ]
+    far = []
+    for i, (by, half) in enumerate(((1, left), (2, right))):
+        passed = out.at[rows(dp ^ by), half]
+        far.append(copy_to(passed, passed, sems, first + 2 + i, (dp ^ 3 ^ by, row, col)))
+    return near, far
 
 
 def dp_peers(dps):
@@ -286,10 +304,15 @@
     )(tokens, w_value, small, vec)
 
 
-def conv_rows(raw_ref, taps, start, size):
-    total = taps[4:5, :] + jnp.zeros((size, taps.shape[1]), F32)
-    for k in range(4):
-        total = total + taps[k : k + 1, :] * raw_ref[pl.ds(HALO - 3 + k + start, size), :]
+def conv_window(raw_ref, start, size):
+    window = raw_ref[HALO + start - 8 : HALO + start + size, :]
+    return [pltpu.roll(window, 3 - k, 0)[8:, :] for k in range(3)] + [window[8:, :]]
+
+
+def conv_rows(moved, taps):
+    total = taps[4:5, :] + taps[0:1, :] * moved[0]
+    for k in range(1, 4):
+        total = total + taps[k : k + 1, :] * moved[k]
     return total
 
 
@@ -336,11 +359,11 @@
 
 def activate(raw_ref, taps, act_ref, copy_ref):
     tokens = act_ref.shape[0]
-    for at in range(0, tokens, Q):
-        pre = conv_rows(raw_ref, taps, at, Q)
+    for at in range(0, tokens, ROWS):
+        pre = conv_rows(conv_window(raw_ref, at, ROWS), taps)
         act = (pre * sigmoid(pre)).astype(BF)
-        act_ref[at : at + Q, :] = act
-        copy_ref[at : at + Q, :] = act
+        act_ref[at : at + ROWS, :] = act
+        copy_ref[at : at + ROWS, :] = act
 
 
 def expand(per_head, spread):
@@ -350,22 +373,33 @@
 
 def transpose_bf(values):
     return values.astype(F32).T.astype(BF)
+
+
+def expand_rows(per_head, spread):
+    high, low = split2(jnp.concatenate(per_head, 0))
+    return mm(jnp.concatenate([high, low], 1), spread)
+
+
+def eight(row):
+    return jnp.broadcast_to(row, (8, row.shape[1]))
+
+
+def spans(total, size):
+    size = min(size, total)
+    return [slice(at, at + size) for at in range(0, total, size)]
 
 
 def state_block(x_ref, b_ref, step_ref, cum_ref, spread_ref, held):
     cum = cum_ref[...]
     end = cum[Q - 1 : Q, :]
     tail = jnp.exp(end - cum) * step_ref[...]
-    fall = jnp.broadcast_to(jnp.exp(end), (8, 128))
     b_t = transpose_bf(b_ref[...])
     b_t2 = jnp.concatenate([b_t, b_t], 1)
-    for start in range(0, x_ref.shape[1], TILE):
-        lanes = slice(start, start + TILE)
-        spread = spread_ref[:, lanes]
-        scaled = expand(tail, spread) * x_ref[:, lanes].astype(F32)
-        high, low = split2(scaled)
+    for lanes in spans(x_ref.shape[1], 1536):
+        wide = expand_rows([tail, eight(jnp.exp(end))], spread_ref[:, lanes])
+        high, low = split2(wide[:Q] * x_ref[:, lanes].astype(F32))
         fresh = mm(b_t2, jnp.concatenate([high, low], 0))
-        held[:, lanes] = held[:, lanes] * expand(fall, spread)[0:1, :] + fresh
+        held[:, lanes] = held[:, lanes] * wide[Q : Q + 1, :] + fresh
 
 
 def forward_block(x_ref, b_ref, c_ref, step_ref, cum_ref, spread_ref, state_ref, y_ref):
@@ -379,12 +413,10 @@
     growth = jnp.exp(cum)
     c2 = jnp.concatenate([c_blk, c_blk], 1)
     zero = jnp.zeros((Q, 128), BF)
-    for start in range(0, x_ref.shape[1], TILE):
-        lanes = slice(start, start + TILE)
+    for lanes in spans(x_ref.shape[1], 1536):
         s_high, s_low = split2(state_ref[0, :, lanes])
-        reached = mm(c2, jnp.concatenate([s_high, s_low], 0)) * expand(growth, spread_ref[:, lanes])
-        for pair in range(2):
-            at = start + pair * 128
+        reached = mm(c2, jnp.concatenate([s_high, s_low], 0)) * expand_rows([growth], spread_ref[:, lanes])
+        for at in range(lanes.start, lanes.stop, 128):
             x_pair = x_ref[:, at : at + 128]
             x0, x1 = jnp.where(first, x_pair, zero), jnp.where(first, zero, x_pair)
             pieces = []
@@ -392,10 +424,10 @@
                 h = at // HEAD + half
                 spread_h = cum[:, h : h + 1] - cum_t[h : h + 1, :]
                 decay = jnp.exp(jnp.where(causal, spread_h, -1e30))
-                mixing = affinity * decay * step_t[h : h + 1, :]
-                pieces += split2(mixing)
+                pieces += split2(affinity * decay * step_t[h : h + 1, :])
             intra = mm(jnp.concatenate(pieces, 1), jnp.concatenate([x0, x0, x1, x1], 0))
-            y_ref[:, at : at + 128] = intra + reached[:, pair * 128 : pair * 128 + 128]
+            inside = at - lanes.start
+            y_ref[:, at : at + 128] = intra + reached[:, inside : inside + 128]
 
 
 def forward_all_kernel(
@@ -710,17 +742,15 @@
 
 def grad_state_block(dy_tiles, c_ref, cum_ref, spread_ref, after_ref, held):
     after_ref[0] = held[...]
-    cum = cum_ref[...]
-    growth = jnp.exp(cum)
-    fall = jnp.broadcast_to(growth[Q - 1 : Q, :], (8, 128))
+    growth = jnp.exp(cum_ref[...])
     c_t = transpose_bf(c_ref[...])
     c_t2 = jnp.concatenate([c_t, c_t], 1)
+    wide = expand_rows([growth], spread_ref[...])
     for tile in range(held.shape[1] // TILE):
         lanes = slice(tile * TILE, tile * TILE + TILE)
-        spread = spread_ref[:, lanes]
-        high, low = split2(dy_tiles[tile] * expand(growth, spread))
+        high, low = split2(dy_tiles[tile] * wide[:, lanes])
         direct = mm(c_t2, jnp.concatenate([high, low], 0))
-        held[:, lanes] = held[:, lanes] * expand(fall, spread)[0:1, :] + direct
+        held[:, lanes] = held[:, lanes] * wide[Q - 1 : Q, lanes] + direct
 
 
 def near_block(
@@ -735,23 +765,21 @@
     cum_t = cum.T
     step = step_ref[...]
     growth = jnp.exp(cum)
-    early_fall = jnp.broadcast_to(jnp.exp(offs_ref[pl.ds(at_block, 1), :]), (8, 128))
+    early_fall = eight(jnp.exp(offs_ref[pl.ds(at_block, 1), :]))
     zero = jnp.zeros((Q, 128), BF)
     grad_affinity_t = jnp.zeros((Q, Q), F32)
     grad_c = jnp.zeros((Q, N), F32)
-    for start in range(0, x_ref.shape[1], TILE):
-        lanes = slice(start, start + TILE)
-        spread = spread_ref[:, lanes]
-        before = state_ref[0, :, lanes] + expand(early_fall, spread)[0:1, :] * early_ref[:, lanes]
-        dy_quad = dy_ref[:, lanes]
+    for lanes in spans(x_ref.shape[1], 768):
+        wide = expand_rows([growth, early_fall], spread_ref[:, lanes])
+        before = state_ref[0, :, lanes] + wide[Q : Q + 1, :] * early_ref[:, lanes]
+        dy_wide = dy_ref[:, lanes]
         s_high, s_low = split2(before)
-        g_high, g_low = split2(dy_quad * expand(growth, spread))
+        g_high, g_low = split2(dy_wide * wide[:Q])
         grad_c = grad_c + mm_nt(
             jnp.concatenate([g_high, g_low, g_high], 1), jnp.concatenate([s_high, s_high, s_low], 1)
         )
-        for pair in range(2):
-            at = start + pair * 128
-            d_high, d_low = split2(dy_quad[:, pair * 128 : pair * 128 + 128])
+        for at in range(lanes.start, lanes.stop, 128):
+            d_high, d_low = split2(dy_ref[:, at : at + 128])
             x_pair = x_ref[:, at : at + 128]
             x0, x1 = jnp.where(first, x_pair, zero), jnp.where(first, zero, x_pair)
             grad_mixing = mm_nt(
@@ -789,39 +817,31 @@
     b2 = jnp.concatenate([b_blk, b_blk], 1)
     cum, step = cum_ref[...], step_ref[...]
     tail = jnp.exp(cum[Q - 1 : Q, :] - cum)
-    tail_step = tail * step
     offs_after = offs_ref[pl.ds(at_block + 1, 1), :]
-    offs_end = offs_ref[pl.ds(blocks, 1), :]
-    late_fall = jnp.broadcast_to(jnp.exp(offs_end - offs_after), (8, 128))
-    early_fall = jnp.broadcast_to(jnp.exp(offs_after), (8, 128))
-    row_dots = jnp.zeros((Q, 128), F32)
-    col_dots = jnp.zeros((Q, 128), F32)
-    last_add = jnp.zeros((8, 128), F32)
+    late_fall = eight(jnp.exp(offs_ref[pl.ds(blocks, 1), :] - offs_after))
+    early_fall = eight(jnp.exp(offs_after))
+    dots = jnp.zeros((2 * Q + 8, 128), F32)
     grad_b = gbc_ref[here_rows, 0:N]
-    for start in range(0, x_ref.shape[1], TILE):
-        lanes = slice(start, start + TILE)
-        spread = spread_ref[:, lanes]
-        gather = gather_ref[lanes, :]
-        gather2 = jnp.concatenate([gather, gather], 0)
-        x_quad = x_ref[:, lanes].astype(F32)
-        dy_quad = dy_ref[:, lanes]
+    for lanes in spans(x_ref.shape[1], 512):
+        wide = expand_rows([tail, step, late_fall, early_fall], spread_ref[:, lanes])
+        tail_wide, step_wide = wide[:Q], wide[Q : 2 * Q]
+        x = x_ref[:, lanes].astype(F32)
+        dy = dy_ref[:, lanes]
         skip = skip_ref[0:1, lanes]
-        d_state = after_ref[0, :, lanes] + expand(late_fall, spread)[0:1, :] * late_ref[:, lanes]
-        state = state_ref[0, :, lanes] + expand(early_fall, spread)[0:1, :] * early_ref[:, lanes]
-        touch = jnp.broadcast_to(jnp.sum(d_state * state, axis=0, keepdims=True), (8, TILE))
-        t_high, t_low = split2(touch)
-        last_add = last_add + mm(jnp.concatenate([t_high, t_low], 1), gather2)
+        d_state = after_ref[0, :, lanes] + wide[2 * Q : 2 * Q + 1, :] * late_ref[:, lanes]
+        state = state_ref[0, :, lanes] + wide[2 * Q + 8 : 2 * Q + 9, :] * early_ref[:, lanes]
+        touch = eight(jnp.sum(d_state * state, axis=0, keepdims=True))
         s_high, s_low = split2(d_state)
-        gx = gx_ref[here_rows, lanes] + expand(tail, spread) * mm(b2, jnp.concatenate([s_high, s_low], 0))
-        w_high, w_low = split2(expand(tail_step, spread) * x_quad)
+        gx = gx_ref[here_rows, lanes] + tail_wide * mm(b2, jnp.concatenate([s_high, s_low], 0))
+        w_high, w_low = split2(tail_wide * step_wide * x)
         grad_b = grad_b + mm_nt(
             jnp.concatenate([w_high, w_low, w_high], 1), jnp.concatenate([s_high, s_high, s_low], 1)
         )
-        p_high, p_low = split2(dy_quad * (y_ref[:, lanes] - skip * x_quad))
-        row_dots = row_dots + mm(jnp.concatenate([p_high, p_low], 1), gather2)
-        r_high, r_low = split2(x_quad * gx)
-        col_dots = col_dots + mm(jnp.concatenate([r_high, r_low], 1), gather2)
-        ga_ref[:, lanes] = expand(step, spread) * gx + skip * dy_quad
+        ga_ref[:, lanes] = step_wide * gx + skip * dy
+        high, low = split2(jnp.concatenate([dy * (y_ref[:, lanes] - skip * x), x * gx, touch], 0))
+        gather = gather_ref[lanes, :]
+        dots = dots + mm(jnp.concatenate([high, low], 1), jnp.concatenate([gather, gather], 0))
+    row_dots, col_dots, last_add = dots[:Q], dots[Q : 2 * Q], dots[2 * Q :]
     last_row = iota2((Q, 128), 0) == Q - 1
     grad_cum = row_dots - step * col_dots + jnp.where(last_row, last_add[0:1, :], 0.0)
     upper = (iota2((Q, Q), 1) >= iota2((Q, Q), 0)).astype(F32)
@@ -999,7 +1019,7 @@
         for move in part_moves():
             move.start()
 
-    @pl.when(step_at == near_at + blocks // 2)
+    @pl.when(step_at == near_at + blocks - 1)
     def _():
         for move in o_moves():
             move.wait_recv()
@@ -1295,122 +1315,188 @@
     taps = taps_ref[...]
     g_pad[0:HALO, :] = jnp.zeros((HALO, width), F32)
     g_pad[HALO + tokens :, :] = jnp.zeros((HALO, width), F32)
-    sums = [jnp.zeros((1, width), F32)] * 5
-    for row in range(0, tokens, Q):
-        pre = conv_rows(raw_ref, taps, row, Q)
+    sums = [jnp.zeros((8, width), F32)] * 5
+    by_eight = lambda values: jnp.sum(values.reshape(ROWS // 8, 8, width), axis=0)
+    for row in range(0, tokens, ROWS):
+        moved = conv_window(raw_ref, row, ROWS)
+        pre = conv_rows(moved, taps)
         sig = sigmoid(pre)
-        g = ga_ref[row : row + Q, :] * (sig * (1.0 + pre * (1.0 - sig)))
-        g_pad[HALO + row : HALO + row + Q, :] = g
+        g = ga_ref[row : row + ROWS, :] * (sig * (1.0 + pre * (1.0 - sig)))
+        g_pad[HALO + row : HALO + row + ROWS, :] = g
         for k in range(4):
-            moved = raw_ref[pl.ds(HALO - 3 + k + row, Q), :]
-            sums[k] = sums[k] + jnp.sum(g * moved, axis=0, keepdims=True)
-        sums[4] = sums[4] + jnp.sum(g, axis=0, keepdims=True)
-    for row in list(range(HALO, HALO + tokens, Q)) + [0]:
-        size = HALO if row == 0 else Q
-        total = jnp.zeros((size, width), F32)
-        for k in range(4):
-            total = total + taps[k : k + 1, :] * g_pad[pl.ds(row + 3 - k, size), :]
+            sums[k] = sums[k] + by_eight(g * moved[k])
+        sums[4] = sums[4] + by_eight(g)
+    for row in list(range(HALO, HALO + tokens, ROWS)) + [0]:
+        size = HALO if row == 0 else ROWS
+        window = g_pad[row : row + size + 8, :]
+        total = taps[3:4, :] * window[:size, :]
+        for k in range(3):
+            total = total + taps[k : k + 1, :] * pltpu.roll(window, size + 5 + k, 0)[:size, :]
         gv_ref[row : row + size, :] = total.astype(BF)
-    sums_ref[...] = jnp.zeros_like(sums_ref)
     for k in range(5):
-        sums_ref[k : k + 1, :] = sums[k]
-
-
-def input_grad_tile(
-    gv_ref, gg_ref, gs_ref, gt_ref, v_ref, g_ref, s_ref, t_ref, tok_ref, inv_ref, out_ref, low_ref, sums_ref
-):
-    rows = gv_ref.shape[0]
-    total = mm_nt(gv_ref[...], v_ref[...]) + mm_nt(gs_ref[...], s_ref[...])
-    inner = mm_nt(gg_ref[...], g_ref[...]) + mm_nt(gt_ref[...], t_ref[...])
-    out_ref[0:HALO, :] = total[0:HALO, :]
-    out_ref[HALO:, :] = total[HALO:, :] + inner
-    sums = jnp.zeros((1, TILE), F32)
-    for at in [0] + list(range(HALO, rows, Q)):
-        size = HALO if at == 0 else Q
-        part = out_ref[at : at + size, :]
-        low_ref[at : at + size, :] = part.astype(BF)
-        unit = tok_ref[at : at + size, :].astype(F32) * inv_ref[at : at + size, 0:1]
-        sums = sums + jnp.sum(part * unit, axis=0, keepdims=True)
-    sums_ref[...] = jnp.broadcast_to(sums, (8, TILE))
+        sums_ref[k : k + 1, :] = jnp.sum(sums[k], axis=0, keepdims=True)
+
+
+SMALL_ROWS = 16
 
 
 def finish_kernel(
-    cols, dps, part, whole_state,
-    ga_ref, raw_ref, taps_ref, gg_ref, gt_ref, v_ref, g_ref, picked_ref, tok_ref, inv_ref, g_own_ref,
-    o_total, g_cross, gbc, normed, gt_hbm,
-    sums_ref, gn_ref, low_ref, norm_ref, joint_ref, o_out, g_out,
-    gv_vm, gv_sib, gs_vm, gs_sib, gt_sib, bc_own, bc_land, g_pad,
-    raw_part, taps_part, sums_part, g_pad_part, n_own, n_sib, o_vm, g_vm, g_land, sems, local,
+    cols, dps, heads, part, whole_state,
+    ga_ref, raw_ref, taps_ref, gg_ref, gt_ref, v_ref, g_ref, pick_v_ref, tok_ref, inv_ref, g_own_ref,
+    mix_ref, headsum_ref, gain_ref, o_total, g_cross, gbc, normed, gt_hbm, tok, cot,
+    tg_out, o_out, g_out, v_out, ext_out, sm_out,
+    gv_vm, gv_sib, gs_vm, gs_sib, gt_sib, bc_own, bc_land, g_pad, raw_part, taps_part, g_pad_part,
+    n_own, n_sib, o_vm, g_vm, g_land, gn_tile, gn_own, gn_parts, gn_land, gn_halo, halo_land,
+    joint_low, rec, tot, z_send, z_land, step_land, state_land, ext, small, small_land, tok_vm, cot_vm, sems, local,
 ):
     step = pl.program_id(0)
-    conv_steps = gv_vm.shape[1] // TILE
-    input_steps = 2 * n_own.shape[1] // TILE
+    channels, half = gv_vm.shape[1], n_own.shape[1]
+    shard, piece, span = channels // 2, tot.shape[0], gs_vm.shape[1]
+    count, width = gn_own.shape
+    tokens = bc_own.shape[0]
+    tiles, weight_steps, input_steps = channels // TILE, half // WEIGHT_TILE, width // TILE
+    weight_at = tiles + 1
+    input_at = weight_at + weight_steps
+    last = input_at + input_steps
     dp, row, col = here()
     group = cols // 2
     place = lax.rem(col, group)
-    sibling = (dp, 1 - row, col)
-    peers = [(dp, row, col ^ by) for by in range(1, group)]
-    half = n_own.shape[1]
-    piece = o_total.shape[0]
-    span = gs_vm.shape[1]
+    sibling, mirror = (dp, 1 - row, col), mirror_of(cols)
+    col_peer = lambda by: (dp, row, col ^ by)
+    peers = [col_peer(by) for by in range(1, group)]
     others = dps - 1
-    out_rows = pl.ds(dp * piece, piece)
-    g_rows = pl.ds(dp * g_vm.shape[0], g_vm.shape[0])
+    o_rows = pl.ds(dp * piece_of(o_vm), piece_of(o_vm))
+    g_rows = pl.ds(dp * piece, piece)
+    cols_a, cols_b = pl.ds(shard, tot.shape[1] - shard), pl.ds(0, shard)
+    used = [0]
+
+    def take(size):
+        used[0] += size
+        return used[0] - size
 
     def part_at(at):
         return pl.ds(0, span) if whole_state else lanes_at(at, span)
 
-    def o_moves():
-        return dp_copies(dps, sems, lambda to, i: o_total, lambda to, i: o_out.at[out_rows, :])
-
-    def g_moves():
-        return dp_copies(dps, sems, lambda to, i: g_vm, lambda to, i: g_out.at[g_rows, :], others)
-
-    first = 2 * others
-    g_move = lambda: copy_to(g_cross, g_land, sems, first, mirror_of(cols))
-    n_move = lambda: copy_to(normed.at[:, lanes_at(1 - row, half)], n_sib, sems, first + 1, sibling)
-    t_move = lambda: copy_to(gt_hbm, gt_sib, sems, first + 2, sibling)
-    s_move = lambda: copy_to(gs_vm, gs_sib, sems, first + 3, sibling)
-
-    def bc_moves():
-        return [
-            copy_to(gbc.at[:, part_at(place ^ by)], bc_land.at[by - 1], sems, first + 3 + by, peers[by - 1])
-            for by in range(1, group)
+    def to_dp(src_of, dst_of):
+        first = take(others)
+        return lambda: dp_copies(dps, sems, src_of, dst_of, first)
+
+    def to_all_dp(src, out):
+        first = take(max(others, 4))
+        return (lambda: hand_out(dps, sems, first, src, out)[0]), (lambda: hand_out(dps, sems, first, src, out)[1])
+
+    def one(src, dst, device):
+        at = take(1)
+        return lambda: [copy_to(src, dst, sems, at, device)]
+
+    def to_peers(src_of, dst_of):
+        first = take(group - 1)
+        return lambda: [
+            copy_to(src_of(by), dst_of(by), sems, first + by - 1, col_peer(by)) for by in range(1, group)
         ]
 
-    def v_move(tile):
+    def to_cols(src, dst):
+        first = take(cols - 1)
+        return lambda: [copy_to(src, dst, sems, first + by - 1, col_peer(by)) for by in range(1, cols)]
+
+    o_moves, o_passed = to_all_dp(o_total, o_out)
+    g_moves, g_passed = to_all_dp(g_vm, g_out)
+    a_moves = to_dp(lambda to, i: joint_low.at[to, :, cols_a], lambda to, i: rec.at[i, :, cols_a])
+    b_moves = to_dp(lambda to, i: joint_low.at[to, :, cols_b], lambda to, i: rec.at[i, :, cols_b])
+    v_moves, v_passed = to_all_dp(tot.at[:, cols_b], v_out)
+    e_moves, e_passed = to_all_dp(ext, ext_out)
+    g_move = one(g_cross, g_land, mirror)
+    n_move = one(normed.at[:, lanes_at(1 - row, half)], n_sib, sibling)
+    t_move = one(gt_hbm, gt_sib, sibling)
+    s_move = one(gs_vm, gs_sib, sibling)
+    z_move = one(z_send, z_land, mirror)
+    step_move = one(tot.at[:, pl.ds(channels + span, 128)], step_land, mirror)
+    state_moves = to_cols(tot.at[:, pl.ds(channels, span)], state_land.at[col])
+    bc_moves = to_peers(lambda by: gbc.at[:, part_at(place ^ by)], lambda by: bc_land.at[by - 1])
+    early_rows, late_rows = pl.ds(0, count // 2), pl.ds(count // 2, count - count // 2)
+    gn_early = to_peers(lambda by: gn_parts.at[by - 1, early_rows, :], lambda by: gn_land.at[by - 1, early_rows, :])
+    gn_late = to_peers(lambda by: gn_parts.at[by - 1, late_rows, :], lambda by: gn_land.at[by - 1, late_rows, :])
+    gn_moves = lambda: gn_early() + gn_late()
+    tile_first = take(tiles)
+
+    def v_tile(tile):
         lanes = lanes_at(tile, TILE)
-        return copy_to(gv_vm.at[:, lanes], gv_sib.at[:, lanes], sems, first + 3 + group + tile, sibling)
+        return copy_to(gv_vm.at[:, lanes], gv_sib.at[:, lanes], sems, tile_first + tile, sibling)
+
+    halo_first = take(group)
+    halos = lambda: [
+        copy_to(gn_halo, halo_land.at[j], sems, halo_first + j, (dp, row, group - 1)) for j in range(group)
+    ]
+    small_steps = [sibling]
+    by = 1
+    while by < dps:
+        small_steps.append((dp ^ by, row, col))
+        by *= 2
+    small_first = take(len(small_steps))
+    small_move = lambda i: copy_to(small, small_land.at[i], sems, small_first + i, small_steps[i])
+    small_cols = to_cols(small, sm_out.at[col])
+
+    def small_next(i):
+        move = small_move(i)
+        move.wait()
+        small[...] += small_land[i]
+        if i + 1 < len(small_steps):
+            small_move(i + 1).start()
+
+    def start(moves):
+        for move in moves:
+            move.start()
+
+    def arrive(moves):
+        for move in moves:
+            move.wait_recv()
+
+    def sent(moves):
+        for move in moves:
+            move.wait_send()
 
     load_bc = pltpu.make_async_copy(gbc.at[:, part_at(place)], bc_own, local.at[0])
     load_n = pltpu.make_async_copy(normed.at[:, lanes_at(row, half)], n_own, local.at[1])
     load_o = pltpu.make_async_copy(o_total, o_vm, local.at[2])
-    store_o = pltpu.make_async_copy(o_vm, o_out.at[out_rows, :], local.at[3])
-    store_g = pltpu.make_async_copy(g_vm, g_out.at[g_rows, :], local.at[4])
+    load_tok = pltpu.make_async_copy(tok, tok_vm, local.at[3])
+    load_cot = pltpu.make_async_copy(cot, cot_vm, local.at[4])
+    store_o = pltpu.make_async_copy(o_vm, o_out.at[o_rows, :], local.at[2])
+    store_g = pltpu.make_async_copy(g_vm, g_out.at[g_rows, :], local.at[0])
+    store_v = pltpu.make_async_copy(tot.at[:, cols_b], v_out.at[g_rows, :], local.at[1])
+    store_e = pltpu.make_async_copy(ext, ext_out.at[g_rows, :], local.at[5])
+    store_tg = pltpu.make_async_copy(gn_own, tg_out, local.at[3])
+    store_small = pltpu.make_async_copy(small, sm_out.at[col], local.at[6])
 
     @at_step(0)
     def _():
         load_o.start()
         load_bc.start()
         load_n.start()
-        greet([sibling, mirror_of(cols)] + peers + dp_peers(dps))
-        for move in bc_moves() + [g_move()] + o_moves() + [t_move(), n_move()]:
-            move.start()
+        load_tok.start()
+        load_cot.start()
+        greet([sibling] + [col_peer(by) for by in range(1, cols)] + dp_peers(dps))
+        start(bc_moves() + o_moves() + t_move() + n_move() + g_move())
+        small[...] = jnp.zeros_like(small)
+        small[5:7, 0:channels] = mix_ref[0:2, :]
+        small[7:9, 0:128] = headsum_ref[0:2, :]
         load_o.wait()
         store_o.start()
 
-    @pl.when(step < conv_steps)
-    def _():
-        conv_back_tile(
-            ga_ref, raw_ref, taps_ref, gv_vm.at[:, lanes_at(step, TILE)], sums_ref, g_pad
-        )
-        v_move(step).start()
-
-    @pl.when(step == conv_steps)
+    @pl.when(step < tiles)
+    def _():
+        lanes = lanes_at(step, TILE)
+        conv_back_tile(ga_ref, raw_ref, taps_ref, gv_vm.at[:, lanes], small.at[0:5, lanes], g_pad)
+        v_tile(step).start()
+
+    @pl.when(step == tiles - 1)
+    def _():
+        arrive(o_moves())
+        start(o_passed())
+
+    @pl.when(step == tiles)
     def _():
         load_bc.wait()
-        for move in bc_moves():
-            move.wait_recv()
+        arrive(bc_moves())
         for i in range(group - 1):
             bc_own[...] += bc_land[i]
         if whole_state:
@@ -1418,345 +1504,223 @@
             mine = (lane >= place * part) & (lane < place * part + part)
             bc_own[...] = jnp.where(mine, bc_own[...], 0.0)
         lanes = part_at(place)
-        sums_ref[...] = jnp.zeros_like(sums_ref)
         raw_part[...] = raw_ref[:, lanes]
         taps_part[...] = taps_ref[:, lanes]
-        conv_back_tile(bc_own, raw_part, taps_part, gs_vm, sums_part, g_pad_part)
-        sums_ref[:, 0:span] = sums_part[...]
-        s_move().start()
-        g_move().wait_recv()
+        conv_back_tile(bc_own, raw_part, taps_part, gs_vm, small.at[10:15, 0:span], g_pad_part)
+        start(s_move())
+        arrive(g_move())
         g_vm[...] = g_own_ref[...] + g_land[...].astype(F32)
-        for move in g_moves():
-            move.start()
+        start(g_moves())
         store_g.start()
 
-    @pl.when((step > conv_steps) & (step <= conv_steps + input_steps))
-    def _():
-        input_grad_tile(
-            gv_vm, gg_ref, gs_vm, gt_ref, v_ref, g_ref, picked_ref.at[:, part_at(place)],
-            picked_ref.at[:, pl.ds(TILE, 128)], tok_ref, inv_ref, gn_ref, low_ref, norm_ref,
+    @pl.when(step == weight_at)
+    def _():
+        load_n.wait()
+        arrive(n_move() + t_move() + s_move() + [v_tile(tile) for tile in range(tiles)])
+
+    @pl.when((step >= weight_at) & (step < input_at))
+    def _():
+        at = step - weight_at
+        lanes = lanes_at(at, WEIGHT_TILE)
+        left, left_sib = n_own[:, lanes], n_sib[:, lanes]
+        per = WEIGHT_TILE // piece
+
+        def keep(first, size, total):
+            for p in range(per):
+                rows = total[p * piece : p * piece + piece, :]
+                joint_low[at * per + p, :, first : first + size] = rows.astype(BF)
+
+                @pl.when(dp == at * per + p)
+                def _():
+                    tot[:, first : first + size] = rows
+
+        keep(0, channels, mm_tn(left, gv_vm[...]) + mm_tn(left_sib, gv_sib[...]))
+        keep(channels, span, mm_tn(left, gs_vm[...]) + mm_tn(left_sib, gs_sib[...]))
+        keep(
+            channels + span, 128,
+            mm_tn(left[HALO:, :], gt_ref[...]) + mm_tn(left_sib[HALO:, :], gt_sib[...]),
         )
 
-    @pl.when(step == conv_steps + input_steps + 1)
-    def _():
-        load_n.wait()
-        for move in [n_move(), t_move(), s_move()]:
-            move.wait_recv()
-        for tile in range(conv_steps):
-            v_move(tile).wait_recv()
-
-    @pl.when(step > conv_steps + input_steps)
-    def _():
-        lanes = lanes_at(step - conv_steps - input_steps - 1, TILE)
-        channels = gv_vm.shape[1]
-        left, left_sib = n_own[:, lanes], n_sib[:, lanes]
-        joint_ref[:, 0:channels] = mm_tn(left, gv_vm[...]) + mm_tn(left_sib, gv_sib[...])
-        joint_ref[:, channels : channels + span] = mm_tn(left, gs_vm[...]) + mm_tn(left_sib, gs_sib[...])
-        joint_ref[:, channels + span :] = mm_tn(left[HALO:, :], gt_ref[...]) + mm_tn(left_sib[HALO:, :], gt_sib[...])
-
-    @at_step(pl.num_programs(0) - 1)
-    def _():
+    @pl.when(step == input_at)
+    def _():
+        start(a_moves())
+        arrive(g_moves())
+        start(g_passed())
+
+    @pl.when((step >= input_at) & (step < last))
+    def _():
+        at = step - input_at
+        lanes = lanes_at(at, TILE)
+        gn_tile[...] = mm_nt(gv_vm[...], v_ref[...]) + mm_nt(gs_vm[...], pick_v_ref[:, part_at(place)])
+        gn_tile[HALO:, :] += mm_nt(gg_ref[...], g_ref[...]) + mm_nt(gt_ref[...], pick_v_ref[:, TILE:])
+        rows = lambda index: pl.ds(pl.multiple_of(HALO + index * count, HALO), count)
+        gn_own[:, lanes] = gn_tile[rows(place), :]
+        for by in range(1, group):
+            gn_parts[by - 1, :, lanes] = gn_tile[rows(place ^ by), :].astype(BF)
+        gn_halo[:, lanes] = gn_tile[0:HALO, :].astype(BF)
+        sums = jnp.zeros((1, TILE), F32)
+        for first in [0] + list(range(HALO, HALO + tokens, Q)):
+            size = HALO if first == 0 else Q
+            unit = tok_ref[first : first + size, :].astype(F32) * inv_ref[first : first + size, 0:1]
+            sums = sums + jnp.sum(gn_tile[first : first + size, :] * unit, axis=0, keepdims=True)
+        small[9:10, lanes] = sums
+
+    @pl.when(step == last)
+    def _():
+        start(gn_early())
+        for j in range(group):
+            pl.when(col == group + j)(halos()[j].start)
+        small_move(0).start()
+        arrive(a_moves())
+        start(b_moves())
+        for i in range(others):
+            tot[:, cols_a] += rec[i, :, cols_a].astype(F32)
+        z_send[...] = tot[:, shard:channels].astype(BF)
+        start(z_move() + step_move() + state_moves())
+        state_land[col] = tot[:, channels : channels + span]
+        small_next(0)
+        arrive(b_moves())
+        for i in range(others):
+            tot[:, cols_b] += rec[i, :, cols_b].astype(F32)
+        arrive(z_move() + step_move())
+        start(gn_late())
+        tot[:, cols_b] += z_land[...].astype(F32)
+        start(v_moves())
+        store_v.start()
+        ext[:, 0:128] = tot[:, channels + span :] + pltpu.roll(step_land[...], 128 - heads, 1)
+        arrive(state_moves())
+        if whole_state:
+            ext[:, 128:] = sum(state_land[i] for i in range(cols))
+        else:
+            ext[:, 128:] = state_land[col // 2] + state_land[col // 2 + group]
+        start(e_moves())
+        store_e.start()
+        for i in range(1, len(small_steps)):
+            small_next(i)
+        start(small_cols())
+        store_small.start()
+        load_tok.wait()
+        load_cot.wait()
+        arrive(gn_moves())
+        for i in range(group - 1):
+            gn_own[...] += gn_land[i].astype(F32)
+
+        @pl.when(col == group - 1)
+        def _():
+            arrive(halos())
+            for j in range(group):
+                gn_own[count - HALO :, :] += halo_land[j].astype(F32)
+
+        for j in range(group):
+            pl.when(col == group + j)(halos()[j].wait_send)
+        for first in range(0, count, ROWS):
+            rows = slice(first, first + ROWS)
+            values = tok_vm[rows, :].astype(F32)
+            inv = lax.rsqrt(jnp.mean(values * values, axis=-1, keepdims=True) + EPSILON)
+            unit = values * inv
+            pulled = gn_own[rows, :] * gain_ref[0:1, :]
+            mean = jnp.mean(pulled * unit, axis=-1, keepdims=True)
+            gn_own[rows, :] = cot_vm[rows, :].astype(F32) + inv * (pulled - unit * mean)
+        store_tg.start()
+        arrive(v_moves())
+        start(v_passed())
+        arrive(e_moves())
+        start(e_passed())
         store_o.wait()
         store_g.wait()
-        for move in o_moves() + g_moves():
-            move.wait()
-        for move in bc_moves() + [g_move(), n_move(), t_move(), s_move()]:
-            move.wait_send()
-        for tile in range(conv_steps):
-            v_move(tile).wait_send()
+        store_small.wait()
+        store_v.wait()
+        store_e.wait()
+        arrive(o_passed() + g_passed() + v_passed() + e_passed() + small_cols())
+        sent(o_passed() + g_passed() + v_passed() + e_passed())
+        sent(bc_moves() + o_moves() + t_move() + n_move() + g_move() + s_move() + a_moves() + b_moves())
+        sent([v_tile(tile) for tile in range(tiles)])
+        sent(gn_moves() + z_move() + step_move() + state_moves() + g_moves() + v_moves() + e_moves() + small_cols())
+        store_tg.wait()
+
+
+def piece_of(ref):
+    return ref.shape[0]
 
 
 def finish(
-    cols, dps, part, ga, raw, taps, gg, gt, w_value, w_gate, picked, tokens_in, inv_rms, g_own, o_total, g_cross,
-    gbc, normed,
+    cols, dps, heads, part, ga, raw, taps, gg, gt, w_value, w_gate, picked, tokens_in, inv_rms, g_own, mix_sums,
+    head_sums, gain, o_total, g_cross, gbc, normed, tokens_own, cotangent,
 ):
     tokens, channels = ga.shape
     rows, width = normed.shape
-    half = width // 2
+    half, shard = width // 2, channels // 2
     whole_state = part % 128 != 0
     span = 2 * N if whole_state else part
     group = cols // 2
-    conv_steps, input_steps, weight_steps = channels // TILE, width // TILE, half // TILE
-    piece = o_total.shape[0]
-    joint_width = channels + span + 128
-
-    def clamp(first, count):
-        return lambda i: jnp.clip(i - first, 0, count - 1)
-
-    conv, input_at = clamp(0, conv_steps), clamp(conv_steps + 1, input_steps)
-    both = clamp(0, conv_steps + 1)
-    weight_at = clamp(conv_steps + 1 + input_steps, weight_steps)
-    lanes = lambda at, count: pl.BlockSpec((count, TILE), lambda i: (0, at(i)))
+    tiles, weight_steps, input_steps = channels // TILE, half // WEIGHT_TILE, width // TILE
+    piece, wide = g_own.shape[0], channels + span + 128
+    count = tokens_own.shape[0]
+    input_at = tiles + 1 + weight_steps
+    small_steps = dps.bit_length()
+
+    def clamp(first, size):
+        return lambda i: jnp.clip(i - first, 0, size - 1)
+
+    conv, both, input_tile = clamp(0, tiles), clamp(0, tiles + 1), clamp(input_at, input_steps)
+    lanes = lambda at, size: pl.BlockSpec((size, TILE), lambda i: (0, at(i)))
     slab = lambda at, size: pl.BlockSpec((TILE, size), lambda i: (at(i), 0))
+    once = lambda values: pl.BlockSpec(
+        values.shape, lambda *_: (0,) * len(values.shape), pipeline_mode=pl.Buffered(1)
+    )
     vmem = pltpu.VMEM
-    copies = 2 * (dps - 1) + 3 + group + conv_steps
+    dma = pltpu.SemaphoreType.DMA
+    more = max(group - 1, 1)
+    copies = 2 * (dps - 1) + 4 * max(dps - 1, 4) + 6 + 2 * (cols - 1) + 3 * (group - 1) + tiles + group + small_steps
     return pl.pallas_call(
-        partial(finish_kernel, cols, dps, part, whole_state),
-        grid=(conv_steps + 1 + input_steps + weight_steps,),
+        partial(finish_kernel, cols, dps, heads, part, whole_state),
+        grid=(input_at + input_steps + 1,),
         in_specs=[
             lanes(conv, tokens),
             lanes(both, rows),
             lanes(both, 8),
-            whole(gg.shape),
-            whole(gt.shape),
-            slab(input_at, channels),
-            slab(input_at, channels),
-            slab(input_at, TILE + 128),
-            lanes(input_at, rows),
-            whole(inv_rms.shape),
-            whole(g_own.shape),
-        ] + [ANY] * 5,
-        out_specs=[
-            lanes(both, 8), lanes(input_at, rows), lanes(input_at, rows), lanes(input_at, 8),
-            slab(weight_at, joint_width), ANY, ANY,
-        ],
+            once(gg),
+            once(gt),
+            slab(input_tile, channels),
+            slab(input_tile, channels),
+            slab(input_tile, TILE + 128),
+            lanes(input_tile, rows),
+            once(inv_rms),
+            once(g_own),
+            once(mix_sums),
+            once(head_sums),
+            once(gain),
+        ] + [ANY] * 7,
+        out_specs=[ANY] * 6,
         out_shape=[
-            sds((8, channels + TILE)), sds((rows, width)), sds((rows, width), BF), sds((8, width)),
-            sds((half, joint_width)), sds((dps * piece, o_total.shape[1])),
-            sds((dps * g_own.shape[0], g_own.shape[1])),
+            sds((count, width)), sds((dps * o_total.shape[0], o_total.shape[1])), sds((half, shard)),
+            sds((half, shard)), sds((half, 128 + span)), sds((cols, SMALL_ROWS, width)),
         ],
         scratch_shapes=[
             vmem((rows, channels), BF), vmem((rows, channels), BF), vmem((rows, span), BF), vmem((rows, span), BF),
-            vmem((tokens, 128), BF), vmem((tokens, span), F32), vmem((max(group - 1, 1), tokens, span), F32),
+            vmem((tokens, 128), BF), vmem((tokens, span), F32), vmem((more, tokens, span), F32),
             vmem((tokens + 2 * HALO, TILE), F32), vmem((rows, span), F32), vmem((8, span), F32),
-            vmem((8, span), F32), vmem((tokens + 2 * HALO, span), F32),
+            vmem((tokens + 2 * HALO, span), F32),
             vmem((rows, half), BF), vmem((rows, half), BF),
             vmem(o_total.shape, F32), vmem(g_own.shape, F32), vmem(g_own.shape, BF),
-            pltpu.SemaphoreType.DMA((2, copies)),
-            pltpu.SemaphoreType.DMA((5,)),
+            vmem((rows, TILE), F32),
+            vmem((count, width), F32), vmem((more, count, width), BF), vmem((more, count, width), BF),
+            vmem((HALO, width), BF), vmem((group, HALO, width), BF),
+            vmem((dps, piece, wide), BF), vmem((dps - 1, piece, wide), BF), vmem((piece, wide), F32),
+            vmem((piece, shard), BF), vmem((piece, shard), BF), vmem((piece, 128), F32),
+            vmem((cols, piece, span), F32), vmem((piece, 128 + span), F32),
+            vmem((SMALL_ROWS, width), F32), vmem((small_steps, SMALL_ROWS, width), F32),
+            vmem((count, width), BF), vmem((count, width), BF),
+            dma((2, copies)),
+            dma((7,)),
         ],
         compiler_params=remote_params(5),
-        cost_estimate=cost(55),
+        cost_estimate=cost(110),
         name="finish",
     )(
-        ga, raw, taps, gg, gt, w_value, w_gate, picked, tokens_in, inv_rms, g_own, o_total, g_cross, gbc, normed, gt,
+        ga, raw, taps, gg, gt, w_value, w_gate, picked, tokens_in, inv_rms, g_own, mix_sums, head_sums, gain,
+        o_total, g_cross, gbc, normed, gt, tokens_own, cotangent,
     )
-
-
-def settle_kernel(
-    cols, dps, heads, span, gn, gnb, joint, flat, tok, cot, gain,
-    tg_out, v_out, ext_out, flat_out,
-    mine_a, mine_b, send_a, rec_a, send_b, rec_b, tot_a, tot_b,
-    z_send, z_land, step_land, state_land, ext, acc, flat_land,
-    gn_own, gn_land, halo_land, tok_vm, cot_vm, gain_vm, local, send, recv,
-):
-    dp, row, col = here()
-    group = cols // 2
-    place = lax.rem(col, group)
-    half, wide_a = mine_a.shape
-    shard = mine_b.shape[1]
-    piece = tot_a.shape[0]
-    count, width = gn_own.shape
-    sibling = (dp, 1 - row, col)
-    mirror = (dp, row, cols - 1 - col)
-    col_peer = lambda by: (dp, row, col ^ by)
-    dp_peer = lambda by: (dp ^ by, row, col)
-    used = [0]
-    started = []
-
-    def remote(src, dst, device):
-        i = used[0]
-        used[0] += 1
-        return pltpu.make_async_remote_copy(
-            src_ref=src, dst_ref=dst, send_sem=send.at[i], recv_sem=recv.at[i],
-            device_id=device, device_id_type=pl.DeviceIdType.MESH,
-        )
-
-    def launch(src, dst, device):
-        copy = remote(src, dst, device)
-        copy.start()
-        started.append(copy)
-        return copy
-
-    def arrive(copies):
-        for copy in copies:
-            copy.wait_recv()
-
-    kept = [0]
-
-    def keep(src, dst):
-        copy = pltpu.make_async_copy(src, dst, local.at[kept[0]])
-        kept[0] += 1
-        copy.start()
-        return copy
-
-    part_a, part_b = pl.ds(shard, wide_a), pl.ds(0, shard)
-    load_a = keep(joint.at[:, part_a], mine_a)
-    load_b = keep(joint.at[:, part_b], mine_b)
-    load_flat = keep(flat, acc)
-    loads = [
-        keep(gn.at[pl.ds(HALO + place * count, count), :], gn_own),
-        keep(tok, tok_vm),
-        keep(cot, cot_vm),
-        keep(gain, gain_vm),
-    ]
-    greet(
-        [sibling]
-        + [col_peer(by) for by in range(1, cols)]
-        + [dp_peer(by) for by in range(1, dps)]
-    )
-    gn_moves = [
-        launch(gnb.at[pl.ds(HALO + (place ^ by) * count, count), :], gn_land.at[by - 1], col_peer(by))
-        for by in range(1, group)
-    ]
-    halo_at = used[0]
-    used[0] += group
-    halos = [
-        pltpu.make_async_remote_copy(
-            src_ref=gnb.at[pl.ds(0, HALO), :], dst_ref=halo_land.at[j], send_sem=send.at[halo_at + j],
-            recv_sem=recv.at[halo_at + j], device_id=(dp, row, group - 1),
-            device_id_type=pl.DeviceIdType.MESH,
-        )
-        for j in range(group)
-    ]
-    for j in range(group):
-        pl.when(col == group + j)(halos[j].start)
-
-    flat_steps = [sibling]
-    by = 1
-    while by < dps:
-        flat_steps.append(dp_peer(by))
-        by *= 2
-    by = 1
-    while by < cols:
-        flat_steps.append(col_peer(by))
-        by *= 2
-    flat_moves = []
-    flat_taken = [0]
-
-    def flat_next():
-        if flat_taken[0] < len(flat_moves):
-            flat_moves[-1].wait_recv()
-            flat_moves[-1].wait_send()
-            acc[...] += flat_land[flat_taken[0]]
-            flat_taken[0] += 1
-        if len(flat_moves) < len(flat_steps):
-            at = len(flat_moves)
-            move = remote(acc, flat_land.at[at], flat_steps[at])
-            move.start()
-            flat_moves.append(move)
-
-    load_flat.wait()
-    flat_next()
-
-    def hand_out(load, mine, total, sends, recs):
-        load.wait()
-        moves = []
-        for by in range(1, dps):
-            rows = pl.ds(pl.multiple_of((dp ^ by) * piece, 16), piece)
-            sends[by - 1] = mine[rows, :].astype(BF)
-            moves.append(launch(sends.at[by - 1], recs.at[by - 1], dp_peer(by)))
-        total[...] = mine[pl.ds(pl.multiple_of(dp * piece, 16), piece), :]
-        return moves
-
-    moves_a = hand_out(load_a, mine_a, tot_a, send_a, rec_a)
-    flat_next()
-    moves_b = hand_out(load_b, mine_b, tot_b, send_b, rec_b)
-    flat_next()
-    arrive(moves_a)
-    for by in range(1, dps):
-        tot_a[...] += rec_a[by - 1].astype(F32)
-    z_send[...] = tot_a[:, 0:shard].astype(BF)
-    z_move = launch(z_send, z_land, mirror)
-    step_move = launch(tot_a.at[:, pl.ds(shard + span, 128)], step_land, mirror)
-    state_block = tot_a.at[:, pl.ds(shard, span)]
-    state_moves = [launch(state_block, state_land.at[col], col_peer(by)) for by in range(1, cols)]
-    state_land[col] = tot_a[:, shard : shard + span]
-    flat_next()
-    arrive(moves_b)
-    for by in range(1, dps):
-        tot_b[...] += rec_b[by - 1].astype(F32)
-    arrive([z_move, step_move])
-    tot_b[...] += z_land[...].astype(F32)
-    ext[:, 0:128] = tot_a[:, shard + span : shard + span + 128] + pltpu.roll(step_land[...], 128 - heads, 1)
-    out_rows = pl.ds(dp * piece, piece)
-    v_moves = [launch(tot_b, v_out.at[out_rows, :], dp_peer(by)) for by in range(1, dps)]
-    v_keep = keep(tot_b, v_out.at[out_rows, :])
-    arrive(state_moves)
-    if span == 2 * N:
-        ext[:, 128:] = sum(state_land[i] for i in range(cols))
-    else:
-        part = col // 2
-        ext[:, 128:] = state_land[part] + state_land[part + group]
-    e_moves = [launch(ext, ext_out.at[out_rows, :], dp_peer(by)) for by in range(1, dps)]
-    e_keep = keep(ext, ext_out.at[out_rows, :])
-    flat_next()
-    for copy in loads:
-        copy.wait()
-    arrive(gn_moves)
-    for by in range(1, group):
-        gn_own[...] += gn_land[by - 1].astype(F32)
-
-    @pl.when(col == group - 1)
-    def _():
-        for copy in halos:
-            copy.wait_recv()
-        for j in range(group):
-            gn_own[count - HALO :, :] += halo_land[j].astype(F32)
-
-    for j in range(group):
-        pl.when(col == group + j)(halos[j].wait_send)
-    flat_next()
-    step = 64
-    for at in range(0, count, step):
-        rows = slice(at, at + step)
-        values = tok_vm[rows, :].astype(F32)
-        inv = lax.rsqrt(jnp.mean(values * values, axis=-1, keepdims=True) + EPSILON)
-        unit = values * inv
-        pulled = gn_own[rows, :] * gain_vm[0:1, :]
-        mean = jnp.mean(pulled * unit, axis=-1, keepdims=True)
-        gn_own[rows, :] = cot_vm[rows, :].astype(F32) + inv * (pulled - unit * mean)
-    tg_keep = keep(gn_own, tg_out)
-    while flat_taken[0] < len(flat_steps):
-        flat_next()
-    flat_keep = keep(acc, flat_out)
-    arrive(v_moves)
-    arrive(e_moves)
-    for copy in [v_keep, e_keep, tg_keep, flat_keep]:
-        copy.wait()
-    for copy in started:
-        copy.wait_send()
-
-
-def settle(cols, dps, heads, span, gn, gnb, joint, flat, tokens, cotangent, gain, shard):
-    half, wide = joint.shape
-    width, wide_a = 2 * half, wide - shard
-    piece = half // dps
-    count = tokens.shape[0]
-    group = cols // 2
-    any_spec = pl.BlockSpec(memory_space=pl.ANY)
-    steps = (dps.bit_length() - 1) + (cols.bit_length() - 1) + 1
-    copies = (group - 1) + group + steps + 4 * (dps - 1) + 2 + (cols - 1)
-    vmem = pltpu.VMEM
-    return pl.pallas_call(
-        partial(settle_kernel, cols, dps, heads, span),
-        in_specs=[any_spec] * 7,
-        out_specs=[any_spec] * 4,
-        out_shape=[
-            sds((count, width)), sds((half, shard)), sds((half, 128 + span)), sds(flat.shape),
-        ],
-        scratch_shapes=[
-            vmem((half, wide_a), F32), vmem((half, shard), F32),
-            vmem((dps - 1, piece, wide_a), BF), vmem((dps - 1, piece, wide_a), BF),
-            vmem((dps - 1, piece, shard), BF), vmem((dps - 1, piece, shard), BF),
-            vmem((piece, wide_a), F32), vmem((piece, shard), F32),
-            vmem((piece, shard), BF), vmem((piece, shard), BF),
-            vmem((piece, 128), F32), vmem((cols, piece, span), F32),
-            vmem((piece, 128 + span), F32),
-            vmem(flat.shape, F32), vmem((steps,) + flat.shape, F32),
-            vmem((count, width), F32), vmem((max(group - 1, 1), count, width), BF),
-            vmem((group, HALO, width), BF),
-            vmem((count, width), BF), vmem((count, width), BF), vmem((1, width), F32),
-            pltpu.SemaphoreType.DMA((11,)),
-            pltpu.SemaphoreType.DMA((copies,)),
-            pltpu.SemaphoreType.DMA((copies,)),
-        ],
-        compiler_params=pltpu.CompilerParams(
-            collective_id=2, has_side_effects=True, vmem_limit_bytes=VMEM_LIMIT
-        ),
-        cost_estimate=cost(90),
-        name="settle",
-    )(gn, gnb, joint, flat, tokens, cotangent, gain)
 
 
 def flips(size, by):
@@ -1887,47 +1851,34 @@
     block_out = (tokens.astype(F32) + branch + jnp.sum(branch_in.astype(F32), axis=0)).astype(BF)
     state_part = state_all // group
 
-    value_sums, grad_normed, grad_normed_low, norm_sums, joint, sum_out, sum_gate = finish(
-        cols, dps, state_part, ga, raw, taps, grad_gate, grad_step, value_full, gate_full, picked, group_tokens,
-        inv_rms, gate_own, out_total, gate_cross, gbc, normed,
-    )
-    whole_state = state_part % 128 != 0
-    span = state_all if whole_state else state_part
-
-    wide = jnp.concatenate([value_sums[:5, :channels], mix_sums[0:1]], axis=0)
-    wide_all = jnp.zeros((6, inner_channels), F32)
-    wide_all = lax.dynamic_update_slice_in_dim(wide_all, wide[:, :shard], col * shard, 1)
-    wide_all = lax.dynamic_update_slice_in_dim(wide_all, wide[:, shard:], (cols - 1 - col) * shard, 1)
-    state_wide = jnp.zeros((5, state_all), F32)
-    state_wide = lax.dynamic_update_slice_in_dim(
-        state_wide, value_sums[:5, channels : channels + span], 0 if whole_state else place * state_part, 1
-    )
-    skip_heads = jnp.sum(mix_sums[1].reshape(2 * heads, HEAD), axis=1)
-    head_parts = jnp.stack([head_sums[0, : 2 * heads] * rate, skip_heads, head_sums[1, : 2 * heads]])
-    head_all = jnp.zeros((3, heads * cols), F32)
-    head_all = lax.dynamic_update_slice_in_dim(head_all, head_parts[:, :heads], col * heads, 1)
-    head_all = lax.dynamic_update_slice_in_dim(head_all, head_parts[:, heads:], (cols - 1 - col) * heads, 1)
-    lengths = [wide_all.size, state_wide.size, head_all.size, width]
-    flat = jnp.concatenate(
-        [wide_all.reshape(-1), state_wide.reshape(-1), head_all.reshape(-1), norm_sums[0]]
-    )
-    flat = jnp.pad(flat, (0, -flat.size % 1024)).reshape(-1, 128)
-    tokens_grad, sum_value, extra, flat = settle(
-        cols, dps, heads, span, grad_normed, grad_normed_low, joint, flat, tokens, cotangent, gain[None], shard
+    tokens_grad, sum_out, sum_gate, sum_value, extra, small_sums = finish(
+        cols, dps, heads, state_part, ga, raw, taps, grad_gate, grad_step, value_full, gate_full, picked,
+        group_tokens, inv_rms, gate_own, mix_sums, head_sums, gain[None], out_total, gate_cross, gbc, normed,
+        tokens, cotangent,
     )
     sum_step = extra[:, :heads]
-    sum_state = lax.dynamic_slice_in_dim(
-        extra, 128 + (col if whole_state else lax.rem(col, cols // group)) * state_width, state_width, axis=1
-    )
-    flat = flat.reshape(-1)
-    ends = [sum(lengths[: i + 1]) for i in range(4)]
-    wide_all = flat[: ends[0]].reshape(6, inner_channels)
-    state_wide = flat[ends[0] : ends[1]].reshape(5, state_all)
-    head_all = flat[ends[1] : ends[2]].reshape(3, heads * cols)
-    norm_total = flat[ends[2] : ends[3]]
-    wide_own = lax.dynamic_slice_in_dim(wide_all, col * shard, shard, axis=1)
-    state_own = lax.dynamic_slice_in_dim(state_wide, col * state_width, state_width, axis=1)
-    head_own = lax.dynamic_slice_in_dim(head_all, col * heads, heads, axis=1)
+    whole_state = state_part % 128 != 0
+    first = 128 + (col if whole_state else lax.rem(col, cols // group)) * state_width
+    sum_state = lax.dynamic_slice_in_dim(extra, first, state_width, axis=1)
+    own_sums = lax.dynamic_index_in_dim(small_sums, col, 0, keepdims=False)
+    mirror_sums = lax.dynamic_index_in_dim(small_sums, cols - 1 - col, 0, keepdims=False)
+    wide = own_sums[0:7, :shard] + mirror_sums[0:7, shard:channels]
+    head_own = own_sums[7:9, :heads] + mirror_sums[7:9, heads : 2 * heads]
+    skip_own = jnp.sum(wide[6].reshape(heads, HEAD), axis=1)
+    norm_total = small_sums[0, 9]
+    for i in range(1, cols):
+        norm_total = norm_total + small_sums[i, 9]
+    if whole_state:
+        state_sums = jnp.sum(small_sums[:, 10:15, :state_all], axis=0)
+        state_first = col * state_width
+    else:
+        half_at = col * state_width // state_part
+        state_sums = lax.dynamic_index_in_dim(small_sums, half_at, 0, keepdims=False)[10:15, :state_part]
+        state_sums = state_sums + lax.dynamic_index_in_dim(
+            small_sums, half_at + group, 0, keepdims=False
+        )[10:15, :state_part]
+        state_first = lax.rem(col * state_width, state_part)
+    state_own = lax.dynamic_slice_in_dim(state_sums, state_first, state_width, axis=1)
 
     return (
         block_out,
@@ -1937,14 +1888,14 @@
         sum_value,
         sum_state,
         sum_step,
-        wide_own[:4].T,
-        wide_own[4],
+        wide[:4].T,
+        wide[4],
         state_own[:4].T,
         state_own[4],
-        head_own[0],
+        head_own[0] * rate[:heads],
+        skip_own,
         head_own[1],
-        head_own[2],
-        wide_own[5],
+        wide[5],
         sum_out,
     )
 

time: 461 us -> 407 us (0.88)
  Pallas kernels: 413 us -> 368 us
  local copies, waits for them, and re-layouts: 30.8 us -> 23.5 us
    pallas_call x2 -> x1, Pallas kernels: 146 us -> 120 us  [finish(): pl.pallas_call(partial(finish_kernel, cols, dps, heads, part, whole_state...]
    pallas_call x1, Pallas kernels: 50.2 us -> 34.4 us  [gate_and_mix(): pl.pallas_call(partial(gate_kernel, cols, inner_channels), grid=(2 * tile...]
    slice x9 -> x1, local copies, waits for them, and re-layouts: 6.92 us -> 0.62 us  [per_device(): wide[5]]
where the time goes in v5:
time: 407 us; the launch traced here: 406 us
  Pallas kernels  368 us (90%)
  local copies, waits for them, and re-layouts  23.5 us (6%)
  other arithmetic  13.6 us (3%)
    pallas_call x1, Pallas kernels, finish(): pl.pallas_call(partial(finish_kernel, cols, dps, heads, part, whole_state...  120 us
    pallas_call x1, Pallas kernels, scan_backward(): pl.pallas_call(partial(backward_kernel, cols, dps), grid=(far_at + blocks...  87.9 us
    pallas_call x1, Pallas kernels, forward_all(): pl.pallas_call(partial(forward_all_kernel, cols, dps), grid=(gate_at + 2...  74.6 us
    pallas_call x1, Pallas kernels, import_all(): pl.pallas_call(partial(import_kernel, cols, dps), in_specs=[any_spec] * 4...  51.6 us
    pallas_call x1, Pallas kernels, gate_and_mix(): pl.pallas_call(partial(gate_kernel, cols, inner_channels), grid=(2 * tile...  34.4 us
    unnamed x22, local copies, waits for them, and re-layouts  12.8 us

profile of v5, /device:TPU:0, one launch (start us, length us, event | category | flops | bytes accessed | tf_op | source)
XLA Modules:
  0.0 406.1 jit_solution(4916359644385067854)
XLA Ops:
  0.7 1.1 copy.34
  1.7 0.9 copy.35
  2.6 0.8 fusion.15.sw
  3.5 0.7 fusion.25
  4.2 0.8 fusion.34
  4.9 0.7 broadcast_in_dim.27
  5.6 0.7 broadcast_in_dim.28
  6.3 1.9 concatenate.42.vec
  8.2 51.6 %import_all.1 = (bf16[1040,1536]{1,0:T(8,128)(2,1)}, bf16[1536,1536]{1,0:T(8,128)(2,1)}, bf16[1536,512]{1,0:T(8,128)(2,1)}, bf16[4,16,768]{2,1,0:T(8,128)(2,1)}) custom-call(bf16[512,1536]{1,0:T(8,128)(2,1)} %tok.3, bf16[768,768]{1,0:T(8,128)(2,1)} %wv.1, bf16[768,128]{1,0:T(8,128)(2,1)} %fusion.15.sw, bf16[16,768]{1,0:T(8,128)(2,1)} %concatenate.42.vec), custom_call_target="tpu_custom_call" | custom-call | bytes 135000000 | tf_op jit(solution)/shard_map/import_all/pallas_call | solution.py:279
  59.8 0.9 convert_element_type.24
  60.7 0.1 slice_bitcast_fusion.9
  60.8 0.1 maximum_bitcast_fusion
  60.9 0.1 fusion.41
  61.0 0.6 select_maximum_fusion.1.head_ref
  61.6 0.1 pad_maximum_fusion.1
  61.7 0.1 broadcast_in_dim_reshape.3
  61.8 0.1 pad.24.clone
  61.9 0.7 fusion.18
  62.6 0.1 reshape.68
  62.7 0.6 pad_maximum_fusion.taps_ref
  63.4 1.6 fusion.4.pick_ref
  65.0 0.6 reshape.69.gain_ref
  65.6 74.6 %forward_all.1 = (f32[1040,1792]{1,0:T(8,128)}, bf16[1024,1792]{1,0:T(8,128)(2,1)}, bf16[1040,1536]{1,0:T(8,128)(2,1)}, f32[1024,128]{1,0:T(8,128)}, f32[1024,12...) custom-call(bf16[1040,1536]{1,0:T(8,128)(2,1)} %get-tuple-element.60, ...), custom_call_target="tpu_custom_call" | custom-call | bytes 210000000 | tf_op jit(solution)/shard_map/forward_all/pallas_call | solution.py:672
  140.2 34.4 %gate_and_mix.1 = (f32[1024,1536]{1,0:T(8,128)}, bf16[1024,1536]{1,0:T(8,128)(2,1)}, bf16[1024,1536]{1,0:T(8,128)(2,1)}, f32[1024,1536]{1,0:T(8,128)}, f32[8,153...) custom-call(f32[1024,1536]{1,0:T(8,128)} %get-tuple-element.64.y0_ref, ...), custom_call_target="tpu_custom_call" | custom-call | bytes 120000000 | tf_op jit(solution)/shard_map/gate_and_mix/pallas_call | solution.py:1276
  174.6 87.9 %scan_backward.1 = (f32[1024,1536]{1,0:T(8,128)}, bf16[1024,128]{1,0:T(8,128)(2,1)}, f32[1024,256]{1,0:T(8,128)}, f32[8,128]{1,0:T(8,128)}, f32[192,768]{1,0:T(8...) custom-call(f32[1024,1536]{1,0:T(8,128)} %get-tuple-element.71.dy_re, ...), custom_call_target="tpu_custom_call" | custom-call | bytes 240000000 | tf_op jit(solution)/shard_map/scan_backward/pallas_call | solution.py:1095
  262.5 119.7 %finish.1 = (f32[512,1536]{1,0:T(8,128)}, f32[768,768]{1,0:T(8,128)}, f32[768,768]{1,0:T(8,128)}, f32[768,768]{1,0:T(8,128)}, f32[768,256]{1,0:T(8,128)}, /*index=5*/f32[4,16,1536]{2,1,0:T(8,128)}) custom-call(f32[1024,1536]{1,0:T(8,128)} %get-tuple-element.86.ga_ref, f32[1040,1792]{1,0:T(8,128)} %get-tuple-element.87.raw_ref, ...), custom_call_target="tpu_custom_call" | custom-call | bytes 330000000 | tf_op jit(solution)/shard_map/finish/pallas_call | solution.py:1675
  382.3 1.2 dynamic-slice_bitcast_fusion.1
  383.6 0.1 fusion.42
  383.7 0.5 bitcast_multiply_fusion
  384.2 0.5 slice_bitcast_fusion.7
  384.8 0.6 slice_bitcast_fusion.2
  385.4 0.5 slice_bitcast_fusion.8
  385.9 0.6 slice_reduce_fusion
  386.6 0.6 reduce_sum.19
  387.2 0.6 slice_bitcast_fusion.1
  387.8 1.2 constant_dynamic-slice_fusion.1
  389.0 0.8 copy.37
  389.8 1.0 slice.100
  390.8 0.8 copy.38
  391.6 1.5 add_reduce_fusion
  393.1 3.8 fusion
  396.9 1.7 copy.43
  398.6 1.1 copy-done.4
  399.7 1.4 copy.44
  401.1 1.1 copy-done.3
  402.2 1.4 copy.45
  403.6 1.1 copy-done.2
  404.7 1.4 copy.46
  (30 shorter events, 0.4 us)
Async XLA Ops:
  0.6 64.4 %copy-start.6 = (bf16[1536]{0:T(1024)(128)(2,1)S(1)}, bf16[1536]{0:T(1024)(128)(2,1)}, u32[]{:S(2)}) copy-start(bf16[1536]{0:T(1024)(128)(2,1)} %param.19) | copy-start | bytes 9220
  382.2 10.9 %copy-start = (bf16[512,1536]{1,0:T(8,128)(2,1)S(1)}, bf16[512,1536]{1,0:T(8,128)(2,1)}, u32[]{:S(2)}) copy-start(bf16[512,1536]{1,0:T(8,128)(2,1)} %tok.3) | copy-start | bytes 4718596
  382.2 10.9 %copy-start.5 = (bf16[1,512,1536]{2,1,0:T(8,128)(2,1)S(1)}, bf16[1,512,1536]{2,1,0:T(8,128)(2,1)}, u32[]{:S(2)}) copy-start(bf16[1,512,1536]{2,1,0:T(8,128)(2,1)} %get-tuple-element.85) | copy-start | bytes 4718596
  393.1 3.8 copy-start.1
  396.9 2.8 copy-start.4
  399.7 2.5 copy-start.3
  402.2 2.5 copy-start.2

commit v6 on v5

--- a/solution.py
+++ b/solution.py
@@ -110,13 +110,12 @@
     rows = lambda d: pl.ds(d * piece, piece)
     if dps != 4:
         return dp_copies(dps, sems, lambda to, i: src, lambda to, i: out.at[rows(dp), :], first), []
-    left, right = pl.ds(0, lanes // 2), pl.ds(lanes // 2, lanes // 2)
     near = [
         copy_to(src, out.at[rows(dp), :], sems, first + i, (dp ^ by, row, col)) for i, by in enumerate((1, 2))
     ]
     far = []
-    for i, (by, half) in enumerate(((1, left), (2, right))):
-        passed = out.at[rows(dp ^ by), half]
+    for i, by in enumerate((1, 2)):
+        passed = out.at[pl.ds((dp ^ by) * piece + i * (piece // 2), piece // 2), :]
         far.append(copy_to(passed, passed, sems, first + 2 + i, (dp ^ 3 ^ by, row, col)))
     return near, far
 
@@ -1014,7 +1013,7 @@
             early_ref, offs_ref, gx_ref, gbc_ref,
         )
 
-    @pl.when(step_at == near_at + 2)
+    @pl.when(step_at == g_at)
     def _():
         for move in part_moves():
             move.start()
@@ -1338,6 +1337,7 @@
 
 
 SMALL_ROWS = 16
+A_TAKEN = 4
 
 
 def finish_kernel(
@@ -1347,14 +1347,14 @@
     tg_out, o_out, g_out, v_out, ext_out, sm_out,
     gv_vm, gv_sib, gs_vm, gs_sib, gt_sib, bc_own, bc_land, g_pad, raw_part, taps_part, g_pad_part,
     n_own, n_sib, o_vm, g_vm, g_land, gn_tile, gn_own, gn_parts, gn_land, gn_halo, halo_land,
-    joint_low, rec, tot, z_send, z_land, step_land, state_land, ext, small, small_land, tok_vm, cot_vm, sems, local,
+    joint_low, rec, tot, z_send, z_land, state_send, state_land, ext, small, small_land, tok_vm, cot_vm, sems, local,
 ):
     step = pl.program_id(0)
     channels, half = gv_vm.shape[1], n_own.shape[1]
     shard, piece, span = channels // 2, tot.shape[0], gs_vm.shape[1]
     count, width = gn_own.shape
     tokens = bc_own.shape[0]
-    tiles, weight_steps, input_steps = channels // TILE, half // WEIGHT_TILE, width // TILE
+    tiles, weight_steps, input_steps = channels // TILE, 2, width // TILE
     weight_at = tiles + 1
     input_at = weight_at + weight_steps
     last = input_at + input_steps
@@ -1410,8 +1410,7 @@
     t_move = one(gt_hbm, gt_sib, sibling)
     s_move = one(gs_vm, gs_sib, sibling)
     z_move = one(z_send, z_land, mirror)
-    step_move = one(tot.at[:, pl.ds(channels + span, 128)], step_land, mirror)
-    state_moves = to_cols(tot.at[:, pl.ds(channels, span)], state_land.at[col])
+    state_moves = to_cols(state_send, state_land.at[col])
     bc_moves = to_peers(lambda by: gbc.at[:, part_at(place ^ by)], lambda by: bc_land.at[by - 1])
     early_rows, late_rows = pl.ds(0, count // 2), pl.ds(count // 2, count - count // 2)
     gn_early = to_peers(lambda by: gn_parts.at[by - 1, early_rows, :], lambda by: gn_land.at[by - 1, early_rows, :])
@@ -1518,34 +1517,42 @@
         load_n.wait()
         arrive(n_move() + t_move() + s_move() + [v_tile(tile) for tile in range(tiles)])
 
-    @pl.when((step >= weight_at) & (step < input_at))
-    def _():
-        at = step - weight_at
-        lanes = lanes_at(at, WEIGHT_TILE)
-        left, left_sib = n_own[:, lanes], n_sib[:, lanes]
-        per = WEIGHT_TILE // piece
-
-        def keep(first, size, total):
-            for p in range(per):
-                rows = total[p * piece : p * piece + piece, :]
-                joint_low[at * per + p, :, first : first + size] = rows.astype(BF)
-
-                @pl.when(dp == at * per + p)
-                def _():
-                    tot[:, first : first + size] = rows
-
-        keep(0, channels, mm_tn(left, gv_vm[...]) + mm_tn(left_sib, gv_sib[...]))
-        keep(channels, span, mm_tn(left, gs_vm[...]) + mm_tn(left_sib, gs_sib[...]))
-        keep(
-            channels + span, 128,
-            mm_tn(left[HALO:, :], gt_ref[...]) + mm_tn(left_sib[HALO:, :], gt_sib[...]),
-        )
+    def keep(first, size, total):
+        for p in range(dps):
+            rows = total[p * piece : p * piece + piece, :]
+            joint_low[p, :, first : first + size] = rows.astype(BF)
+
+            @pl.when(dp == p)
+            def _():
+                tot[:, first : first + size] = rows
+
+    @pl.when(step == weight_at)
+    def _():
+        keep(shard, shard, mm_tn(n_own[...], gv_vm[:, shard:]) + mm_tn(n_sib[...], gv_sib[:, shard:]))
+        keep(channels, span, mm_tn(n_own[...], gs_vm[...]) + mm_tn(n_sib[...], gs_sib[...]))
+        keep(channels + span, 128, mm_tn(n_own[HALO:, :], gt_ref[...]) + mm_tn(n_sib[HALO:, :], gt_sib[...]))
+        start(a_moves())
+
+    @pl.when(step == weight_at + 1)
+    def _():
+        keep(0, shard, mm_tn(n_own[...], gv_vm[:, :shard]) + mm_tn(n_sib[...], gv_sib[:, :shard]))
 
     @pl.when(step == input_at)
     def _():
-        start(a_moves())
         arrive(g_moves())
         start(g_passed())
+
+    @pl.when(step == input_at + A_TAKEN)
+    def _():
+        arrive(a_moves())
+        start(b_moves())
+        for i in range(others):
+            tot[:, cols_a] += rec[i, :, cols_a].astype(F32)
+        z_send[:, 0:shard] = tot[:, shard:channels].astype(BF)
+        z_send[:, shard:] = tot[:, channels + span :].astype(BF)
+        state_send[...] = tot[:, channels : channels + span].astype(BF)
+        start(z_move() + state_moves())
+        state_land[col] = state_send[...]
 
     @pl.when((step >= input_at) & (step < last))
     def _():
@@ -1571,34 +1578,34 @@
         for j in range(group):
             pl.when(col == group + j)(halos()[j].start)
         small_move(0).start()
-        arrive(a_moves())
-        start(b_moves())
-        for i in range(others):
-            tot[:, cols_a] += rec[i, :, cols_a].astype(F32)
-        z_send[...] = tot[:, shard:channels].astype(BF)
-        start(z_move() + step_move() + state_moves())
-        state_land[col] = tot[:, channels : channels + span]
         small_next(0)
         arrive(b_moves())
         for i in range(others):
             tot[:, cols_b] += rec[i, :, cols_b].astype(F32)
-        arrive(z_move() + step_move())
+        arrive(z_move())
         start(gn_late())
-        tot[:, cols_b] += z_land[...].astype(F32)
+        tot[:, cols_b] += z_land[:, 0:shard].astype(F32)
         start(v_moves())
         store_v.start()
-        ext[:, 0:128] = tot[:, channels + span :] + pltpu.roll(step_land[...], 128 - heads, 1)
+        steps = tot[:, channels + span :] + pltpu.roll(z_land[:, shard:].astype(F32), 128 - heads, 1)
         arrive(state_moves())
         if whole_state:
-            ext[:, 128:] = sum(state_land[i] for i in range(cols))
+            ext[:, 0:128] = steps
+            ext[:, 128:] = sum(state_land[i].astype(F32) for i in range(cols))
         else:
-            ext[:, 128:] = state_land[col // 2] + state_land[col // 2 + group]
+            states = state_land[col // 2].astype(F32) + state_land[col // 2 + group].astype(F32)
+            moved = jnp.where(lax.rem(col, 2) == 1, states, pltpu.roll(states, 64, 1))
+            ext[...] = jnp.where(iota2(steps.shape, 1) < 64, steps, moved)
         start(e_moves())
         store_e.start()
         for i in range(1, len(small_steps)):
             small_next(i)
         start(small_cols())
         store_small.start()
+        arrive(v_moves())
+        start(v_passed())
+        arrive(e_moves())
+        start(e_passed())
         load_tok.wait()
         load_cot.wait()
         arrive(gn_moves())
@@ -1622,10 +1629,6 @@
             mean = jnp.mean(pulled * unit, axis=-1, keepdims=True)
             gn_own[rows, :] = cot_vm[rows, :].astype(F32) + inv * (pulled - unit * mean)
         store_tg.start()
-        arrive(v_moves())
-        start(v_passed())
-        arrive(e_moves())
-        start(e_passed())
         store_o.wait()
         store_g.wait()
         store_small.wait()
@@ -1635,7 +1638,7 @@
         sent(o_passed() + g_passed() + v_passed() + e_passed())
         sent(bc_moves() + o_moves() + t_move() + n_move() + g_move() + s_move() + a_moves() + b_moves())
         sent([v_tile(tile) for tile in range(tiles)])
-        sent(gn_moves() + z_move() + step_move() + state_moves() + g_moves() + v_moves() + e_moves() + small_cols())
+        sent(gn_moves() + z_move() + state_moves() + g_moves() + v_moves() + e_moves() + small_cols())
         store_tg.wait()
 
 
@@ -1652,8 +1655,9 @@
     half, shard = width // 2, channels // 2
     whole_state = part % 128 != 0
     span = 2 * N if whole_state else part
+    extra = 128 + span if whole_state else 128
     group = cols // 2
-    tiles, weight_steps, input_steps = channels // TILE, half // WEIGHT_TILE, width // TILE
+    tiles, weight_steps, input_steps = channels // TILE, 2, width // TILE
     piece, wide = g_own.shape[0], channels + span + 128
     count = tokens_own.shape[0]
     input_at = tiles + 1 + weight_steps
@@ -1694,7 +1698,7 @@
         out_specs=[ANY] * 6,
         out_shape=[
             sds((count, width)), sds((dps * o_total.shape[0], o_total.shape[1])), sds((half, shard)),
-            sds((half, shard)), sds((half, 128 + span)), sds((cols, SMALL_ROWS, width)),
+            sds((half, shard)), sds((half, extra)), sds((cols, SMALL_ROWS, width)),
         ],
         scratch_shapes=[
             vmem((rows, channels), BF), vmem((rows, channels), BF), vmem((rows, span), BF), vmem((rows, span), BF),
@@ -1707,8 +1711,8 @@
             vmem((count, width), F32), vmem((more, count, width), BF), vmem((more, count, width), BF),
             vmem((HALO, width), BF), vmem((group, HALO, width), BF),
             vmem((dps, piece, wide), BF), vmem((dps - 1, piece, wide), BF), vmem((piece, wide), F32),
-            vmem((piece, shard), BF), vmem((piece, shard), BF), vmem((piece, 128), F32),
-            vmem((cols, piece, span), F32), vmem((piece, 128 + span), F32),
+            vmem((piece, shard + 128), BF), vmem((piece, shard + 128), BF), vmem((piece, span), BF),
+            vmem((cols, piece, span), BF), vmem((piece, extra), F32),
             vmem((SMALL_ROWS, width), F32), vmem((small_steps, SMALL_ROWS, width), F32),
             vmem((count, width), BF), vmem((count, width), BF),
             dma((2, copies)),
@@ -1858,8 +1862,10 @@
     )
     sum_step = extra[:, :heads]
     whole_state = state_part % 128 != 0
-    first = 128 + (col if whole_state else lax.rem(col, cols // group)) * state_width
-    sum_state = lax.dynamic_slice_in_dim(extra, first, state_width, axis=1)
+    if whole_state:
+        sum_state = lax.dynamic_slice_in_dim(extra, 128 + col * state_width, state_width, axis=1)
+    else:
+        sum_state = extra[:, 64:]
     own_sums = lax.dynamic_index_in_dim(small_sums, col, 0, keepdims=False)
     mirror_sums = lax.dynamic_index_in_dim(small_sums, cols - 1 - col, 0, keepdims=False)
     wide = own_sums[0:7, :shard] + mirror_sums[0:7, shard:channels]

time: 407 us -> 411 us (level)
    pallas_call x1, Pallas kernels: 120 us -> 127 us  [finish(): pl.pallas_call(partial(finish_kernel, cols, dps, heads, part, whole_state...]
    pallas_call x1, Pallas kernels: 87.9 us -> 82.3 us  [scan_backward(): pl.pallas_call(partial(backward_kernel, cols, dps), grid=(far_at + blocks...]
where the time goes in v6:
time: 411 us; the launch traced here: 408 us
  Pallas kernels  370 us (90%)
  local copies, waits for them, and re-layouts  23.5 us (6%)
  other arithmetic  13.6 us (3%)
    pallas_call x1, Pallas kernels, finish(): pl.pallas_call(partial(finish_kernel, cols, dps, heads, part, whole_state...  127 us
    pallas_call x1, Pallas kernels, scan_backward(): pl.pallas_call(partial(backward_kernel, cols, dps), grid=(far_at + blocks...  82.3 us
    pallas_call x1, Pallas kernels, forward_all(): pl.pallas_call(partial(forward_all_kernel, cols, dps), grid=(gate_at + 2...  74.6 us
    pallas_call x1, Pallas kernels, import_all(): pl.pallas_call(partial(import_kernel, cols, dps), in_specs=[any_spec] * 4...  51.6 us
    pallas_call x1, Pallas kernels, gate_and_mix(): pl.pallas_call(partial(gate_kernel, cols, inner_channels), grid=(2 * tile...  34.5 us
    unnamed x22, local copies, waits for them, and re-layouts  13.8 us

profile of v6, /device:TPU:0, one launch (start us, length us, event | category | flops | bytes accessed | tf_op | source)
XLA Modules:
  0.0 408.3 jit_solution(15976649927857048129)
XLA Ops:
  0.7 1.1 copy.34
  1.7 0.9 copy.35
  2.6 0.8 fusion.15.sw
  3.5 0.7 fusion.25
  4.2 0.8 fusion.34
  4.9 0.7 broadcast_in_dim.27
  5.6 0.7 broadcast_in_dim.28
  6.3 1.9 concatenate.42.vec
  8.2 51.6 %import_all.1 = (bf16[1040,1536]{1,0:T(8,128)(2,1)}, bf16[1536,1536]{1,0:T(8,128)(2,1)}, bf16[1536,512]{1,0:T(8,128)(2,1)}, bf16[4,16,768]{2,1,0:T(8,128)(2,1)}) custom-call(bf16[512,1536]{1,0:T(8,128)(2,1)} %tok.3, bf16[768,768]{1,0:T(8,128)(2,1)} %wv.1, bf16[768,128]{1,0:T(8,128)(2,1)} %fusion.15.sw, bf16[16,768]{1,0:T(8,128)(2,1)} %concatenate.42.vec), custom_call_target="tpu_custom_call" | custom-call | bytes 135000000 | tf_op jit(solution)/shard_map/import_all/pallas_call | solution.py:278
  59.8 0.9 convert_element_type.24
  60.7 0.1 slice_bitcast_fusion.9
  60.8 0.1 maximum_bitcast_fusion
  60.9 0.1 fusion.41
  61.0 0.6 select_maximum_fusion.1.head_ref
  61.6 0.1 pad_maximum_fusion.1
  61.7 0.1 broadcast_in_dim_reshape.3
  61.8 0.1 pad.24.clone
  61.9 0.7 fusion.18
  62.6 0.1 reshape.68
  62.7 0.6 pad_maximum_fusion.taps_ref
  63.4 1.6 fusion.4.pick_ref
  65.0 0.6 reshape.69.gain_ref
  65.6 74.6 %forward_all.1 = (f32[1040,1792]{1,0:T(8,128)}, bf16[1024,1792]{1,0:T(8,128)(2,1)}, bf16[1040,1536]{1,0:T(8,128)(2,1)}, f32[1024,128]{1,0:T(8,128)}, f32[1024,12...) custom-call(bf16[1040,1536]{1,0:T(8,128)(2,1)} %get-tuple-element.60, ...), custom_call_target="tpu_custom_call" | custom-call | bytes 210000000 | tf_op jit(solution)/shard_map/forward_all/pallas_call | solution.py:671
  140.2 34.5 %gate_and_mix.1 = (f32[1024,1536]{1,0:T(8,128)}, bf16[1024,1536]{1,0:T(8,128)(2,1)}, bf16[1024,1536]{1,0:T(8,128)(2,1)}, f32[1024,1536]{1,0:T(8,128)}, f32[8,153...) custom-call(f32[1024,1536]{1,0:T(8,128)} %get-tuple-element.64.y0_ref, ...), custom_call_target="tpu_custom_call" | custom-call | bytes 120000000 | tf_op jit(solution)/shard_map/gate_and_mix/pallas_call | solution.py:1275
  174.7 82.3 %scan_backward.1 = (f32[1024,1536]{1,0:T(8,128)}, bf16[1024,128]{1,0:T(8,128)(2,1)}, f32[1024,256]{1,0:T(8,128)}, f32[8,128]{1,0:T(8,128)}, f32[192,768]{1,0:T(8...) custom-call(f32[1024,1536]{1,0:T(8,128)} %get-tuple-element.71.dy_re, ...), custom_call_target="tpu_custom_call" | custom-call | bytes 240000000 | tf_op jit(solution)/shard_map/scan_backward/pallas_call | solution.py:1094
  257.0 127.3 %finish.1 = (f32[512,1536]{1,0:T(8,128)}, f32[768,768]{1,0:T(8,128)}, f32[768,768]{1,0:T(8,128)}, f32[768,768]{1,0:T(8,128)}, f32[768,128]{1,0:T(8,128)}, /*index=5*/f32[4,16,1536]{2,1,0:T(8,128)}) custom-call(f32[1024,1536]{1,0:T(8,128)} %get-tuple-element.86.ga_ref, f32[1040,1792]{1,0:T(8,128)} %get-tuple-element.87.raw_ref, ...), custom_call_target="tpu_custom_call" | custom-call | bytes 330000000 | tf_op jit(solution)/shard_map/finish/pallas_call | solution.py:1679
  384.4 1.2 dynamic-slice_bitcast_fusion.1
  385.6 0.1 fusion.42
  385.7 0.5 bitcast_multiply_fusion
  386.2 0.5 slice_bitcast_fusion.7
  386.7 0.1 constant_dynamic-slice_fusion
  386.8 0.6 slice_bitcast_fusion.2
  387.4 0.5 slice_bitcast_fusion.8
  387.9 0.6 slice_reduce_fusion
  388.6 0.6 reduce_sum.19
  389.2 0.6 slice_bitcast_fusion.1
  389.8 1.2 slice.103
  391.0 0.8 copy.37
  391.8 1.8 copy.38
  393.6 1.5 add_reduce_fusion
  395.1 3.8 fusion
  398.9 1.7 copy.43
  400.6 1.1 copy-done.4
  401.7 1.4 copy.44
  403.1 1.1 copy-done.3
  404.2 1.4 copy.45
  405.6 1.1 copy-done.2
  406.8 1.4 copy.46
  (29 shorter events, 0.3 us)
Async XLA Ops:
  0.6 64.4 %copy-start.6 = (bf16[1536]{0:T(1024)(128)(2,1)S(1)}, bf16[1536]{0:T(1024)(128)(2,1)}, u32[]{:S(2)}) copy-start(bf16[1536]{0:T(1024)(128)(2,1)} %param.19) | copy-start | bytes 9220
  257.0 138.1 %copy-start.5 = (bf16[1,512,1536]{2,1,0:T(8,128)(2,1)S(1)}, bf16[1,512,1536]{2,1,0:T(8,128)(2,1)}, u32[]{:S(2)}) copy-start(bf16[1,512,1536]{2,1,0:T(8,128)(2,1)} %get-tuple-element.85) | copy-start | bytes 4718596
  384.3 10.8 %copy-start = (bf16[512,1536]{1,0:T(8,128)(2,1)S(1)}, bf16[512,1536]{1,0:T(8,128)(2,1)}, u32[]{:S(2)}) copy-start(bf16[512,1536]{1,0:T(8,128)(2,1)} %tok.3) | copy-start | bytes 4718596
  395.1 3.8 copy-start.1
  398.9 2.8 copy-start.4
  401.7 2.5 copy-start.3
  404.2 2.5 copy-start.2

commit v7 on v6

--- a/solution.py
+++ b/solution.py
@@ -1018,7 +1018,7 @@
         for move in part_moves():
             move.start()
 
-    @pl.when(step_at == near_at + blocks - 1)
+    @pl.when(step_at == near_at + blocks // 2 + 1)
     def _():
         for move in o_moves():
             move.wait_recv()
@@ -1347,7 +1347,7 @@
     tg_out, o_out, g_out, v_out, ext_out, sm_out,
     gv_vm, gv_sib, gs_vm, gs_sib, gt_sib, bc_own, bc_land, g_pad, raw_part, taps_part, g_pad_part,
     n_own, n_sib, o_vm, g_vm, g_land, gn_tile, gn_own, gn_parts, gn_land, gn_halo, halo_land,
-    joint_low, rec, tot, z_send, z_land, state_send, state_land, ext, small, small_land, tok_vm, cot_vm, sems, local,
+    joint_low, rec, tot, z_send, z_land, state_land, ext, small, small_land, tok_vm, cot_vm, sems, local,
 ):
     step = pl.program_id(0)
     channels, half = gv_vm.shape[1], n_own.shape[1]
@@ -1410,7 +1410,17 @@
     t_move = one(gt_hbm, gt_sib, sibling)
     s_move = one(gs_vm, gs_sib, sibling)
     z_move = one(z_send, z_land, mirror)
-    state_moves = to_cols(state_send, state_land.at[col])
+    state_moves = to_cols(tot.at[:, pl.ds(channels, span)], state_land.at[col])
+
+    def state_each(sending, act):
+        for by, move in enumerate(state_moves(), 1):
+            if whole_state:
+                act(move)
+            else:
+                there = col ^ by
+                needed = lax.div(there, 2) == place if sending else lax.rem(there, group) == lax.div(col, 2)
+                pl.when(needed)(partial(act, move))
+
     bc_moves = to_peers(lambda by: gbc.at[:, part_at(place ^ by)], lambda by: bc_land.at[by - 1])
     early_rows, late_rows = pl.ds(0, count // 2), pl.ds(count // 2, count - count // 2)
     gn_early = to_peers(lambda by: gn_parts.at[by - 1, early_rows, :], lambda by: gn_land.at[by - 1, early_rows, :])
@@ -1550,9 +1560,9 @@
             tot[:, cols_a] += rec[i, :, cols_a].astype(F32)
         z_send[:, 0:shard] = tot[:, shard:channels].astype(BF)
         z_send[:, shard:] = tot[:, channels + span :].astype(BF)
-        state_send[...] = tot[:, channels : channels + span].astype(BF)
-        start(z_move() + state_moves())
-        state_land[col] = state_send[...]
+        start(z_move())
+        state_each(True, lambda move: move.start())
+        state_land[col] = tot[:, channels : channels + span]
 
     @pl.when((step >= input_at) & (step < last))
     def _():
@@ -1588,12 +1598,12 @@
         start(v_moves())
         store_v.start()
         steps = tot[:, channels + span :] + pltpu.roll(z_land[:, shard:].astype(F32), 128 - heads, 1)
-        arrive(state_moves())
+        state_each(False, lambda move: move.wait_recv())
         if whole_state:
             ext[:, 0:128] = steps
-            ext[:, 128:] = sum(state_land[i].astype(F32) for i in range(cols))
+            ext[:, 128:] = sum(state_land[i] for i in range(cols))
         else:
-            states = state_land[col // 2].astype(F32) + state_land[col // 2 + group].astype(F32)
+            states = state_land[lax.div(col, 2)] + state_land[lax.div(col, 2) + group]
             moved = jnp.where(lax.rem(col, 2) == 1, states, pltpu.roll(states, 64, 1))
             ext[...] = jnp.where(iota2(steps.shape, 1) < 64, steps, moved)
         start(e_moves())
@@ -1638,7 +1648,8 @@
         sent(o_passed() + g_passed() + v_passed() + e_passed())
         sent(bc_moves() + o_moves() + t_move() + n_move() + g_move() + s_move() + a_moves() + b_moves())
         sent([v_tile(tile) for tile in range(tiles)])
-        sent(gn_moves() + z_move() + state_moves() + g_moves() + v_moves() + e_moves() + small_cols())
+        state_each(True, lambda move: move.wait_send())
+        sent(gn_moves() + z_move() + g_moves() + v_moves() + e_moves() + small_cols())
         store_tg.wait()
 
 
@@ -1711,8 +1722,8 @@
             vmem((count, width), F32), vmem((more, count, width), BF), vmem((more, count, width), BF),
             vmem((HALO, width), BF), vmem((group, HALO, width), BF),
             vmem((dps, piece, wide), BF), vmem((dps - 1, piece, wide), BF), vmem((piece, wide), F32),
-            vmem((piece, shard + 128), BF), vmem((piece, shard + 128), BF), vmem((piece, span), BF),
-            vmem((cols, piece, span), BF), vmem((piece, extra), F32),
+            vmem((piece, shard + 128), BF), vmem((piece, shard + 128), BF),
+            vmem((cols, piece, span), F32), vmem((piece, extra), F32),
             vmem((SMALL_ROWS, width), F32), vmem((small_steps, SMALL_ROWS, width), F32),
             vmem((count, width), BF), vmem((count, width), BF),
             dma((2, copies)),
@@ -1725,6 +1736,33 @@
         ga, raw, taps, gg, gt, w_value, w_gate, picked, tokens_in, inv_rms, g_own, mix_sums, head_sums, gain,
         o_total, g_cross, gbc, normed, gt, tokens_own, cotangent,
     )
+
+
+def collect_kernel(tok_ref, branch_ref, in_ref, *refs):
+    half = (len(refs) - 1) // 2
+    refs[half][...] = (
+        tok_ref[...].astype(F32) + branch_ref[...] + jnp.sum(in_ref[...].astype(F32), axis=0)
+    ).astype(BF)
+    for source, target in zip(refs[:half], refs[half + 1 :]):
+        target[...] = source[...]
+
+
+def collect(tokens, branch, branch_in, results):
+    steps = 4
+    slab = lambda v: pl.BlockSpec((v.shape[0] // steps, v.shape[1]), lambda i: (i, 0))
+    more, count, width = branch_in.shape
+    return pl.pallas_call(
+        collect_kernel,
+        grid=(steps,),
+        in_specs=[
+            slab(tokens), slab(branch), pl.BlockSpec((more, count // steps, width), lambda i: (0, i, 0)),
+        ] + [slab(v) for v in results],
+        out_specs=[slab(tokens)] + [slab(v) for v in results],
+        out_shape=[sds(tokens.shape, BF)] + [sds(v.shape) for v in results],
+        compiler_params=params(),
+        cost_estimate=cost(8),
+        name="collect",
+    )(tokens, branch, branch_in, *results)
 
 
 def flips(size, by):
@@ -1852,13 +1890,15 @@
         cols, dps, dy, act, y, step, cum, step_in, spread, gather, after, states, early, offs, head_rows, vectors,
         mixed, out_full, grad_gate, first_grad, group_cot, normed,
     )
-    block_out = (tokens.astype(F32) + branch + jnp.sum(branch_in.astype(F32), axis=0)).astype(BF)
     state_part = state_all // group
 
     tokens_grad, sum_out, sum_gate, sum_value, extra, small_sums = finish(
         cols, dps, heads, state_part, ga, raw, taps, grad_gate, grad_step, value_full, gate_full, picked,
         group_tokens, inv_rms, gate_own, mix_sums, head_sums, gain[None], out_total, gate_cross, gbc, normed,
         tokens, cotangent,
+    )
+    block_out, tokens_grad, sum_out, sum_gate, sum_value = collect(
+        tokens, branch, branch_in, [tokens_grad, sum_out, sum_gate, sum_value]
     )
     sum_step = extra[:, :heads]
     whole_state = state_part % 128 != 0

time: 411 us -> 402 us (0.978)
  local copies, waits for them, and re-layouts: 23.5 us -> 12.1 us
  Pallas kernels: 370 us -> 376 us
    unnamed x22 -> x8, local copies, waits for them, and re-layouts: 13.8 us -> 3.59 us
    pallas_call x0 -> x1, Pallas kernels: none -> 9.76 us  [collect(): pl.pallas_call(collect_kernel, grid=(steps,), in_specs=[slab(tokens), sla...]
where the time goes in v7:
time: 402 us; the launch traced here: 399 us
  Pallas kernels  376 us (94%)
  local copies, waits for them, and re-layouts  12.1 us (3%)
  other arithmetic  9.83 us (2%)
    pallas_call x1, Pallas kernels, finish(): pl.pallas_call(partial(finish_kernel, cols, dps, heads, part, whole_state...  126 us
    pallas_call x1, Pallas kernels, scan_backward(): pl.pallas_call(partial(backward_kernel, cols, dps), grid=(far_at + blocks...  80.1 us
    pallas_call x1, Pallas kernels, forward_all(): pl.pallas_call(partial(forward_all_kernel, cols, dps), grid=(gate_at + 2...  74.6 us
    pallas_call x1, Pallas kernels, import_all(): pl.pallas_call(partial(import_kernel, cols, dps), in_specs=[any_spec] * 4...  51.6 us
    pallas_call x1, Pallas kernels, gate_and_mix(): pl.pallas_call(partial(gate_kernel, cols, inner_channels), grid=(2 * tile...  34.5 us
    pallas_call x1, Pallas kernels, collect(): pl.pallas_call(collect_kernel, grid=(steps,), in_specs=[slab(tokens), sla...  9.76 us

profile of v7, /device:TPU:0, one launch (start us, length us, event | category | flops | bytes accessed | tf_op | source)
XLA Modules:
  0.0 399.1 jit_solution(7032747183384334287)
XLA Ops:
  0.6 0.0 copy-start.1
  0.7 1.1 copy.34
  1.7 0.9 copy.35
  2.6 0.8 fusion.14.sw
  3.5 0.7 fusion.24
  4.2 0.8 fusion.33
  4.9 0.7 broadcast_in_dim.27
  5.6 0.7 broadcast_in_dim.28
  6.3 1.9 concatenate.42.vec
  8.2 51.6 %import_all.1 = (bf16[1040,1536]{1,0:T(8,128)(2,1)}, bf16[1536,1536]{1,0:T(8,128)(2,1)}, bf16[1536,512]{1,0:T(8,128)(2,1)}, bf16[4,16,768]{2,1,0:T(8,128)(2,1)}) custom-call(bf16[512,1536]{1,0:T(8,128)(2,1)} %tok_ref.1, bf16[768,768]{1,0:T(8,128)(2,1)} %wv.1, bf16[768,128]{1,0:T(8,128)(2,1)} %fusion.14.sw, bf16[16,768]{1,0:T(8,128)(2,1)} %concatenate.42.vec), custom_call_target="tpu_custom_call" | custom-call | bytes 135000000 | tf_op jit(solution)/shard_map/import_all/pallas_call | solution.py:278
  59.8 0.9 convert_element_type.16
  60.7 0.1 slice_bitcast_fusion.9
  60.8 0.1 maximum_bitcast_fusion
  60.9 0.1 fusion.40
  61.0 0.6 select_maximum_fusion.1.head_ref
  61.6 0.1 pad_maximum_fusion.1
  61.7 0.1 broadcast_in_dim.34
  61.7 0.1 broadcast_in_dim_reshape.3
  61.8 0.1 pad.24.clone
  61.9 0.7 fusion.17
  62.6 0.1 reshape.66
  62.7 0.6 pad_maximum_fusion.taps_ref
  63.4 1.6 fusion.3.pick_ref
  65.0 0.0 copy-done.1
  65.0 0.6 reshape.67.gain_ref
  65.6 74.6 %forward_all.1 = (f32[1040,1792]{1,0:T(8,128)}, bf16[1024,1792]{1,0:T(8,128)(2,1)}, bf16[1040,1536]{1,0:T(8,128)(2,1)}, f32[1024,128]{1,0:T(8,128)}, f32[1024,12...) custom-call(bf16[1040,1536]{1,0:T(8,128)(2,1)} %get-tuple-element.65, ...), custom_call_target="tpu_custom_call" | custom-call | bytes 210000000 | tf_op jit(solution)/shard_map/forward_all/pallas_call | solution.py:671
  140.2 34.5 %gate_and_mix.1 = (f32[1024,1536]{1,0:T(8,128)}, bf16[1024,1536]{1,0:T(8,128)(2,1)}, bf16[1024,1536]{1,0:T(8,128)(2,1)}, f32[1024,1536]{1,0:T(8,128)}, f32[8,153...) custom-call(f32[1024,1536]{1,0:T(8,128)} %get-tuple-element.69.y0_ref, ...), custom_call_target="tpu_custom_call" | custom-call | bytes 120000000 | tf_op jit(solution)/shard_map/gate_and_mix/pallas_call | solution.py:1275
  174.7 80.1 %scan_backward.1 = (f32[1024,1536]{1,0:T(8,128)}, bf16[1024,128]{1,0:T(8,128)(2,1)}, f32[1024,256]{1,0:T(8,128)}, f32[8,128]{1,0:T(8,128)}, f32[192,768]{1,0:T(8...) custom-call(f32[1024,1536]{1,0:T(8,128)} %get-tuple-element.76.dy_re, ...), custom_call_target="tpu_custom_call" | custom-call | bytes 240000000 | tf_op jit(solution)/shard_map/scan_backward/pallas_call | solution.py:1094
  254.9 125.6 %finish.1 = (f32[512,1536]{1,0:T(8,128)}, f32[768,768]{1,0:T(8,128)}, f32[768,768]{1,0:T(8,128)}, f32[768,768]{1,0:T(8,128)}, f32[768,128]{1,0:T(8,128)}, /*index=5*/f32[4,16,1536]{2,1,0:T(8,128)}) custom-call(f32[1024,1536]{1,0:T(8,128)} %get-tuple-element.91.ga_ref, f32[1040,1792]{1,0:T(8,128)} %get-tuple-element.92.raw_ref, ...), custom_call_target="tpu_custom_call" | custom-call | bytes 330000000 | tf_op jit(solution)/shard_map/finish/pallas_call | solution.py:1690
  380.5 1.1 dynamic-slice_bitcast_fusion.1
  381.5 0.1 slice_add_fusion.2
  381.6 0.1 fusion.41
  381.7 0.5 bitcast_multiply_fusion
  382.2 0.5 slice_bitcast_fusion.7
  382.7 0.1 constant_dynamic-slice_fusion
  382.8 0.6 slice_bitcast_fusion.2
  383.4 0.5 slice_bitcast_fusion.8
  383.9 0.6 slice_reduce_fusion
  384.5 0.1 reshape_squeeze.3
  384.6 0.6 reduce_sum.9
  385.2 0.6 slice_bitcast_fusion.1
  385.8 0.0 copy-start
  385.8 9.8 %collect.1 = (bf16[512,1536]{1,0:T(8,128)(2,1)}, f32[512,1536]{1,0:T(8,128)}, f32[768,768]{1,0:T(8,128)}, f32[768,768]{1,0:T(8,128)}, f32[768,768]{1,0:T(8,128)}) custom-call(bf16[512,1536]{1,0:T(8,128)(2,1)} %tok_ref.1, f32[512,1536]{1,0:T(8,128)} %get-tuple-element.89.branch_ref, bf16[1,512,1536]{2,1,0:T(8,128)(2,1)} %get-tuple-element.90.in_ref, ...), custom_call_target="tpu_custom_call" | custom-call | bytes 24000000 | tf_op jit(solution)/shard_map/collect/pallas_call | solution.py:1754
  395.6 0.0 copy-done
  395.6 0.2 slice.103
  395.8 0.8 copy.37
  396.6 0.8 copy.38
  397.4 1.5 add_reduce_fusion
  (15 shorter events, 0.1 us)
Async XLA Ops:
  0.6 64.4 %copy-start.1 = (bf16[1536]{0:T(1024)(128)(2,1)S(1)}, bf16[1536]{0:T(1024)(128)(2,1)}, u32[]{:S(2)}) copy-start(bf16[1536]{0:T(1024)(128)(2,1)} %param.19) | copy-start | bytes 9220
  385.8 9.8 %copy-start = (f32[768,128]{1,0:T(8,128)S(1)}, f32[768,128]{1,0:T(8,128)}, u32[]{:S(2)}) copy-start(f32[768,128]{1,0:T(8,128)} %get-tuple-element.112) | copy-start | bytes 1179652

commit v8 on v7

--- a/solution.py
+++ b/solution.py
@@ -1338,6 +1338,7 @@
 
 SMALL_ROWS = 16
 A_TAKEN = 4
+EARLY_TILES = 3
 
 
 def finish_kernel(
@@ -1422,9 +1423,10 @@
                 pl.when(needed)(partial(act, move))
 
     bc_moves = to_peers(lambda by: gbc.at[:, part_at(place ^ by)], lambda by: bc_land.at[by - 1])
-    early_rows, late_rows = pl.ds(0, count // 2), pl.ds(count // 2, count - count // 2)
-    gn_early = to_peers(lambda by: gn_parts.at[by - 1, early_rows, :], lambda by: gn_land.at[by - 1, early_rows, :])
-    gn_late = to_peers(lambda by: gn_parts.at[by - 1, late_rows, :], lambda by: gn_land.at[by - 1, late_rows, :])
+    early_lanes = pl.ds(0, EARLY_TILES * TILE)
+    late_lanes = pl.ds(EARLY_TILES * TILE, width - EARLY_TILES * TILE)
+    gn_early = to_peers(lambda by: gn_parts.at[by - 1, :, early_lanes], lambda by: gn_land.at[by - 1, :, early_lanes])
+    gn_late = to_peers(lambda by: gn_parts.at[by - 1, :, late_lanes], lambda by: gn_land.at[by - 1, :, late_lanes])
     gn_moves = lambda: gn_early() + gn_late()
     tile_first = take(tiles)
 
@@ -1552,6 +1554,10 @@
         arrive(g_moves())
         start(g_passed())
 
+    @pl.when(step == input_at + EARLY_TILES)
+    def _():
+        start(gn_early())
+
     @pl.when(step == input_at + A_TAKEN)
     def _():
         arrive(a_moves())
@@ -1584,7 +1590,6 @@
 
     @pl.when(step == last)
     def _():
-        start(gn_early())
         for j in range(group):
             pl.when(col == group + j)(halos()[j].start)
         small_move(0).start()

time: 402 us -> 395 us (0.983)
  Pallas kernels: 376 us -> 369 us
    pallas_call x1, Pallas kernels: 126 us -> 119 us  [finish(): pl.pallas_call(partial(finish_kernel, cols, dps, heads, part, whole_state...]
where the time goes in v8:
time: 395 us; the launch traced here: 392 us
  Pallas kernels  369 us (93%)
  local copies, waits for them, and re-layouts  12.1 us (3%)
  other arithmetic  9.83 us (2%)
    pallas_call x1, Pallas kernels, finish(): pl.pallas_call(partial(finish_kernel, cols, dps, heads, part, whole_state...  119 us
    pallas_call x1, Pallas kernels, scan_backward(): pl.pallas_call(partial(backward_kernel, cols, dps), grid=(far_at + blocks...  80.1 us
    pallas_call x1, Pallas kernels, forward_all(): pl.pallas_call(partial(forward_all_kernel, cols, dps), grid=(gate_at + 2...  74.6 us
    pallas_call x1, Pallas kernels, import_all(): pl.pallas_call(partial(import_kernel, cols, dps), in_specs=[any_spec] * 4...  51.6 us
    pallas_call x1, Pallas kernels, gate_and_mix(): pl.pallas_call(partial(gate_kernel, cols, inner_channels), grid=(2 * tile...  34.5 us
    pallas_call x1, Pallas kernels, collect(): pl.pallas_call(collect_kernel, grid=(steps,), in_specs=[slab(tokens), sla...  9.76 us

profile of v8, /device:TPU:0, one launch (start us, length us, event | category | flops | bytes accessed | tf_op | source)
XLA Modules:
  0.0 392.4 jit_solution(150352934188005078)
XLA Ops:
  0.6 0.0 copy-start.1
  0.7 1.1 copy.34
  1.7 0.9 copy.35
  2.6 0.8 fusion.14.sw
  3.5 0.7 fusion.24
  4.2 0.8 fusion.33
  4.9 0.7 broadcast_in_dim.27
  5.6 0.7 broadcast_in_dim.28
  6.3 1.9 concatenate.42.vec
  8.2 51.6 %import_all.1 = (bf16[1040,1536]{1,0:T(8,128)(2,1)}, bf16[1536,1536]{1,0:T(8,128)(2,1)}, bf16[1536,512]{1,0:T(8,128)(2,1)}, bf16[4,16,768]{2,1,0:T(8,128)(2,1)}) custom-call(bf16[512,1536]{1,0:T(8,128)(2,1)} %tok_ref.1, bf16[768,768]{1,0:T(8,128)(2,1)} %wv.1, bf16[768,128]{1,0:T(8,128)(2,1)} %fusion.14.sw, bf16[16,768]{1,0:T(8,128)(2,1)} %concatenate.42.vec), custom_call_target="tpu_custom_call" | custom-call | bytes 135000000 | tf_op jit(solution)/shard_map/import_all/pallas_call | solution.py:278
  59.8 0.9 convert_element_type.16
  60.7 0.1 slice_bitcast_fusion.9
  60.8 0.1 maximum_bitcast_fusion
  60.9 0.1 fusion.40
  61.0 0.6 select_maximum_fusion.1.head_ref
  61.6 0.1 pad_maximum_fusion.1
  61.7 0.1 broadcast_in_dim.34
  61.7 0.1 broadcast_in_dim_reshape.3
  61.8 0.1 pad.24.clone
  61.9 0.7 fusion.17
  62.6 0.1 reshape.66
  62.7 0.6 pad_maximum_fusion.taps_ref
  63.4 1.6 fusion.3.pick_ref
  65.0 0.0 copy-done.1
  65.0 0.6 reshape.67.gain_ref
  65.6 74.6 %forward_all.1 = (f32[1040,1792]{1,0:T(8,128)}, bf16[1024,1792]{1,0:T(8,128)(2,1)}, bf16[1040,1536]{1,0:T(8,128)(2,1)}, f32[1024,128]{1,0:T(8,128)}, f32[1024,12...) custom-call(bf16[1040,1536]{1,0:T(8,128)(2,1)} %get-tuple-element.65, ...), custom_call_target="tpu_custom_call" | custom-call | bytes 210000000 | tf_op jit(solution)/shard_map/forward_all/pallas_call | solution.py:671
  140.2 34.5 %gate_and_mix.1 = (f32[1024,1536]{1,0:T(8,128)}, bf16[1024,1536]{1,0:T(8,128)(2,1)}, bf16[1024,1536]{1,0:T(8,128)(2,1)}, f32[1024,1536]{1,0:T(8,128)}, f32[8,153...) custom-call(f32[1024,1536]{1,0:T(8,128)} %get-tuple-element.69.y0_ref, ...), custom_call_target="tpu_custom_call" | custom-call | bytes 120000000 | tf_op jit(solution)/shard_map/gate_and_mix/pallas_call | solution.py:1275
  174.7 80.1 %scan_backward.1 = (f32[1024,1536]{1,0:T(8,128)}, bf16[1024,128]{1,0:T(8,128)(2,1)}, f32[1024,256]{1,0:T(8,128)}, f32[8,128]{1,0:T(8,128)}, f32[192,768]{1,0:T(8...) custom-call(f32[1024,1536]{1,0:T(8,128)} %get-tuple-element.76.dy_re, ...), custom_call_target="tpu_custom_call" | custom-call | bytes 240000000 | tf_op jit(solution)/shard_map/scan_backward/pallas_call | solution.py:1094
  254.9 118.9 %finish.1 = (f32[512,1536]{1,0:T(8,128)}, f32[768,768]{1,0:T(8,128)}, f32[768,768]{1,0:T(8,128)}, f32[768,768]{1,0:T(8,128)}, f32[768,128]{1,0:T(8,128)}, /*index=5*/f32[4,16,1536]{2,1,0:T(8,128)}) custom-call(f32[1024,1536]{1,0:T(8,128)} %get-tuple-element.91.ga_ref, f32[1040,1792]{1,0:T(8,128)} %get-tuple-element.92.raw_ref, ...), custom_call_target="tpu_custom_call" | custom-call | bytes 330000000 | tf_op jit(solution)/shard_map/finish/pallas_call | solution.py:1695
  373.8 1.1 dynamic-slice_bitcast_fusion.1
  374.9 0.1 slice_add_fusion.2
  375.0 0.1 fusion.41
  375.0 0.5 bitcast_multiply_fusion
  375.6 0.5 slice_bitcast_fusion.7
  376.1 0.1 constant_dynamic-slice_fusion
  376.2 0.6 slice_bitcast_fusion.2
  376.7 0.5 slice_bitcast_fusion.8
  377.3 0.6 slice_reduce_fusion
  377.9 0.1 reshape_squeeze.3
  378.0 0.6 reduce_sum.9
  378.6 0.6 slice_bitcast_fusion.1
  379.2 0.0 copy-start
  379.2 9.8 %collect.1 = (bf16[512,1536]{1,0:T(8,128)(2,1)}, f32[512,1536]{1,0:T(8,128)}, f32[768,768]{1,0:T(8,128)}, f32[768,768]{1,0:T(8,128)}, f32[768,768]{1,0:T(8,128)}) custom-call(bf16[512,1536]{1,0:T(8,128)(2,1)} %tok_ref.1, f32[512,1536]{1,0:T(8,128)} %get-tuple-element.89.branch_ref, bf16[1,512,1536]{2,1,0:T(8,128)(2,1)} %get-tuple-element.90.in_ref, ...), custom_call_target="tpu_custom_call" | custom-call | bytes 24000000 | tf_op jit(solution)/shard_map/collect/pallas_call | solution.py:1759
  388.9 0.0 copy-done
  389.0 0.2 slice.103
  389.1 0.8 copy.37
  390.0 0.8 copy.38
  390.7 1.5 add_reduce_fusion
  (15 shorter events, 0.1 us)
Async XLA Ops:
  0.6 64.4 %copy-start.1 = (bf16[1536]{0:T(1024)(128)(2,1)S(1)}, bf16[1536]{0:T(1024)(128)(2,1)}, u32[]{:S(2)}) copy-start(bf16[1536]{0:T(1024)(128)(2,1)} %param.19) | copy-start | bytes 9220
  379.2 9.8 %copy-start = (f32[768,128]{1,0:T(8,128)S(1)}, f32[768,128]{1,0:T(8,128)}, u32[]{:S(2)}) copy-start(f32[768,128]{1,0:T(8,128)} %get-tuple-element.112) | copy-start | bytes 1179652
